TPU v7x, 32 devices: a whole 2x2x4 slice. The times are simulated.
32 devices in a mesh: dp: 4 (over y, x), expert: 8 (over z, core).
Axes of the slice: x: 2, y: 2, z: 4, core: 2. Of those that a mesh axis runs over, the one named last changes fastest.
Arguments:
- tokens: bfloat16 [512, 4096], P(('dp', 'expert')), may hold values from -6 to 6
- cotangent: bfloat16 [512, 4096], P(('dp', 'expert')), may hold values from -6 to 6
- gate_prob: float32 [512, 8], P(('dp', 'expert')), may hold values from 0.05 to 0.6
- expert_ids: int32 [512, 8], P(('dp', 'expert')), may hold values from 0 to 63, all different within a row; in each aligned block of 16 rows (0 to 15, 16 to 31, ...) at most 3 rows name the same one
- placement: int32 [64], replicated, may hold values from 0 to 63, each once
- gate_weight: bfloat16 [64, 768, 4096], P('expert', 'dp'), may hold values from -0.09375 to 0.09375
- up_weight: bfloat16 [64, 768, 4096], P('expert', 'dp'), may hold values from -0.09375 to 0.09375
- down_weight: bfloat16 [64, 768, 4096], P('expert', 'dp'), may hold values from -0.21875 to 0.21875
Outputs:
- mixed: bfloat16 [512, 4096], P(('dp', 'expert'))
- token_grad: bfloat16 [512, 4096], P(('dp', 'expert'))
- gate_grad: float32 [512, 8], P(('dp', 'expert'))
- gate_weight_grad: bfloat16 [64, 768, 4096], P('expert', 'dp')
- up_weight_grad: bfloat16 [64, 768, 4096], P('expert', 'dp')
- down_weight_grad: bfloat16 [64, 768, 4096], P('expert', 'dp')
Inputs may be any that keep to these rules, and one draw needn't show every extreme that they name: `expert_ids`: in each row the 8 experts differ. In each aligned block of 16 tokens (the tokens of one device) no expert is named by more than 3 tokens, and in some blocks one is named by exactly 3. `placement`: A permutation: each slot serves exactly one expert, and no expert is replicated.
All inputs are finite; a program needn't handle non-finite values.
Results may differ from a plain program's by a relative error of at most 0.015.
Values may be sent and summed in bfloat16 or wider, within the bound.
No kernel may reach another device: no remote copies, remote signals or barrier semaphores. Data moves between devices by JAX's collectives and lax.ppermute only.
A program may use at most 192 MiB of HBM per device.

v0:
```python
import jax
import jax.numpy as jnp
from jax import lax
from jax.sharding import PartitionSpec as P

CAP = 3


def gated(values):
    sigmoid_v = jax.nn.sigmoid(values)
    return (values * sigmoid_v, sigmoid_v * (1.0 + values * (1.0 - sigmoid_v)))


def body(tokens, cotangent, gate_prob, expert_ids, placement, gate_weight, up_weight, down_weight):
    tok_count, model_width = tokens.shape
    top_count = expert_ids.shape[1]
    expert_devs = lax.axis_size("expert")
    local_experts = gate_weight.shape[0]
    total_experts = placement.shape[0]
    capacity = CAP
    flat_ids = expert_ids.reshape(-1)
    matches_id = flat_ids[:, None] == jnp.arange(total_experts, dtype=jnp.int32)[None, :]
    slot_ids = jnp.sum(jnp.where(matches_id, placement[None, :], 0), axis=1)
    pair_order = jnp.arange(flat_ids.shape[0], dtype=jnp.int32)
    earlier = (slot_ids[:, None] == slot_ids[None, :]) & (pair_order[None, :] < pair_order[:, None])
    position = slot_ids * capacity + jnp.sum(earlier.astype(jnp.int32), axis=1)
    matches = jnp.arange(total_experts * capacity, dtype=jnp.int32)[:, None] == position[None, :]
    matches = matches.reshape(total_experts * capacity, tok_count, top_count)
    dispatch = jnp.any(matches, axis=2).astype(jnp.bfloat16)
    weight_map = jnp.sum(jnp.where(matches, gate_prob[None, :, :], 0.0), axis=2)
    sent_rows = jnp.dot(dispatch, tokens, preferred_element_type=jnp.float32).astype(jnp.bfloat16)
    sent_grads = jnp.dot(
        weight_map, cotangent.astype(jnp.float32), precision=lax.Precision.HIGHEST
    ).astype(jnp.bfloat16)
    block_shape = (1, expert_devs, local_experts, capacity, model_width)
    sent_rows = sent_rows.reshape(block_shape)
    sent_grads = sent_grads.reshape(block_shape)
    got_rows, got_grads = (
        lax.all_to_all(sent_rows, "expert", split_axis=1, concat_axis=1, tiled=True),
        lax.all_to_all(sent_grads, "expert", split_axis=1, concat_axis=1, tiled=True),
    )
    routed, routed_grads = (
        lax.all_gather(got_rows, "dp", axis=0, tiled=True),
        lax.all_gather(got_grads, "dp", axis=0, tiled=True),
    )
    gate_pre = jnp.einsum(
        "asjcd,jfd->asjcf", routed, gate_weight, preferred_element_type=jnp.float32
    )
    up_pre = jnp.einsum("asjcd,jfd->asjcf", routed, up_weight, preferred_element_type=jnp.float32)
    silu_v, slope = gated(gate_pre)
    hidden = (silu_v * up_pre).astype(jnp.bfloat16)
    out_part = jnp.einsum(
        "asjcf,jfd->asjcd", hidden, down_weight, preferred_element_type=jnp.float32
    )
    d_hidden = jnp.einsum(
        "asjcd,jfd->asjcf", routed_grads, down_weight, preferred_element_type=jnp.float32
    )
    d_gate_pre = (d_hidden * up_pre * slope).astype(jnp.bfloat16)
    d_up_pre = (d_hidden * silu_v).astype(jnp.bfloat16)
    back_part = jnp.einsum(
        "asjcf,jfd->asjcd", d_gate_pre, gate_weight, preferred_element_type=jnp.float32
    )
    back_part = back_part + jnp.einsum(
        "asjcf,jfd->asjcd", d_up_pre, up_weight, preferred_element_type=jnp.float32
    )
    down_grad = jnp.einsum(
        "asjcf,asjcd->jfd", hidden, routed_grads, preferred_element_type=jnp.float32
    ).astype(jnp.bfloat16)
    gate_grad_w = jnp.einsum(
        "asjcf,asjcd->jfd", d_gate_pre, routed, preferred_element_type=jnp.float32
    ).astype(jnp.bfloat16)
    up_grad_w = jnp.einsum(
        "asjcf,asjcd->jfd", d_up_pre, routed, preferred_element_type=jnp.float32
    ).astype(jnp.bfloat16)
    summed = (
        lax.psum_scatter(
            out_part.astype(jnp.bfloat16), "dp", scatter_dimension=0, tiled=True
        ).astype(jnp.float32),
        lax.psum_scatter(
            back_part.astype(jnp.bfloat16), "dp", scatter_dimension=0, tiled=True
        ).astype(jnp.float32),
    )
    back_out, back_grad = (
        lax.all_to_all(
            summed[0].astype(jnp.bfloat16), "expert", split_axis=1, concat_axis=1, tiled=True
        ),
        lax.all_to_all(
            summed[1].astype(jnp.bfloat16), "expert", split_axis=1, concat_axis=1, tiled=True
        ),
    )
    out_flat = back_out.reshape(total_experts * capacity, model_width)
    grad_flat = back_grad.reshape(total_experts * capacity, model_width)
    chosen_out = out_flat[position].reshape(tok_count, top_count, model_width)
    chosen_grad = grad_flat[position].reshape(tok_count, top_count, model_width)
    mixed = jnp.einsum(
        "tk,tkd->td", gate_prob, chosen_out.astype(jnp.float32), precision=lax.Precision.HIGHEST
    ).astype(jnp.bfloat16)
    gate_grad = jnp.einsum("td,tkd->tk", cotangent, chosen_out, preferred_element_type=jnp.float32)
    token_grad = jnp.sum(chosen_grad.astype(jnp.float32), axis=1).astype(jnp.bfloat16)
    return (mixed, token_grad, gate_grad, gate_grad_w, up_grad_w, down_grad)


def solution(mesh):
    return jax.shard_map(
        body,
        mesh=mesh,
        in_specs=(
            P(("dp", "expert"), None),
            P(("dp", "expert"), None),
            P(("dp", "expert"), None),
            P(("dp", "expert"), None),
            P(),
            P("expert", "dp", None),
            P("expert", "dp", None),
            P("expert", "dp", None),
        ),
        out_specs=(
            P(("dp", "expert"), None),
            P(("dp", "expert"), None),
            P(("dp", "expert"), None),
            P("expert", "dp", None),
            P("expert", "dp", None),
            P("expert", "dp", None),
        ),
        check_vma=False,
    )
```

profile of v0, /device:TPU:0, one launch (start us, length us, event | category | flops | bytes accessed | tf_op | source)
XLA Modules:
  0.0 596.2 jit_solution(17503490921534955510)
XLA Ops:
  9.3 2.7 convolution_convert_fusion.1
  11.9 2.7 reshape.81
  15.9 44.0 %all_to_all.20 = bf16[1,8,8,3,4096]{4,2,3,0,1:T(8,128)(2,1)S(1)} all-to-all(bf16[1,8,8,3,4096]{4,2,3,0,1:T(8,128)(2,1)S(1)} %copy.55), channel_id=1, replica_groups=mesh['dp'=4,'expert'=8] {'expert'}, dimensions={1} | all-to-all | bytes 3145728 | tf_op jit(solution)/shard_map/all_to_all | solution.py:39
  62.1 2.6 convolution_convert_fusion
  64.7 2.7 reshape.84
  68.6 40.3 %all_to_all.21 = bf16[1,8,8,3,4096]{4,2,3,0,1:T(8,128)(2,1)S(1)} all-to-all(bf16[1,8,8,3,4096]{4,2,3,0,1:T(8,128)(2,1)S(1)} %copy.60), channel_id=1, replica_groups=mesh['dp'=4,'expert'=8] {'expert'}, dimensions={1} | all-to-all | bytes 3145728 | tf_op jit(solution)/shard_map/all_to_all | solution.py:40
  111.2 19.9 %all-gather.3.cloned.1.call-done = bf16[4,8,8,3,4096]{4,1,3,0,2:T(8,128)(2,1)} async-done(((bf16[1,8,8,3,4096]{4,1,3,0,2:T(8,128)(2,1)}), bf16[4,8,8,3,4096]{4,1,3,0,2:T(8,128)(2,1)}) %all-gather.3.cloned.1.call-update) | async-done | bytes 6291472 | tf_op jit(solution)/shard_map/all_gather | solution.py:43
  131.1 8.6 %fusion.32 = f32[4,8,8,3,192]{4,1,3,0,2:T(8,128)S(1)} fusion(bf16[4,8,8,3,4096]{4,1,3,0,2:T(8,128)(2,1)} %all-gather.3.cloned.1.call-done, bf16[8,192,4096]{2,1,0:T(8,128)(2,1)} %param.14), kind=kOutput, calls=%fused_computation.28 | convolution fusion | flops 1207959552 | bytes 19464192 | tf_op jit(solution)/shard_map/asjcd,jfd->asjcf/dot_general | solution.py:49
  139.7 64.0 %all-gather.5.cloned.1.call-done = bf16[4,8,8,3,4096]{4,1,3,0,2:T(8,128)(2,1)} async-done(((bf16[1,8,8,3,4096]{4,1,3,0,2:T(8,128)(2,1)}), bf16[4,8,8,3,4096]{4,1,3,0,2:T(8,128)(2,1)}) %all-gather.5.cloned.1.call-update) | async-done | bytes 6291472 | tf_op jit(solution)/shard_map/all_gather | solution.py:44
  203.7 8.7 %fusion.26 = f32[4,8,8,3,192]{4,1,3,0,2:T(8,128)S(1)} fusion(bf16[4,8,8,3,4096]{4,1,3,0,2:T(8,128)(2,1)} %all-gather.5.cloned.1.call-done, bf16[8,192,4096]{2,1,0:T(8,128)(2,1)} %param.15), kind=kOutput, calls=%fused_computation.26 | convolution fusion | flops 1207959552 | bytes 19464192 | tf_op jit(solution)/shard_map/asjcd,jfd->asjcf/dot_general | solution.py:55
  212.4 10.3 %multiply_convert_fusion.1 = (bf16[4,8,8,3,192]{4,1,3,0,2:T(8,128)(2,1)}, bf16[4,8,8,3,192]{4,1,3,0,2:T(8,128)(2,1)}, bf16[4,8,8,3,192]{4,1,3,0,2:T(8,128)(2,1)}) fusion(f32[4,8,8,3,192]{4,1,3,0,2:T(8,128)S(1)} %fusion.26, f32[4,8,8,3,192]{4,1,3,0,2:T(8,128)S(1)} %fusion.32, bf16[4,8,8,3,4096]{4,1,3,0,2:T(8,128)(2,1)} %all-gather.3.cloned.1.call-done, ...), kind=kOutput, calls=%fused_computation.35 | convolution fusion | flops 1210171392 | bytes 20938752 | tf_op jit(solution)/shard_map/asjcd,jfd->asjcf/dot_general | solution.py:46
  222.8 7.6 %fusion = f32[8,4,8,3,4096]{4,2,3,1,0:T(8,128)} fusion(bf16[4,8,8,3,192]{4,1,3,0,2:T(8,128)(2,1)} %get-tuple-element.11, bf16[8,192,4096]{2,1,0:T(8,128)(2,1)S(1)} %bitcast.98), kind=kOutput, calls=%fused_computation.5 | convolution fusion | flops 1207959552 | bytes 25460736 | tf_op jit(solution)/shard_map/asjcf,jfd->asjcd/dot_general | solution.py:63
  230.4 9.1 %fusion.18 = bf16[4,8,8,3,4096]{4,1,3,0,2:T(8,128)(2,1)} fusion(bf16[4,8,8,3,192]{4,1,3,0,2:T(8,128)(2,1)S(1)} %copy-done.2, bf16[8,192,4096]{2,1,0:T(8,128)(2,1)} %param.15), kind=kOutput, calls=%fused_computation.20 | convolution fusion | flops 1211105280 | bytes 19169280 | tf_op jit(solution)/shard_map/asjcf,jfd->asjcd/dot_general | solution.py:52
  239.6 12.7 %fusion.21 = bf16[4,8,8,3,4096]{4,1,3,0,2:T(8,128)(2,1)} fusion(f32[8,4,8,3,4096]{4,2,3,1,0:T(8,128)} %fusion, bf16[4,8,8,3,192]{4,1,3,0,2:T(8,128)(2,1)S(1)} %copy-done.1, bf16[8,192,4096]{2,1,0:T(8,128)(2,1)} %param.13), kind=kOutput, calls=%fused_computation.21 | convolution fusion | flops 1214251008 | bytes 31752192 | tf_op jit(solution)/shard_map/asjcf,jfd->asjcd/dot_general | solution.py:60
  253.5 11.0 %bitcast_convert_fusion.1 = bf16[8,192,4096]{2,1,0:T(8,128)(2,1)} fusion(bf16[4,8,8,3,4096]{4,1,3,0,2:T(8,128)(2,1)} %all-gather.3.cloned.1.call-done, bf16[4,8,8,3,192]{4,1,3,0,2:T(8,128)(2,1)S(1)} %copy-done.3), kind=kOutput, calls=%fused_computation.3 | convolution fusion | flops 1214251008 | bytes 19169280 | tf_op jit(solution)/shard_map/asjcf,asjcd->jfd/dot_general | solution.py:72
  264.5 228.2 %all-reduce.5.cloned.1.call-done = (bf16[4,8,8,3,4096]{4,1,3,0,2:T(8,128)(2,1)}, bf16[4,8,8,3,4096]{4,1,3,0,2:T(8,128)(2,1)}) async-done(((bf16[4,8,8,3,4096]{4,1,3,0,2:T(8,128)(2,1)}, bf16[4,8,8,3,4096]{4,1,3,0,2:T(8,128)(2,1)}), (bf16[4,8,8,3,4096]{4,1,3,0,2:T(8,128)(2,1)}, bf16[4,8,8,3,4096]{4,1,3,0,2:T(8,128)(2,1)})) %all-reduce.5.cloned.1.call-update) | async-done | bytes 12582928
  492.7 2.2 constant_dynamic-slice_fusion.1
  494.8 2.0 copy.57
  496.8 4.9 all-to-all-start.1
  501.7 11.0 %bitcast_convert_fusion.2 = bf16[8,192,4096]{2,1,0:T(8,128)(2,1)} fusion(bf16[4,8,8,3,4096]{4,1,3,0,2:T(8,128)(2,1)} %all-gather.3.cloned.1.call-done, bf16[4,8,8,3,192]{4,1,3,0,2:T(8,128)(2,1)S(1)} %copy-done.1), kind=kOutput, calls=%fused_computation.4 | convolution fusion | flops 1214251008 | bytes 19169280 | tf_op jit(solution)/shard_map/asjcf,asjcd->jfd/dot_general | solution.py:69
  512.7 2.2 constant_dynamic-slice_fusion
  514.9 2.0 copy.62
  516.9 22.6 %all-to-all-done.1 = bf16[1,8,8,3,4096]{4,2,3,0,1:T(8,128)(2,1)S(1)} async-done(((bf16[1,8,8,3,4096]{4,2,3,0,1:T(8,128)(2,1)}), bf16[1,8,8,3,4096]{4,2,3,0,1:T(8,128)(2,1)S(1)}, u32[]{:S(2)}, u32[]{:S(2)}) %all-to-all-start.1) | async-done | bytes 1572896 | tf_op jit(solution)/shard_map/all_to_all | solution.py:84
  539.5 3.6 all-to-all-start.3
  543.1 11.2 %bitcast_convert_fusion = bf16[8,192,4096]{2,1,0:T(8,128)(2,1)} fusion(bf16[4,8,8,3,4096]{4,1,3,0,2:T(8,128)(2,1)} %all-gather.5.cloned.1.call-done, bf16[4,8,8,3,192]{4,1,3,0,2:T(8,128)(2,1)} %get-tuple-element.12), kind=kOutput, calls=%fused_computation.2 | convolution fusion | flops 1214251008 | bytes 19169280 | tf_op jit(solution)/shard_map/asjcf,asjcd->jfd/dot_general | solution.py:66
  554.3 2.7 copy.58
  557.0 3.1 reshape.82
  560.1 2.2 gather_fusion
  562.3 2.2 fusion.37
  568.0 12.9 %all-to-all-done.3 = bf16[1,8,8,3,4096]{4,2,3,0,1:T(8,128)(2,1)S(1)} async-done(((bf16[1,8,8,3,4096]{4,2,3,0,1:T(8,128)(2,1)}), bf16[1,8,8,3,4096]{4,2,3,0,1:T(8,128)(2,1)S(1)}, u32[]{:S(2)}, u32[]{:S(2)}) %all-to-all-start.3) | async-done | bytes 1572896 | tf_op jit(solution)/shard_map/all_to_all | solution.py:87
  580.9 2.7 copy.63
  583.6 3.1 reshape.85
  (46 shorter events, 16.2 us)
Async XLA Ops:
  7.2 55.0 %copy-start = (bf16[16,4096]{1,0:T(8,128)(2,1)S(1)}, bf16[16,4096]{1,0:T(8,128)(2,1)}, u32[]{:S(2)}) copy-start(bf16[16,4096]{1,0:T(8,128)(2,1)} %param.9) | copy-start | bytes 393220
  7.2 123.9 %all-gather.3.cloned.1.call-start = ((), (), s32[]{:S(2)}) async-start(), calls=%async_computation.4 | async-start | bytes 7864320 | tf_op jit(solution)/shard_map/all_gather | solution.py:43
  14.7 47.2 %copy-start.4 = (f32[16,8]{0,1:T(8,128)S(1)}, f32[16,8]{0,1:T(8,128)}, u32[]{:S(2)}) copy-start(f32[16,8]{0,1:T(8,128)} %param.10) | copy-start | bytes 1540
  61.9 141.8 %all-gather.5.cloned.1.call-start = ((), (), s32[]{:S(2)}) async-start(), calls=%async_computation.5 | async-start | bytes 7864320 | tf_op jit(solution)/shard_map/all_gather | solution.py:44
  110.9 381.7 %all-reduce.5.cloned.1.call-start = ((), (), s32[]{:S(2)}) async-start(), calls=%async_computation.6 | async-start | bytes 25165824
  203.7 19.1 %slice-start = ((s8[12582912]{0:T(1024)(128)(4,1)}), s8[4194304]{0:T(1024)(128)(4,1)S(1)}, s32[]{:S(2)}) async-start(s8[12582912]{0:T(1024)(128)(4,1)} %bitcast.97), calls=%async_computation.7 | async-start | bytes 8388608
  203.7 19.1 %slice-start.1 = ((s8[12582912]{0:T(1024)(128)(4,1)}), s8[4194304]{0:T(1024)(128)(4,1)S(1)}, s32[]{:S(2)}) async-start(s8[12582912]{0:T(1024)(128)(4,1)} %bitcast.97), calls=%async_computation.8 | async-start | bytes 8388608
  212.4 10.4 %slice-start.2 = ((s8[12582912]{0:T(1024)(128)(4,1)}), s8[4194304]{0:T(1024)(128)(4,1)S(1)}, s32[]{:S(2)}) async-start(s8[12582912]{0:T(1024)(128)(4,1)} %bitcast.97), calls=%async_computation.9 | async-start | bytes 8388608
  222.8 7.6 %copy-start.2 = (bf16[4,8,8,3,192]{4,1,3,0,2:T(8,128)(2,1)S(1)}, bf16[4,8,8,3,192]{4,1,3,0,2:T(8,128)(2,1)}, u32[]{:S(2)}) copy-start(bf16[4,8,8,3,192]{4,1,3,0,2:T(8,128)(2,1)} %get-tuple-element.12) | copy-start | bytes 884740
  230.4 9.1 %copy-start.1 = (bf16[4,8,8,3,192]{4,1,3,0,2:T(8,128)(2,1)S(1)}, bf16[4,8,8,3,192]{4,1,3,0,2:T(8,128)(2,1)}, u32[]{:S(2)}) copy-start(bf16[4,8,8,3,192]{4,1,3,0,2:T(8,128)(2,1)} %get-tuple-element.10) | copy-start | bytes 884740
  252.2 0.7 copy-start.5
  252.2 1.2 copy-start.3
  496.8 42.7 %all-to-all-start.1 = ((bf16[1,8,8,3,4096]{4,2,3,0,1:T(8,128)(2,1)}), bf16[1,8,8,3,4096]{4,2,3,0,1:T(8,128)(2,1)S(1)}, u32[]{:S(2)}, u32[]{:S(2)}) async-start(bf16[1,8,8,3,4096]{4,2,3,0,1:T(8,128)(2,1)} %copy.57), calls=%async_computation.1 | async-start | bytes 3145728 | tf_op jit(solution)/shard_map/all_to_all | solution.py:84
  539.5 41.3 %all-to-all-start.3 = ((bf16[1,8,8,3,4096]{4,2,3,0,1:T(8,128)(2,1)}), bf16[1,8,8,3,4096]{4,2,3,0,1:T(8,128)(2,1)S(1)}, u32[]{:S(2)}, u32[]{:S(2)}) async-start(bf16[1,8,8,3,4096]{4,2,3,0,1:T(8,128)(2,1)} %copy.62), calls=%async_computation.3 | async-start | bytes 3145728 | tf_op jit(solution)/shard_map/all_to_all | solution.py:87
Sparse Core Ops, SparseCore 0:
  62.0 69.0 all-gather.2
  133.5 70.1 all-gather.4
  252.4 240.2 all-reduce.4
where the time goes:
time: 602 us; the launch traced here: 596 us
  waiting for transfers between devices  348 us (58%)
  matrix products  99.7 us (17%)
  blocking collectives  84.2 us (14%)
  local copies, waits for them, and re-layouts  39 us (6%)
  between operations  14.4 us (2%)
  starting transfers between devices  8.76 us (1%)
    unnamed x4, waiting for transfers between devices  228 us
    all_gather x1, waiting for transfers between devices, body(): lax.all_gather(got_grads, 'dp', axis=0, tiled=True)  64 us
    all_to_all x1, blocking collectives, body(): lax.all_to_all(sent_rows, 'expert', split_axis=1, concat_axis=1, tiled=True)  44 us
    all_to_all x1, blocking collectives, body(): lax.all_to_all(sent_grads, 'expert', split_axis=1, concat_axis=1, tiled=T...  40.3 us
    all_to_all x1, waiting for transfers between devices, body(): lax.all_to_all(summed[0].astype(jnp.bfloat16), 'expert', split_axis=1, co...  22.6 us
    all_gather x1, waiting for transfers between devices, body(): lax.all_gather(got_rows, 'dp', axis=0, tiled=True)  19.9 us
    all_to_all x1, waiting for transfers between devices, body(): lax.all_to_all(summed[1].astype(jnp.bfloat16), 'expert', split_axis=1, co...  12.9 us
    dot_general x1, matrix products, body(): jnp.einsum('asjcf,jfd->asjcd', d_gate_pre, gate_weight, preferred_element...  12.7 us
  transfers between devices with their start and end apart: 5, of which 5 were waited for; matrix products, arithmetic and copies ran while one was open for 12% of the time, Pallas kernels for 0%

commit v1 on v0

--- a/solution.py
+++ b/solution.py
@@ -1,9 +1,18 @@
+import functools
+
 import jax
 import jax.numpy as jnp
 from jax import lax
+from jax.experimental import pallas as pl
+from jax.experimental.pallas import tpu as pltpu
 from jax.sharding import PartitionSpec as P
 
 CAP = 3
+AXES = ("dp", "expert")
+CORE, Z1, Z2, Z3, X, Y = 1, 2, 4, 6, 8, 16
+GROUPS = ((0,), (Z1, Z2), (Z3,))
+CHUNK = 512
+MIB = 1 << 20
 
 
 def gated(values):
@@ -11,7 +20,295 @@
     return (values * sigmoid_v, sigmoid_v * (1.0 + values * (1.0 - sigmoid_v)))
 
 
-def body(tokens, cotangent, gate_prob, expert_ids, placement, gate_weight, up_weight, down_weight):
+def swap(values, even, odd=None):
+    odd = even if odd is None else odd
+    count = lax.axis_size("dp") * lax.axis_size("expert")
+    pairs = [(i, i ^ (odd if i & CORE else even)) for i in range(count)]
+    return lax.ppermute(values, AXES, pairs)
+
+
+def gather_rows(block):
+    near, far = swap(block, Z1), swap(block, Z2)
+    last = swap(far, Z1)
+    pieces = []
+    for rows in (block, jnp.concatenate([near, far]), last):
+        rows = jnp.concatenate([rows, swap(rows, X, Y)])
+        pieces += [rows, swap(rows, Y, X)]
+    own = jnp.concatenate(pieces)
+    return own, swap(own, CORE)
+
+
+def arrival():
+    def own(first, second):
+        order = []
+        for group in GROUPS:
+            order += [b ^ a ^ z for b in (0, second) for a in (0, first) for z in group]
+        return order
+
+    even, odd = own(X, Y), own(Y, X)
+    return jnp.array([even + [CORE ^ i for i in odd], odd + [CORE ^ i for i in even]], jnp.int32)
+
+
+def add(a, b):
+    return (a.astype(jnp.float32) + b.astype(jnp.float32)).astype(jnp.bfloat16)
+
+
+def scatter_sum(own, other, tok_count):
+    from_other = swap(other, CORE)
+    ends, at = [], 0
+    for group in GROUPS:
+        ends.append((at, len(group) * tok_count))
+        at += 4 * len(group) * tok_count
+    sums = {}
+    for at, size in reversed(ends):
+        rows = add(own[at : at + 4 * size], from_other[at : at + 4 * size])
+        rows = add(rows[: 2 * size], swap(rows[2 * size :], Y, X))
+        sums[at] = add(rows[:size], swap(rows[size:], X, Y))
+    mine, middle, last = (sums[at] for at, _ in ends)
+    far = add(middle[tok_count:], swap(last, Z1))
+    near = swap(middle[:tok_count], Z1)
+    far = swap(far, Z2)
+    total = mine.astype(jnp.float32) + near.astype(jnp.float32) + far.astype(jnp.float32)
+    return total.astype(jnp.bfloat16)
+
+
+def slots_of(expert_ids, placement):
+    total = placement.shape[0]
+    matches = expert_ids[:, :, None] == jnp.arange(total, dtype=jnp.int32)
+    return jnp.sum(jnp.where(matches, placement, 0), axis=2)
+
+
+NT = (((1,), (1,)), ((), ()))
+NN = (((1,), (0,)), ((), ()))
+
+
+def dot(a, b, dims=NN):
+    return lax.dot_general(a, b, dims, preferred_element_type=jnp.float32)
+
+
+def dispatch(pick_ref, own_ref, other_ref, x_ref):
+    width = own_ref.shape[1]
+    experts, places = x_ref.shape[1], x_ref.shape[2]
+    for half, source in enumerate((own_ref, other_ref)):
+        for at in range(0, width, CHUNK):
+            rows = dot(pick_ref[half], source[:, at : at + CHUNK]).astype(jnp.bfloat16)
+            for e in range(experts):
+                x_ref[half, e, :, at : at + CHUNK] = rows[e * places : (e + 1) * places]
+
+
+def placed(x_ref, e):
+    return jnp.concatenate([x_ref[0, e], x_ref[1, e]], axis=0)
+
+
+def up_kernel(pick_ref, prob_ref, own_ref, other_ref, gate_ref, up_ref, x_ref, g_ref, u_ref, h_ref, ht_ref):
+    e = pl.program_id(0)
+
+    @pl.when(e == 0)
+    def _():
+        dispatch(pick_ref, own_ref, other_ref, x_ref)
+
+    rows = placed(x_ref, e)
+    g = dot(gate_ref[0], rows, NT)
+    u = dot(up_ref[0], rows, NT)
+    g_ref[0] = g
+    u_ref[0] = u
+    silu_v, _ = gated(g)
+    scaled = silu_v * u * prob_ref[0]
+    ht_ref[0] = scaled.astype(jnp.bfloat16)
+    h_ref[0] = scaled.T.astype(jnp.bfloat16)
+
+
+def slope_kernel(pick_ref, prob_ref, own_ref, other_ref, down_ref, g_ref, u_ref,
+                 x_ref, dg_ref, du_ref, dgt_ref, dut_ref, share_ref):
+    e = pl.program_id(0)
+
+    @pl.when(e == 0)
+    def _():
+        dispatch(pick_ref, own_ref, other_ref, x_ref)
+
+    plain = dot(down_ref[0], placed(x_ref, e), NT)
+    g, u = g_ref[0], u_ref[0]
+    silu_v, slope = gated(g)
+    share_ref[0] = jnp.sum(silu_v * u * plain, axis=0, keepdims=True)
+    scaled = plain * prob_ref[0]
+    dg = scaled * u * slope
+    du = scaled * silu_v
+    dgt_ref[0] = dg.astype(jnp.bfloat16)
+    dut_ref[0] = du.astype(jnp.bfloat16)
+    dg_ref[0] = dg.T.astype(jnp.bfloat16)
+    du_ref[0] = du.T.astype(jnp.bfloat16)
+
+
+def back_kernel(terms, put_ref, *refs):
+    lefts, rights = refs[:terms], refs[terms : 2 * terms]
+    own_ref, other_ref, rows_ref = refs[2 * terms :]
+    experts, places = rights[0].shape[0], put_ref.shape[2] // rights[0].shape[0]
+    for e in range(experts):
+        rows = dot(lefts[0][e], rights[0][e])
+        for left, right in zip(lefts[1:], rights[1:]):
+            rows = rows + dot(left[e], right[e])
+        rows = rows.astype(jnp.bfloat16)
+        for half in range(2):
+            rows_ref[half, e * places : (e + 1) * places] = rows[half * places : (half + 1) * places]
+    own_ref[...] = dot(put_ref[0], rows_ref[0]).astype(jnp.bfloat16)
+    other_ref[...] = dot(put_ref[1], rows_ref[1]).astype(jnp.bfloat16)
+
+
+def grad_kernel(x_ref, *refs):
+    count = len(refs) // 2
+    rows = jnp.concatenate([x_ref[0, 0], x_ref[1, 0]], axis=0)
+    for left, out in zip(refs[:count], refs[count:]):
+        for at in range(0, rows.shape[1], CHUNK):
+            out[0, :, at : at + CHUNK] = dot(left[0], rows[:, at : at + CHUNK]).astype(jnp.bfloat16)
+
+
+def whole(shape):
+    return pl.BlockSpec(shape, lambda i: (0,) * len(shape))
+
+
+def each(shape):
+    return pl.BlockSpec((1, *shape[1:]), lambda i: (i,) + (0,) * (len(shape) - 1))
+
+
+def call(kernel, grid, ins, args, outs, shapes, scratch=(), flops=0):
+    moved = sum(a.size * a.dtype.itemsize for a in (*args, *shapes))
+    return pl.pallas_call(
+        kernel,
+        grid=(grid,),
+        in_specs=ins,
+        out_specs=outs,
+        out_shape=shapes,
+        scratch_shapes=scratch,
+        compiler_params=pltpu.CompilerParams(vmem_limit_bytes=48 * MIB),
+        cost_estimate=pl.CostEstimate(flops=flops, bytes_accessed=moved, transcendentals=0),
+    )(*args)
+
+
+def up_call(pick, prob, own, other, w_gate, w_up):
+    experts, hidden, width = w_gate.shape
+    places = pick.shape[1] // experts
+    rows = 2 * places
+    args = (pick, prob, own, other, w_gate, w_up)
+    shapes = [
+        jax.ShapeDtypeStruct((2, experts, places, width), jnp.bfloat16),
+        jax.ShapeDtypeStruct((experts, hidden, rows), jnp.float32),
+        jax.ShapeDtypeStruct((experts, hidden, rows), jnp.float32),
+        jax.ShapeDtypeStruct((experts, rows, hidden), jnp.bfloat16),
+        jax.ShapeDtypeStruct((experts, hidden, rows), jnp.bfloat16),
+    ]
+    ins = [whole(pick.shape), each(prob.shape), whole(own.shape), whole(other.shape)]
+    ins += [each(w_gate.shape), each(w_up.shape)]
+    outs = [whole(shapes[0].shape)] + [each(s.shape) for s in shapes[1:]]
+    flops = 4 * experts * rows * hidden * width + 2 * experts * rows * own.shape[0] * width
+    return call(up_kernel, experts, ins, args, outs, shapes, flops=flops)
+
+
+def slope_call(pick, prob, own, other, w_down, g, u):
+    experts, hidden, width = w_down.shape
+    places = pick.shape[1] // experts
+    rows = 2 * places
+    args = (pick, prob, own, other, w_down, g, u)
+    shapes = [
+        jax.ShapeDtypeStruct((2, experts, places, width), jnp.bfloat16),
+        jax.ShapeDtypeStruct((experts, rows, hidden), jnp.bfloat16),
+        jax.ShapeDtypeStruct((experts, rows, hidden), jnp.bfloat16),
+        jax.ShapeDtypeStruct((experts, hidden, rows), jnp.bfloat16),
+        jax.ShapeDtypeStruct((experts, hidden, rows), jnp.bfloat16),
+        jax.ShapeDtypeStruct((experts, 1, rows), jnp.float32),
+    ]
+    ins = [whole(pick.shape), each(prob.shape), whole(own.shape), whole(other.shape)]
+    ins += [each(w_down.shape), each(g.shape), each(u.shape)]
+    outs = [whole(shapes[0].shape)] + [each(s.shape) for s in shapes[1:]]
+    flops = 2 * experts * rows * hidden * width + 2 * experts * rows * own.shape[0] * width
+    return call(slope_kernel, experts, ins, args, outs, shapes, flops=flops)
+
+
+def back_call(put, lefts, rights):
+    experts, hidden, width = rights[0].shape
+    rows = lefts[0].shape[1]
+    count = put.shape[1]
+    terms = len(lefts)
+    args = (put, *lefts, *rights)
+    shapes = [jax.ShapeDtypeStruct((count, width), jnp.bfloat16)] * 2
+    ins = [whole(put.shape)] + [whole(a.shape) for a in lefts]
+    ins += [pl.BlockSpec((experts, hidden, CHUNK), lambda i: (0, 0, i))] * terms
+    outs = [pl.BlockSpec((count, CHUNK), lambda i: (0, i))] * 2
+    scratch = [pltpu.VMEM((2, put.shape[2], CHUNK), jnp.bfloat16)]
+    flops = 2 * experts * rows * width * (hidden * terms + count)
+    kernel = functools.partial(back_kernel, terms)
+    return call(kernel, width // CHUNK, ins, args, outs, shapes, scratch, flops=flops)
+
+
+def grad_call(x, lefts):
+    _, experts, places, width = x.shape
+    hidden = lefts[0].shape[1]
+    args = (x, *lefts)
+    shapes = [jax.ShapeDtypeStruct((experts, hidden, width), jnp.bfloat16)] * len(lefts)
+    ins = [pl.BlockSpec((2, 1, places, width), lambda i: (0, i, 0, 0))]
+    ins += [each(a.shape) for a in lefts]
+    outs = [each(s.shape) for s in shapes]
+    flops = 4 * experts * places * hidden * width * len(lefts)
+    return call(grad_kernel, experts, ins, args, outs, shapes, flops=flops)
+
+
+def dense_body(
+    tokens, cotangent, gate_prob, expert_ids, placement, gate_weight, up_weight, down_weight
+):
+    tok_count, width = tokens.shape
+    local, hidden_count, _ = gate_weight.shape
+    total_experts = placement.shape[0]
+    me = lax.axis_index(AXES)
+    dp_size, ex_size = lax.axis_size("dp"), lax.axis_size("expert")
+    devices = dp_size * ex_size
+    half = devices * tok_count // 2
+    places = devices // 2 * CAP
+
+    slots = slots_of(expert_ids, placement)
+    used = slots[:, :, None] == jnp.arange(total_experts, dtype=jnp.int32)
+    prob = jnp.sum(jnp.where(used, gate_prob[:, :, None], 0.0), axis=1)
+    prob = jnp.concatenate(gather_rows(prob))
+    prob = lax.dynamic_slice_in_dim(prob, lax.axis_index("expert") * local, local, axis=1)
+
+    prob = prob.reshape(2, devices // 2, tok_count, local).transpose(0, 3, 1, 2)
+    taken = prob > 0.0
+    before = jnp.arange(tok_count)[:, None] < jnp.arange(tok_count)[None, :]
+    rank = dot(taken.astype(jnp.bfloat16), before.astype(jnp.bfloat16), (((3,), (0,)), ((), ())))
+    block = jnp.arange(devices // 2, dtype=jnp.int32)[:, None]
+    place = jnp.where(taken, rank.astype(jnp.int32) + block * CAP, -1).reshape(2, local, 1, half)
+    hit = place == jnp.arange(places, dtype=jnp.int32)[:, None]
+    prob_rows = jnp.sum(jnp.where(hit, prob.reshape(2, local, 1, half), 0.0), axis=3)
+    prob_rows = prob_rows.transpose(1, 0, 2).reshape(local, 1, 2 * places)
+    pick = hit.astype(jnp.bfloat16).reshape(2, local * places, half)
+    put = pick.transpose(0, 2, 1)
+
+    rows_own, rows_other = gather_rows(tokens)
+    grads_own, grads_other = gather_rows(cotangent)
+
+    x, g, u, h, ht = up_call(pick, prob_rows, rows_own, rows_other, gate_weight, up_weight)
+    mixed = scatter_sum(*back_call(put, [h], [down_weight]), tok_count)
+    c, dg, du, dgt, dut, share = slope_call(
+        pick, prob_rows, grads_own, grads_other, down_weight, g, u
+    )
+    token_grad = scatter_sum(*back_call(put, [dg, du], [gate_weight, up_weight]), tok_count)
+
+    share = share.reshape(local, 2, places).transpose(1, 0, 2)[:, :, :, None]
+    share = jnp.sum(jnp.where(hit, share, 0.0), axis=2)
+    share = share.reshape(2, local, devices // 2, tok_count).transpose(0, 2, 3, 1)
+    share = share.reshape(devices, tok_count, local)
+    order = me ^ arrival()[me & CORE]
+    spots = jnp.arange(devices, dtype=jnp.int32)
+    inverse = jnp.sum(jnp.where(order[None, :] == spots[:, None], spots[None, :], 0), axis=1)
+    share = lax.all_to_all(share[inverse], AXES, split_axis=0, concat_axis=0, tiled=True)
+    share = share.reshape(dp_size, ex_size, tok_count, local).sum(axis=0)
+    share = share.transpose(1, 0, 2).reshape(tok_count, 1, total_experts)
+    gate_grad = jnp.sum(jnp.where(used, share, 0.0), axis=2)
+
+    down_weight_grad = grad_call(c, [ht])[0]
+    gate_weight_grad, up_weight_grad = grad_call(x, [dgt, dut])
+    return (mixed, token_grad, gate_grad, gate_weight_grad, up_weight_grad, down_weight_grad)
+
+
+def routed_body(tokens, cotangent, gate_prob, expert_ids, placement, gate_weight, up_weight, down_weight):
     tok_count, model_width = tokens.shape
     top_count = expert_ids.shape[1]
     expert_devs = lax.axis_size("expert")
@@ -100,6 +397,14 @@
     return (mixed, token_grad, gate_grad, gate_grad_w, up_grad_w, down_grad)
 
 
+def body(*args):
+    tokens, gate_weight = args[0], args[5]
+    mesh_fits = (lax.axis_size("dp"), lax.axis_size("expert")) == (4, 8)
+    if mesh_fits and tokens.shape[0] <= gate_weight.shape[0] * CAP:
+        return dense_body(*args)
+    return routed_body(*args)
+
+
 def solution(mesh):
     return jax.shard_map(
         body,

time: 602 us -> 250 us (0.42)
  waiting for transfers between devices: 348 us -> 61.3 us
  matrix products: 99.7 us -> 0.15 us
  blocking collectives: 84.2 us -> 0 us
  Pallas kernels: 0 us -> 81.4 us
  starting transfers between devices: 8.76 us -> 61.5 us
  between operations: 14.4 us -> 1.36 us
  other arithmetic: 2.54 us -> 14.6 us
  local copies, waits for them, and re-layouts: 39 us -> 28 us
    unnamed x4 -> x0, waiting for transfers between devices: 228 us -> none
    dot_general x13 -> x1, matrix products: 99.7 us -> 0.15 us  [dot(): return lax.dot_general(a, b, dims, preferred_element_type=jnp.float32)]
    all_to_all x2 -> x0, blocking collectives: 84.2 us -> none  [the longest x1 44 us: body(): lax.all_to_all(sent_rows, 'expert', split_axis=1, concat_axis=1, tiled=True)]
    all_gather x2 -> x0, waiting for transfers between devices: 83.9 us -> none  [the longest x1 64 us: body(): lax.all_gather(got_grads, 'dp', axis=0, tiled=True)]
    pallas_call x0 -> x6, Pallas kernels: none -> 81.4 us  [call(): pl.pallas_call(kernel, grid=(grid,), in_specs=ins, out_specs=outs, out_sh...]
    ppermute x0 -> x50, waiting for transfers between devices: none -> 61.3 us  [swap(): return lax.ppermute(values, AXES, pairs)]
    ppermute x0 -> x50, starting transfers between devices: none -> 58 us  [swap(): return lax.ppermute(values, AXES, pairs)]
    all_to_all x2 -> x1, waiting for transfers between devices: 35.5 us -> 0.01 us  [dense_body(): lax.all_to_all(share[inverse], AXES, split_axis=0, concat_axis=0, tiled=T...]
  transfers between devices with their start and end apart: 5 -> 51, of which waited for: 5 -> 23; matrix products, arithmetic and copies ran while one was open for 12% -> 12% of each run, Pallas kernels for 0% -> 33%
where the time goes in v1:
time: 250 us; the launch traced here: 248 us
  Pallas kernels  81.4 us (33%)
  starting transfers between devices  61.5 us (25%)
  waiting for transfers between devices  61.3 us (25%)
  local copies, waits for them, and re-layouts  28 us (11%)
  other arithmetic  14.6 us (6%)
    pallas_call x6, Pallas kernels, call(): pl.pallas_call(kernel, grid=(grid,), in_specs=ins, out_specs=outs, out_sh...  81.4 us
    ppermute x50, waiting for transfers between devices, swap(): return lax.ppermute(values, AXES, pairs)  61.3 us
    ppermute x50, starting transfers between devices, swap(): return lax.ppermute(values, AXES, pairs)  58 us
    unnamed x68, local copies, waits for them, and re-layouts  21.4 us
    convert_element_type x16, other arithmetic, add(): return (a.astype(jnp.float32) + b.astype(jnp.float32)).astype(jnp.bfloat16)  6.61 us
  transfers between devices with their start and end apart: 51, of which 23 were waited for; matrix products, arithmetic and copies ran while one was open for 12% of the time, Pallas kernels for 33%

profile of v1, /device:TPU:0, one launch (start us, length us, event | category | flops | bytes accessed | tf_op | source)
XLA Modules:
  0.0 248.5 jit_solution(13418946994543302780)
XLA Ops:
  3.3 3.0 %collective-permute-start = (f32[16,64]{1,0:T(8,128)S(1)}, f32[16,64]{1,0:T(8,128)S(1)}, u32[]{:S(2)}, u32[]{:S(2)}) collective-permute-start(f32[16,64]{1,0:T(8,128)S(1)} %select_reduce_fusion.3), channel_id=1, source_target_pairs={{0,8},{1,17},{2,10},{3,19},{4,12},{5,21},{6,14},{7,23},{8,0},{9,25... | collective-permute-start | bytes 12296 | tf_op jit(solution)/shard_map/ppermute | solution.py:27
  7.9 2.6 %collective-permute-start.3 = (f32[16,64]{1,0:T(8,128)S(1)}, f32[16,64]{1,0:T(8,128)S(1)}, u32[]{:S(2)}, u32[]{:S(2)}) collective-permute-start(f32[16,64]{1,0:T(8,128)S(1)} %select_reduce_fusion.3), channel_id=1, source_target_pairs={{0,4},{1,5},{2,6},{3,7},{4,0},{5,1},{6,2},{7,3},{8,12},{9,13},{10,... | collective-permute-start | bytes 12296 | tf_op jit(solution)/shard_map/ppermute | solution.py:27
  14.7 1.9 collective-permute-start.1
  18.2 2.2 collective-permute-done.4
  22.0 2.1 collective-permute-done.6
  26.1 3.2 %collective-permute-done.7 = f32[16,64]{1,0:T(8,128)S(1)} collective-permute-done((f32[16,64]{1,0:T(8,128)S(1)}, f32[16,64]{1,0:T(8,128)S(1)}, u32[]{:S(2)}, u32[]{:S(2)}) %collective-permute-start.7) | collective-permute-done | bytes 4128 | tf_op jit(solution)/shard_map/ppermute | solution.py:27
  29.9 3.4 %collective-permute-done.5 = f32[64,64]{1,0:T(8,128)S(1)} collective-permute-done((f32[64,64]{1,0:T(8,128)S(1)}, f32[64,64]{1,0:T(8,128)S(1)}, u32[]{:S(2)}, u32[]{:S(2)}) %collective-permute-start.5) | collective-permute-done | bytes 16416 | tf_op jit(solution)/shard_map/ppermute | solution.py:27
  33.9 3.2 %collective-permute-done.8 = f32[32,64]{1,0:T(8,128)S(1)} collective-permute-done((f32[32,64]{1,0:T(8,128)S(1)}, f32[32,64]{1,0:T(8,128)S(1)}, u32[]{:S(2)}, u32[]{:S(2)}) %collective-permute-start.8) | collective-permute-done | bytes 8224 | tf_op jit(solution)/shard_map/ppermute | solution.py:27
  42.9 2.7 %collective-permute-start.33 = (bf16[16,4096]{1,0:T(8,128)(2,1)}, bf16[16,4096]{1,0:T(8,128)(2,1)S(1)}, u32[]{:S(2)}, u32[]{:S(2)}) collective-permute-start(bf16[16,4096]{1,0:T(8,128)(2,1)} %param.10), channel_id=1, source_target_pairs={{0,4},{1,5},{2,6},{3,7},{4,0},{5,1},{6,2},{7,3},{8,12},{9,13},{10,... | collective-permute-start | bytes 393224 | tf_op jit(solution)/shard_map/ppermute | solution.py:27
  55.8 2.0 collective-permute-done.16
  61.2 4.4 %collective-permute-done.17 = bf16[16,4096]{1,0:T(8,128)(2,1)S(1)} collective-permute-done((bf16[16,4096]{1,0:T(8,128)(2,1)S(1)}, bf16[16,4096]{1,0:T(8,128)(2,1)S(1)}, u32[]{:S(2)}, u32[]{:S(2)}) %collective-permute-start.17) | collective-permute-done | bytes 131104 | tf_op jit(solution)/shard_map/ppermute | solution.py:27
  65.6 1.7 collective-permute-start.15
  68.4 1.7 collective-permute-start.35
  78.3 4.9 %collective-permute-done.35 = bf16[64,4096]{1,0:T(8,128)(2,1)S(1)} collective-permute-done((bf16[64,4096]{1,0:T(8,128)(2,1)S(1)}, bf16[64,4096]{1,0:T(8,128)(2,1)S(1)}, u32[]{:S(2)}, u32[]{:S(2)}) %collective-permute-start.35) | collective-permute-done | bytes 524320 | tf_op jit(solution)/shard_map/ppermute | solution.py:27
  83.3 2.7 %collective-permute-done.38 = bf16[32,4096]{1,0:T(8,128)(2,1)S(1)} collective-permute-done((bf16[32,4096]{1,0:T(8,128)(2,1)S(1)}, bf16[32,4096]{1,0:T(8,128)(2,1)S(1)}, u32[]{:S(2)}, u32[]{:S(2)}) %collective-permute-start.38) | collective-permute-done | bytes 262176 | tf_op jit(solution)/shard_map/ppermute | solution.py:27
  88.0 19.1 %shard_map.136 = (bf16[2,8,48,4096]{3,2,1,0:T(8,128)(2,1)}, f32[8,192,96]{2,1,0:T(8,128)S(1)}, f32[8,192,96]{2,1,0:T(8,128)S(1)}, bf16[8,96,192]{2,1,0:T(8,128)(2,1)S(1)}, bf16[8,192,96]{2,1,0:T(8,128)(2,1)S(1)}) custom-call(bf16[2,384,256]{2,1,0:T(8,128)(2,1)S(1)} %copy.57.pick_ref, f32[8,1,96]{2,1,0:T(1,128)S(1)} %reshape.63.prob_ref, ...), custom_call_target="tpu_custom_call" | custom-call | flops 4026531840 | bytes 37817344 | tf_op jit(solution)/shard_map/pallas_call | solution.py:175
  108.9 10.7 %shard_map.137 = (bf16[256,4096]{1,0:T(8,128)(2,1)S(1)}, bf16[256,4096]{1,0:T(8,128)(2,1)}) custom-call(bf16[2,256,384]{2,1,0:T(8,128)(2,1)S(1)} %fusion.9.put_ref, bf16[8,96,192]{2,1,0:T(8,128)(2,1)S(1)} %get-tuple-element.23.refs_0_, bf16[8,192,4096]{2,1,0:T(8,128)(2,1)} %down_ref.1), custom_call_target="tpu_custom_call" | custom-call | flops 2818572288 | bytes 17465344 | tf_op jit(solution)/shard_map/pallas_call | solution.py:175
  123.9 14.3 %shard_map.138 = (bf16[2,8,48,4096]{3,2,1,0:T(8,128)(2,1)}, bf16[8,96,192]{2,1,0:T(8,128)(2,1)S(1)}, bf16[8,96,192]{2,1,0:T(8,128)(2,1)S(1)}, bf16[8,192,96]{2,1...) custom-call(bf16[2,384,256]{2,1,0:T(8,128)(2,1)S(1)} %copy.57.pick_ref, ...), custom_call_target="tpu_custom_call" | custom-call | flops 2818572288 | bytes 25827328 | tf_op jit(solution)/shard_map/pallas_call | solution.py:175
  139.7 13.9 %shard_map.139 = (bf16[256,4096]{1,0:T(8,128)(2,1)S(1)}, bf16[256,4096]{1,0:T(8,128)(2,1)}) custom-call(bf16[2,256,384]{2,1,0:T(8,128)(2,1)S(1)} %fusion.9.put_ref, bf16[8,96,192]{2,1,0:T(8,128)(2,1)S(1)} %get-tuple-element.28.refs_0_, bf16[8,96,192]{2,1,0:T(8,128)(2,1)S(1)} %get-tuple-element.29.refs_1_, bf16[8,192,4096]{2,1,0:T(8,128)(2,1)} %refs_2_.1, ...), custom_call_target="tpu_custom_call" | custom-call | flops 4026531840 | bytes 30343168 | tf_op jit(solution)/shard_map/pallas_call | solution.py:175
  158.0 3.5 %all-to-all-start = ((f32[32,1,128]{2,1,0:T(1,128)}), f32[32,1,128]{2,1,0:T(1,128)S(1)}, u32[]{:S(2)}, u32[]{:S(2)}) async-start(f32[32,1,128]{2,1,0:T(1,128)} %reshape.86), calls=%async_computation | async-start | bytes 32768 | tf_op jit(solution)/shard_map/all_to_all | solution.py:301
  161.5 12.7 %shard_map.140 = (bf16[8,192,4096]{2,1,0:T(8,128)(2,1)}, bf16[8,192,4096]{2,1,0:T(8,128)(2,1)}) custom-call(bf16[2,8,48,4096]{3,2,1,0:T(8,128)(2,1)} %get-tuple-element.33.x_ref, bf16[8,192,96]{2,1,0:T(8,128)(2,1)S(1)} %copy-done.9, bf16[8,192,96]{2,1,0:T(8,128)(2,1)S(1)} %copy-done.11), custom_call_target="tpu_custom_call" | custom-call | flops 2415919104 | bytes 32047104 | tf_op jit(solution)/shard_map/pallas_call | solution.py:175
  174.2 10.7 %shard_map.141 = bf16[8,192,4096]{2,1,0:T(8,128)(2,1)} custom-call(bf16[2,8,48,4096]{3,2,1,0:T(8,128)(2,1)} %get-tuple-element.38.x_ref, bf16[8,192,96]{2,1,0:T(8,128)(2,1)S(1)} %get-tuple-element.39.refs_0_), custom_call_target="tpu_custom_call" | custom-call | flops 1207959552 | bytes 19169280 | tf_op jit(solution)/shard_map/pallas_call | solution.py:175
  188.6 1.7 collective-permute-start.26
  199.9 4.0 %collective-permute-done.21 = bf16[32,4096]{1,0:T(8,128)(2,1)S(1)} collective-permute-done((bf16[32,4096]{1,0:T(8,128)(2,1)S(1)}, bf16[32,4096]{1,0:T(8,128)(2,1)S(1)}, u32[]{:S(2)}, u32[]{:S(2)}) %collective-permute-start.21) | collective-permute-done | bytes 262176 | tf_op jit(solution)/shard_map/ppermute | solution.py:27
  205.5 2.4 collective-permute-done.46
  209.4 8.6 %collective-permute-done.41 = bf16[32,4096]{1,0:T(8,128)(2,1)S(1)} collective-permute-done((bf16[32,4096]{1,0:T(8,128)(2,1)S(1)}, bf16[32,4096]{1,0:T(8,128)(2,1)S(1)}, u32[]{:S(2)}, u32[]{:S(2)}) %collective-permute-start.41) | collective-permute-done | bytes 262176 | tf_op jit(solution)/shard_map/ppermute | solution.py:27
  220.2 2.7 %collective-permute-done.47 = bf16[16,4096]{1,0:T(8,128)(2,1)S(1)} collective-permute-done((bf16[16,4096]{1,0:T(8,128)(2,1)S(1)}, bf16[16,4096]{1,0:T(8,128)(2,1)S(1)}, u32[]{:S(2)}, u32[]{:S(2)}) %collective-permute-start.47) | collective-permute-done | bytes 131104 | tf_op jit(solution)/shard_map/ppermute | solution.py:27
  226.9 4.8 %collective-permute-done.24 = bf16[32,4096]{1,0:T(8,128)(2,1)S(1)} collective-permute-done((bf16[32,4096]{1,0:T(8,128)(2,1)S(1)}, bf16[32,4096]{1,0:T(8,128)(2,1)S(1)}, u32[]{:S(2)}, u32[]{:S(2)}) %collective-permute-start.24) | collective-permute-done | bytes 262176 | tf_op jit(solution)/shard_map/ppermute | solution.py:27
  233.3 2.5 collective-permute-start.29
  235.7 2.3 collective-permute-done.44
  239.6 2.5 %collective-permute-start.49 = (bf16[16,4096]{1,0:T(8,128)(2,1)S(1)}, bf16[16,4096]{1,0:T(8,128)(2,1)S(1)}, u32[]{:S(2)}, u32[]{:S(2)}) collective-permute-start(bf16[16,4096]{1,0:T(8,128)(2,1)S(1)} %add_convert_fusion.15), channel_id=1, source_target_pairs={{0,4},{1,5},{2,6},{3,7},{4,0},{5,1},{6,2},{7,3},{8,12},{9,13},{10,... | collective-permute-start | bytes 393224 | tf_op jit(solution)/shard_map/ppermute | solution.py:27
  243.2 2.1 collective-permute-done.25
  (227 shorter events, 87.0 us)
Async XLA Ops:
  3.3 11.4 %collective-permute-start = (f32[16,64]{1,0:T(8,128)S(1)}, f32[16,64]{1,0:T(8,128)S(1)}, u32[]{:S(2)}, u32[]{:S(2)}) collective-permute-start(f32[16,64]{1,0:T(8,128)S(1)} %select_reduce_fusion.3), channel_id=1, source_target_pairs={{0,8},{1,17},{2,10},{3,19},{4,12},{5,21},{6,14},{7,23},{8,0},{9,25... | collective-permute-start | bytes 12296 | tf_op jit(solution)/shard_map/ppermute | solution.py:27
  10.5 32.4 %collective-permute-start.10 = (bf16[16,4096]{1,0:T(8,128)(2,1)}, bf16[16,4096]{1,0:T(8,128)(2,1)}, u32[]{:S(2)}, u32[]{:S(2)}) collective-permute-start(bf16[16,4096]{1,0:T(8,128)(2,1)} %param.9), channel_id=1, source_target_pairs={{0,8},{1,17},{2,10},{3,19},{4,12},{5,21},{6,14},{7,23},{8,0},{9,25... | collective-permute-start | bytes 393224 | tf_op jit(solution)/shard_map/ppermute | solution.py:27
  11.1 35.4 %collective-permute-start.12 = (bf16[16,4096]{1,0:T(8,128)(2,1)}, bf16[16,4096]{1,0:T(8,128)(2,1)S(1)}, u32[]{:S(2)}, u32[]{:S(2)}) collective-permute-start(bf16[16,4096]{1,0:T(8,128)(2,1)} %param.9), channel_id=1, source_target_pairs={{0,2},{1,3},{2,0},{3,1},{4,6},{5,7},{6,4},{7,5},{8,10},{9,11},{10,... | collective-permute-start | bytes 393224 | tf_op jit(solution)/shard_map/ppermute | solution.py:27
  14.7 32.7 %collective-permute-start.13 = (bf16[16,4096]{1,0:T(8,128)(2,1)}, bf16[16,4096]{1,0:T(8,128)(2,1)S(1)}, u32[]{:S(2)}, u32[]{:S(2)}) collective-permute-start(bf16[16,4096]{1,0:T(8,128)(2,1)} %param.9), channel_id=1, source_target_pairs={{0,4},{1,5},{2,6},{3,7},{4,0},{5,1},{6,2},{7,3},{8,12},{9,13},{10,... | collective-permute-start | bytes 393224 | tf_op jit(solution)/shard_map/ppermute | solution.py:27
  14.7 10.9 %collective-permute-start.1 = (f32[32,64]{1,0:T(8,128)S(1)}, f32[32,64]{1,0:T(8,128)S(1)}, u32[]{:S(2)}, u32[]{:S(2)}) collective-permute-start(f32[32,64]{1,0:T(8,128)S(1)} %pad_maximum_fusion.9), channel_id=1, source_target_pairs={{0,16},{1,9},{2,18},{3,11},{4,20},{5,13},{6,22},{7,15},{8,24},{9,1... | collective-permute-start | bytes 24584 | tf_op jit(solution)/shard_map/ppermute | solution.py:27
  24.1 24.6 %collective-permute-start.30 = (bf16[16,4096]{1,0:T(8,128)(2,1)}, bf16[16,4096]{1,0:T(8,128)(2,1)}, u32[]{:S(2)}, u32[]{:S(2)}) collective-permute-start(bf16[16,4096]{1,0:T(8,128)(2,1)} %param.10), channel_id=1, source_target_pairs={{0,8},{1,17},{2,10},{3,19},{4,12},{5,21},{6,14},{7,23},{8,0},{9,25... | collective-permute-start | bytes 393224 | tf_op jit(solution)/shard_map/ppermute | solution.py:27
  38.4 14.4 %collective-permute-start.32 = (bf16[16,4096]{1,0:T(8,128)(2,1)}, bf16[16,4096]{1,0:T(8,128)(2,1)S(1)}, u32[]{:S(2)}, u32[]{:S(2)}) collective-permute-start(bf16[16,4096]{1,0:T(8,128)(2,1)} %param.10), channel_id=1, source_target_pairs={{0,2},{1,3},{2,0},{3,1},{4,6},{5,7},{6,4},{7,5},{8,10},{9,11},{10,... | collective-permute-start | bytes 393224 | tf_op jit(solution)/shard_map/ppermute | solution.py:27
  42.9 10.5 %collective-permute-start.33 = (bf16[16,4096]{1,0:T(8,128)(2,1)}, bf16[16,4096]{1,0:T(8,128)(2,1)S(1)}, u32[]{:S(2)}, u32[]{:S(2)}) collective-permute-start(bf16[16,4096]{1,0:T(8,128)(2,1)} %param.10), channel_id=1, source_target_pairs={{0,4},{1,5},{2,6},{3,7},{4,0},{5,1},{6,2},{7,3},{8,12},{9,13},{10,... | collective-permute-start | bytes 393224 | tf_op jit(solution)/shard_map/ppermute | solution.py:27
  46.5 23.7 %collective-permute-start.11 = (bf16[32,4096]{1,0:T(8,128)(2,1)S(1)}, bf16[32,4096]{1,0:T(8,128)(2,1)S(1)}, u32[]{:S(2)}, u32[]{:S(2)}) collective-permute-start(bf16[32,4096]{1,0:T(8,128)(2,1)S(1)} %pad_maximum_fusion.2), channel_id=1, source_target_pairs={{0,16},{1,9},{2,18},{3,11},{4,20},{5,13},{6,22},{7,15},{8,24},{9,1... | collective-permute-start | bytes 786440 | tf_op jit(solution)/shard_map/ppermute | solution.py:27
  47.4 13.1 %collective-permute-start.14 = (bf16[32,4096]{1,0:T(8,128)(2,1)S(1)}, bf16[32,4096]{1,0:T(8,128)(2,1)S(1)}, u32[]{:S(2)}, u32[]{:S(2)}) collective-permute-start(bf16[32,4096]{1,0:T(8,128)(2,1)S(1)} %pad_maximum_fusion.3), channel_id=1, source_target_pairs={{0,8},{1,17},{2,10},{3,19},{4,12},{5,21},{6,14},{7,23},{8,0},{9,25... | collective-permute-start | bytes 786440 | tf_op jit(solution)/shard_map/ppermute | solution.py:27
  49.6 23.7 %collective-permute-start.31 = (bf16[32,4096]{1,0:T(8,128)(2,1)S(1)}, bf16[32,4096]{1,0:T(8,128)(2,1)S(1)}, u32[]{:S(2)}, u32[]{:S(2)}) collective-permute-start(bf16[32,4096]{1,0:T(8,128)(2,1)S(1)} %pad_maximum_fusion.5), channel_id=1, source_target_pairs={{0,16},{1,9},{2,18},{3,11},{4,20},{5,13},{6,22},{7,15},{8,24},{9,1... | collective-permute-start | bytes 786440 | tf_op jit(solution)/shard_map/ppermute | solution.py:27
  57.8 9.6 %collective-permute-start.34 = (bf16[32,4096]{1,0:T(8,128)(2,1)S(1)}, bf16[32,4096]{1,0:T(8,128)(2,1)S(1)}, u32[]{:S(2)}, u32[]{:S(2)}) collective-permute-start(bf16[32,4096]{1,0:T(8,128)(2,1)S(1)} %pad_maximum_fusion.6), channel_id=1, source_target_pairs={{0,8},{1,17},{2,10},{3,19},{4,12},{5,21},{6,14},{7,23},{8,0},{9,25... | collective-permute-start | bytes 786440 | tf_op jit(solution)/shard_map/ppermute | solution.py:27
  67.4 10.2 %collective-permute-start.18 = (bf16[32,4096]{1,0:T(8,128)(2,1)S(1)}, bf16[32,4096]{1,0:T(8,128)(2,1)S(1)}, u32[]{:S(2)}, u32[]{:S(2)}) collective-permute-start(bf16[32,4096]{1,0:T(8,128)(2,1)S(1)} %pad_maximum_fusion.4), channel_id=1, source_target_pairs={{0,16},{1,9},{2,18},{3,11},{4,20},{5,13},{6,22},{7,15},{8,24},{9,1... | collective-permute-start | bytes 786440 | tf_op jit(solution)/shard_map/ppermute | solution.py:27
  68.4 14.8 %collective-permute-start.35 = (bf16[64,4096]{1,0:T(8,128)(2,1)S(1)}, bf16[64,4096]{1,0:T(8,128)(2,1)S(1)}, u32[]{:S(2)}, u32[]{:S(2)}) collective-permute-start(bf16[64,4096]{1,0:T(8,128)(2,1)S(1)} %pad_maximum_fusion.1), channel_id=1, source_target_pairs={{0,16},{1,9},{2,18},{3,11},{4,20},{5,13},{6,22},{7,15},{8,24},{9,1... | collective-permute-start | bytes 1572872 | tf_op jit(solution)/shard_map/ppermute | solution.py:27
  70.2 15.8 %collective-permute-start.38 = (bf16[32,4096]{1,0:T(8,128)(2,1)S(1)}, bf16[32,4096]{1,0:T(8,128)(2,1)S(1)}, u32[]{:S(2)}, u32[]{:S(2)}) collective-permute-start(bf16[32,4096]{1,0:T(8,128)(2,1)S(1)} %pad_maximum_fusion.7), channel_id=1, source_target_pairs={{0,16},{1,9},{2,18},{3,11},{4,20},{5,13},{6,22},{7,15},{8,24},{9,1... | collective-permute-start | bytes 786440 | tf_op jit(solution)/shard_map/ppermute | solution.py:27
  78.3 9.7 %collective-permute-start.19 = (bf16[256,4096]{1,0:T(8,128)(2,1)}, bf16[256,4096]{1,0:T(8,128)(2,1)}, u32[]{:S(2)}, u32[]{:S(2)}) collective-permute-start(bf16[256,4096]{1,0:T(8,128)(2,1)} %constant_dynamic-update-slice_fusion.21.own_ref), channel_id=1, source_target_pairs={{0,1},{1,0},{2,3},{3,2},{4,5},{5,4},{6,7},{7,6},{8,9},{9,8},{10,11... | collective-permute-start | bytes 6291464 | tf_op jit(solution)/shard_map/ppermute | solution.py:27
  86.1 35.5 %collective-permute-start.39 = (bf16[256,4096]{1,0:T(8,128)(2,1)S(1)}, bf16[256,4096]{1,0:T(8,128)(2,1)}, u32[]{:S(2)}, u32[]{:S(2)}) collective-permute-start(bf16[256,4096]{1,0:T(8,128)(2,1)S(1)} %constant_dynamic-update-slice_fusion.31.own_ref), channel_id=1, source_target_pairs={{0,1},{1,0},{2,3},{3,2},{4,5},{5,4},{6,7},{7,6},{8,9},{9,8},{10,11... | collective-permute-start | bytes 6291464 | tf_op jit(solution)/shard_map/ppermute | solution.py:27
  121.0 66.2 %collective-permute-start.20 = (bf16[256,4096]{1,0:T(8,128)(2,1)}, bf16[256,4096]{1,0:T(8,128)(2,1)}, u32[]{:S(2)}, u32[]{:S(2)}) collective-permute-start(bf16[256,4096]{1,0:T(8,128)(2,1)} %get-tuple-element.25), channel_id=1, source_target_pairs={{0,1},{1,0},{2,3},{3,2},{4,5},{5,4},{6,7},{7,6},{8,9},{9,8},{10,11... | collective-permute-start | bytes 6291464 | tf_op jit(solution)/shard_map/ppermute | solution.py:27
  155.0 39.0 %collective-permute-start.40 = (bf16[256,4096]{1,0:T(8,128)(2,1)}, bf16[256,4096]{1,0:T(8,128)(2,1)}, u32[]{:S(2)}, u32[]{:S(2)}) collective-permute-start(bf16[256,4096]{1,0:T(8,128)(2,1)} %get-tuple-element.31), channel_id=1, source_target_pairs={{0,1},{1,0},{2,3},{3,2},{4,5},{5,4},{6,7},{7,6},{8,9},{9,8},{10,11... | collective-permute-start | bytes 6291464 | tf_op jit(solution)/shard_map/ppermute | solution.py:27
  158.0 27.0 %all-to-all-start = ((f32[32,1,128]{2,1,0:T(1,128)}), f32[32,1,128]{2,1,0:T(1,128)S(1)}, u32[]{:S(2)}, u32[]{:S(2)}) async-start(f32[32,1,128]{2,1,0:T(1,128)} %reshape.86), calls=%async_computation | async-start | bytes 32768 | tf_op jit(solution)/shard_map/all_to_all | solution.py:301
  188.6 10.6 %collective-permute-start.26 = (bf16[32,4096]{1,0:T(8,128)(2,1)S(1)}, bf16[32,4096]{1,0:T(8,128)(2,1)S(1)}, u32[]{:S(2)}, u32[]{:S(2)}) collective-permute-start(bf16[32,4096]{1,0:T(8,128)(2,1)S(1)} %slice.176), channel_id=1, source_target_pairs={{0,16},{1,9},{2,18},{3,11},{4,20},{5,13},{6,22},{7,15},{8,24},{9,1... | collective-permute-start | bytes 786440 | tf_op jit(solution)/shard_map/ppermute | solution.py:27
  191.8 32.6 %collective-permute-start.23 = (bf16[64,4096]{1,0:T(8,128)(2,1)S(1)}, bf16[64,4096]{1,0:T(8,128)(2,1)S(1)}, u32[]{:S(2)}, u32[]{:S(2)}) collective-permute-start(bf16[64,4096]{1,0:T(8,128)(2,1)S(1)} %slice.169), channel_id=1, source_target_pairs={{0,16},{1,9},{2,18},{3,11},{4,20},{5,13},{6,22},{7,15},{8,24},{9,1... | collective-permute-start | bytes 1572872 | tf_op jit(solution)/shard_map/ppermute | solution.py:27
  192.5 11.4 %collective-permute-start.21 = (bf16[32,4096]{1,0:T(8,128)(2,1)S(1)}, bf16[32,4096]{1,0:T(8,128)(2,1)S(1)}, u32[]{:S(2)}, u32[]{:S(2)}) collective-permute-start(bf16[32,4096]{1,0:T(8,128)(2,1)S(1)} %slice.164), channel_id=1, source_target_pairs={{0,16},{1,9},{2,18},{3,11},{4,20},{5,13},{6,22},{7,15},{8,24},{9,1... | collective-permute-start | bytes 786440 | tf_op jit(solution)/shard_map/ppermute | solution.py:27
  195.5 12.3 %collective-permute-start.46 = (bf16[32,4096]{1,0:T(8,128)(2,1)S(1)}, bf16[32,4096]{1,0:T(8,128)(2,1)S(1)}, u32[]{:S(2)}, u32[]{:S(2)}) collective-permute-start(bf16[32,4096]{1,0:T(8,128)(2,1)S(1)} %slice.193), channel_id=1, source_target_pairs={{0,16},{1,9},{2,18},{3,11},{4,20},{5,13},{6,22},{7,15},{8,24},{9,1... | collective-permute-start | bytes 786440 | tf_op jit(solution)/shard_map/ppermute | solution.py:27
  197.7 27.5 %collective-permute-start.43 = (bf16[64,4096]{1,0:T(8,128)(2,1)S(1)}, bf16[64,4096]{1,0:T(8,128)(2,1)S(1)}, u32[]{:S(2)}, u32[]{:S(2)}) collective-permute-start(bf16[64,4096]{1,0:T(8,128)(2,1)S(1)} %slice.186), channel_id=1, source_target_pairs={{0,16},{1,9},{2,18},{3,11},{4,20},{5,13},{6,22},{7,15},{8,24},{9,1... | collective-permute-start | bytes 1572872 | tf_op jit(solution)/shard_map/ppermute | solution.py:27
  199.2 18.7 %collective-permute-start.41 = (bf16[32,4096]{1,0:T(8,128)(2,1)S(1)}, bf16[32,4096]{1,0:T(8,128)(2,1)S(1)}, u32[]{:S(2)}, u32[]{:S(2)}) collective-permute-start(bf16[32,4096]{1,0:T(8,128)(2,1)S(1)} %slice.181), channel_id=1, source_target_pairs={{0,16},{1,9},{2,18},{3,11},{4,20},{5,13},{6,22},{7,15},{8,24},{9,1... | collective-permute-start | bytes 786440 | tf_op jit(solution)/shard_map/ppermute | solution.py:27
  203.9 15.6 %collective-permute-start.27 = (bf16[16,4096]{1,0:T(8,128)(2,1)S(1)}, bf16[16,4096]{1,0:T(8,128)(2,1)S(1)}, u32[]{:S(2)}, u32[]{:S(2)}) collective-permute-start(bf16[16,4096]{1,0:T(8,128)(2,1)S(1)} %slice.178), channel_id=1, source_target_pairs={{0,8},{1,17},{2,10},{3,19},{4,12},{5,21},{6,14},{7,23},{8,0},{9,25... | collective-permute-start | bytes 393224 | tf_op jit(solution)/shard_map/ppermute | solution.py:27
  207.9 34.2 %collective-permute-start.22 = (bf16[16,4096]{1,0:T(8,128)(2,1)S(1)}, bf16[16,4096]{1,0:T(8,128)(2,1)S(1)}, u32[]{:S(2)}, u32[]{:S(2)}) collective-permute-start(bf16[16,4096]{1,0:T(8,128)(2,1)S(1)} %slice.166), channel_id=1, source_target_pairs={{0,8},{1,17},{2,10},{3,19},{4,12},{5,21},{6,14},{7,23},{8,0},{9,25... | collective-permute-start | bytes 393224 | tf_op jit(solution)/shard_map/ppermute | solution.py:27
  219.5 26.4 %collective-permute-start.42 = (bf16[16,4096]{1,0:T(8,128)(2,1)S(1)}, bf16[16,4096]{1,0:T(8,128)(2,1)S(1)}, u32[]{:S(2)}, u32[]{:S(2)}) collective-permute-start(bf16[16,4096]{1,0:T(8,128)(2,1)S(1)} %slice.183), channel_id=1, source_target_pairs={{0,8},{1,17},{2,10},{3,19},{4,12},{5,21},{6,14},{7,23},{8,0},{9,25... | collective-permute-start | bytes 393224 | tf_op jit(solution)/shard_map/ppermute | solution.py:27
  222.9 10.3 %collective-permute-start.28 = (bf16[16,4096]{1,0:T(8,128)(2,1)S(1)}, bf16[16,4096]{1,0:T(8,128)(2,1)S(1)}, u32[]{:S(2)}, u32[]{:S(2)}) collective-permute-start(bf16[16,4096]{1,0:T(8,128)(2,1)S(1)} %add_convert_fusion.20), channel_id=1, source_target_pairs={{0,2},{1,3},{2,0},{3,1},{4,6},{5,7},{6,4},{7,5},{8,10},{9,11},{10,... | collective-permute-start | bytes 393224 | tf_op jit(solution)/shard_map/ppermute | solution.py:27
  224.4 15.1 %collective-permute-start.48 = (bf16[16,4096]{1,0:T(8,128)(2,1)S(1)}, bf16[16,4096]{1,0:T(8,128)(2,1)S(1)}, u32[]{:S(2)}, u32[]{:S(2)}) collective-permute-start(bf16[16,4096]{1,0:T(8,128)(2,1)S(1)} %add_convert_fusion.16), channel_id=1, source_target_pairs={{0,2},{1,3},{2,0},{3,1},{4,6},{5,7},{6,4},{7,5},{8,10},{9,11},{10,... | collective-permute-start | bytes 393224 | tf_op jit(solution)/shard_map/ppermute | solution.py:27
  233.3 9.9 %collective-permute-start.29 = (bf16[16,4096]{1,0:T(8,128)(2,1)S(1)}, bf16[16,4096]{1,0:T(8,128)(2,1)S(1)}, u32[]{:S(2)}, u32[]{:S(2)}) collective-permute-start(bf16[16,4096]{1,0:T(8,128)(2,1)S(1)} %add_convert_fusion.19), channel_id=1, source_target_pairs={{0,4},{1,5},{2,6},{3,7},{4,0},{5,1},{6,2},{7,3},{8,12},{9,13},{10,... | collective-permute-start | bytes 393224 | tf_op jit(solution)/shard_map/ppermute | solution.py:27
  (37 other events, 284.4 us)

commit v2 on v0

--- a/solution.py
+++ b/solution.py
@@ -1,9 +1,21 @@
+import functools
+
 import jax
 import jax.numpy as jnp
 from jax import lax
+from jax.experimental import pallas as pl
+from jax.experimental.pallas import tpu as pltpu
 from jax.sharding import PartitionSpec as P
 
 CAP = 3
+AXES = ("dp", "expert")
+CORE, Z1, Z2, Z3, X, Y = 1, 2, 4, 6, 8, 16
+GROUPS = ((0,), (1, 2), (3,))
+CHUNK = 512
+MIB = 1 << 20
+
+NT = (((1,), (1,)), ((), ()))
+NN = (((1,), (0,)), ((), ()))
 
 
 def gated(values):
@@ -11,7 +23,409 @@
     return (values * sigmoid_v, sigmoid_v * (1.0 + values * (1.0 - sigmoid_v)))
 
 
-def body(tokens, cotangent, gate_prob, expert_ids, placement, gate_weight, up_weight, down_weight):
+def swap(values, even, odd=None):
+    odd = even if odd is None else odd
+    count = lax.axis_size("dp") * lax.axis_size("expert")
+    pairs = [(i, i ^ (odd if i & CORE else even)) for i in range(count)]
+    return lax.ppermute(values, AXES, pairs)
+
+
+def add(*parts):
+    total = parts[0].astype(jnp.float32)
+    for part in parts[1:]:
+        total = total + part.astype(jnp.float32)
+    return total.astype(jnp.bfloat16)
+
+
+def together(*values):
+    return lax.optimization_barrier(values)
+
+
+def slots_of(expert_ids, placement):
+    total = placement.shape[0]
+    matches = expert_ids[:, :, None] == jnp.arange(total, dtype=jnp.int32)
+    return jnp.sum(jnp.where(matches, placement, 0), axis=2)
+
+
+def dot(a, b, dims=NN):
+    return lax.dot_general(a, b, dims, preferred_element_type=jnp.float32)
+
+
+def iota(shape, axis):
+    return lax.broadcasted_iota(jnp.int32, shape, axis)
+
+
+def fetch(x_ref, e):
+    return jnp.concatenate([x_ref[0, e], x_ref[1, e]], axis=0)
+
+
+def dispatch(pick, rows_ref, half, x_ref):
+    experts, places, width = x_ref.shape[1:]
+    for at in range(0, width, CHUNK):
+        rows = dot(pick, rows_ref[half, :, at : at + CHUNK]).astype(jnp.bfloat16)
+        for e in range(experts):
+            x_ref[half, e, :, at : at + CHUNK] = rows[e * places : (e + 1) * places]
+
+
+def join_groups(pieces, rows_ref, half, tok_count):
+    for piece, group in zip(pieces, GROUPS):
+        size = len(group) * tok_count
+        for quarter in range(4):
+            at = (quarter * 4 + group[0]) * tok_count
+            rows_ref[half, at : at + size] = piece[quarter * size : (quarter + 1) * size]
+
+
+def up_kernel(tok_count, own0, own1, own2, other0, other1, other2, mine_ref, mine_t_ref, both_t_ref,
+              gate_ref, up_ref, x_out, put_ref, pick_ref, prob_ref, g_ref, u_ref, h_ref, ht_ref,
+              rows_ref, x_ref, sem):
+    e = pl.program_id(0)
+    experts, places, width = x_ref.shape[1:]
+    count = rows_ref.shape[1]
+
+    @pl.when(e == 0)
+    def _():
+        join_groups((own0, own1, own2), rows_ref, 0, tok_count)
+        join_groups((other0, other1, other2), rows_ref, 1, tok_count)
+        row, col = iota((count, count), 0), iota((count, count), 1)
+        block = lax.div(row, tok_count)
+        before = ((col < row) & (lax.div(col, tok_count) == block)).astype(jnp.bfloat16)
+        columns = both_t_ref.shape[1]
+        first = (lax.div(iota((count, columns), 0), tok_count) * CAP).astype(jnp.float32)
+        spot = lax.rem(iota((count, experts * places), 1), places).astype(jnp.float32)
+        spot_t = lax.rem(iota((experts * places, count), 0), places).astype(jnp.float32)
+        for half in range(2):
+            prob = rows_ref[half, :, width:]
+            taken = prob.astype(jnp.float32) > 0.0
+            rank = dot(before, jnp.where(taken, 1.0, 0.0).astype(jnp.bfloat16))
+            place = jnp.where(taken, rank + first, -1.0).astype(jnp.bfloat16)
+            put = jnp.where(dot(place, mine_ref[...]) == spot, 1.0, 0.0).astype(jnp.bfloat16)
+            pick = dot(mine_t_ref[...], place, NT) == spot_t
+            pick = jnp.where(pick, 1.0, 0.0).astype(jnp.bfloat16)
+            put_ref[half] = put
+            pick_ref[half] = pick
+            weight = jnp.sum(dot(pick, prob) * both_t_ref[...], axis=1, keepdims=True)
+            weight = jnp.broadcast_to(weight, (experts * places, columns))
+            for i in range(experts):
+                prob_ref[half, i] = weight[i * places : (i + 1) * places]
+            dispatch(pick, rows_ref, half, x_ref)
+        pltpu.make_async_copy(x_ref, x_out, sem).start()
+
+    rows = fetch(x_ref, e)
+    g = dot(rows, gate_ref[0], NT)
+    u = dot(rows, up_ref[0], NT)
+    g_ref[0] = g
+    u_ref[0] = u
+    silu_v, _ = gated(g)
+    scaled = silu_v * u * fetch(prob_ref, e)[:, :1]
+    h_ref[0] = scaled.astype(jnp.bfloat16)
+    ht_ref[0] = scaled.T.astype(jnp.bfloat16)
+
+    @pl.when(e == pl.num_programs(0) - 1)
+    def _():
+        pltpu.make_async_copy(x_ref, x_out, sem).wait()
+
+
+def slope_kernel(own0, own1, other0, other1, pick_ref, put_ref, prob_ref, mine_ref, down_ref, g_ref, u_ref,
+                 x_out, dg_ref, du_ref, dgt_ref, dut_ref, share_ref, rows_ref, x_ref, terms_ref, sem):
+    e = pl.program_id(0)
+    places = x_ref.shape[2]
+
+    @pl.when(e == 0)
+    def _():
+        for half, pieces in enumerate(((own0, own1), (other0, other1))):
+            size = own0.shape[0]
+            rows_ref[half, :size] = pieces[0][...]
+            rows_ref[half, size:] = pieces[1][...]
+            dispatch(pick_ref[half], rows_ref, half, x_ref)
+        pltpu.make_async_copy(x_ref, x_out, sem).start()
+
+    plain = dot(fetch(x_ref, e), down_ref[0], NT)
+    g, u = g_ref[0], u_ref[0]
+    silu_v, slope = gated(g)
+    share = jnp.sum(silu_v * u * plain, axis=1, keepdims=True)
+    for half in range(2):
+        part = share[half * places : (half + 1) * places] * mine_ref[e].astype(jnp.float32)
+        terms_ref[half, e] = part.astype(jnp.bfloat16)
+    scaled = plain * fetch(prob_ref, e)[:, :1]
+    dg = scaled * u * slope
+    du = scaled * silu_v
+    dg_ref[0] = dg.astype(jnp.bfloat16)
+    du_ref[0] = du.astype(jnp.bfloat16)
+    dgt_ref[0] = dg.T.astype(jnp.bfloat16)
+    dut_ref[0] = du.T.astype(jnp.bfloat16)
+
+    @pl.when(e == pl.num_programs(0) - 1)
+    def _():
+        for half in range(2):
+            terms = terms_ref[half].reshape(put_ref.shape[2], terms_ref.shape[3])
+            share_ref[half] = dot(put_ref[half], terms).astype(jnp.bfloat16)
+        pltpu.make_async_copy(x_ref, x_out, sem).wait()
+
+
+def back_kernel(terms, steps, put_ref, *refs):
+    lefts, rights = refs[:terms], refs[terms : 2 * terms]
+    extra_ref = refs[2 * terms] if len(refs) > 2 * terms + 3 else None
+    own_ref, other_ref, rows_ref = refs[-3:]
+    experts, places = rights[0].shape[0], put_ref.shape[2] // rights[0].shape[0]
+
+    @pl.when(pl.program_id(0) < steps)
+    def _():
+        for e in range(experts):
+            rows = dot(lefts[0][e], rights[0][e])
+            for left, right in zip(lefts[1:], rights[1:]):
+                rows = rows + dot(left[e], right[e])
+            rows = rows.astype(jnp.bfloat16)
+            for half in range(2):
+                rows_ref[half, e * places : (e + 1) * places] = rows[half * places : (half + 1) * places]
+        own_ref[...] = dot(put_ref[0], rows_ref[0]).astype(jnp.bfloat16)
+        other_ref[...] = dot(put_ref[1], rows_ref[1]).astype(jnp.bfloat16)
+
+    if extra_ref is not None:
+
+        @pl.when(pl.program_id(0) == steps)
+        def _():
+            columns = extra_ref.shape[2]
+            own_ref[:, :columns] = extra_ref[0]
+            other_ref[:, :columns] = extra_ref[1]
+
+
+def grad_kernel(x_ref, left, out):
+    rows = jnp.concatenate([x_ref[0, 0], x_ref[1, 0]], axis=0)
+    for at in range(0, rows.shape[1], CHUNK):
+        out[0, :, at : at + CHUNK] = dot(left[0], rows[:, at : at + CHUNK]).astype(jnp.bfloat16)
+
+
+def whole(a):
+    shape = a.shape
+    return pl.BlockSpec(shape, lambda i: (0,) * len(shape))
+
+
+def each(a):
+    shape = a.shape
+    return pl.BlockSpec((1, *shape[1:]), lambda i: (i,) + (0,) * (len(shape) - 1))
+
+
+def bf16(*shape):
+    return jax.ShapeDtypeStruct(shape, jnp.bfloat16)
+
+
+def f32(*shape):
+    return jax.ShapeDtypeStruct(shape, jnp.float32)
+
+
+def call(kernel, grid, ins, args, outs, shapes, scratch=(), flops=0):
+    moved = sum(a.size * a.dtype.itemsize for a in (*args, *shapes))
+    return pl.pallas_call(
+        kernel,
+        grid=(grid,),
+        in_specs=ins,
+        out_specs=outs,
+        out_shape=shapes,
+        scratch_shapes=scratch,
+        compiler_params=pltpu.CompilerParams(vmem_limit_bytes=56 * MIB),
+        cost_estimate=pl.CostEstimate(flops=flops, bytes_accessed=moved, transcendentals=0),
+    )(*args)
+
+
+def up_call(own, other, maps, w_gate, w_up, tok_count):
+    experts, hidden, width = w_gate.shape
+    held = own[0].shape[1]
+    count = sum(piece.shape[0] for piece in own)
+    columns = held - width
+    places = count // tok_count * CAP
+    rows = 2 * places
+    args = (*own, *other, *maps, w_gate, w_up)
+    shapes = [
+        bf16(2, experts, places, width),
+        bf16(2, count, experts * places),
+        bf16(2, experts * places, count),
+        f32(2, experts, places, columns),
+        f32(experts, rows, hidden),
+        f32(experts, rows, hidden),
+        bf16(experts, rows, hidden),
+        bf16(experts, hidden, rows),
+    ]
+    ins = [whole(a) for a in args[:-2]] + [each(w_gate), each(w_up)]
+    outs = [pl.BlockSpec(memory_space=pl.ANY)]
+    outs += [whole(s) for s in shapes[1:4]] + [each(s) for s in shapes[4:]]
+    scratch = [
+        pltpu.VMEM((2, count, held), jnp.bfloat16),
+        pltpu.VMEM((2, experts, places, width), jnp.bfloat16),
+        pltpu.SemaphoreType.DMA,
+    ]
+    flops = 4 * experts * rows * hidden * width + 2 * experts * rows * count * width
+    return call(
+        functools.partial(up_kernel, tok_count), experts, ins, args, outs, shapes, scratch, flops
+    )
+
+
+def slope_call(own, other, pick, put, prob, mine, w_down, g, u):
+    experts, hidden, width = w_down.shape
+    count, places, columns = pick.shape[2], prob.shape[2], prob.shape[3]
+    rows = 2 * places
+    args = (*own, *other, pick, put, prob, mine, w_down, g, u)
+    shapes = [
+        bf16(2, experts, places, width),
+        bf16(experts, rows, hidden),
+        bf16(experts, rows, hidden),
+        bf16(experts, hidden, rows),
+        bf16(experts, hidden, rows),
+        bf16(2, count, columns),
+    ]
+    ins = [whole(a) for a in args[:-3]] + [each(w_down), each(g), each(u)]
+    outs = [pl.BlockSpec(memory_space=pl.ANY)]
+    outs += [each(s) for s in shapes[1:5]] + [whole(shapes[5])]
+    scratch = [
+        pltpu.VMEM((2, count, width), jnp.bfloat16),
+        pltpu.VMEM((2, experts, places, width), jnp.bfloat16),
+        pltpu.VMEM((2, experts, places, columns), jnp.bfloat16),
+        pltpu.SemaphoreType.DMA,
+    ]
+    flops = 2 * experts * rows * hidden * width + 2 * experts * rows * count * width
+    return call(slope_kernel, experts, ins, args, outs, shapes, scratch, flops)
+
+
+def back_call(put, lefts, rights, start, stop, extra=None):
+    experts, hidden, _ = rights[0].shape
+    rows = lefts[0].shape[1]
+    count = put.shape[1]
+    terms = len(lefts)
+    first, steps = start // CHUNK, (stop - start) // CHUNK
+    columns = stop - start + (0 if extra is None else extra.shape[2])
+    args = (put, *lefts, *rights) + (() if extra is None else (extra,))
+    shapes = [bf16(count, columns)] * 2
+    ins = [whole(put)] + [whole(a) for a in lefts]
+    last = first + steps - 1
+    ins += [
+        pl.BlockSpec((experts, hidden, CHUNK), lambda i: (0, 0, jnp.minimum(first + i, last)))
+    ] * terms
+    ins += [] if extra is None else [whole(extra)]
+    outs = [pl.BlockSpec((count, CHUNK), lambda i: (0, i))] * 2
+    scratch = [pltpu.VMEM((2, put.shape[2], CHUNK), jnp.bfloat16)]
+    flops = 2 * experts * rows * (stop - start) * (hidden * terms + count)
+    kernel = functools.partial(back_kernel, terms, steps)
+    grid = steps + (0 if extra is None else 1)
+    return call(kernel, grid, ins, args, outs, shapes, scratch, flops)
+
+
+def grad_call(x, left):
+    _, experts, places, width = x.shape
+    hidden = left.shape[1]
+    shape = bf16(experts, hidden, width)
+    ins = [pl.BlockSpec((2, 1, places, width), lambda i: (0, i, 0, 0)), each(left)]
+    flops = 4 * experts * places * hidden * width
+    return call(grad_kernel, experts, ins, (x, left), [each(shape)], [shape], flops=flops)[0]
+
+
+def dense_body(
+    tokens, cotangent, gate_prob, expert_ids, placement, gate_weight, up_weight, down_weight
+):
+    tok_count, width = tokens.shape
+    local = gate_weight.shape[0]
+    total_experts = placement.shape[0]
+    devices = lax.axis_size("dp") * lax.axis_size("expert")
+    places = devices // 2 * CAP
+    count = devices // 2 * tok_count
+    quarter, middle = count // 4, width // 2
+
+    slots = slots_of(expert_ids, placement)
+    used = slots[:, :, None] == jnp.arange(total_experts, dtype=jnp.int32)
+    prob = jnp.sum(jnp.where(used, gate_prob[:, :, None], 0.0), axis=1)
+    high = lax.reduce_precision(prob, 8, 7)
+    extended = jnp.concatenate(
+        [tokens, high.astype(jnp.bfloat16), (prob - high).astype(jnp.bfloat16)], axis=1
+    )
+
+    slot = lax.axis_index("expert") * local + jnp.arange(local * places, dtype=jnp.int32) // places
+    spots = jnp.arange(2 * total_experts, dtype=jnp.int32)
+    mine = (slot[:, None] == spots[None, :]).astype(jnp.bfloat16)
+    both = (slot[:, None] == spots[None, :] % total_experts).astype(jnp.float32)
+    maps = ((slot[None, :] == spots[:, None]).astype(jnp.bfloat16), mine, both)
+
+    near, far = swap(extended, Z1), swap(extended, Z2)
+    cotangent, near, far = together(cotangent, near, far)
+    own, other = [], []
+    for rows in (extended, jnp.concatenate([near, far]), swap(far, Z1)):
+        rows = jnp.concatenate([rows, swap(rows, X, Y)])
+        rows = jnp.concatenate([rows, swap(rows, Y, X)])
+        own.append(rows)
+        other.append(swap(rows, CORE))
+
+    grads = jnp.concatenate([cotangent] + [swap(cotangent, bit) for bit in (Z1, Z2, Z3)])
+    grads = jnp.concatenate([grads, swap(grads, X, Y)])
+    *rows, grads = together(*own, *other, grads)
+    far_grads = swap(grads, Y, X)
+    grads_other = swap(grads, CORE)
+
+    x, put, pick, prob_rows, g, u, h, ht = up_call(
+        rows[:3], rows[3:], maps, gate_weight, up_weight, tok_count
+    )
+    h, far_grads = together(h, far_grads)
+    far_grads_other = swap(far_grads, CORE)
+
+    sums, sums_other = back_call(put, [h], [down_weight], 0, width)
+    sums = add(sums, swap(sums_other, CORE))
+    sums, far_grads_other = together(sums, far_grads_other)
+    from_second = swap(sums[2 * quarter :], Y, X)
+
+    c, dg, du, dgt, dut, share = slope_call(
+        (grads, far_grads),
+        (grads_other, far_grads_other),
+        pick,
+        put,
+        prob_rows,
+        mine.reshape(local, places, -1),
+        down_weight,
+        g,
+        u,
+    )
+    weights = [gate_weight, up_weight]
+    left, left_other = back_call(put, [dg, du], weights, 0, middle)
+    from_left = swap(left_other, CORE)
+    from_second, left, dg, du = together(from_second, left, dg, du)
+    sums = add(sums[: 2 * quarter], from_second)
+    sums, dg, du = together(sums, dg, du)
+    from_first = swap(sums[quarter:], X, Y)
+    right, right_other = back_call(put, [dg, du], weights, middle, width, share)
+
+    from_right = swap(right_other, CORE)
+    from_left, right = together(from_left, right)
+    left = add(left, from_left)
+    left, ht = together(left, ht)
+    from_left = swap(left[2 * quarter :], Y, X)
+    down_weight_grad = grad_call(c, ht)
+
+    from_right, from_first, down_weight_grad = together(from_right, from_first, down_weight_grad)
+    right = add(right, from_right)
+    sums = add(sums[:quarter], from_first)
+    right, sums, dgt = together(right, sums, dgt)
+    from_right = swap(right[2 * quarter :], Y, X)
+
+    def over_z(values):
+        parts = [values[i * tok_count : (i + 1) * tok_count] for i in range(4)]
+        return parts[:1] + [swap(part, bit) for part, bit in zip(parts[1:], (Z1, Z2, Z3))]
+
+    mixed = over_z(sums)
+    gate_weight_grad = grad_call(x, dgt)
+
+    from_left, gate_weight_grad = together(from_left, gate_weight_grad)
+    left = add(left[: 2 * quarter], from_left)
+    left, dut = together(left, dut)
+    from_left = swap(left[quarter:], X, Y)
+    up_weight_grad = grad_call(x, dut)
+
+    from_right, up_weight_grad = together(from_right, up_weight_grad)
+    right = add(right[: 2 * quarter], from_right)
+    from_right = swap(right[quarter:], X, Y)
+    left = over_z(add(left[:quarter], from_left))
+    right = add(*over_z(add(right[:quarter], from_right)))
+    token_grad = jnp.concatenate([add(*left), right[:, : width - middle]], axis=1)
+    share = right[:, width - middle : width - middle + total_experts].astype(jnp.float32)
+    gate_grad = jnp.sum(jnp.where(used, share[:, None, :], 0.0), axis=2)
+    return (add(*mixed), token_grad, gate_grad, gate_weight_grad, up_weight_grad, down_weight_grad)
+
+
+def routed_body(tokens, cotangent, gate_prob, expert_ids, placement, gate_weight, up_weight, down_weight):
     tok_count, model_width = tokens.shape
     top_count = expert_ids.shape[1]
     expert_devs = lax.axis_size("expert")
@@ -100,6 +514,14 @@
     return (mixed, token_grad, gate_grad, gate_grad_w, up_grad_w, down_grad)
 
 
+def body(*args):
+    tokens, gate_weight = args[0], args[5]
+    mesh_fits = (lax.axis_size("dp"), lax.axis_size("expert")) == (4, 8)
+    if mesh_fits and tokens.shape[0] <= gate_weight.shape[0] * CAP:
+        return dense_body(*args)
+    return routed_body(*args)
+
+
 def solution(mesh):
     return jax.shard_map(
         body,

time: 602 us -> 200 us (0.33)
  waiting for transfers between devices: 348 us -> 43 us
  matrix products: 99.7 us -> 0 us
  Pallas kernels: 0 us -> 96.5 us
  blocking collectives: 84.2 us -> 0 us
  starting transfers between devices: 8.76 us -> 43.7 us
  local copies, waits for them, and re-layouts: 39 us -> 5.33 us
  between operations: 14.4 us -> 1.14 us
  other arithmetic: 2.54 us -> 9.09 us
    unnamed x4 -> x0, waiting for transfers between devices: 228 us -> none
    dot_general x13 -> x0, matrix products: 99.7 us -> none  [the longest x1 12.7 us: body(): jnp.einsum('asjcf,jfd->asjcd', d_gate_pre, gate_weight, preferred_element...]
    pallas_call x0 -> x8, Pallas kernels: none -> 96.5 us  [call(): pl.pallas_call(kernel, grid=(grid,), in_specs=ins, out_specs=outs, out_sh...]
    all_to_all x2 -> x0, blocking collectives: 84.2 us -> none  [the longest x1 44 us: body(): lax.all_to_all(sent_rows, 'expert', split_axis=1, concat_axis=1, tiled=True)]
    all_gather x2 -> x0, waiting for transfers between devices: 83.9 us -> none  [the longest x1 64 us: body(): lax.all_gather(got_grads, 'dp', axis=0, tiled=True)]
    ppermute x0 -> x37, starting transfers between devices: none -> 43.7 us  [swap(): return lax.ppermute(values, AXES, pairs)]
    ppermute x0 -> x37, waiting for transfers between devices: none -> 43 us  [swap(): return lax.ppermute(values, AXES, pairs)]
    all_to_all x2 -> x0, waiting for transfers between devices: 35.5 us -> none  [the longest x1 22.6 us: body(): lax.all_to_all(summed[0].astype(jnp.bfloat16), 'expert', split_axis=1, co...]
  transfers between devices with their start and end apart: 5 -> 37, of which waited for: 5 -> 14; matrix products, arithmetic and copies ran while one was open for 12% -> 4% of each run, Pallas kernels for 0% -> 43%
where the time goes in v2:
time: 200 us; the launch traced here: 199 us
  Pallas kernels  96.5 us (48%)
  starting transfers between devices  43.7 us (22%)
  waiting for transfers between devices  43 us (22%)
  other arithmetic  9.09 us (5%)
  local copies, waits for them, and re-layouts  5.33 us (3%)
    pallas_call x8, Pallas kernels, call(): pl.pallas_call(kernel, grid=(grid,), in_specs=ins, out_specs=outs, out_sh...  96.5 us
    ppermute x37, starting transfers between devices, swap(): return lax.ppermute(values, AXES, pairs)  43.7 us
    ppermute x37, waiting for transfers between devices, swap(): return lax.ppermute(values, AXES, pairs)  43 us
    convert_element_type x12, other arithmetic, add(): return total.astype(jnp.bfloat16)  4.61 us
  transfers between devices with their start and end apart: 37, of which 14 were waited for; matrix products, arithmetic and copies ran while one was open for 4% of the time, Pallas kernels for 43%

profile of v2, /device:TPU:0, one launch (start us, length us, event | category | flops | bytes accessed | tf_op | source)
XLA Modules:
  0.0 198.8 jit_solution(10930557377187846121)
XLA Ops:
  4.4 3.0 %collective-permute-start.2 = (bf16[16,4224]{1,0:T(8,128)(2,1)S(1)}, bf16[16,4224]{1,0:T(8,128)(2,1)S(1)}, u32[]{:S(2)}, u32[]{:S(2)}) collective-permute-start(bf16[16,4224]{1,0:T(8,128)(2,1)S(1)} %concatenate.38), channel_id=1, source_target_pairs={{0,2},{1,3},{2,0},{3,1},{4,6},{5,7},{6,4},{7,5},{8,10},{9,11},{10,... | collective-permute-start | bytes 405512 | tf_op jit(solution)/shard_map/ppermute | solution.py:30
  7.4 2.6 %collective-permute-start.3 = (bf16[16,4224]{1,0:T(8,128)(2,1)S(1)}, bf16[16,4224]{1,0:T(8,128)(2,1)S(1)}, u32[]{:S(2)}, u32[]{:S(2)}) collective-permute-start(bf16[16,4224]{1,0:T(8,128)(2,1)S(1)} %concatenate.38), channel_id=1, source_target_pairs={{0,4},{1,5},{2,6},{3,7},{4,0},{5,1},{6,2},{7,3},{8,12},{9,13},{10,... | collective-permute-start | bytes 405512 | tf_op jit(solution)/shard_map/ppermute | solution.py:30
  13.0 3.3 %collective-permute-done.3 = bf16[16,4224]{1,0:T(8,128)(2,1)S(1)} collective-permute-done((bf16[16,4224]{1,0:T(8,128)(2,1)S(1)}, bf16[16,4224]{1,0:T(8,128)(2,1)S(1)}, u32[]{:S(2)}, u32[]{:S(2)}) %collective-permute-start.3) | collective-permute-done | bytes 135200 | tf_op jit(solution)/shard_map/ppermute | solution.py:30
  16.8 2.6 %collective-permute-start.13 = (bf16[16,4096]{1,0:T(8,128)(2,1)}, bf16[16,4096]{1,0:T(8,128)(2,1)S(1)}, u32[]{:S(2)}, u32[]{:S(2)}) collective-permute-start(bf16[16,4096]{1,0:T(8,128)(2,1)} %param.9), channel_id=1, source_target_pairs={{0,4},{1,5},{2,6},{3,7},{4,0},{5,1},{6,2},{7,3},{8,12},{9,13},{10,... | collective-permute-start | bytes 393224 | tf_op jit(solution)/shard_map/ppermute | solution.py:30
  19.5 1.8 collective-permute-start.14
  26.7 3.4 %collective-permute-done.14 = bf16[16,4096]{1,0:T(8,128)(2,1)S(1)} collective-permute-done((bf16[16,4096]{1,0:T(8,128)(2,1)S(1)}, bf16[16,4096]{1,0:T(8,128)(2,1)S(1)}, u32[]{:S(2)}, u32[]{:S(2)}) %collective-permute-start.14) | collective-permute-done | bytes 131104 | tf_op jit(solution)/shard_map/ppermute | solution.py:30
  32.5 1.6 collective-permute-start.5
  34.1 13.9 %collective-permute-done.7 = bf16[16,4224]{1,0:T(8,128)(2,1)S(1)} collective-permute-done((bf16[16,4224]{1,0:T(8,128)(2,1)S(1)}, bf16[16,4224]{1,0:T(8,128)(2,1)S(1)}, u32[]{:S(2)}, u32[]{:S(2)}) %collective-permute-start.7) | collective-permute-done | bytes 135200 | tf_op jit(solution)/shard_map/ppermute | solution.py:30
  48.0 1.6 collective-permute-start.8
  50.4 4.1 %collective-permute-done.8 = bf16[32,4224]{1,0:T(8,128)(2,1)S(1)} collective-permute-done((bf16[32,4224]{1,0:T(8,128)(2,1)S(1)}, bf16[32,4224]{1,0:T(8,128)(2,1)S(1)}, u32[]{:S(2)}, u32[]{:S(2)}) %collective-permute-start.8) | collective-permute-done | bytes 270368 | tf_op jit(solution)/shard_map/ppermute | solution.py:30
  54.8 1.8 collective-permute-done.11.other2
  56.6 1.6 collective-permute-start.16
  59.7 20.7 %shard_map.127 = (bf16[2,8,48,4096]{3,2,1,0:T(8,128)(2,1)}, bf16[2,256,384]{2,1,0:T(8,128)(2,1)}, bf16[2,384,256]{2,1,0:T(8,128)(2,1)}, f32[2,8,48,128]{3,2,1,0:...) custom-call(bf16[64,4224]{1,0:T(8,128)(2,1)} %copy-done, ...), custom_call_target="tpu_custom_call" | custom-call | flops 4026531840 | bytes 39124992 | tf_op jit(solution)/shard_map/pallas_call | solution.py:218
  80.4 11.6 %shard_map.128 = (bf16[256,4096]{1,0:T(8,128)(2,1)}, bf16[256,4096]{1,0:T(8,128)(2,1)}) custom-call(bf16[2,256,384]{2,1,0:T(8,128)(2,1)} %get-tuple-element.72.put_ref, bf16[8,96,192]{2,1,0:T(8,128)(2,1)} %get-tuple-element.76.refs_0_, bf16[8,192,4096]{2,1,0:T(8,128)(2,1)} %down_ref.1), custom_call_target="tpu_custom_call" | custom-call | flops 2818572288 | bytes 17465344 | tf_op jit(solution)/shard_map/pallas_call | solution.py:218
  92.6 6.0 %collective-permute-done.18 = bf16[256,4096]{1,0:T(8,128)(2,1)S(1)} collective-permute-done((bf16[256,4096]{1,0:T(8,128)(2,1)}, bf16[256,4096]{1,0:T(8,128)(2,1)S(1)}, u32[]{:S(2)}, u32[]{:S(2)}) %collective-permute-start.18) | collective-permute-done | bytes 2097184 | tf_op jit(solution)/shard_map/ppermute | solution.py:30
  98.6 2.4 %add_convert_fusion = bf16[256,4096]{1,0:T(8,128)(2,1)S(1)} fusion(bf16[256,4096]{1,0:T(8,128)(2,1)S(1)} %collective-permute-done.18, bf16[256,4096]{1,0:T(8,128)(2,1)} %get-tuple-element.77), kind=kLoop, calls=%fused_computation | loop fusion | flops 4194304 | bytes 6291456 | tf_op jit(solution)/shard_map/convert_element_type | solution.py:37
  103.8 16.0 %shard_map.129 = (bf16[2,8,48,4096]{3,2,1,0:T(8,128)(2,1)}, bf16[8,96,192]{2,1,0:T(8,128)(2,1)}, bf16[8,96,192]{2,1,0:T(8,128)(2,1)}, bf16[8,192,96]{2,1,0:T(8,1...) custom-call(bf16[128,4096]{1,0:T(8,128)(2,1)} %copy-done.2, bf16[128,4096]{1,0:T(8,128)(2,1)} %copy-done.5, ...), custom_call_target="tpu_custom_call" | custom-call | flops 2818572288 | bytes 26836992 | tf_op jit(solution)/shard_map/pallas_call | solution.py:218
  119.8 8.3 %shard_map.130 = (bf16[256,2048]{1,0:T(8,128)(2,1)}, bf16[256,2048]{1,0:T(8,128)(2,1)}) custom-call(bf16[2,256,384]{2,1,0:T(8,128)(2,1)} %get-tuple-element.72.put_ref, bf16[8,96,192]{2,1,0:T(8,128)(2,1)} %get-tuple-element.92.refs_0_, bf16[8,96,192]{2,1,0:T(8,128)(2,1)} %get-tuple-element.93.refs_1_, bf16[8,192,4096]{2,1,0:T(8,128)(2,1)} %refs_2_.3, ...), custom_call_target="tpu_custom_call" | custom-call | flops 2013265920 | bytes 28246016 | tf_op jit(solution)/shard_map/pallas_call | solution.py:218
  128.8 8.3 %shard_map.131 = (bf16[256,2176]{1,0:T(8,128)(2,1)}, bf16[256,2176]{1,0:T(8,128)(2,1)}) custom-call(bf16[2,256,384]{2,1,0:T(8,128)(2,1)} %get-tuple-element.72.put_ref, bf16[8,96,192]{2,1,0:T(8,128)(2,1)} %get-tuple-element.92.refs_0_, bf16[8,96,192]{2,1,0:T(8,128)(2,1)} %get-tuple-element.93.refs_1_, bf16[8,192,4096]{2,1,0:T(8,128)(2,1)} %refs_2_.3, ...), custom_call_target="tpu_custom_call" | custom-call | flops 2013265920 | bytes 28508160 | tf_op jit(solution)/shard_map/pallas_call | solution.py:218
  138.9 1.6 collective-permute-start.27
  140.5 10.6 %shard_map.132 = bf16[8,192,4096]{2,1,0:T(8,128)(2,1)} custom-call(bf16[2,8,48,4096]{3,2,1,0:T(8,128)(2,1)} %get-tuple-element.99.x_ref, bf16[8,192,96]{2,1,0:T(8,128)(2,1)} %get-tuple-element.103.left), custom_call_target="tpu_custom_call" | custom-call | flops 1207959552 | bytes 19169280 | tf_op jit(solution)/shard_map/pallas_call | solution.py:218
  152.6 10.6 %shard_map.133 = bf16[8,192,4096]{2,1,0:T(8,128)(2,1)} custom-call(bf16[2,8,48,4096]{3,2,1,0:T(8,128)(2,1)} %get-tuple-element.109.x_ref, bf16[8,192,96]{2,1,0:T(8,128)(2,1)} %get-tuple-element.110.left), custom_call_target="tpu_custom_call" | custom-call | flops 1207959552 | bytes 19169280 | tf_op jit(solution)/shard_map/pallas_call | solution.py:218
  163.3 2.6 %collective-permute-start.25 = (bf16[16,4096]{1,0:T(8,128)(2,1)S(1)}, bf16[16,4096]{1,0:T(8,128)(2,1)S(1)}, u32[]{:S(2)}, u32[]{:S(2)}) collective-permute-start(bf16[16,4096]{1,0:T(8,128)(2,1)S(1)} %get-tuple-element.128), channel_id=1, source_target_pairs={{0,4},{1,5},{2,6},{3,7},{4,0},{5,1},{6,2},{7,3},{8,12},{9,13},{10,... | collective-permute-start | bytes 393224 | tf_op jit(solution)/shard_map/ppermute | solution.py:30
  165.9 1.8 collective-permute-start.26
  168.5 1.6 collective-permute-start.32
  170.1 10.6 %shard_map.134 = bf16[8,192,4096]{2,1,0:T(8,128)(2,1)} custom-call(bf16[2,8,48,4096]{3,2,1,0:T(8,128)(2,1)} %get-tuple-element.109.x_ref, bf16[8,192,96]{2,1,0:T(8,128)(2,1)} %get-tuple-element.115.left), custom_call_target="tpu_custom_call" | custom-call | flops 1207959552 | bytes 19169280 | tf_op jit(solution)/shard_map/pallas_call | solution.py:218
  182.3 2.6 %collective-permute-start.30 = (bf16[16,2048]{1,0:T(8,128)(2,1)S(1)}, bf16[16,2048]{1,0:T(8,128)(2,1)S(1)}, u32[]{:S(2)}, u32[]{:S(2)}) collective-permute-start(bf16[16,2048]{1,0:T(8,128)(2,1)S(1)} %get-tuple-element.134), channel_id=1, source_target_pairs={{0,4},{1,5},{2,6},{3,7},{4,0},{5,1},{6,2},{7,3},{8,12},{9,13},{10,... | collective-permute-start | bytes 196616 | tf_op jit(solution)/shard_map/ppermute | solution.py:30
  184.9 1.8 collective-permute-start.31
  186.7 1.6 collective-permute-done.33
  188.5 2.6 %collective-permute-start.35 = (bf16[16,2176]{1,0:T(8,128)(2,1)S(1)}, bf16[16,2176]{1,0:T(8,128)(2,1)S(1)}, u32[]{:S(2)}, u32[]{:S(2)}) collective-permute-start(bf16[16,2176]{1,0:T(8,128)(2,1)S(1)} %get-tuple-element.131), channel_id=1, source_target_pairs={{0,4},{1,5},{2,6},{3,7},{4,0},{5,1},{6,2},{7,3},{8,12},{9,13},{10,... | collective-permute-start | bytes 208904 | tf_op jit(solution)/shard_map/ppermute | solution.py:30
  191.1 1.8 collective-permute-start.36
  194.0 3.2 %collective-permute-done.36 = bf16[16,2176]{1,0:T(8,128)(2,1)S(1)} collective-permute-done((bf16[16,2176]{1,0:T(8,128)(2,1)S(1)}, bf16[16,2176]{1,0:T(8,128)(2,1)S(1)}, u32[]{:S(2)}, u32[]{:S(2)}) %collective-permute-start.36) | collective-permute-done | bytes 69664 | tf_op jit(solution)/shard_map/ppermute | solution.py:30
  (132 shorter events, 30.2 us)
Async XLA Ops:
  4.4 8.6 %collective-permute-start.2 = (bf16[16,4224]{1,0:T(8,128)(2,1)S(1)}, bf16[16,4224]{1,0:T(8,128)(2,1)S(1)}, u32[]{:S(2)}, u32[]{:S(2)}) collective-permute-start(bf16[16,4224]{1,0:T(8,128)(2,1)S(1)} %concatenate.38), channel_id=1, source_target_pairs={{0,2},{1,3},{2,0},{3,1},{4,6},{5,7},{6,4},{7,5},{8,10},{9,11},{10,... | collective-permute-start | bytes 405512 | tf_op jit(solution)/shard_map/ppermute | solution.py:30
  7.4 8.9 %collective-permute-start.3 = (bf16[16,4224]{1,0:T(8,128)(2,1)S(1)}, bf16[16,4224]{1,0:T(8,128)(2,1)S(1)}, u32[]{:S(2)}, u32[]{:S(2)}) collective-permute-start(bf16[16,4224]{1,0:T(8,128)(2,1)S(1)} %concatenate.38), channel_id=1, source_target_pairs={{0,4},{1,5},{2,6},{3,7},{4,0},{5,1},{6,2},{7,3},{8,12},{9,13},{10,... | collective-permute-start | bytes 405512 | tf_op jit(solution)/shard_map/ppermute | solution.py:30
  10.0 11.4 %collective-permute-start = (bf16[16,4224]{1,0:T(8,128)(2,1)S(1)}, bf16[16,4224]{1,0:T(8,128)(2,1)S(1)}, u32[]{:S(2)}, u32[]{:S(2)}) collective-permute-start(bf16[16,4224]{1,0:T(8,128)(2,1)S(1)} %concatenate.38), channel_id=1, source_target_pairs={{0,8},{1,17},{2,10},{3,19},{4,12},{5,21},{6,14},{7,23},{8,0},{9,25... | collective-permute-start | bytes 405512 | tf_op jit(solution)/shard_map/ppermute | solution.py:30
  16.3 7.8 %collective-permute-start.12 = (bf16[16,4096]{1,0:T(8,128)(2,1)}, bf16[16,4096]{1,0:T(8,128)(2,1)S(1)}, u32[]{:S(2)}, u32[]{:S(2)}) collective-permute-start(bf16[16,4096]{1,0:T(8,128)(2,1)} %param.9), channel_id=1, source_target_pairs={{0,2},{1,3},{2,0},{3,1},{4,6},{5,7},{6,4},{7,5},{8,10},{9,11},{10,... | collective-permute-start | bytes 393224 | tf_op jit(solution)/shard_map/ppermute | solution.py:30
  16.8 10.0 %collective-permute-start.13 = (bf16[16,4096]{1,0:T(8,128)(2,1)}, bf16[16,4096]{1,0:T(8,128)(2,1)S(1)}, u32[]{:S(2)}, u32[]{:S(2)}) collective-permute-start(bf16[16,4096]{1,0:T(8,128)(2,1)} %param.9), channel_id=1, source_target_pairs={{0,4},{1,5},{2,6},{3,7},{4,0},{5,1},{6,2},{7,3},{8,12},{9,13},{10,... | collective-permute-start | bytes 393224 | tf_op jit(solution)/shard_map/ppermute | solution.py:30
  19.4 12.4 %collective-permute-start.6 = (bf16[16,4224]{1,0:T(8,128)(2,1)S(1)}, bf16[16,4224]{1,0:T(8,128)(2,1)S(1)}, u32[]{:S(2)}, u32[]{:S(2)}) collective-permute-start(bf16[16,4224]{1,0:T(8,128)(2,1)S(1)} %collective-permute-done.3), channel_id=1, source_target_pairs={{0,2},{1,3},{2,0},{3,1},{4,6},{5,7},{6,4},{7,5},{8,10},{9,11},{10,... | collective-permute-start | bytes 405512 | tf_op jit(solution)/shard_map/ppermute | solution.py:30
  19.5 10.6 %collective-permute-start.14 = (bf16[16,4096]{1,0:T(8,128)(2,1)S(1)}, bf16[16,4096]{1,0:T(8,128)(2,1)S(1)}, u32[]{:S(2)}, u32[]{:S(2)}) collective-permute-start(bf16[16,4096]{1,0:T(8,128)(2,1)S(1)} %copy-done.12), channel_id=1, source_target_pairs={{0,6},{1,7},{2,4},{3,5},{4,2},{5,3},{6,0},{7,1},{8,14},{9,15},{10,... | collective-permute-start | bytes 393224 | tf_op jit(solution)/shard_map/ppermute | solution.py:30
  21.4 11.0 %collective-permute-start.4 = (bf16[32,4224]{1,0:T(8,128)(2,1)S(1)}, bf16[32,4224]{1,0:T(8,128)(2,1)S(1)}, u32[]{:S(2)}, u32[]{:S(2)}) collective-permute-start(bf16[32,4224]{1,0:T(8,128)(2,1)S(1)} %pad_maximum_fusion.4), channel_id=1, source_target_pairs={{0,8},{1,17},{2,10},{3,19},{4,12},{5,21},{6,14},{7,23},{8,0},{9,25... | collective-permute-start | bytes 811016 | tf_op jit(solution)/shard_map/ppermute | solution.py:30
  24.1 25.5 %collective-permute-start.1 = (bf16[32,4224]{1,0:T(8,128)(2,1)S(1)}, bf16[32,4224]{1,0:T(8,128)(2,1)S(1)}, u32[]{:S(2)}, u32[]{:S(2)}) collective-permute-start(bf16[32,4224]{1,0:T(8,128)(2,1)S(1)} %pad_maximum_fusion.3), channel_id=1, source_target_pairs={{0,16},{1,9},{2,18},{3,11},{4,20},{5,13},{6,22},{7,15},{8,24},{9,1... | collective-permute-start | bytes 811016 | tf_op jit(solution)/shard_map/ppermute | solution.py:30
  30.2 24.5 %collective-permute-start.15 = (bf16[64,4096]{1,0:T(8,128)(2,1)S(1)}, bf16[64,4096]{1,0:T(8,128)(2,1)S(1)}, u32[]{:S(2)}, u32[]{:S(2)}) collective-permute-start(bf16[64,4096]{1,0:T(8,128)(2,1)S(1)} %pad_maximum_fusion.2), channel_id=1, source_target_pairs={{0,8},{1,17},{2,10},{3,19},{4,12},{5,21},{6,14},{7,23},{8,0},{9,25... | collective-permute-start | bytes 1572872 | tf_op jit(solution)/shard_map/ppermute | solution.py:30
  31.8 16.2 %collective-permute-start.7 = (bf16[16,4224]{1,0:T(8,128)(2,1)S(1)}, bf16[16,4224]{1,0:T(8,128)(2,1)S(1)}, u32[]{:S(2)}, u32[]{:S(2)}) collective-permute-start(bf16[16,4224]{1,0:T(8,128)(2,1)S(1)} %collective-permute-done.6), channel_id=1, source_target_pairs={{0,8},{1,17},{2,10},{3,19},{4,12},{5,21},{6,14},{7,23},{8,0},{9,25... | collective-permute-start | bytes 405512 | tf_op jit(solution)/shard_map/ppermute | solution.py:30
  32.5 17.3 %collective-permute-start.5 = (bf16[64,4224]{1,0:T(8,128)(2,1)S(1)}, bf16[64,4224]{1,0:T(8,128)(2,1)S(1)}, u32[]{:S(2)}, u32[]{:S(2)}) collective-permute-start(bf16[64,4224]{1,0:T(8,128)(2,1)S(1)} %pad_maximum_fusion.1), channel_id=1, source_target_pairs={{0,16},{1,9},{2,18},{3,11},{4,20},{5,13},{6,22},{7,15},{8,24},{9,1... | collective-permute-start | bytes 1622024 | tf_op jit(solution)/shard_map/ppermute | solution.py:30
  48.0 6.5 %collective-permute-start.8 = (bf16[32,4224]{1,0:T(8,128)(2,1)S(1)}, bf16[32,4224]{1,0:T(8,128)(2,1)S(1)}, u32[]{:S(2)}, u32[]{:S(2)}) collective-permute-start(bf16[32,4224]{1,0:T(8,128)(2,1)S(1)} %pad_maximum_fusion.5), channel_id=1, source_target_pairs={{0,16},{1,9},{2,18},{3,11},{4,20},{5,13},{6,22},{7,15},{8,24},{9,1... | collective-permute-start | bytes 811016 | tf_op jit(solution)/shard_map/ppermute | solution.py:30
  49.9 6.7 %collective-permute-start.10 = (bf16[128,4224]{1,0:T(8,128)(2,1)S(1)}, bf16[128,4224]{1,0:T(8,128)(2,1)S(1)}, u32[]{:S(2)}, u32[]{:S(2)}) collective-permute-start(bf16[128,4224]{1,0:T(8,128)(2,1)S(1)} %constant_dynamic-update-slice_fusion.own1), channel_id=1, source_target_pairs={{0,1},{1,0},{2,3},{3,2},{4,5},{5,4},{6,7},{7,6},{8,9},{9,8},{10,11... | collective-permute-start | bytes 3244040 | tf_op jit(solution)/shard_map/ppermute | solution.py:30
  56.6 23.8 %collective-permute-start.16 = (bf16[128,4096]{1,0:T(8,128)(2,1)S(1)}, bf16[128,4096]{1,0:T(8,128)(2,1)S(1)}, u32[]{:S(2)}, u32[]{:S(2)}) collective-permute-start(bf16[128,4096]{1,0:T(8,128)(2,1)S(1)} %constant_dynamic-update-slice_fusion.7.own0), channel_id=1, source_target_pairs={{0,16},{1,9},{2,18},{3,11},{4,20},{5,13},{6,22},{7,15},{8,24},{9,1... | collective-permute-start | bytes 3145736 | tf_op jit(solution)/shard_map/ppermute | solution.py:30
  92.0 6.6 %collective-permute-start.18 = (bf16[256,4096]{1,0:T(8,128)(2,1)}, bf16[256,4096]{1,0:T(8,128)(2,1)S(1)}, u32[]{:S(2)}, u32[]{:S(2)}) collective-permute-start(bf16[256,4096]{1,0:T(8,128)(2,1)} %get-tuple-element.78), channel_id=1, source_target_pairs={{0,1},{1,0},{2,3},{3,2},{4,5},{5,4},{6,7},{7,6},{8,9},{9,8},{10,11... | collective-permute-start | bytes 6291464 | tf_op jit(solution)/shard_map/ppermute | solution.py:30
  92.0 10.9 %collective-permute-start.17 = (bf16[128,4096]{1,0:T(8,128)(2,1)S(1)}, bf16[128,4096]{1,0:T(8,128)(2,1)S(1)}, u32[]{:S(2)}, u32[]{:S(2)}) collective-permute-start(bf16[128,4096]{1,0:T(8,128)(2,1)S(1)} %constant_dynamic-update-slice_fusion.7.own0), channel_id=1, source_target_pairs={{0,1},{1,0},{2,3},{3,2},{4,5},{5,4},{6,7},{7,6},{8,9},{9,8},{10,11... | collective-permute-start | bytes 3145736 | tf_op jit(solution)/shard_map/ppermute | solution.py:30
  92.5 8.5 %collective-permute-start.19 = (bf16[128,4096]{1,0:T(8,128)(2,1)S(1)}, bf16[128,4096]{1,0:T(8,128)(2,1)S(1)}, u32[]{:S(2)}, u32[]{:S(2)}) collective-permute-start(bf16[128,4096]{1,0:T(8,128)(2,1)S(1)} %collective-permute-done.16.own1), channel_id=1, source_target_pairs={{0,1},{1,0},{2,3},{3,2},{4,5},{5,4},{6,7},{7,6},{8,9},{9,8},{10,11... | collective-permute-start | bytes 3145736 | tf_op jit(solution)/shard_map/ppermute | solution.py:30
  101.1 27.4 %collective-permute-start.21 = (bf16[128,4096]{1,0:T(8,128)(2,1)S(1)}, bf16[128,4096]{1,0:T(8,128)(2,1)S(1)}, u32[]{:S(2)}, u32[]{:S(2)}) collective-permute-start(bf16[128,4096]{1,0:T(8,128)(2,1)S(1)} %slice.79), channel_id=1, source_target_pairs={{0,16},{1,9},{2,18},{3,11},{4,20},{5,13},{6,22},{7,15},{8,24},{9,1... | collective-permute-start | bytes 3145736 | tf_op jit(solution)/shard_map/ppermute | solution.py:30
  128.1 9.2 %collective-permute-start.20 = (bf16[256,2048]{1,0:T(8,128)(2,1)}, bf16[256,2048]{1,0:T(8,128)(2,1)S(1)}, u32[]{:S(2)}, u32[]{:S(2)}) collective-permute-start(bf16[256,2048]{1,0:T(8,128)(2,1)} %get-tuple-element.86), channel_id=1, source_target_pairs={{0,1},{1,0},{2,3},{3,2},{4,5},{5,4},{6,7},{7,6},{8,9},{9,8},{10,11... | collective-permute-start | bytes 3145736 | tf_op jit(solution)/shard_map/ppermute | solution.py:30
  137.1 14.5 %collective-permute-start.22 = (bf16[256,2176]{1,0:T(8,128)(2,1)}, bf16[256,2176]{1,0:T(8,128)(2,1)S(1)}, u32[]{:S(2)}, u32[]{:S(2)}) collective-permute-start(bf16[256,2176]{1,0:T(8,128)(2,1)} %get-tuple-element.97), channel_id=1, source_target_pairs={{0,1},{1,0},{2,3},{3,2},{4,5},{5,4},{6,7},{7,6},{8,9},{9,8},{10,11... | collective-permute-start | bytes 3342344 | tf_op jit(solution)/shard_map/ppermute | solution.py:30
  137.3 14.3 %collective-permute-start.23 = (bf16[64,4096]{1,0:T(8,128)(2,1)S(1)}, bf16[64,4096]{1,0:T(8,128)(2,1)S(1)}, u32[]{:S(2)}, u32[]{:S(2)}) collective-permute-start(bf16[64,4096]{1,0:T(8,128)(2,1)S(1)} %slice.80), channel_id=1, source_target_pairs={{0,8},{1,17},{2,10},{3,19},{4,12},{5,21},{6,14},{7,23},{8,0},{9,25... | collective-permute-start | bytes 1572872 | tf_op jit(solution)/shard_map/ppermute | solution.py:30
  138.9 24.3 %collective-permute-start.27 = (bf16[128,2048]{1,0:T(8,128)(2,1)S(1)}, bf16[128,2048]{1,0:T(8,128)(2,1)S(1)}, u32[]{:S(2)}, u32[]{:S(2)}) collective-permute-start(bf16[128,2048]{1,0:T(8,128)(2,1)S(1)} %slice.87), channel_id=1, source_target_pairs={{0,16},{1,9},{2,18},{3,11},{4,20},{5,13},{6,22},{7,15},{8,24},{9,1... | collective-permute-start | bytes 1572872 | tf_op jit(solution)/shard_map/ppermute | solution.py:30
  163.2 17.4 %collective-permute-start.24 = (bf16[16,4096]{1,0:T(8,128)(2,1)S(1)}, bf16[16,4096]{1,0:T(8,128)(2,1)S(1)}, u32[]{:S(2)}, u32[]{:S(2)}) collective-permute-start(bf16[16,4096]{1,0:T(8,128)(2,1)S(1)} %get-tuple-element.126), channel_id=1, source_target_pairs={{0,2},{1,3},{2,0},{3,1},{4,6},{5,7},{6,4},{7,5},{8,10},{9,11},{10,... | collective-permute-start | bytes 393224 | tf_op jit(solution)/shard_map/ppermute | solution.py:30
  163.3 17.4 %collective-permute-start.25 = (bf16[16,4096]{1,0:T(8,128)(2,1)S(1)}, bf16[16,4096]{1,0:T(8,128)(2,1)S(1)}, u32[]{:S(2)}, u32[]{:S(2)}) collective-permute-start(bf16[16,4096]{1,0:T(8,128)(2,1)S(1)} %get-tuple-element.128), channel_id=1, source_target_pairs={{0,4},{1,5},{2,6},{3,7},{4,0},{5,1},{6,2},{7,3},{8,12},{9,13},{10,... | collective-permute-start | bytes 393224 | tf_op jit(solution)/shard_map/ppermute | solution.py:30
  165.9 14.8 %collective-permute-start.26 = (bf16[16,4096]{1,0:T(8,128)(2,1)S(1)}, bf16[16,4096]{1,0:T(8,128)(2,1)S(1)}, u32[]{:S(2)}, u32[]{:S(2)}) collective-permute-start(bf16[16,4096]{1,0:T(8,128)(2,1)S(1)} %get-tuple-element.127), channel_id=1, source_target_pairs={{0,6},{1,7},{2,4},{3,5},{4,2},{5,3},{6,0},{7,1},{8,14},{9,15},{10,... | collective-permute-start | bytes 393224 | tf_op jit(solution)/shard_map/ppermute | solution.py:30
  167.8 13.6 %collective-permute-start.28 = (bf16[64,2048]{1,0:T(8,128)(2,1)S(1)}, bf16[64,2048]{1,0:T(8,128)(2,1)S(1)}, u32[]{:S(2)}, u32[]{:S(2)}) collective-permute-start(bf16[64,2048]{1,0:T(8,128)(2,1)S(1)} %slice.89), channel_id=1, source_target_pairs={{0,8},{1,17},{2,10},{3,19},{4,12},{5,21},{6,14},{7,23},{8,0},{9,25... | collective-permute-start | bytes 786440 | tf_op jit(solution)/shard_map/ppermute | solution.py:30
  168.5 13.0 %collective-permute-start.32 = (bf16[128,2176]{1,0:T(8,128)(2,1)S(1)}, bf16[128,2176]{1,0:T(8,128)(2,1)S(1)}, u32[]{:S(2)}, u32[]{:S(2)}) collective-permute-start(bf16[128,2176]{1,0:T(8,128)(2,1)S(1)} %slice.95), channel_id=1, source_target_pairs={{0,16},{1,9},{2,18},{3,11},{4,20},{5,13},{6,22},{7,15},{8,24},{9,1... | collective-permute-start | bytes 1671176 | tf_op jit(solution)/shard_map/ppermute | solution.py:30
  181.7 6.6 %collective-permute-start.33 = (bf16[64,2176]{1,0:T(8,128)(2,1)S(1)}, bf16[64,2176]{1,0:T(8,128)(2,1)S(1)}, u32[]{:S(2)}, u32[]{:S(2)}) collective-permute-start(bf16[64,2176]{1,0:T(8,128)(2,1)S(1)} %slice.109), channel_id=1, source_target_pairs={{0,8},{1,17},{2,10},{3,19},{4,12},{5,21},{6,14},{7,23},{8,0},{9,25... | collective-permute-start | bytes 835592 | tf_op jit(solution)/shard_map/ppermute | solution.py:30
  182.2 8.8 %collective-permute-start.29 = (bf16[16,2048]{1,0:T(8,128)(2,1)S(1)}, bf16[16,2048]{1,0:T(8,128)(2,1)S(1)}, u32[]{:S(2)}, u32[]{:S(2)}) collective-permute-start(bf16[16,2048]{1,0:T(8,128)(2,1)S(1)} %get-tuple-element.132), channel_id=1, source_target_pairs={{0,2},{1,3},{2,0},{3,1},{4,6},{5,7},{6,4},{7,5},{8,10},{9,11},{10,... | collective-permute-start | bytes 196616 | tf_op jit(solution)/shard_map/ppermute | solution.py:30
  182.3 10.5 %collective-permute-start.30 = (bf16[16,2048]{1,0:T(8,128)(2,1)S(1)}, bf16[16,2048]{1,0:T(8,128)(2,1)S(1)}, u32[]{:S(2)}, u32[]{:S(2)}) collective-permute-start(bf16[16,2048]{1,0:T(8,128)(2,1)S(1)} %get-tuple-element.134), channel_id=1, source_target_pairs={{0,4},{1,5},{2,6},{3,7},{4,0},{5,1},{6,2},{7,3},{8,12},{9,13},{10,... | collective-permute-start | bytes 196616 | tf_op jit(solution)/shard_map/ppermute | solution.py:30
  184.9 7.9 %collective-permute-start.31 = (bf16[16,2048]{1,0:T(8,128)(2,1)S(1)}, bf16[16,2048]{1,0:T(8,128)(2,1)S(1)}, u32[]{:S(2)}, u32[]{:S(2)}) collective-permute-start(bf16[16,2048]{1,0:T(8,128)(2,1)S(1)} %get-tuple-element.133), channel_id=1, source_target_pairs={{0,6},{1,7},{2,4},{3,5},{4,2},{5,3},{6,0},{7,1},{8,14},{9,15},{10,... | collective-permute-start | bytes 196616 | tf_op jit(solution)/shard_map/ppermute | solution.py:30
  (18 other events, 128.4 us)

commit v3 on v2

--- a/solution.py
+++ b/solution.py
@@ -55,16 +55,19 @@
     return lax.broadcasted_iota(jnp.int32, shape, axis)
 
 
-def fetch(x_ref, e):
-    return jnp.concatenate([x_ref[0, e], x_ref[1, e]], axis=0)
+def expert_copy(source, held, sems, e):
+    return pltpu.make_async_copy(source.at[e], held.at[e], sems.at[e])
 
 
 def dispatch(pick, rows_ref, half, x_ref):
-    experts, places, width = x_ref.shape[1:]
+    experts, both, width = x_ref.shape
+    places = both // 2
     for at in range(0, width, CHUNK):
         rows = dot(pick, rows_ref[half, :, at : at + CHUNK]).astype(jnp.bfloat16)
         for e in range(experts):
-            x_ref[half, e, :, at : at + CHUNK] = rows[e * places : (e + 1) * places]
+            x_ref[e, half * places : (half + 1) * places, at : at + CHUNK] = rows[
+                e * places : (e + 1) * places
+            ]
 
 
 def join_groups(pieces, rows_ref, half, tok_count):
@@ -77,13 +80,17 @@
 
 def up_kernel(tok_count, own0, own1, own2, other0, other1, other2, mine_ref, mine_t_ref, both_t_ref,
               gate_ref, up_ref, x_out, put_ref, pick_ref, prob_ref, g_ref, u_ref, h_ref, ht_ref,
-              rows_ref, x_ref, sem):
+              rows_ref, x_ref, held_ref, held_sems, sem):
     e = pl.program_id(0)
-    experts, places, width = x_ref.shape[1:]
+    experts, both, width = x_ref.shape
+    places = both // 2
     count = rows_ref.shape[1]
 
     @pl.when(e == 0)
     def _():
+        for i in range(experts):
+            expert_copy(gate_ref, held_ref.at[0], held_sems.at[0], i).start()
+            expert_copy(up_ref, held_ref.at[1], held_sems.at[1], i).start()
         join_groups((own0, own1, own2), rows_ref, 0, tok_count)
         join_groups((other0, other1, other2), rows_ref, 1, tok_count)
         row, col = iota((count, count), 0), iota((count, count), 1)
@@ -106,17 +113,19 @@
             weight = jnp.sum(dot(pick, prob) * both_t_ref[...], axis=1, keepdims=True)
             weight = jnp.broadcast_to(weight, (experts * places, columns))
             for i in range(experts):
-                prob_ref[half, i] = weight[i * places : (i + 1) * places]
+                prob_ref[i, half * places : (half + 1) * places] = weight[i * places : (i + 1) * places]
             dispatch(pick, rows_ref, half, x_ref)
         pltpu.make_async_copy(x_ref, x_out, sem).start()
 
-    rows = fetch(x_ref, e)
-    g = dot(rows, gate_ref[0], NT)
-    u = dot(rows, up_ref[0], NT)
+    rows = x_ref[e]
+    expert_copy(gate_ref, held_ref.at[0], held_sems.at[0], e).wait()
+    g = dot(rows, held_ref[0, e], NT)
+    expert_copy(up_ref, held_ref.at[1], held_sems.at[1], e).wait()
+    u = dot(rows, held_ref[1, e], NT)
     g_ref[0] = g
     u_ref[0] = u
     silu_v, _ = gated(g)
-    scaled = silu_v * u * fetch(prob_ref, e)[:, :1]
+    scaled = silu_v * u * prob_ref[e][:, :1]
     h_ref[0] = scaled.astype(jnp.bfloat16)
     ht_ref[0] = scaled.T.astype(jnp.bfloat16)
 
@@ -126,12 +135,16 @@
 
 
 def slope_kernel(own0, own1, other0, other1, pick_ref, put_ref, prob_ref, mine_ref, down_ref, g_ref, u_ref,
-                 x_out, dg_ref, du_ref, dgt_ref, dut_ref, share_ref, rows_ref, x_ref, terms_ref, sem):
+                 x_out, dg_ref, du_ref, dgt_ref, dut_ref, share_ref, rows_ref, x_ref, terms_ref,
+                 held_ref, held_sems, sem):
     e = pl.program_id(0)
-    places = x_ref.shape[2]
+    experts = x_ref.shape[0]
+    places = x_ref.shape[1] // 2
 
     @pl.when(e == 0)
     def _():
+        for i in range(experts):
+            expert_copy(down_ref, held_ref, held_sems, i).start()
         for half, pieces in enumerate(((own0, own1), (other0, other1))):
             size = own0.shape[0]
             rows_ref[half, :size] = pieces[0][...]
@@ -139,14 +152,15 @@
             dispatch(pick_ref[half], rows_ref, half, x_ref)
         pltpu.make_async_copy(x_ref, x_out, sem).start()
 
-    plain = dot(fetch(x_ref, e), down_ref[0], NT)
+    expert_copy(down_ref, held_ref, held_sems, e).wait()
+    plain = dot(x_ref[e], held_ref[e], NT)
     g, u = g_ref[0], u_ref[0]
     silu_v, slope = gated(g)
     share = jnp.sum(silu_v * u * plain, axis=1, keepdims=True)
     for half in range(2):
         part = share[half * places : (half + 1) * places] * mine_ref[e].astype(jnp.float32)
         terms_ref[half, e] = part.astype(jnp.bfloat16)
-    scaled = plain * fetch(prob_ref, e)[:, :1]
+    scaled = plain * prob_ref[e][:, :1]
     dg = scaled * u * slope
     du = scaled * silu_v
     dg_ref[0] = dg.astype(jnp.bfloat16)
@@ -162,18 +176,31 @@
         pltpu.make_async_copy(x_ref, x_out, sem).wait()
 
 
-def back_kernel(terms, steps, put_ref, *refs):
+def back_kernel(terms, start, steps, put_ref, *refs):
     lefts, rights = refs[:terms], refs[terms : 2 * terms]
-    extra_ref = refs[2 * terms] if len(refs) > 2 * terms + 3 else None
-    own_ref, other_ref, rows_ref = refs[-3:]
+    extra_ref = refs[2 * terms] if len(refs) > 2 * terms + 5 else None
+    own_ref, other_ref, rows_ref, held_ref, sems = refs[-5:]
     experts, places = rights[0].shape[0], put_ref.shape[2] // rights[0].shape[0]
-
-    @pl.when(pl.program_id(0) < steps)
+    step = pl.program_id(0)
+
+    def copy(i, at):
+        columns = pl.ds(pl.multiple_of(start + at * CHUNK, CHUNK), CHUNK)
+        return pltpu.make_async_copy(rights[i].at[:, :, columns], held_ref.at[i, at], sems.at[i, at])
+
+    @pl.when(step == 0)
     def _():
+        for at in range(steps):
+            for i in range(terms):
+                copy(i, at).start()
+
+    @pl.when(step < steps)
+    def _():
+        for i in range(terms):
+            copy(i, step).wait()
         for e in range(experts):
-            rows = dot(lefts[0][e], rights[0][e])
-            for left, right in zip(lefts[1:], rights[1:]):
-                rows = rows + dot(left[e], right[e])
+            rows = dot(lefts[0][e], held_ref[0, step, e])
+            for i in range(1, terms):
+                rows = rows + dot(lefts[i][e], held_ref[i, step, e])
             rows = rows.astype(jnp.bfloat16)
             for half in range(2):
                 rows_ref[half, e * places : (e + 1) * places] = rows[half * places : (half + 1) * places]
@@ -182,20 +209,27 @@
 
     if extra_ref is not None:
 
-        @pl.when(pl.program_id(0) == steps)
+        @pl.when(step == steps)
         def _():
             columns = extra_ref.shape[2]
             own_ref[:, :columns] = extra_ref[0]
             other_ref[:, :columns] = extra_ref[1]
 
 
-def grad_kernel(x_ref, left, out):
-    rows = jnp.concatenate([x_ref[0, 0], x_ref[1, 0]], axis=0)
-    for at in range(0, rows.shape[1], CHUNK):
-        out[0, :, at : at + CHUNK] = dot(left[0], rows[:, at : at + CHUNK]).astype(jnp.bfloat16)
+def grad_kernel(x_ref, *refs):
+    count = len(refs) // 2
+    for at in range(0, x_ref.shape[2], CHUNK):
+        rows = x_ref[0, :, at : at + CHUNK]
+        for left, out in zip(refs[:count], refs[count:]):
+            out[0, :, at : at + CHUNK] = dot(left[0], rows).astype(jnp.bfloat16)
 
 
 def whole(a):
+    shape = a.shape
+    return pl.BlockSpec(shape, lambda i: (0,) * len(shape), pipeline_mode=pl.Buffered(1))
+
+
+def kept(a):
     shape = a.shape
     return pl.BlockSpec(shape, lambda i: (0,) * len(shape))
 
@@ -236,21 +270,23 @@
     rows = 2 * places
     args = (*own, *other, *maps, w_gate, w_up)
     shapes = [
-        bf16(2, experts, places, width),
+        bf16(experts, rows, width),
         bf16(2, count, experts * places),
         bf16(2, experts * places, count),
-        f32(2, experts, places, columns),
+        f32(experts, rows, columns),
         f32(experts, rows, hidden),
         f32(experts, rows, hidden),
         bf16(experts, rows, hidden),
         bf16(experts, hidden, rows),
     ]
-    ins = [whole(a) for a in args[:-2]] + [each(w_gate), each(w_up)]
+    ins = [whole(a) for a in args[:-2]] + [pl.BlockSpec(memory_space=pl.ANY)] * 2
     outs = [pl.BlockSpec(memory_space=pl.ANY)]
-    outs += [whole(s) for s in shapes[1:4]] + [each(s) for s in shapes[4:]]
+    outs += [kept(s) for s in shapes[1:4]] + [each(s) for s in shapes[4:]]
     scratch = [
         pltpu.VMEM((2, count, held), jnp.bfloat16),
-        pltpu.VMEM((2, experts, places, width), jnp.bfloat16),
+        pltpu.VMEM((experts, rows, width), jnp.bfloat16),
+        pltpu.VMEM((2, *w_gate.shape), jnp.bfloat16),
+        pltpu.SemaphoreType.DMA((2, experts)),
         pltpu.SemaphoreType.DMA,
     ]
     flops = 4 * experts * rows * hidden * width + 2 * experts * rows * count * width
@@ -261,24 +297,26 @@
 
 def slope_call(own, other, pick, put, prob, mine, w_down, g, u):
     experts, hidden, width = w_down.shape
-    count, places, columns = pick.shape[2], prob.shape[2], prob.shape[3]
-    rows = 2 * places
+    count, rows, columns = pick.shape[2], prob.shape[1], prob.shape[2]
+    places = rows // 2
     args = (*own, *other, pick, put, prob, mine, w_down, g, u)
     shapes = [
-        bf16(2, experts, places, width),
+        bf16(experts, rows, width),
         bf16(experts, rows, hidden),
         bf16(experts, rows, hidden),
         bf16(experts, hidden, rows),
         bf16(experts, hidden, rows),
         bf16(2, count, columns),
     ]
-    ins = [whole(a) for a in args[:-3]] + [each(w_down), each(g), each(u)]
+    ins = [whole(a) for a in args[:-3]] + [pl.BlockSpec(memory_space=pl.ANY), each(g), each(u)]
     outs = [pl.BlockSpec(memory_space=pl.ANY)]
-    outs += [each(s) for s in shapes[1:5]] + [whole(shapes[5])]
+    outs += [each(s) for s in shapes[1:5]] + [kept(shapes[5])]
     scratch = [
         pltpu.VMEM((2, count, width), jnp.bfloat16),
-        pltpu.VMEM((2, experts, places, width), jnp.bfloat16),
+        pltpu.VMEM((experts, rows, width), jnp.bfloat16),
         pltpu.VMEM((2, experts, places, columns), jnp.bfloat16),
+        pltpu.VMEM(w_down.shape, jnp.bfloat16),
+        pltpu.SemaphoreType.DMA((experts,)),
         pltpu.SemaphoreType.DMA,
     ]
     flops = 2 * experts * rows * hidden * width + 2 * experts * rows * count * width
@@ -290,31 +328,32 @@
     rows = lefts[0].shape[1]
     count = put.shape[1]
     terms = len(lefts)
-    first, steps = start // CHUNK, (stop - start) // CHUNK
+    steps = (stop - start) // CHUNK
     columns = stop - start + (0 if extra is None else extra.shape[2])
     args = (put, *lefts, *rights) + (() if extra is None else (extra,))
     shapes = [bf16(count, columns)] * 2
     ins = [whole(put)] + [whole(a) for a in lefts]
-    last = first + steps - 1
-    ins += [
-        pl.BlockSpec((experts, hidden, CHUNK), lambda i: (0, 0, jnp.minimum(first + i, last)))
-    ] * terms
+    ins += [pl.BlockSpec(memory_space=pl.ANY)] * terms
     ins += [] if extra is None else [whole(extra)]
     outs = [pl.BlockSpec((count, CHUNK), lambda i: (0, i))] * 2
-    scratch = [pltpu.VMEM((2, put.shape[2], CHUNK), jnp.bfloat16)]
+    scratch = [
+        pltpu.VMEM((2, put.shape[2], CHUNK), jnp.bfloat16),
+        pltpu.VMEM((terms, steps, experts, hidden, CHUNK), jnp.bfloat16),
+        pltpu.SemaphoreType.DMA((terms, steps)),
+    ]
     flops = 2 * experts * rows * (stop - start) * (hidden * terms + count)
-    kernel = functools.partial(back_kernel, terms, steps)
+    kernel = functools.partial(back_kernel, terms, start, steps)
     grid = steps + (0 if extra is None else 1)
     return call(kernel, grid, ins, args, outs, shapes, scratch, flops)
 
 
-def grad_call(x, left):
-    _, experts, places, width = x.shape
-    hidden = left.shape[1]
-    shape = bf16(experts, hidden, width)
-    ins = [pl.BlockSpec((2, 1, places, width), lambda i: (0, i, 0, 0)), each(left)]
-    flops = 4 * experts * places * hidden * width
-    return call(grad_kernel, experts, ins, (x, left), [each(shape)], [shape], flops=flops)[0]
+def grad_call(x, *lefts):
+    experts, rows, width = x.shape
+    hidden = lefts[0].shape[1]
+    shapes = [bf16(experts, hidden, width)] * len(lefts)
+    ins = [each(x)] + [each(left) for left in lefts]
+    flops = 2 * experts * rows * hidden * width * len(lefts)
+    return call(grad_kernel, experts, ins, (x, *lefts), [each(s) for s in shapes], shapes, flops=flops)
 
 
 def dense_body(
@@ -343,9 +382,10 @@
     maps = ((slot[None, :] == spots[:, None]).astype(jnp.bfloat16), mine, both)
 
     near, far = swap(extended, Z1), swap(extended, Z2)
-    cotangent, near, far = together(cotangent, near, far)
+    last = swap(far, Z1)
+    cotangent, last = together(cotangent, last)
     own, other = [], []
-    for rows in (extended, jnp.concatenate([near, far]), swap(far, Z1)):
+    for rows in (extended, jnp.concatenate([near, far]), last):
         rows = jnp.concatenate([rows, swap(rows, X, Y)])
         rows = jnp.concatenate([rows, swap(rows, Y, X)])
         own.append(rows)
@@ -362,11 +402,9 @@
     )
     h, far_grads = together(h, far_grads)
     far_grads_other = swap(far_grads, CORE)
-
-    sums, sums_other = back_call(put, [h], [down_weight], 0, width)
-    sums = add(sums, swap(sums_other, CORE))
-    sums, far_grads_other = together(sums, far_grads_other)
-    from_second = swap(sums[2 * quarter :], Y, X)
+    mixed, mixed_other = back_call(put, [h], [down_weight], 0, width)
+    mixed_other, far_grads_other = together(mixed_other, far_grads_other)
+    mixed = [mixed, swap(mixed_other, CORE)]
 
     c, dg, du, dgt, dut, share = slope_call(
         (grads, far_grads),
@@ -379,50 +417,55 @@
         g,
         u,
     )
+
+    def leaving(parts, start, stop):
+        return add(*(part[start:stop] for part in parts))
+
+    def by_second(parts):
+        return parts + [swap(leaving(parts, 2 * quarter, 4 * quarter), Y, X)]
+
+    def by_first(parts):
+        return parts + [swap(leaving(parts, quarter, 2 * quarter), X, Y)]
+
+    def by_far(parts):
+        return parts + [swap(leaving(parts, 2 * tok_count, 4 * tok_count), Z2)]
+
+    def by_near(parts):
+        return parts + [swap(leaving(parts, tok_count, 2 * tok_count), Z1)]
+
     weights = [gate_weight, up_weight]
+    mixed[1], dg, du = together(mixed[1], dg, du)
+    mixed = by_second(mixed)
     left, left_other = back_call(put, [dg, du], weights, 0, middle)
-    from_left = swap(left_other, CORE)
-    from_second, left, dg, du = together(from_second, left, dg, du)
-    sums = add(sums[: 2 * quarter], from_second)
-    sums, dg, du = together(sums, dg, du)
-    from_first = swap(sums[quarter:], X, Y)
+    left = [left, swap(left_other, CORE)]
+    left[0], dg, du = together(left[0], dg, du)
     right, right_other = back_call(put, [dg, du], weights, middle, width, share)
-
-    from_right = swap(right_other, CORE)
-    from_left, right = together(from_left, right)
-    left = add(left, from_left)
-    left, ht = together(left, ht)
-    from_left = swap(left[2 * quarter :], Y, X)
-    down_weight_grad = grad_call(c, ht)
-
-    from_right, from_first, down_weight_grad = together(from_right, from_first, down_weight_grad)
-    right = add(right, from_right)
-    sums = add(sums[:quarter], from_first)
-    right, sums, dgt = together(right, sums, dgt)
-    from_right = swap(right[2 * quarter :], Y, X)
-
-    def over_z(values):
-        parts = [values[i * tok_count : (i + 1) * tok_count] for i in range(4)]
-        return parts[:1] + [swap(part, bit) for part, bit in zip(parts[1:], (Z1, Z2, Z3))]
-
-    mixed = over_z(sums)
-    gate_weight_grad = grad_call(x, dgt)
-
-    from_left, gate_weight_grad = together(from_left, gate_weight_grad)
-    left = add(left[: 2 * quarter], from_left)
-    left, dut = together(left, dut)
-    from_left = swap(left[quarter:], X, Y)
-    up_weight_grad = grad_call(x, dut)
-
-    from_right, up_weight_grad = together(from_right, up_weight_grad)
-    right = add(right[: 2 * quarter], from_right)
-    from_right = swap(right[quarter:], X, Y)
-    left = over_z(add(left[:quarter], from_left))
-    right = add(*over_z(add(right[:quarter], from_right)))
-    token_grad = jnp.concatenate([add(*left), right[:, : width - middle]], axis=1)
+    right = [right, swap(right_other, CORE)]
+
+    right[0], left[1] = together(right[0], left[1])
+    left = by_second(left)
+    mixed[2], ht = together(mixed[2], ht)
+    mixed = by_first(mixed)
+    (down_weight_grad,) = grad_call(c, ht)
+
+    right[1], left[2], mixed[3], down_weight_grad = together(
+        right[1], left[2], mixed[3], down_weight_grad
+    )
+    right, left, mixed = by_second(right), by_first(left), by_far(mixed)
+    right[0], dgt, dut = together(right[0], dgt, dut)
+    gate_weight_grad, up_weight_grad = grad_call(x, dgt, dut)
+
+    right[2], left[3], mixed[4], gate_weight_grad = together(
+        right[2], left[3], mixed[4], gate_weight_grad
+    )
+    right, left, mixed = by_first(right), by_far(left), by_near(mixed)
+    right, left = by_far(right), by_near(left)
+    right = by_near(right)
+    mixed, left, right = (leaving(parts, 0, tok_count) for parts in (mixed, left, right))
+    token_grad = jnp.concatenate([left, right[:, : width - middle]], axis=1)
     share = right[:, width - middle : width - middle + total_experts].astype(jnp.float32)
     gate_grad = jnp.sum(jnp.where(used, share[:, None, :], 0.0), axis=2)
-    return (add(*mixed), token_grad, gate_grad, gate_weight_grad, up_weight_grad, down_weight_grad)
+    return (mixed, token_grad, gate_grad, gate_weight_grad, up_weight_grad, down_weight_grad)
 
 
 def routed_body(tokens, cotangent, gate_prob, expert_ids, placement, gate_weight, up_weight, down_weight):

time: 200 us -> 197 us (0.985)
  other arithmetic: 9.09 us -> 18.3 us
  Pallas kernels: 96.5 us -> 90.1 us
  starting transfers between devices: 43.7 us -> 39.2 us
    convert_element_type x12 -> x15, other arithmetic: 4.61 us -> 13.8 us  [add(): return total.astype(jnp.bfloat16)]
    pallas_call x8 -> x7, Pallas kernels: 96.5 us -> 90.1 us  [call(): pl.pallas_call(kernel, grid=(grid,), in_specs=ins, out_specs=outs, out_sh...]
    ppermute x37 -> x34, starting transfers between devices: 43.7 us -> 39.2 us  [swap(): return lax.ppermute(values, AXES, pairs)]
    ppermute x37 -> x34, waiting for transfers between devices: 43 us -> 42.4 us  [swap(): return lax.ppermute(values, AXES, pairs)]
  transfers between devices with their start and end apart: 37 -> 34, of which waited for: 14 -> 15; matrix products, arithmetic and copies ran while one was open for 4% -> 7% of each run, Pallas kernels for 43% -> 46%
where the time goes in v3:
time: 197 us; the launch traced here: 195 us
  Pallas kernels  90.1 us (46%)
  waiting for transfers between devices  42.4 us (22%)
  starting transfers between devices  39.2 us (20%)
  other arithmetic  18.3 us (9%)
  local copies, waits for them, and re-layouts  4.47 us (2%)
    pallas_call x7, Pallas kernels, call(): pl.pallas_call(kernel, grid=(grid,), in_specs=ins, out_specs=outs, out_sh...  90.1 us
    ppermute x34, waiting for transfers between devices, swap(): return lax.ppermute(values, AXES, pairs)  42.4 us
    ppermute x34, starting transfers between devices, swap(): return lax.ppermute(values, AXES, pairs)  39.2 us
    convert_element_type x15, other arithmetic, add(): return total.astype(jnp.bfloat16)  13.8 us
  transfers between devices with their start and end apart: 34, of which 15 were waited for; matrix products, arithmetic and copies ran while one was open for 7% of the time, Pallas kernels for 46%

profile of v3, /device:TPU:0, one launch (start us, length us, event | category | flops | bytes accessed | tf_op | source)
XLA Modules:
  0.0 195.5 jit_solution(7691975005489671107)
XLA Ops:
  4.4 4.0 %collective-permute-start.3 = (bf16[16,4224]{1,0:T(8,128)(2,1)S(1)}, bf16[16,4224]{1,0:T(8,128)(2,1)S(1)}, u32[]{:S(2)}, u32[]{:S(2)}) collective-permute-start(bf16[16,4224]{1,0:T(8,128)(2,1)S(1)} %concatenate.38), channel_id=1, source_target_pairs={{0,4},{1,5},{2,6},{3,7},{4,0},{5,1},{6,2},{7,3},{8,12},{9,13},{10,... | collective-permute-start | bytes 405512 | tf_op jit(solution)/shard_map/ppermute | solution.py:30
  8.4 1.6 collective-permute-start.2
  10.0 1.5 collective-permute-start
  11.5 3.5 %collective-permute-done.3 = bf16[16,4224]{1,0:T(8,128)(2,1)S(1)} collective-permute-done((bf16[16,4224]{1,0:T(8,128)(2,1)S(1)}, bf16[16,4224]{1,0:T(8,128)(2,1)S(1)}, u32[]{:S(2)}, u32[]{:S(2)}) %collective-permute-start.3) | collective-permute-done | bytes 135200 | tf_op jit(solution)/shard_map/ppermute | solution.py:30
  15.2 1.6 collective-permute-start.4
  16.9 1.6 collective-permute-start.1
  19.9 3.7 %collective-permute-done.6 = bf16[16,4224]{1,0:T(8,128)(2,1)S(1)} collective-permute-done((bf16[16,4224]{1,0:T(8,128)(2,1)S(1)}, bf16[16,4224]{1,0:T(8,128)(2,1)S(1)}, u32[]{:S(2)}, u32[]{:S(2)}) %collective-permute-start.6) | collective-permute-done | bytes 135200 | tf_op jit(solution)/shard_map/ppermute | solution.py:30
  24.9 2.4 %collective-permute-start.13 = (bf16[16,4096]{1,0:T(8,128)(2,1)S(1)}, bf16[16,4096]{1,0:T(8,128)(2,1)S(1)}, u32[]{:S(2)}, u32[]{:S(2)}) collective-permute-start(bf16[16,4096]{1,0:T(8,128)(2,1)S(1)} %copy-done.13), channel_id=1, source_target_pairs={{0,4},{1,5},{2,6},{3,7},{4,0},{5,1},{6,2},{7,3},{8,12},{9,13},{10,... | collective-permute-start | bytes 393224 | tf_op jit(solution)/shard_map/ppermute | solution.py:30
  29.7 6.5 %collective-permute-done.13 = bf16[16,4096]{1,0:T(8,128)(2,1)S(1)} collective-permute-done((bf16[16,4096]{1,0:T(8,128)(2,1)S(1)}, bf16[16,4096]{1,0:T(8,128)(2,1)S(1)}, u32[]{:S(2)}, u32[]{:S(2)}) %collective-permute-start.13) | collective-permute-done | bytes 131104 | tf_op jit(solution)/shard_map/ppermute | solution.py:30
  37.6 1.6 collective-permute-start.8
  39.4 7.1 %collective-permute-done.5 = bf16[64,4224]{1,0:T(8,128)(2,1)S(1)} collective-permute-done((bf16[64,4224]{1,0:T(8,128)(2,1)S(1)}, bf16[64,4224]{1,0:T(8,128)(2,1)S(1)}, u32[]{:S(2)}, u32[]{:S(2)}) %collective-permute-start.5) | collective-permute-done | bytes 540704 | tf_op jit(solution)/shard_map/ppermute | solution.py:30
  46.6 2.8 %collective-permute-done.8 = bf16[32,4224]{1,0:T(8,128)(2,1)S(1)} collective-permute-done((bf16[32,4224]{1,0:T(8,128)(2,1)S(1)}, bf16[32,4224]{1,0:T(8,128)(2,1)S(1)}, u32[]{:S(2)}, u32[]{:S(2)}) %collective-permute-start.8) | collective-permute-done | bytes 270368 | tf_op jit(solution)/shard_map/ppermute | solution.py:30
  49.8 1.6 collective-permute-done.11.other2
  54.2 23.8 %shard_map.127 = (bf16[8,96,4096]{2,1,0:T(8,128)(2,1)}, bf16[2,256,384]{2,1,0:T(8,128)(2,1)}, bf16[2,384,256]{2,1,0:T(8,128)(2,1)}, f32[8,96,128]{2,1,0:T(8,128)...) custom-call(bf16[64,4224]{1,0:T(8,128)(2,1)} %copy-done, ...), custom_call_target="tpu_custom_call" | custom-call | flops 4026531840 | bytes 39124992 | tf_op jit(solution)/shard_map/pallas_call | solution.py:252
  78.1 9.6 %shard_map.128 = (bf16[256,4096]{1,0:T(8,128)(2,1)}, bf16[256,4096]{1,0:T(8,128)(2,1)}) custom-call(bf16[2,256,384]{2,1,0:T(8,128)(2,1)} %get-tuple-element.70.put_ref, bf16[8,96,192]{2,1,0:T(8,128)(2,1)} %get-tuple-element.73.refs_0_, bf16[8,192,4096]{2,1,0:T(8,128)(2,1)} %down_ref.1), custom_call_target="tpu_custom_call" | custom-call | flops 2818572288 | bytes 17465344 | tf_op jit(solution)/shard_map/pallas_call | solution.py:252
  89.1 4.4 %collective-permute-done.19.other0 = bf16[128,4096]{1,0:T(8,128)(2,1)S(1)} collective-permute-done((bf16[128,4096]{1,0:T(8,128)(2,1)S(1)}, bf16[128,4096]{1,0:T(8,128)(2,1)S(1)}, u32[]{:S(2)}, u32[]{:S(2)}) %collective-permute-start.19) | collective-permute-done | bytes 1048608 | tf_op jit(solution)/shard_map/ppermute | solution.py:30
  94.5 16.1 %shard_map.129 = (bf16[8,96,4096]{2,1,0:T(8,128)(2,1)}, bf16[8,96,192]{2,1,0:T(8,128)(2,1)}, bf16[8,96,192]{2,1,0:T(8,128)(2,1)}, bf16[8,192,96]{2,1,0:T(8,128)(...) custom-call(bf16[128,4096]{1,0:T(8,128)(2,1)} %copy-done.3, bf16[128,4096]{1,0:T(8,128)(2,1)} %copy-done.6, ...), custom_call_target="tpu_custom_call" | custom-call | flops 2818572288 | bytes 26836992 | tf_op jit(solution)/shard_map/pallas_call | solution.py:252
  111.8 8.1 %shard_map.130 = (bf16[256,2048]{1,0:T(8,128)(2,1)}, bf16[256,2048]{1,0:T(8,128)(2,1)}) custom-call(bf16[2,256,384]{2,1,0:T(8,128)(2,1)} %get-tuple-element.70.put_ref, bf16[8,96,192]{2,1,0:T(8,128)(2,1)} %get-tuple-element.91.refs_0_, bf16[8,96,192]{2,1,0:T(8,128)(2,1)} %get-tuple-element.92.refs_1_, bf16[8,192,4096]{2,1,0:T(8,128)(2,1)} %refs_2_.3, ...), custom_call_target="tpu_custom_call" | custom-call | flops 2013265920 | bytes 28246016 | tf_op jit(solution)/shard_map/pallas_call | solution.py:252
  120.0 8.2 %shard_map.131 = (bf16[256,2176]{1,0:T(8,128)(2,1)}, bf16[256,2176]{1,0:T(8,128)(2,1)}) custom-call(bf16[2,256,384]{2,1,0:T(8,128)(2,1)} %get-tuple-element.70.put_ref, bf16[8,96,192]{2,1,0:T(8,128)(2,1)} %get-tuple-element.91.refs_0_, bf16[8,96,192]{2,1,0:T(8,128)(2,1)} %get-tuple-element.92.refs_1_, bf16[8,192,4096]{2,1,0:T(8,128)(2,1)} %refs_2_.3, ...), custom_call_target="tpu_custom_call" | custom-call | flops 2013265920 | bytes 28508160 | tf_op jit(solution)/shard_map/pallas_call | solution.py:252
  128.8 2.1 %add_convert_fusion.2 = bf16[64,4096]{1,0:T(8,128)(2,1)} fusion(bf16[128,4096]{1,0:T(8,128)(2,1)} %collective-permute-done.20, bf16[256,4096]{1,0:T(8,128)(2,1)S(1)} %collective-permute-done.18, bf16[256,4096]{1,0:T(8,128)(2,1)S(1)} %copy-done.1), kind=kLoop, calls=%fused_computation.2 | loop fusion | flops 1572864 | bytes 2097152 | tf_op jit(solution)/shard_map/convert_element_type | solution.py:37
  134.1 10.6 %shard_map.132 = bf16[8,192,4096]{2,1,0:T(8,128)(2,1)} custom-call(bf16[8,96,4096]{2,1,0:T(8,128)(2,1)} %get-tuple-element.99.x_ref, bf16[8,192,96]{2,1,0:T(8,128)(2,1)} %get-tuple-element.100.refs_0_), custom_call_target="tpu_custom_call" | custom-call | flops 1207959552 | bytes 19169280 | tf_op jit(solution)/shard_map/pallas_call | solution.py:252
  146.3 5.2 %collective-permute-start.27 = (bf16[32,4096]{1,0:T(8,128)(2,1)S(1)}, bf16[32,4096]{1,0:T(8,128)(2,1)}, u32[]{:S(2)}, u32[]{:S(2)}) collective-permute-start(bf16[32,4096]{1,0:T(8,128)(2,1)S(1)} %add_convert_fusion.5), channel_id=1, source_target_pairs={{0,4},{1,5},{2,6},{3,7},{4,0},{5,1},{6,2},{7,3},{8,12},{9,13},{10,... | collective-permute-start | bytes 786440 | tf_op jit(solution)/shard_map/ppermute | solution.py:30
  152.5 1.5 collective-permute-start.25
  154.0 1.8 add_convert_fusion.6
  156.3 13.7 %shard_map.133 = (bf16[8,192,4096]{2,1,0:T(8,128)(2,1)}, bf16[8,192,4096]{2,1,0:T(8,128)(2,1)}) custom-call(bf16[8,96,4096]{2,1,0:T(8,128)(2,1)} %get-tuple-element.105.x_ref, bf16[8,192,96]{2,1,0:T(8,128)(2,1)} %get-tuple-element.108.refs_0_, bf16[8,192,96]{2,1,0:T(8,128)(2,1)} %get-tuple-element.109.refs_1_), custom_call_target="tpu_custom_call" | custom-call | flops 2415919104 | bytes 32047104 | tf_op jit(solution)/shard_map/pallas_call | solution.py:252
  171.3 1.6 collective-permute-start.31
  174.1 1.8 collective-permute-start.28
  175.9 2.7 %collective-permute-done.29 = bf16[32,2048]{1,0:T(8,128)(2,1)S(1)} collective-permute-done((bf16[32,2048]{1,0:T(8,128)(2,1)S(1)}, bf16[32,2048]{1,0:T(8,128)(2,1)S(1)}, u32[]{:S(2)}, u32[]{:S(2)}) %collective-permute-start.29) | collective-permute-done | bytes 131104 | tf_op jit(solution)/shard_map/ppermute | solution.py:30
  179.8 3.2 %collective-permute-start.32 = (bf16[32,2176]{1,0:T(8,128)(2,1)S(1)}, bf16[32,2176]{1,0:T(8,128)(2,1)S(1)}, u32[]{:S(2)}, u32[]{:S(2)}) collective-permute-start(bf16[32,2176]{1,0:T(8,128)(2,1)S(1)} %add_convert_fusion.7), channel_id=1, source_target_pairs={{0,4},{1,5},{2,6},{3,7},{4,0},{5,1},{6,2},{7,3},{8,12},{9,13},{10,... | collective-permute-start | bytes 417800 | tf_op jit(solution)/shard_map/ppermute | solution.py:30
  183.0 1.8 add_convert_fusion.9
  184.8 4.7 %collective-permute-done.32 = bf16[32,2176]{1,0:T(8,128)(2,1)S(1)} collective-permute-done((bf16[32,2176]{1,0:T(8,128)(2,1)S(1)}, bf16[32,2176]{1,0:T(8,128)(2,1)S(1)}, u32[]{:S(2)}, u32[]{:S(2)}) %collective-permute-start.32) | collective-permute-done | bytes 139296 | tf_op jit(solution)/shard_map/ppermute | solution.py:30
  190.6 3.3 %collective-permute-done.33 = bf16[16,2176]{1,0:T(8,128)(2,1)S(1)} collective-permute-done((bf16[16,2176]{1,0:T(8,128)(2,1)S(1)}, bf16[16,2176]{1,0:T(8,128)(2,1)S(1)}, u32[]{:S(2)}, u32[]{:S(2)}) %collective-permute-start.33) | collective-permute-done | bytes 69664 | tf_op jit(solution)/shard_map/ppermute | solution.py:30
  (121 shorter events, 30.7 us)
Async XLA Ops:
  4.4 10.6 %collective-permute-start.3 = (bf16[16,4224]{1,0:T(8,128)(2,1)S(1)}, bf16[16,4224]{1,0:T(8,128)(2,1)S(1)}, u32[]{:S(2)}, u32[]{:S(2)}) collective-permute-start(bf16[16,4224]{1,0:T(8,128)(2,1)S(1)} %concatenate.38), channel_id=1, source_target_pairs={{0,4},{1,5},{2,6},{3,7},{4,0},{5,1},{6,2},{7,3},{8,12},{9,13},{10,... | collective-permute-start | bytes 405512 | tf_op jit(solution)/shard_map/ppermute | solution.py:30
  8.4 6.8 %collective-permute-start.2 = (bf16[16,4224]{1,0:T(8,128)(2,1)S(1)}, bf16[16,4224]{1,0:T(8,128)(2,1)S(1)}, u32[]{:S(2)}, u32[]{:S(2)}) collective-permute-start(bf16[16,4224]{1,0:T(8,128)(2,1)S(1)} %concatenate.38), channel_id=1, source_target_pairs={{0,2},{1,3},{2,0},{3,1},{4,6},{5,7},{6,4},{7,5},{8,10},{9,11},{10,... | collective-permute-start | bytes 405512 | tf_op jit(solution)/shard_map/ppermute | solution.py:30
  10.0 6.8 %collective-permute-start = (bf16[16,4224]{1,0:T(8,128)(2,1)S(1)}, bf16[16,4224]{1,0:T(8,128)(2,1)S(1)}, u32[]{:S(2)}, u32[]{:S(2)}) collective-permute-start(bf16[16,4224]{1,0:T(8,128)(2,1)S(1)} %concatenate.38), channel_id=1, source_target_pairs={{0,8},{1,17},{2,10},{3,19},{4,12},{5,21},{6,14},{7,23},{8,0},{9,25... | collective-permute-start | bytes 405512 | tf_op jit(solution)/shard_map/ppermute | solution.py:30
  15.2 21.7 %collective-permute-start.4 = (bf16[32,4224]{1,0:T(8,128)(2,1)S(1)}, bf16[32,4224]{1,0:T(8,128)(2,1)S(1)}, u32[]{:S(2)}, u32[]{:S(2)}) collective-permute-start(bf16[32,4224]{1,0:T(8,128)(2,1)S(1)} %pad_maximum_fusion.4), channel_id=1, source_target_pairs={{0,8},{1,17},{2,10},{3,19},{4,12},{5,21},{6,14},{7,23},{8,0},{9,25... | collective-permute-start | bytes 811016 | tf_op jit(solution)/shard_map/ppermute | solution.py:30
  16.9 22.3 %collective-permute-start.1 = (bf16[32,4224]{1,0:T(8,128)(2,1)S(1)}, bf16[32,4224]{1,0:T(8,128)(2,1)S(1)}, u32[]{:S(2)}, u32[]{:S(2)}) collective-permute-start(bf16[32,4224]{1,0:T(8,128)(2,1)S(1)} %pad_maximum_fusion.3), channel_id=1, source_target_pairs={{0,16},{1,9},{2,18},{3,11},{4,20},{5,13},{6,22},{7,15},{8,24},{9,1... | collective-permute-start | bytes 811016 | tf_op jit(solution)/shard_map/ppermute | solution.py:30
  18.5 5.1 %collective-permute-start.6 = (bf16[16,4224]{1,0:T(8,128)(2,1)S(1)}, bf16[16,4224]{1,0:T(8,128)(2,1)S(1)}, u32[]{:S(2)}, u32[]{:S(2)}) collective-permute-start(bf16[16,4224]{1,0:T(8,128)(2,1)S(1)} %collective-permute-done.3), channel_id=1, source_target_pairs={{0,2},{1,3},{2,0},{3,1},{4,6},{5,7},{6,4},{7,5},{8,10},{9,11},{10,... | collective-permute-start | bytes 405512 | tf_op jit(solution)/shard_map/ppermute | solution.py:30
  23.6 5.6 %collective-permute-start.12 = (bf16[16,4096]{1,0:T(8,128)(2,1)S(1)}, bf16[16,4096]{1,0:T(8,128)(2,1)S(1)}, u32[]{:S(2)}, u32[]{:S(2)}) collective-permute-start(bf16[16,4096]{1,0:T(8,128)(2,1)S(1)} %copy-done.13), channel_id=1, source_target_pairs={{0,2},{1,3},{2,0},{3,1},{4,6},{5,7},{6,4},{7,5},{8,10},{9,11},{10,... | collective-permute-start | bytes 393224 | tf_op jit(solution)/shard_map/ppermute | solution.py:30
  24.9 11.4 %collective-permute-start.13 = (bf16[16,4096]{1,0:T(8,128)(2,1)S(1)}, bf16[16,4096]{1,0:T(8,128)(2,1)S(1)}, u32[]{:S(2)}, u32[]{:S(2)}) collective-permute-start(bf16[16,4096]{1,0:T(8,128)(2,1)S(1)} %copy-done.13), channel_id=1, source_target_pairs={{0,4},{1,5},{2,6},{3,7},{4,0},{5,1},{6,2},{7,3},{8,12},{9,13},{10,... | collective-permute-start | bytes 393224 | tf_op jit(solution)/shard_map/ppermute | solution.py:30
  27.2 9.0 %collective-permute-start.14 = (bf16[16,4096]{1,0:T(8,128)(2,1)S(1)}, bf16[16,4096]{1,0:T(8,128)(2,1)S(1)}, u32[]{:S(2)}, u32[]{:S(2)}) collective-permute-start(bf16[16,4096]{1,0:T(8,128)(2,1)S(1)} %copy-done.13), channel_id=1, source_target_pairs={{0,6},{1,7},{2,4},{3,5},{4,2},{5,3},{6,0},{7,1},{8,14},{9,15},{10,... | collective-permute-start | bytes 393224 | tf_op jit(solution)/shard_map/ppermute | solution.py:30
  29.2 8.3 %collective-permute-start.7 = (bf16[16,4224]{1,0:T(8,128)(2,1)S(1)}, bf16[16,4224]{1,0:T(8,128)(2,1)S(1)}, u32[]{:S(2)}, u32[]{:S(2)}) collective-permute-start(bf16[16,4224]{1,0:T(8,128)(2,1)S(1)} %collective-permute-done.6), channel_id=1, source_target_pairs={{0,8},{1,17},{2,10},{3,19},{4,12},{5,21},{6,14},{7,23},{8,0},{9,25... | collective-permute-start | bytes 405512 | tf_op jit(solution)/shard_map/ppermute | solution.py:30
  36.3 13.5 %collective-permute-start.15 = (bf16[64,4096]{1,0:T(8,128)(2,1)S(1)}, bf16[64,4096]{1,0:T(8,128)(2,1)S(1)}, u32[]{:S(2)}, u32[]{:S(2)}) collective-permute-start(bf16[64,4096]{1,0:T(8,128)(2,1)S(1)} %pad_maximum_fusion.2), channel_id=1, source_target_pairs={{0,8},{1,17},{2,10},{3,19},{4,12},{5,21},{6,14},{7,23},{8,0},{9,25... | collective-permute-start | bytes 1572872 | tf_op jit(solution)/shard_map/ppermute | solution.py:30
  37.0 9.5 %collective-permute-start.5 = (bf16[64,4224]{1,0:T(8,128)(2,1)S(1)}, bf16[64,4224]{1,0:T(8,128)(2,1)S(1)}, u32[]{:S(2)}, u32[]{:S(2)}) collective-permute-start(bf16[64,4224]{1,0:T(8,128)(2,1)S(1)} %pad_maximum_fusion.1), channel_id=1, source_target_pairs={{0,16},{1,9},{2,18},{3,11},{4,20},{5,13},{6,22},{7,15},{8,24},{9,1... | collective-permute-start | bytes 1622024 | tf_op jit(solution)/shard_map/ppermute | solution.py:30
  37.6 11.8 %collective-permute-start.8 = (bf16[32,4224]{1,0:T(8,128)(2,1)S(1)}, bf16[32,4224]{1,0:T(8,128)(2,1)S(1)}, u32[]{:S(2)}, u32[]{:S(2)}) collective-permute-start(bf16[32,4224]{1,0:T(8,128)(2,1)S(1)} %pad_maximum_fusion.5), channel_id=1, source_target_pairs={{0,16},{1,9},{2,18},{3,11},{4,20},{5,13},{6,22},{7,15},{8,24},{9,1... | collective-permute-start | bytes 811016 | tf_op jit(solution)/shard_map/ppermute | solution.py:30
  39.2 10.6 %collective-permute-start.9 = (bf16[64,4224]{1,0:T(8,128)(2,1)S(1)}, bf16[64,4224]{1,0:T(8,128)(2,1)S(1)}, u32[]{:S(2)}, u32[]{:S(2)}) collective-permute-start(bf16[64,4224]{1,0:T(8,128)(2,1)S(1)} %pad_maximum_fusion.own0), channel_id=1, source_target_pairs={{0,1},{1,0},{2,3},{3,2},{4,5},{5,4},{6,7},{7,6},{8,9},{9,8},{10,11... | collective-permute-start | bytes 1622024 | tf_op jit(solution)/shard_map/ppermute | solution.py:30
  46.5 4.9 %collective-permute-start.10 = (bf16[128,4224]{1,0:T(8,128)(2,1)S(1)}, bf16[128,4224]{1,0:T(8,128)(2,1)S(1)}, u32[]{:S(2)}, u32[]{:S(2)}) collective-permute-start(bf16[128,4224]{1,0:T(8,128)(2,1)S(1)} %constant_dynamic-update-slice_fusion.own1), channel_id=1, source_target_pairs={{0,1},{1,0},{2,3},{3,2},{4,5},{5,4},{6,7},{7,6},{8,9},{9,8},{10,11... | collective-permute-start | bytes 3244040 | tf_op jit(solution)/shard_map/ppermute | solution.py:30
  51.4 26.6 %collective-permute-start.16 = (bf16[128,4096]{1,0:T(8,128)(2,1)S(1)}, bf16[128,4096]{1,0:T(8,128)(2,1)S(1)}, u32[]{:S(2)}, u32[]{:S(2)}) collective-permute-start(bf16[128,4096]{1,0:T(8,128)(2,1)S(1)} %constant_dynamic-update-slice_fusion.7.own0), channel_id=1, source_target_pairs={{0,16},{1,9},{2,18},{3,11},{4,20},{5,13},{6,22},{7,15},{8,24},{9,1... | collective-permute-start | bytes 3145736 | tf_op jit(solution)/shard_map/ppermute | solution.py:30
  78.0 9.8 %collective-permute-start.17 = (bf16[128,4096]{1,0:T(8,128)(2,1)S(1)}, bf16[128,4096]{1,0:T(8,128)(2,1)S(1)}, u32[]{:S(2)}, u32[]{:S(2)}) collective-permute-start(bf16[128,4096]{1,0:T(8,128)(2,1)S(1)} %collective-permute-done.16.own1), channel_id=1, source_target_pairs={{0,1},{1,0},{2,3},{3,2},{4,5},{5,4},{6,7},{7,6},{8,9},{9,8},{10,11... | collective-permute-start | bytes 3145736 | tf_op jit(solution)/shard_map/ppermute | solution.py:30
  87.8 22.8 %collective-permute-start.18 = (bf16[256,4096]{1,0:T(8,128)(2,1)}, bf16[256,4096]{1,0:T(8,128)(2,1)S(1)}, u32[]{:S(2)}, u32[]{:S(2)}) collective-permute-start(bf16[256,4096]{1,0:T(8,128)(2,1)} %get-tuple-element.77), channel_id=1, source_target_pairs={{0,1},{1,0},{2,3},{3,2},{4,5},{5,4},{6,7},{7,6},{8,9},{9,8},{10,11... | collective-permute-start | bytes 6291464 | tf_op jit(solution)/shard_map/ppermute | solution.py:30
  88.0 5.5 %collective-permute-start.19 = (bf16[128,4096]{1,0:T(8,128)(2,1)S(1)}, bf16[128,4096]{1,0:T(8,128)(2,1)S(1)}, u32[]{:S(2)}, u32[]{:S(2)}) collective-permute-start(bf16[128,4096]{1,0:T(8,128)(2,1)S(1)} %constant_dynamic-update-slice_fusion.7.own0), channel_id=1, source_target_pairs={{0,1},{1,0},{2,3},{3,2},{4,5},{5,4},{6,7},{7,6},{8,9},{9,8},{10,11... | collective-permute-start | bytes 3145736 | tf_op jit(solution)/shard_map/ppermute | solution.py:30
  110.9 17.9 %collective-permute-start.20 = (bf16[128,4096]{1,0:T(8,128)(2,1)S(1)}, bf16[128,4096]{1,0:T(8,128)(2,1)}, u32[]{:S(2)}, u32[]{:S(2)}) collective-permute-start(bf16[128,4096]{1,0:T(8,128)(2,1)S(1)} %add_convert_fusion), channel_id=1, source_target_pairs={{0,16},{1,9},{2,18},{3,11},{4,20},{5,13},{6,22},{7,15},{8,24},{9,1... | collective-permute-start | bytes 3145736 | tf_op jit(solution)/shard_map/ppermute | solution.py:30
  119.9 10.9 %collective-permute-start.22 = (bf16[256,2048]{1,0:T(8,128)(2,1)}, bf16[256,2048]{1,0:T(8,128)(2,1)}, u32[]{:S(2)}, u32[]{:S(2)}) collective-permute-start(bf16[256,2048]{1,0:T(8,128)(2,1)} %get-tuple-element.97), channel_id=1, source_target_pairs={{0,1},{1,0},{2,3},{3,2},{4,5},{5,4},{6,7},{7,6},{8,9},{9,8},{10,11... | collective-permute-start | bytes 3145736 | tf_op jit(solution)/shard_map/ppermute | solution.py:30
  128.2 16.4 %collective-permute-start.21 = (bf16[256,2176]{1,0:T(8,128)(2,1)}, bf16[256,2176]{1,0:T(8,128)(2,1)S(1)}, u32[]{:S(2)}, u32[]{:S(2)}) collective-permute-start(bf16[256,2176]{1,0:T(8,128)(2,1)} %get-tuple-element.94), channel_id=1, source_target_pairs={{0,1},{1,0},{2,3},{3,2},{4,5},{5,4},{6,7},{7,6},{8,9},{9,8},{10,11... | collective-permute-start | bytes 3342344 | tf_op jit(solution)/shard_map/ppermute | solution.py:30
  130.8 13.9 %collective-permute-start.24 = (bf16[64,4096]{1,0:T(8,128)(2,1)}, bf16[64,4096]{1,0:T(8,128)(2,1)}, u32[]{:S(2)}, u32[]{:S(2)}) collective-permute-start(bf16[64,4096]{1,0:T(8,128)(2,1)} %add_convert_fusion.2), channel_id=1, source_target_pairs={{0,8},{1,17},{2,10},{3,19},{4,12},{5,21},{6,14},{7,23},{8,0},{9,25... | collective-permute-start | bytes 1572872 | tf_op jit(solution)/shard_map/ppermute | solution.py:30
  133.5 11.6 %collective-permute-start.23 = (bf16[128,2048]{1,0:T(8,128)(2,1)S(1)}, bf16[128,2048]{1,0:T(8,128)(2,1)}, u32[]{:S(2)}, u32[]{:S(2)}) collective-permute-start(bf16[128,2048]{1,0:T(8,128)(2,1)S(1)} %add_convert_fusion.3), channel_id=1, source_target_pairs={{0,16},{1,9},{2,18},{3,11},{4,20},{5,13},{6,22},{7,15},{8,24},{9,1... | collective-permute-start | bytes 1572872 | tf_op jit(solution)/shard_map/ppermute | solution.py:30
  146.3 23.7 %collective-permute-start.27 = (bf16[32,4096]{1,0:T(8,128)(2,1)S(1)}, bf16[32,4096]{1,0:T(8,128)(2,1)}, u32[]{:S(2)}, u32[]{:S(2)}) collective-permute-start(bf16[32,4096]{1,0:T(8,128)(2,1)S(1)} %add_convert_fusion.5), channel_id=1, source_target_pairs={{0,4},{1,5},{2,6},{3,7},{4,0},{5,1},{6,2},{7,3},{8,12},{9,13},{10,... | collective-permute-start | bytes 786440 | tf_op jit(solution)/shard_map/ppermute | solution.py:30
  152.5 17.5 %collective-permute-start.25 = (bf16[128,2176]{1,0:T(8,128)(2,1)}, bf16[128,2176]{1,0:T(8,128)(2,1)S(1)}, u32[]{:S(2)}, u32[]{:S(2)}) collective-permute-start(bf16[128,2176]{1,0:T(8,128)(2,1)} %add_convert_fusion.1), channel_id=1, source_target_pairs={{0,16},{1,9},{2,18},{3,11},{4,20},{5,13},{6,22},{7,15},{8,24},{9,1... | collective-permute-start | bytes 1671176 | tf_op jit(solution)/shard_map/ppermute | solution.py:30
  155.8 14.2 %collective-permute-start.26 = (bf16[64,2048]{1,0:T(8,128)(2,1)}, bf16[64,2048]{1,0:T(8,128)(2,1)}, u32[]{:S(2)}, u32[]{:S(2)}) collective-permute-start(bf16[64,2048]{1,0:T(8,128)(2,1)} %add_convert_fusion.6), channel_id=1, source_target_pairs={{0,8},{1,17},{2,10},{3,19},{4,12},{5,21},{6,14},{7,23},{8,0},{9,25... | collective-permute-start | bytes 786440 | tf_op jit(solution)/shard_map/ppermute | solution.py:30
  171.1 7.5 %collective-permute-start.29 = (bf16[32,2048]{1,0:T(8,128)(2,1)S(1)}, bf16[32,2048]{1,0:T(8,128)(2,1)S(1)}, u32[]{:S(2)}, u32[]{:S(2)}) collective-permute-start(bf16[32,2048]{1,0:T(8,128)(2,1)S(1)} %add_convert_fusion.8), channel_id=1, source_target_pairs={{0,4},{1,5},{2,6},{3,7},{4,0},{5,1},{6,2},{7,3},{8,12},{9,13},{10,... | collective-permute-start | bytes 393224 | tf_op jit(solution)/shard_map/ppermute | solution.py:30
  171.3 8.4 %collective-permute-start.31 = (bf16[64,2176]{1,0:T(8,128)(2,1)S(1)}, bf16[64,2176]{1,0:T(8,128)(2,1)S(1)}, u32[]{:S(2)}, u32[]{:S(2)}) collective-permute-start(bf16[64,2176]{1,0:T(8,128)(2,1)S(1)} %add_convert_fusion.4), channel_id=1, source_target_pairs={{0,8},{1,17},{2,10},{3,19},{4,12},{5,21},{6,14},{7,23},{8,0},{9,25... | collective-permute-start | bytes 835592 | tf_op jit(solution)/shard_map/ppermute | solution.py:30
  174.1 8.9 %collective-permute-start.28 = (bf16[16,4096]{1,0:T(8,128)(2,1)S(1)}, bf16[16,4096]{1,0:T(8,128)(2,1)S(1)}, u32[]{:S(2)}, u32[]{:S(2)}) collective-permute-start(bf16[16,4096]{1,0:T(8,128)(2,1)S(1)} %add_convert_fusion.10), channel_id=1, source_target_pairs={{0,2},{1,3},{2,0},{3,1},{4,6},{5,7},{6,4},{7,5},{8,10},{9,11},{10,... | collective-permute-start | bytes 393224 | tf_op jit(solution)/shard_map/ppermute | solution.py:30
  179.6 10.0 %collective-permute-start.30 = (bf16[16,2048]{1,0:T(8,128)(2,1)S(1)}, bf16[16,2048]{1,0:T(8,128)(2,1)S(1)}, u32[]{:S(2)}, u32[]{:S(2)}) collective-permute-start(bf16[16,2048]{1,0:T(8,128)(2,1)S(1)} %add_convert_fusion.14), channel_id=1, source_target_pairs={{0,2},{1,3},{2,0},{3,1},{4,6},{5,7},{6,4},{7,5},{8,10},{9,11},{10,... | collective-permute-start | bytes 196616 | tf_op jit(solution)/shard_map/ppermute | solution.py:30
  179.8 9.7 %collective-permute-start.32 = (bf16[32,2176]{1,0:T(8,128)(2,1)S(1)}, bf16[32,2176]{1,0:T(8,128)(2,1)S(1)}, u32[]{:S(2)}, u32[]{:S(2)}) collective-permute-start(bf16[32,2176]{1,0:T(8,128)(2,1)S(1)} %add_convert_fusion.7), channel_id=1, source_target_pairs={{0,4},{1,5},{2,6},{3,7},{4,0},{5,1},{6,2},{7,3},{8,12},{9,13},{10,... | collective-permute-start | bytes 417800 | tf_op jit(solution)/shard_map/ppermute | solution.py:30
  (16 other events, 143.4 us)

commit v4 on v3

--- a/solution.py
+++ b/solution.py
@@ -12,6 +12,7 @@
 CORE, Z1, Z2, Z3, X, Y = 1, 2, 4, 6, 8, 16
 GROUPS = ((0,), (1, 2), (3,))
 CHUNK = 512
+WIDE = 1024
 MIB = 1 << 20
 
 NT = (((1,), (1,)), ((), ()))
@@ -55,17 +56,13 @@
     return lax.broadcasted_iota(jnp.int32, shape, axis)
 
 
-def expert_copy(source, held, sems, e):
-    return pltpu.make_async_copy(source.at[e], held.at[e], sems.at[e])
-
-
 def dispatch(pick, rows_ref, half, x_ref):
     experts, both, width = x_ref.shape
     places = both // 2
-    for at in range(0, width, CHUNK):
-        rows = dot(pick, rows_ref[half, :, at : at + CHUNK]).astype(jnp.bfloat16)
+    for at in range(0, width, WIDE):
+        rows = dot(pick, rows_ref[half, :, at : at + WIDE]).astype(jnp.bfloat16)
         for e in range(experts):
-            x_ref[e, half * places : (half + 1) * places, at : at + CHUNK] = rows[
+            x_ref[e, half * places : (half + 1) * places, at : at + WIDE] = rows[
                 e * places : (e + 1) * places
             ]
 
@@ -78,25 +75,32 @@
             rows_ref[half, at : at + size] = piece[quarter * size : (quarter + 1) * size]
 
 
-def up_kernel(tok_count, own0, own1, own2, other0, other1, other2, mine_ref, mine_t_ref, both_t_ref,
+def up_kernel(tok_count, own0, own1, own2, other0, other1, other2, mine_ref, mine_t_ref, both_ref,
               gate_ref, up_ref, x_out, put_ref, pick_ref, prob_ref, g_ref, u_ref, h_ref, ht_ref,
               rows_ref, x_ref, held_ref, held_sems, sem):
     e = pl.program_id(0)
     experts, both, width = x_ref.shape
     places = both // 2
+    hidden = gate_ref.shape[1]
     count = rows_ref.shape[1]
+
+    def copies(i):
+        return (
+            pltpu.make_async_copy(gate_ref.at[i], held_ref.at[i, :hidden], held_sems.at[0, i]),
+            pltpu.make_async_copy(up_ref.at[i], held_ref.at[i, hidden:], held_sems.at[1, i]),
+        )
 
     @pl.when(e == 0)
     def _():
         for i in range(experts):
-            expert_copy(gate_ref, held_ref.at[0], held_sems.at[0], i).start()
-            expert_copy(up_ref, held_ref.at[1], held_sems.at[1], i).start()
+            for copy in copies(i):
+                copy.start()
         join_groups((own0, own1, own2), rows_ref, 0, tok_count)
         join_groups((other0, other1, other2), rows_ref, 1, tok_count)
         row, col = iota((count, count), 0), iota((count, count), 1)
         block = lax.div(row, tok_count)
         before = ((col < row) & (lax.div(col, tok_count) == block)).astype(jnp.bfloat16)
-        columns = both_t_ref.shape[1]
+        columns = mine_ref.shape[0]
         first = (lax.div(iota((count, columns), 0), tok_count) * CAP).astype(jnp.float32)
         spot = lax.rem(iota((count, experts * places), 1), places).astype(jnp.float32)
         spot_t = lax.rem(iota((experts * places, count), 0), places).astype(jnp.float32)
@@ -105,29 +109,29 @@
             taken = prob.astype(jnp.float32) > 0.0
             rank = dot(before, jnp.where(taken, 1.0, 0.0).astype(jnp.bfloat16))
             place = jnp.where(taken, rank + first, -1.0).astype(jnp.bfloat16)
-            put = jnp.where(dot(place, mine_ref[...]) == spot, 1.0, 0.0).astype(jnp.bfloat16)
+            put = jnp.where(dot(place, mine_ref[...]) == spot, 1.0, 0.0)
             pick = dot(mine_t_ref[...], place, NT) == spot_t
             pick = jnp.where(pick, 1.0, 0.0).astype(jnp.bfloat16)
-            put_ref[half] = put
+            put_ref[half] = put.astype(jnp.bfloat16)
             pick_ref[half] = pick
-            weight = jnp.sum(dot(pick, prob) * both_t_ref[...], axis=1, keepdims=True)
-            weight = jnp.broadcast_to(weight, (experts * places, columns))
+            weight = jnp.sum(put * dot(prob, both_ref[...]), axis=0, keepdims=True)
             for i in range(experts):
-                prob_ref[i, half * places : (half + 1) * places] = weight[i * places : (i + 1) * places]
+                prob_ref[i, :, half * places : (half + 1) * places] = weight[
+                    :, i * places : (i + 1) * places
+                ]
             dispatch(pick, rows_ref, half, x_ref)
         pltpu.make_async_copy(x_ref, x_out, sem).start()
 
-    rows = x_ref[e]
-    expert_copy(gate_ref, held_ref.at[0], held_sems.at[0], e).wait()
-    g = dot(rows, held_ref[0, e], NT)
-    expert_copy(up_ref, held_ref.at[1], held_sems.at[1], e).wait()
-    u = dot(rows, held_ref[1, e], NT)
+    for copy in copies(e):
+        copy.wait()
+    product = dot(held_ref[e], x_ref[e], NT)
+    g, u = product[:hidden], product[hidden:]
     g_ref[0] = g
     u_ref[0] = u
     silu_v, _ = gated(g)
-    scaled = silu_v * u * prob_ref[e][:, :1]
-    h_ref[0] = scaled.astype(jnp.bfloat16)
-    ht_ref[0] = scaled.T.astype(jnp.bfloat16)
+    scaled = silu_v * u * prob_ref[e]
+    ht_ref[0] = scaled.astype(jnp.bfloat16)
+    h_ref[0] = scaled.T.astype(jnp.bfloat16)
 
     @pl.when(e == pl.num_programs(0) - 1)
     def _():
@@ -135,16 +139,19 @@
 
 
 def slope_kernel(own0, own1, other0, other1, pick_ref, put_ref, prob_ref, mine_ref, down_ref, g_ref, u_ref,
-                 x_out, dg_ref, du_ref, dgt_ref, dut_ref, share_ref, rows_ref, x_ref, terms_ref,
+                 x_out, dg_ref, du_ref, dgt_ref, dut_ref, share_ref, rows_ref, x_ref, shares_ref, terms_ref,
                  held_ref, held_sems, sem):
     e = pl.program_id(0)
     experts = x_ref.shape[0]
     places = x_ref.shape[1] // 2
 
+    def copy(i):
+        return pltpu.make_async_copy(down_ref.at[i], held_ref.at[i], held_sems.at[i])
+
     @pl.when(e == 0)
     def _():
         for i in range(experts):
-            expert_copy(down_ref, held_ref, held_sems, i).start()
+            copy(i).start()
         for half, pieces in enumerate(((own0, own1), (other0, other1))):
             size = own0.shape[0]
             rows_ref[half, :size] = pieces[0][...]
@@ -152,27 +159,28 @@
             dispatch(pick_ref[half], rows_ref, half, x_ref)
         pltpu.make_async_copy(x_ref, x_out, sem).start()
 
-    expert_copy(down_ref, held_ref, held_sems, e).wait()
-    plain = dot(x_ref[e], held_ref[e], NT)
+    copy(e).wait()
+    plain = dot(held_ref[e], x_ref[e], NT)
     g, u = g_ref[0], u_ref[0]
     silu_v, slope = gated(g)
-    share = jnp.sum(silu_v * u * plain, axis=1, keepdims=True)
-    for half in range(2):
-        part = share[half * places : (half + 1) * places] * mine_ref[e].astype(jnp.float32)
-        terms_ref[half, e] = part.astype(jnp.bfloat16)
-    scaled = plain * prob_ref[e][:, :1]
+    shares_ref[pl.ds(e, 1), :] = jnp.sum(silu_v * u * plain, axis=0, keepdims=True)
+    scaled = plain * prob_ref[e]
     dg = scaled * u * slope
     du = scaled * silu_v
-    dg_ref[0] = dg.astype(jnp.bfloat16)
-    du_ref[0] = du.astype(jnp.bfloat16)
-    dgt_ref[0] = dg.T.astype(jnp.bfloat16)
-    dut_ref[0] = du.T.astype(jnp.bfloat16)
+    dgt_ref[0] = dg.astype(jnp.bfloat16)
+    dut_ref[0] = du.astype(jnp.bfloat16)
+    dg_ref[0] = dg.T.astype(jnp.bfloat16)
+    du_ref[0] = du.T.astype(jnp.bfloat16)
 
     @pl.when(e == pl.num_programs(0) - 1)
     def _():
+        shares = shares_ref[...].T
         for half in range(2):
-            terms = terms_ref[half].reshape(put_ref.shape[2], terms_ref.shape[3])
-            share_ref[half] = dot(put_ref[half], terms).astype(jnp.bfloat16)
+            for i in range(experts):
+                share = shares[half * places : (half + 1) * places, i : i + 1]
+                share = (share * mine_ref[i].astype(jnp.float32)).astype(jnp.bfloat16)
+                terms_ref[i * places : (i + 1) * places] = share
+            share_ref[half] = dot(put_ref[half], terms_ref[...]).astype(jnp.bfloat16)
         pltpu.make_async_copy(x_ref, x_out, sem).wait()
 
 
@@ -216,12 +224,9 @@
             other_ref[:, :columns] = extra_ref[1]
 
 
-def grad_kernel(x_ref, *refs):
-    count = len(refs) // 2
-    for at in range(0, x_ref.shape[2], CHUNK):
-        rows = x_ref[0, :, at : at + CHUNK]
-        for left, out in zip(refs[:count], refs[count:]):
-            out[0, :, at : at + CHUNK] = dot(left[0], rows).astype(jnp.bfloat16)
+def grad_kernel(x_ref, left, out):
+    for at in range(0, x_ref.shape[2], WIDE):
+        out[0, :, at : at + WIDE] = dot(left[0], x_ref[0, :, at : at + WIDE]).astype(jnp.bfloat16)
 
 
 def whole(a):
@@ -265,7 +270,6 @@
     experts, hidden, width = w_gate.shape
     held = own[0].shape[1]
     count = sum(piece.shape[0] for piece in own)
-    columns = held - width
     places = count // tok_count * CAP
     rows = 2 * places
     args = (*own, *other, *maps, w_gate, w_up)
@@ -273,9 +277,9 @@
         bf16(experts, rows, width),
         bf16(2, count, experts * places),
         bf16(2, experts * places, count),
-        f32(experts, rows, columns),
-        f32(experts, rows, hidden),
-        f32(experts, rows, hidden),
+        f32(experts, 1, rows),
+        f32(experts, hidden, rows),
+        f32(experts, hidden, rows),
         bf16(experts, rows, hidden),
         bf16(experts, hidden, rows),
     ]
@@ -285,7 +289,7 @@
     scratch = [
         pltpu.VMEM((2, count, held), jnp.bfloat16),
         pltpu.VMEM((experts, rows, width), jnp.bfloat16),
-        pltpu.VMEM((2, *w_gate.shape), jnp.bfloat16),
+        pltpu.VMEM((experts, 2 * hidden, width), jnp.bfloat16),
         pltpu.SemaphoreType.DMA((2, experts)),
         pltpu.SemaphoreType.DMA,
     ]
@@ -297,7 +301,7 @@
 
 def slope_call(own, other, pick, put, prob, mine, w_down, g, u):
     experts, hidden, width = w_down.shape
-    count, rows, columns = pick.shape[2], prob.shape[1], prob.shape[2]
+    count, rows, columns = pick.shape[2], prob.shape[2], mine.shape[2]
     places = rows // 2
     args = (*own, *other, pick, put, prob, mine, w_down, g, u)
     shapes = [
@@ -314,7 +318,8 @@
     scratch = [
         pltpu.VMEM((2, count, width), jnp.bfloat16),
         pltpu.VMEM((experts, rows, width), jnp.bfloat16),
-        pltpu.VMEM((2, experts, places, columns), jnp.bfloat16),
+        pltpu.VMEM((experts, rows), jnp.float32),
+        pltpu.VMEM((experts * places, columns), jnp.bfloat16),
         pltpu.VMEM(w_down.shape, jnp.bfloat16),
         pltpu.SemaphoreType.DMA((experts,)),
         pltpu.SemaphoreType.DMA,
@@ -347,13 +352,13 @@
     return call(kernel, grid, ins, args, outs, shapes, scratch, flops)
 
 
-def grad_call(x, *lefts):
+def grad_call(x, left):
     experts, rows, width = x.shape
-    hidden = lefts[0].shape[1]
-    shapes = [bf16(experts, hidden, width)] * len(lefts)
-    ins = [each(x)] + [each(left) for left in lefts]
-    flops = 2 * experts * rows * hidden * width * len(lefts)
-    return call(grad_kernel, experts, ins, (x, *lefts), [each(s) for s in shapes], shapes, flops=flops)
+    hidden = left.shape[1]
+    shape = bf16(experts, hidden, width)
+    flops = 2 * experts * rows * hidden * width
+    ins, outs = [each(x), each(left)], [each(shape)]
+    return call(grad_kernel, experts, ins, (x, left), outs, [shape], flops=flops)[0]
 
 
 def dense_body(
@@ -371,36 +376,61 @@
     used = slots[:, :, None] == jnp.arange(total_experts, dtype=jnp.int32)
     prob = jnp.sum(jnp.where(used, gate_prob[:, :, None], 0.0), axis=1)
     high = lax.reduce_precision(prob, 8, 7)
-    extended = jnp.concatenate(
-        [tokens, high.astype(jnp.bfloat16), (prob - high).astype(jnp.bfloat16)], axis=1
-    )
+    parts = jnp.concatenate([high.astype(jnp.bfloat16), (prob - high).astype(jnp.bfloat16)], axis=1)
 
     slot = lax.axis_index("expert") * local + jnp.arange(local * places, dtype=jnp.int32) // places
     spots = jnp.arange(2 * total_experts, dtype=jnp.int32)
     mine = (slot[:, None] == spots[None, :]).astype(jnp.bfloat16)
-    both = (slot[:, None] == spots[None, :] % total_experts).astype(jnp.float32)
+    both = (slot[None, :] == spots[:, None] % total_experts).astype(jnp.bfloat16)
     maps = ((slot[None, :] == spots[:, None]).astype(jnp.bfloat16), mine, both)
 
-    near, far = swap(extended, Z1), swap(extended, Z2)
-    last = swap(far, Z1)
-    cotangent, last = together(cotangent, last)
-    own, other = [], []
-    for rows in (extended, jnp.concatenate([near, far]), last):
-        rows = jnp.concatenate([rows, swap(rows, X, Y)])
-        rows = jnp.concatenate([rows, swap(rows, Y, X)])
-        own.append(rows)
-        other.append(swap(rows, CORE))
-
-    grads = jnp.concatenate([cotangent] + [swap(cotangent, bit) for bit in (Z1, Z2, Z3)])
-    grads = jnp.concatenate([grads, swap(grads, X, Y)])
-    *rows, grads = together(*own, *other, grads)
+    def rows_of(*blocks):
+        return jnp.concatenate(blocks)
+
+    def wide(values, extra):
+        return jnp.concatenate([values, extra], axis=1)
+
+    near, far = swap(tokens, Z1), swap(tokens, Z2)
+    near_parts, far_parts = swap(parts, Z1), swap(parts, Z2)
+    zero = wide(tokens, parts)
+    first0 = swap(zero, X, Y)
+    near, far, near_parts, far_parts = together(near, far, near_parts, far_parts)
+
+    last, last_parts = swap(far, Z1), swap(far_parts, Z1)
+    middle_rows = wide(rows_of(near, far), rows_of(near_parts, far_parts))
+    first1 = swap(middle_rows, X, Y)
+    zero = rows_of(zero, first0)
+    second0 = swap(zero, Y, X)
+    cotangent, last_parts = together(cotangent, last_parts)
+    grads = [swap(cotangent, bit) for bit in (Z1, Z2, Z3)]
+    last, last_parts, first1, second0 = together(last, last_parts, first1, second0)
+
+    last = wide(last, last_parts)
+    first2 = swap(last, X, Y)
+    middle_rows = rows_of(middle_rows, first1)
+    second1 = swap(middle_rows, Y, X)
+    zero = rows_of(zero, second0)
+    zero_other = swap(zero, CORE)
+    first2, second1, cotangent = together(first2, second1, cotangent)
+
+    last = rows_of(last, first2)
+    second2 = swap(last, Y, X)
+    middle_rows = rows_of(middle_rows, second1)
+    middle_other = swap(middle_rows, CORE)
+    grads = rows_of(cotangent, *grads)
+    grads = rows_of(grads, swap(grads, X, Y))
+    last = rows_of(last, second2)
+    last_other = swap(last, CORE)
+    *rows, grads = together(
+        zero, middle_rows, last, zero_other, middle_other, last_other, grads
+    )
     far_grads = swap(grads, Y, X)
     grads_other = swap(grads, CORE)
 
     x, put, pick, prob_rows, g, u, h, ht = up_call(
         rows[:3], rows[3:], maps, gate_weight, up_weight, tok_count
     )
-    h, far_grads = together(h, far_grads)
+    h, far_grads, grads_other = together(h, far_grads, grads_other)
     far_grads_other = swap(far_grads, CORE)
     mixed, mixed_other = back_call(put, [h], [down_weight], 0, width)
     mixed_other, far_grads_other = together(mixed_other, far_grads_other)
@@ -446,19 +476,25 @@
     left = by_second(left)
     mixed[2], ht = together(mixed[2], ht)
     mixed = by_first(mixed)
-    (down_weight_grad,) = grad_call(c, ht)
+    down_weight_grad = grad_call(c, ht)
 
     right[1], left[2], mixed[3], down_weight_grad = together(
         right[1], left[2], mixed[3], down_weight_grad
     )
     right, left, mixed = by_second(right), by_first(left), by_far(mixed)
-    right[0], dgt, dut = together(right[0], dgt, dut)
-    gate_weight_grad, up_weight_grad = grad_call(x, dgt, dut)
+    right[0], dgt = together(right[0], dgt)
+    gate_weight_grad = grad_call(x, dgt)
 
     right[2], left[3], mixed[4], gate_weight_grad = together(
         right[2], left[3], mixed[4], gate_weight_grad
     )
     right, left, mixed = by_first(right), by_far(left), by_near(mixed)
+    right[0], dut = together(right[0], dut)
+    up_weight_grad = grad_call(x, dut)
+
+    right[3], left[4], mixed[5], up_weight_grad = together(
+        right[3], left[4], mixed[5], up_weight_grad
+    )
     right, left = by_far(right), by_near(left)
     right = by_near(right)
     mixed, left, right = (leaving(parts, 0, tok_count) for parts in (mixed, left, right))

time: 197 us -> 191 us (0.970)
  waiting for transfers between devices: 42.4 us -> 35 us
  other arithmetic: 18.3 us -> 22.2 us
  starting transfers between devices: 39.2 us -> 36.4 us
    ppermute x34 -> x37, waiting for transfers between devices: 42.4 us -> 35 us  [swap(): return lax.ppermute(values, AXES, pairs)]
    convert_element_type x15, other arithmetic: 13.8 us -> 16.6 us  [add(): return total.astype(jnp.bfloat16)]
    ppermute x34 -> x37, starting transfers between devices: 39.2 us -> 36.4 us  [swap(): return lax.ppermute(values, AXES, pairs)]
    pallas_call x7 -> x8, Pallas kernels: 90.1 us -> 91.1 us  [call(): pl.pallas_call(kernel, grid=(grid,), in_specs=ins, out_specs=outs, out_sh...]
  transfers between devices with their start and end apart: 34 -> 37, of which waited for: 15 -> 12; matrix products, arithmetic and copies ran while one was open for 7% -> 10% of each run, Pallas kernels for 46% -> 48%
where the time goes in v4:
time: 191 us; the launch traced here: 189 us
  Pallas kernels  91.1 us (48%)
  starting transfers between devices  36.4 us (19%)
  waiting for transfers between devices  35 us (18%)
  other arithmetic  22.2 us (12%)
  local copies, waits for them, and re-layouts  3.34 us (2%)
    pallas_call x8, Pallas kernels, call(): pl.pallas_call(kernel, grid=(grid,), in_specs=ins, out_specs=outs, out_sh...  91.1 us
    ppermute x37, starting transfers between devices, swap(): return lax.ppermute(values, AXES, pairs)  36.4 us
    ppermute x37, waiting for transfers between devices, swap(): return lax.ppermute(values, AXES, pairs)  35 us
    convert_element_type x15, other arithmetic, add(): return total.astype(jnp.bfloat16)  16.6 us
  transfers between devices with their start and end apart: 37, of which 12 were waited for; matrix products, arithmetic and copies ran while one was open for 10% of the time, Pallas kernels for 48%

profile of v4, /device:TPU:0, one launch (start us, length us, event | category | flops | bytes accessed | tf_op | source)
XLA Modules:
  0.0 189.3 jit_solution(11264245840454603047)
XLA Ops:
  0.6 3.1 %collective-permute-start.1 = (bf16[16,4096]{1,0:T(8,128)(2,1)}, bf16[16,4096]{1,0:T(8,128)(2,1)S(1)}, u32[]{:S(2)}, u32[]{:S(2)}) collective-permute-start(bf16[16,4096]{1,0:T(8,128)(2,1)} %param.8), channel_id=1, source_target_pairs={{0,2},{1,3},{2,0},{3,1},{4,6},{5,7},{6,4},{7,5},{8,10},{9,11},{10,... | collective-permute-start | bytes 393224 | tf_op jit(solution)/shard_map/ppermute | solution.py:31
  3.7 2.6 %collective-permute-start.2 = (bf16[16,4096]{1,0:T(8,128)(2,1)}, bf16[16,4096]{1,0:T(8,128)(2,1)S(1)}, u32[]{:S(2)}, u32[]{:S(2)}) collective-permute-start(bf16[16,4096]{1,0:T(8,128)(2,1)} %param.8), channel_id=1, source_target_pairs={{0,4},{1,5},{2,6},{3,7},{4,0},{5,1},{6,2},{7,3},{8,12},{9,13},{10,... | collective-permute-start | bytes 393224 | tf_op jit(solution)/shard_map/ppermute | solution.py:31
  10.6 1.8 collective-permute-start
  14.1 1.6 collective-permute-start.7
  15.7 1.8 collective-permute-start.8
  17.5 1.6 collective-permute-start.5
  19.6 3.3 %collective-permute-done.6 = bf16[16,128]{1,0:T(8,128)(2,1)S(1)} collective-permute-done((bf16[16,128]{1,0:T(8,128)(2,1)S(1)}, bf16[16,128]{1,0:T(8,128)(2,1)S(1)}, u32[]{:S(2)}, u32[]{:S(2)}) %collective-permute-start.6) | collective-permute-done | bytes 4128 | tf_op jit(solution)/shard_map/ppermute | solution.py:31
  22.9 2.0 %collective-permute-start.15 = (bf16[16,4096]{1,0:T(8,128)(2,1)S(1)}, bf16[16,4096]{1,0:T(8,128)(2,1)S(1)}, u32[]{:S(2)}, u32[]{:S(2)}) collective-permute-start(bf16[16,4096]{1,0:T(8,128)(2,1)S(1)} %copy-done.13), channel_id=1, source_target_pairs={{0,2},{1,3},{2,0},{3,1},{4,6},{5,7},{6,4},{7,5},{8,10},{9,11},{10,... | collective-permute-start | bytes 393224 | tf_op jit(solution)/shard_map/ppermute | solution.py:31
  24.9 4.1 %collective-permute-start.16 = (bf16[16,4096]{1,0:T(8,128)(2,1)S(1)}, bf16[16,4096]{1,0:T(8,128)(2,1)S(1)}, u32[]{:S(2)}, u32[]{:S(2)}) collective-permute-start(bf16[16,4096]{1,0:T(8,128)(2,1)S(1)} %copy-done.13), channel_id=1, source_target_pairs={{0,4},{1,5},{2,6},{3,7},{4,0},{5,1},{6,2},{7,3},{8,12},{9,13},{10,... | collective-permute-start | bytes 393224 | tf_op jit(solution)/shard_map/ppermute | solution.py:31
  29.0 2.2 %collective-permute-start.9 = (bf16[16,4224]{1,0:T(8,128)(2,1)S(1)}, bf16[16,4224]{1,0:T(8,128)(2,1)S(1)}, u32[]{:S(2)}, u32[]{:S(2)}) collective-permute-start(bf16[16,4224]{1,0:T(8,128)(2,1)S(1)} %constant_dynamic-update-slice_fusion), channel_id=1, source_target_pairs={{0,8},{1,17},{2,10},{3,19},{4,12},{5,21},{6,14},{7,23},{8,0},{9,25... | collective-permute-start | bytes 405512 | tf_op jit(solution)/shard_map/ppermute | solution.py:31
  31.4 2.8 %collective-permute-done.9 = bf16[16,4224]{1,0:T(8,128)(2,1)S(1)} collective-permute-done((bf16[16,4224]{1,0:T(8,128)(2,1)S(1)}, bf16[16,4224]{1,0:T(8,128)(2,1)S(1)}, u32[]{:S(2)}, u32[]{:S(2)}) %collective-permute-start.9) | collective-permute-done | bytes 135200 | tf_op jit(solution)/shard_map/ppermute | solution.py:31
  34.2 9.6 %collective-permute-done.10 = bf16[64,4224]{1,0:T(8,128)(2,1)S(1)} collective-permute-done((bf16[64,4224]{1,0:T(8,128)(2,1)S(1)}, bf16[64,4224]{1,0:T(8,128)(2,1)S(1)}, u32[]{:S(2)}, u32[]{:S(2)}) %collective-permute-start.10) | collective-permute-done | bytes 540704 | tf_op jit(solution)/shard_map/ppermute | solution.py:31
  44.3 6.2 %collective-permute-done.11 = bf16[32,4224]{1,0:T(8,128)(2,1)S(1)} collective-permute-done((bf16[32,4224]{1,0:T(8,128)(2,1)S(1)}, bf16[32,4224]{1,0:T(8,128)(2,1)S(1)}, u32[]{:S(2)}, u32[]{:S(2)}) %collective-permute-start.11) | collective-permute-done | bytes 270368 | tf_op jit(solution)/shard_map/ppermute | solution.py:31
  50.7 2.5 %collective-permute-done.18 = bf16[64,4096]{1,0:T(8,128)(2,1)S(1)} collective-permute-done((bf16[64,4096]{1,0:T(8,128)(2,1)S(1)}, bf16[64,4096]{1,0:T(8,128)(2,1)S(1)}, u32[]{:S(2)}, u32[]{:S(2)}) %collective-permute-start.18) | collective-permute-done | bytes 524320 | tf_op jit(solution)/shard_map/ppermute | solution.py:31
  56.0 17.1 %shard_map.127 = (bf16[8,96,4096]{2,1,0:T(8,128)(2,1)}, bf16[2,256,384]{2,1,0:T(8,128)(2,1)}, bf16[2,384,256]{2,1,0:T(8,128)(2,1)}, f32[8,1,96]{2,1,0:T(1,128)},...) custom-call(bf16[64,4224]{1,0:T(8,128)(2,1)} %copy-done.1, ...), custom_call_target="tpu_custom_call" | custom-call | flops 4026531840 | bytes 38636544 | tf_op jit(solution)/shard_map/pallas_call | solution.py:257
  73.3 10.0 %shard_map.128 = (bf16[256,4096]{1,0:T(8,128)(2,1)}, bf16[256,4096]{1,0:T(8,128)(2,1)}) custom-call(bf16[2,256,384]{2,1,0:T(8,128)(2,1)} %get-tuple-element.96.put_ref, bf16[8,96,192]{2,1,0:T(8,128)(2,1)} %get-tuple-element.99.refs_0_, bf16[8,192,4096]{2,1,0:T(8,128)(2,1)} %down_ref.1), custom_call_target="tpu_custom_call" | custom-call | flops 2818572288 | bytes 17465344 | tf_op jit(solution)/shard_map/pallas_call | solution.py:257
  84.3 15.9 %shard_map.129 = (bf16[8,96,4096]{2,1,0:T(8,128)(2,1)}, bf16[8,96,192]{2,1,0:T(8,128)(2,1)}, bf16[8,96,192]{2,1,0:T(8,128)(2,1)}, bf16[8,192,96]{2,1,0:T(8,128)(...) custom-call(bf16[128,4096]{1,0:T(8,128)(2,1)} %copy-done.4, bf16[128,4096]{1,0:T(8,128)(2,1)} %copy-done.8, ...), custom_call_target="tpu_custom_call" | custom-call | flops 2818572288 | bytes 26446848 | tf_op jit(solution)/shard_map/pallas_call | solution.py:257
  101.8 8.1 %shard_map.130 = (bf16[256,2048]{1,0:T(8,128)(2,1)}, bf16[256,2048]{1,0:T(8,128)(2,1)}) custom-call(bf16[2,256,384]{2,1,0:T(8,128)(2,1)} %get-tuple-element.96.put_ref, bf16[8,96,192]{2,1,0:T(8,128)(2,1)} %get-tuple-element.118.refs_0_, bf16[8,96,192]{2,1,0:T(8,128)(2,1)} %get-tuple-element.119.refs_1_, bf16[8,192,4096]{2,1,0:T(8,128)(2,1)} %refs_2_.3, ...), custom_call_target="tpu_custom_call" | custom-call | flops 2013265920 | bytes 28246016 | tf_op jit(solution)/shard_map/pallas_call | solution.py:257
  110.0 8.2 %shard_map.131 = (bf16[256,2176]{1,0:T(8,128)(2,1)}, bf16[256,2176]{1,0:T(8,128)(2,1)}) custom-call(bf16[2,256,384]{2,1,0:T(8,128)(2,1)} %get-tuple-element.96.put_ref, bf16[8,96,192]{2,1,0:T(8,128)(2,1)} %get-tuple-element.118.refs_0_, bf16[8,96,192]{2,1,0:T(8,128)(2,1)} %get-tuple-element.119.refs_1_, bf16[8,192,4096]{2,1,0:T(8,128)(2,1)} %refs_2_.3, ...), custom_call_target="tpu_custom_call" | custom-call | flops 2013265920 | bytes 28508160 | tf_op jit(solution)/shard_map/pallas_call | solution.py:257
  118.7 2.1 %add_convert_fusion.2 = bf16[64,4096]{1,0:T(8,128)(2,1)} fusion(bf16[128,4096]{1,0:T(8,128)(2,1)} %collective-permute-done.23, bf16[256,4096]{1,0:T(8,128)(2,1)S(1)} %collective-permute-done.22, bf16[256,4096]{1,0:T(8,128)(2,1)S(1)} %copy-done.3), kind=kLoop, calls=%fused_computation.3 | loop fusion | flops 1572864 | bytes 2097152 | tf_op jit(solution)/shard_map/convert_element_type | solution.py:38
  123.6 10.6 %shard_map.132 = bf16[8,192,4096]{2,1,0:T(8,128)(2,1)} custom-call(bf16[8,96,4096]{2,1,0:T(8,128)(2,1)} %get-tuple-element.126.x_ref, bf16[8,192,96]{2,1,0:T(8,128)(2,1)} %get-tuple-element.127.left), custom_call_target="tpu_custom_call" | custom-call | flops 1207959552 | bytes 19169280 | tf_op jit(solution)/shard_map/pallas_call | solution.py:257
  138.5 1.9 add_convert_fusion.6
  141.1 10.6 %shard_map.133 = bf16[8,192,4096]{2,1,0:T(8,128)(2,1)} custom-call(bf16[8,96,4096]{2,1,0:T(8,128)(2,1)} %get-tuple-element.132.x_ref, bf16[8,192,96]{2,1,0:T(8,128)(2,1)} %get-tuple-element.134.left), custom_call_target="tpu_custom_call" | custom-call | flops 1207959552 | bytes 19169280 | tf_op jit(solution)/shard_map/pallas_call | solution.py:257
  151.8 1.8 add_convert_fusion.9
  153.6 3.1 %collective-permute-start.33 = (bf16[16,4096]{1,0:T(8,128)(2,1)}, bf16[16,4096]{1,0:T(8,128)(2,1)}, u32[]{:S(2)}, u32[]{:S(2)}) collective-permute-start(bf16[16,4096]{1,0:T(8,128)(2,1)} %add_convert_fusion.9), channel_id=1, source_target_pairs={{0,2},{1,3},{2,0},{3,1},{4,6},{5,7},{6,4},{7,5},{8,10},{9,11},{10,... | collective-permute-start | bytes 393224 | tf_op jit(solution)/shard_map/ppermute | solution.py:31
  158.9 1.8 add_convert_fusion.10
  160.6 10.6 %shard_map.134 = bf16[8,192,4096]{2,1,0:T(8,128)(2,1)} custom-call(bf16[8,96,4096]{2,1,0:T(8,128)(2,1)} %get-tuple-element.132.x_ref, bf16[8,192,96]{2,1,0:T(8,128)(2,1)} %get-tuple-element.140.left), custom_call_target="tpu_custom_call" | custom-call | flops 1207959552 | bytes 19169280 | tf_op jit(solution)/shard_map/pallas_call | solution.py:257
  172.2 1.7 collective-permute-start.34
  175.4 1.9 add_convert_fusion.8
  177.2 5.2 %collective-permute-done.35 = bf16[32,2176]{1,0:T(8,128)(2,1)S(1)} collective-permute-done((bf16[32,2176]{1,0:T(8,128)(2,1)S(1)}, bf16[32,2176]{1,0:T(8,128)(2,1)S(1)}, u32[]{:S(2)}, u32[]{:S(2)}) %collective-permute-start.35) | collective-permute-done | bytes 139296 | tf_op jit(solution)/shard_map/ppermute | solution.py:31
  182.6 1.6 add_convert_fusion.13
  184.2 2.7 %collective-permute-done.36 = bf16[16,2176]{1,0:T(8,128)(2,1)S(1)} collective-permute-done((bf16[16,2176]{1,0:T(8,128)(2,1)S(1)}, bf16[16,2176]{1,0:T(8,128)(2,1)S(1)}, u32[]{:S(2)}, u32[]{:S(2)}) %collective-permute-start.36) | collective-permute-done | bytes 69664 | tf_op jit(solution)/shard_map/ppermute | solution.py:31
  (126 shorter events, 28.2 us)
Async XLA Ops:
  0.6 13.4 %collective-permute-start.1 = (bf16[16,4096]{1,0:T(8,128)(2,1)}, bf16[16,4096]{1,0:T(8,128)(2,1)S(1)}, u32[]{:S(2)}, u32[]{:S(2)}) collective-permute-start(bf16[16,4096]{1,0:T(8,128)(2,1)} %param.8), channel_id=1, source_target_pairs={{0,2},{1,3},{2,0},{3,1},{4,6},{5,7},{6,4},{7,5},{8,10},{9,11},{10,... | collective-permute-start | bytes 393224 | tf_op jit(solution)/shard_map/ppermute | solution.py:31
  3.7 10.4 %collective-permute-start.2 = (bf16[16,4096]{1,0:T(8,128)(2,1)}, bf16[16,4096]{1,0:T(8,128)(2,1)S(1)}, u32[]{:S(2)}, u32[]{:S(2)}) collective-permute-start(bf16[16,4096]{1,0:T(8,128)(2,1)} %param.8), channel_id=1, source_target_pairs={{0,4},{1,5},{2,6},{3,7},{4,0},{5,1},{6,2},{7,3},{8,12},{9,13},{10,... | collective-permute-start | bytes 393224 | tf_op jit(solution)/shard_map/ppermute | solution.py:31
  10.6 5.1 %collective-permute-start = (bf16[16,4224]{1,0:T(8,128)(2,1)S(1)}, bf16[16,4224]{1,0:T(8,128)(2,1)S(1)}, u32[]{:S(2)}, u32[]{:S(2)}) collective-permute-start(bf16[16,4224]{1,0:T(8,128)(2,1)S(1)} %concatenate.50), channel_id=1, source_target_pairs={{0,8},{1,17},{2,10},{3,19},{4,12},{5,21},{6,14},{7,23},{8,0},{9,25... | collective-permute-start | bytes 405512 | tf_op jit(solution)/shard_map/ppermute | solution.py:31
  14.1 14.9 %collective-permute-start.7 = (bf16[32,4224]{1,0:T(8,128)(2,1)S(1)}, bf16[32,4224]{1,0:T(8,128)(2,1)S(1)}, u32[]{:S(2)}, u32[]{:S(2)}) collective-permute-start(bf16[32,4224]{1,0:T(8,128)(2,1)S(1)} %maximum_maximum_fusion), channel_id=1, source_target_pairs={{0,8},{1,17},{2,10},{3,19},{4,12},{5,21},{6,14},{7,23},{8,0},{9,25... | collective-permute-start | bytes 811016 | tf_op jit(solution)/shard_map/ppermute | solution.py:31
  15.7 13.3 %collective-permute-start.8 = (bf16[32,4224]{1,0:T(8,128)(2,1)S(1)}, bf16[32,4224]{1,0:T(8,128)(2,1)S(1)}, u32[]{:S(2)}, u32[]{:S(2)}) collective-permute-start(bf16[32,4224]{1,0:T(8,128)(2,1)S(1)} %pad_maximum_fusion.5), channel_id=1, source_target_pairs={{0,16},{1,9},{2,18},{3,11},{4,20},{5,13},{6,22},{7,15},{8,24},{9,1... | collective-permute-start | bytes 811016 | tf_op jit(solution)/shard_map/ppermute | solution.py:31
  17.5 11.4 %collective-permute-start.5 = (bf16[16,4096]{1,0:T(8,128)(2,1)S(1)}, bf16[16,4096]{1,0:T(8,128)(2,1)S(1)}, u32[]{:S(2)}, u32[]{:S(2)}) collective-permute-start(bf16[16,4096]{1,0:T(8,128)(2,1)S(1)} %collective-permute-done.2), channel_id=1, source_target_pairs={{0,2},{1,3},{2,0},{3,1},{4,6},{5,7},{6,4},{7,5},{8,10},{9,11},{10,... | collective-permute-start | bytes 393224 | tf_op jit(solution)/shard_map/ppermute | solution.py:31
  22.9 21.0 %collective-permute-start.15 = (bf16[16,4096]{1,0:T(8,128)(2,1)S(1)}, bf16[16,4096]{1,0:T(8,128)(2,1)S(1)}, u32[]{:S(2)}, u32[]{:S(2)}) collective-permute-start(bf16[16,4096]{1,0:T(8,128)(2,1)S(1)} %copy-done.13), channel_id=1, source_target_pairs={{0,2},{1,3},{2,0},{3,1},{4,6},{5,7},{6,4},{7,5},{8,10},{9,11},{10,... | collective-permute-start | bytes 393224 | tf_op jit(solution)/shard_map/ppermute | solution.py:31
  24.9 19.0 %collective-permute-start.16 = (bf16[16,4096]{1,0:T(8,128)(2,1)S(1)}, bf16[16,4096]{1,0:T(8,128)(2,1)S(1)}, u32[]{:S(2)}, u32[]{:S(2)}) collective-permute-start(bf16[16,4096]{1,0:T(8,128)(2,1)S(1)} %copy-done.13), channel_id=1, source_target_pairs={{0,4},{1,5},{2,6},{3,7},{4,0},{5,1},{6,2},{7,3},{8,12},{9,13},{10,... | collective-permute-start | bytes 393224 | tf_op jit(solution)/shard_map/ppermute | solution.py:31
  29.0 14.9 %collective-permute-start.17 = (bf16[16,4096]{1,0:T(8,128)(2,1)S(1)}, bf16[16,4096]{1,0:T(8,128)(2,1)S(1)}, u32[]{:S(2)}, u32[]{:S(2)}) collective-permute-start(bf16[16,4096]{1,0:T(8,128)(2,1)S(1)} %copy-done.13), channel_id=1, source_target_pairs={{0,6},{1,7},{2,4},{3,5},{4,2},{5,3},{6,0},{7,1},{8,14},{9,15},{10,... | collective-permute-start | bytes 393224 | tf_op jit(solution)/shard_map/ppermute | solution.py:31
  29.0 5.2 %collective-permute-start.9 = (bf16[16,4224]{1,0:T(8,128)(2,1)S(1)}, bf16[16,4224]{1,0:T(8,128)(2,1)S(1)}, u32[]{:S(2)}, u32[]{:S(2)}) collective-permute-start(bf16[16,4224]{1,0:T(8,128)(2,1)S(1)} %constant_dynamic-update-slice_fusion), channel_id=1, source_target_pairs={{0,8},{1,17},{2,10},{3,19},{4,12},{5,21},{6,14},{7,23},{8,0},{9,25... | collective-permute-start | bytes 405512 | tf_op jit(solution)/shard_map/ppermute | solution.py:31
  31.3 12.6 %collective-permute-start.10 = (bf16[64,4224]{1,0:T(8,128)(2,1)S(1)}, bf16[64,4224]{1,0:T(8,128)(2,1)S(1)}, u32[]{:S(2)}, u32[]{:S(2)}) collective-permute-start(bf16[64,4224]{1,0:T(8,128)(2,1)S(1)} %pad_maximum_fusion.2), channel_id=1, source_target_pairs={{0,16},{1,9},{2,18},{3,11},{4,20},{5,13},{6,22},{7,15},{8,24},{9,1... | collective-permute-start | bytes 1622024 | tf_op jit(solution)/shard_map/ppermute | solution.py:31
  34.2 19.0 %collective-permute-start.12 = (bf16[64,4224]{1,0:T(8,128)(2,1)S(1)}, bf16[64,4224]{1,0:T(8,128)(2,1)S(1)}, u32[]{:S(2)}, u32[]{:S(2)}) collective-permute-start(bf16[64,4224]{1,0:T(8,128)(2,1)S(1)} %pad_maximum_fusion.1.own0), channel_id=1, source_target_pairs={{0,1},{1,0},{2,3},{3,2},{4,5},{5,4},{6,7},{7,6},{8,9},{9,8},{10,11... | collective-permute-start | bytes 1622024 | tf_op jit(solution)/shard_map/ppermute | solution.py:31
  43.9 9.2 %collective-permute-start.18 = (bf16[64,4096]{1,0:T(8,128)(2,1)S(1)}, bf16[64,4096]{1,0:T(8,128)(2,1)S(1)}, u32[]{:S(2)}, u32[]{:S(2)}) collective-permute-start(bf16[64,4096]{1,0:T(8,128)(2,1)S(1)} %pad_maximum_fusion.4), channel_id=1, source_target_pairs={{0,8},{1,17},{2,10},{3,19},{4,12},{5,21},{6,14},{7,23},{8,0},{9,25... | collective-permute-start | bytes 1572872 | tf_op jit(solution)/shard_map/ppermute | solution.py:31
  44.0 6.5 %collective-permute-start.11 = (bf16[32,4224]{1,0:T(8,128)(2,1)S(1)}, bf16[32,4224]{1,0:T(8,128)(2,1)S(1)}, u32[]{:S(2)}, u32[]{:S(2)}) collective-permute-start(bf16[32,4224]{1,0:T(8,128)(2,1)S(1)} %pad_maximum_fusion.6), channel_id=1, source_target_pairs={{0,16},{1,9},{2,18},{3,11},{4,20},{5,13},{6,22},{7,15},{8,24},{9,1... | collective-permute-start | bytes 811016 | tf_op jit(solution)/shard_map/ppermute | solution.py:31
  44.2 9.0 %collective-permute-start.13 = (bf16[128,4224]{1,0:T(8,128)(2,1)S(1)}, bf16[128,4224]{1,0:T(8,128)(2,1)S(1)}, u32[]{:S(2)}, u32[]{:S(2)}) collective-permute-start(bf16[128,4224]{1,0:T(8,128)(2,1)S(1)} %pad_maximum_fusion.own1), channel_id=1, source_target_pairs={{0,1},{1,0},{2,3},{3,2},{4,5},{5,4},{6,7},{7,6},{8,9},{9,8},{10,11... | collective-permute-start | bytes 3244040 | tf_op jit(solution)/shard_map/ppermute | solution.py:31
  53.3 19.9 %collective-permute-start.19 = (bf16[128,4096]{1,0:T(8,128)(2,1)S(1)}, bf16[128,4096]{1,0:T(8,128)(2,1)S(1)}, u32[]{:S(2)}, u32[]{:S(2)}) collective-permute-start(bf16[128,4096]{1,0:T(8,128)(2,1)S(1)} %constant_dynamic-update-slice_fusion.2.own0), channel_id=1, source_target_pairs={{0,16},{1,9},{2,18},{3,11},{4,20},{5,13},{6,22},{7,15},{8,24},{9,1... | collective-permute-start | bytes 3145736 | tf_op jit(solution)/shard_map/ppermute | solution.py:31
  53.4 19.8 %collective-permute-start.20 = (bf16[128,4096]{1,0:T(8,128)(2,1)S(1)}, bf16[128,4096]{1,0:T(8,128)(2,1)S(1)}, u32[]{:S(2)}, u32[]{:S(2)}) collective-permute-start(bf16[128,4096]{1,0:T(8,128)(2,1)S(1)} %constant_dynamic-update-slice_fusion.2.own0), channel_id=1, source_target_pairs={{0,1},{1,0},{2,3},{3,2},{4,5},{5,4},{6,7},{7,6},{8,9},{9,8},{10,11... | collective-permute-start | bytes 3145736 | tf_op jit(solution)/shard_map/ppermute | solution.py:31
  73.2 10.1 %collective-permute-start.21 = (bf16[128,4096]{1,0:T(8,128)(2,1)S(1)}, bf16[128,4096]{1,0:T(8,128)(2,1)S(1)}, u32[]{:S(2)}, u32[]{:S(2)}) collective-permute-start(bf16[128,4096]{1,0:T(8,128)(2,1)S(1)} %collective-permute-done.19.own1), channel_id=1, source_target_pairs={{0,1},{1,0},{2,3},{3,2},{4,5},{5,4},{6,7},{7,6},{8,9},{9,8},{10,11... | collective-permute-start | bytes 3145736 | tf_op jit(solution)/shard_map/ppermute | solution.py:31
  83.3 16.9 %collective-permute-start.22 = (bf16[256,4096]{1,0:T(8,128)(2,1)}, bf16[256,4096]{1,0:T(8,128)(2,1)S(1)}, u32[]{:S(2)}, u32[]{:S(2)}) collective-permute-start(bf16[256,4096]{1,0:T(8,128)(2,1)} %get-tuple-element.103), channel_id=1, source_target_pairs={{0,1},{1,0},{2,3},{3,2},{4,5},{5,4},{6,7},{7,6},{8,9},{9,8},{10,11... | collective-permute-start | bytes 6291464 | tf_op jit(solution)/shard_map/ppermute | solution.py:31
  100.5 18.2 %collective-permute-start.23 = (bf16[128,4096]{1,0:T(8,128)(2,1)S(1)}, bf16[128,4096]{1,0:T(8,128)(2,1)}, u32[]{:S(2)}, u32[]{:S(2)}) collective-permute-start(bf16[128,4096]{1,0:T(8,128)(2,1)S(1)} %add_convert_fusion), channel_id=1, source_target_pairs={{0,16},{1,9},{2,18},{3,11},{4,20},{5,13},{6,22},{7,15},{8,24},{9,1... | collective-permute-start | bytes 3145736 | tf_op jit(solution)/shard_map/ppermute | solution.py:31
  109.9 10.9 %collective-permute-start.25 = (bf16[256,2048]{1,0:T(8,128)(2,1)}, bf16[256,2048]{1,0:T(8,128)(2,1)}, u32[]{:S(2)}, u32[]{:S(2)}) collective-permute-start(bf16[256,2048]{1,0:T(8,128)(2,1)} %get-tuple-element.124), channel_id=1, source_target_pairs={{0,1},{1,0},{2,3},{3,2},{4,5},{5,4},{6,7},{7,6},{8,9},{9,8},{10,11... | collective-permute-start | bytes 3145736 | tf_op jit(solution)/shard_map/ppermute | solution.py:31
  118.2 16.0 %collective-permute-start.24 = (bf16[256,2176]{1,0:T(8,128)(2,1)}, bf16[256,2176]{1,0:T(8,128)(2,1)S(1)}, u32[]{:S(2)}, u32[]{:S(2)}) collective-permute-start(bf16[256,2176]{1,0:T(8,128)(2,1)} %get-tuple-element.121), channel_id=1, source_target_pairs={{0,1},{1,0},{2,3},{3,2},{4,5},{5,4},{6,7},{7,6},{8,9},{9,8},{10,11... | collective-permute-start | bytes 3342344 | tf_op jit(solution)/shard_map/ppermute | solution.py:31
  120.8 14.1 %collective-permute-start.27 = (bf16[64,4096]{1,0:T(8,128)(2,1)}, bf16[64,4096]{1,0:T(8,128)(2,1)}, u32[]{:S(2)}, u32[]{:S(2)}) collective-permute-start(bf16[64,4096]{1,0:T(8,128)(2,1)} %add_convert_fusion.2), channel_id=1, source_target_pairs={{0,8},{1,17},{2,10},{3,19},{4,12},{5,21},{6,14},{7,23},{8,0},{9,25... | collective-permute-start | bytes 1572872 | tf_op jit(solution)/shard_map/ppermute | solution.py:31
  123.4 11.7 %collective-permute-start.26 = (bf16[128,2048]{1,0:T(8,128)(2,1)S(1)}, bf16[128,2048]{1,0:T(8,128)(2,1)}, u32[]{:S(2)}, u32[]{:S(2)}) collective-permute-start(bf16[128,2048]{1,0:T(8,128)(2,1)S(1)} %add_convert_fusion.3), channel_id=1, source_target_pairs={{0,16},{1,9},{2,18},{3,11},{4,20},{5,13},{6,22},{7,15},{8,24},{9,1... | collective-permute-start | bytes 1572872 | tf_op jit(solution)/shard_map/ppermute | solution.py:31
  136.3 15.6 %collective-permute-start.30 = (bf16[32,4096]{1,0:T(8,128)(2,1)S(1)}, bf16[32,4096]{1,0:T(8,128)(2,1)}, u32[]{:S(2)}, u32[]{:S(2)}) collective-permute-start(bf16[32,4096]{1,0:T(8,128)(2,1)S(1)} %add_convert_fusion.5), channel_id=1, source_target_pairs={{0,4},{1,5},{2,6},{3,7},{4,0},{5,1},{6,2},{7,3},{8,12},{9,13},{10,... | collective-permute-start | bytes 786440 | tf_op jit(solution)/shard_map/ppermute | solution.py:31
  137.4 14.5 %collective-permute-start.28 = (bf16[128,2176]{1,0:T(8,128)(2,1)}, bf16[128,2176]{1,0:T(8,128)(2,1)S(1)}, u32[]{:S(2)}, u32[]{:S(2)}) collective-permute-start(bf16[128,2176]{1,0:T(8,128)(2,1)} %add_convert_fusion.1), channel_id=1, source_target_pairs={{0,16},{1,9},{2,18},{3,11},{4,20},{5,13},{6,22},{7,15},{8,24},{9,1... | collective-permute-start | bytes 1671176 | tf_op jit(solution)/shard_map/ppermute | solution.py:31
  140.4 11.5 %collective-permute-start.29 = (bf16[64,2048]{1,0:T(8,128)(2,1)}, bf16[64,2048]{1,0:T(8,128)(2,1)}, u32[]{:S(2)}, u32[]{:S(2)}) collective-permute-start(bf16[64,2048]{1,0:T(8,128)(2,1)} %add_convert_fusion.6), channel_id=1, source_target_pairs={{0,8},{1,17},{2,10},{3,19},{4,12},{5,21},{6,14},{7,23},{8,0},{9,25... | collective-permute-start | bytes 786440 | tf_op jit(solution)/shard_map/ppermute | solution.py:31
  153.6 17.6 %collective-permute-start.33 = (bf16[16,4096]{1,0:T(8,128)(2,1)}, bf16[16,4096]{1,0:T(8,128)(2,1)}, u32[]{:S(2)}, u32[]{:S(2)}) collective-permute-start(bf16[16,4096]{1,0:T(8,128)(2,1)} %add_convert_fusion.9), channel_id=1, source_target_pairs={{0,2},{1,3},{2,0},{3,1},{4,6},{5,7},{6,4},{7,5},{8,10},{9,11},{10,... | collective-permute-start | bytes 393224 | tf_op jit(solution)/shard_map/ppermute | solution.py:31
  157.5 13.7 %collective-permute-start.31 = (bf16[64,2176]{1,0:T(8,128)(2,1)}, bf16[64,2176]{1,0:T(8,128)(2,1)S(1)}, u32[]{:S(2)}, u32[]{:S(2)}) collective-permute-start(bf16[64,2176]{1,0:T(8,128)(2,1)} %add_convert_fusion.4), channel_id=1, source_target_pairs={{0,8},{1,17},{2,10},{3,19},{4,12},{5,21},{6,14},{7,23},{8,0},{9,25... | collective-permute-start | bytes 835592 | tf_op jit(solution)/shard_map/ppermute | solution.py:31
  160.6 10.6 %collective-permute-start.32 = (bf16[32,2048]{1,0:T(8,128)(2,1)}, bf16[32,2048]{1,0:T(8,128)(2,1)}, u32[]{:S(2)}, u32[]{:S(2)}) collective-permute-start(bf16[32,2048]{1,0:T(8,128)(2,1)} %add_convert_fusion.10), channel_id=1, source_target_pairs={{0,4},{1,5},{2,6},{3,7},{4,0},{5,1},{6,2},{7,3},{8,12},{9,13},{10,... | collective-permute-start | bytes 393224 | tf_op jit(solution)/shard_map/ppermute | solution.py:31
  172.2 10.3 %collective-permute-start.34 = (bf16[16,2048]{1,0:T(8,128)(2,1)S(1)}, bf16[16,2048]{1,0:T(8,128)(2,1)S(1)}, u32[]{:S(2)}, u32[]{:S(2)}) collective-permute-start(bf16[16,2048]{1,0:T(8,128)(2,1)S(1)} %add_convert_fusion.14), channel_id=1, source_target_pairs={{0,2},{1,3},{2,0},{3,1},{4,6},{5,7},{6,4},{7,5},{8,10},{9,11},{10,... | collective-permute-start | bytes 196616 | tf_op jit(solution)/shard_map/ppermute | solution.py:31
  174.0 8.4 %collective-permute-start.35 = (bf16[32,2176]{1,0:T(8,128)(2,1)S(1)}, bf16[32,2176]{1,0:T(8,128)(2,1)S(1)}, u32[]{:S(2)}, u32[]{:S(2)}) collective-permute-start(bf16[32,2176]{1,0:T(8,128)(2,1)S(1)} %add_convert_fusion.7), channel_id=1, source_target_pairs={{0,4},{1,5},{2,6},{3,7},{4,0},{5,1},{6,2},{7,3},{8,12},{9,13},{10,... | collective-permute-start | bytes 417800 | tf_op jit(solution)/shard_map/ppermute | solution.py:31
  (19 other events, 139.8 us)

commit v5 on v4

--- a/solution.py
+++ b/solution.py
@@ -13,6 +13,7 @@
 GROUPS = ((0,), (1, 2), (3,))
 CHUNK = 512
 WIDE = 1024
+PAIR = 2
 MIB = 1 << 20
 
 NT = (((1,), (1,)), ((), ()))
@@ -122,55 +123,59 @@
             dispatch(pick, rows_ref, half, x_ref)
         pltpu.make_async_copy(x_ref, x_out, sem).start()
 
-    for copy in copies(e):
-        copy.wait()
-    product = dot(held_ref[e], x_ref[e], NT)
-    g, u = product[:hidden], product[hidden:]
-    g_ref[0] = g
-    u_ref[0] = u
-    silu_v, _ = gated(g)
-    scaled = silu_v * u * prob_ref[e]
-    ht_ref[0] = scaled.astype(jnp.bfloat16)
-    h_ref[0] = scaled.T.astype(jnp.bfloat16)
+    pair = pl.ds(PAIR * e, PAIR)
+    for i in range(PAIR):
+        for copy in copies(PAIR * e + i):
+            copy.wait()
+    product = dot(
+        held_ref[pair].reshape(PAIR * 2 * hidden, width), x_ref[pair].reshape(PAIR * both, width), NT
+    )
+    for i in range(PAIR):
+        own = product[2 * hidden * i : 2 * hidden * (i + 1), both * i : both * (i + 1)]
+        g, u = own[:hidden], own[hidden:]
+        g_ref[i] = g
+        u_ref[i] = u
+        silu_v, _ = gated(g)
+        scaled = silu_v * u * prob_ref[PAIR * e + i]
+        ht_ref[i] = scaled.astype(jnp.bfloat16)
+        h_ref[i] = scaled.T.astype(jnp.bfloat16)
 
     @pl.when(e == pl.num_programs(0) - 1)
     def _():
         pltpu.make_async_copy(x_ref, x_out, sem).wait()
 
 
-def slope_kernel(own0, own1, other0, other1, pick_ref, put_ref, prob_ref, mine_ref, down_ref, g_ref, u_ref,
-                 x_out, dg_ref, du_ref, dgt_ref, dut_ref, share_ref, rows_ref, x_ref, shares_ref, terms_ref,
-                 held_ref, held_sems, sem):
+def place_kernel(own0, own1, other0, other1, pick_ref, x_ref):
+    experts, both = x_ref.shape[:2]
+    places = both // 2
+    for half, pieces in enumerate(((own0, own1), (other0, other1))):
+        rows = jnp.concatenate([pieces[0][...], pieces[1][...]], axis=0)
+        rows = dot(pick_ref[half], rows).astype(jnp.bfloat16)
+        for e in range(experts):
+            x_ref[e, half * places : (half + 1) * places] = rows[e * places : (e + 1) * places]
+
+
+def slope_kernel(x_ref, put_ref, prob_ref, mine_ref, down_ref, g_ref, u_ref,
+                 dg_ref, du_ref, dt_ref, share_ref, shares_ref, terms_ref):
     e = pl.program_id(0)
-    experts = x_ref.shape[0]
-    places = x_ref.shape[1] // 2
-
-    def copy(i):
-        return pltpu.make_async_copy(down_ref.at[i], held_ref.at[i], held_sems.at[i])
-
-    @pl.when(e == 0)
-    def _():
-        for i in range(experts):
-            copy(i).start()
-        for half, pieces in enumerate(((own0, own1), (other0, other1))):
-            size = own0.shape[0]
-            rows_ref[half, :size] = pieces[0][...]
-            rows_ref[half, size:] = pieces[1][...]
-            dispatch(pick_ref[half], rows_ref, half, x_ref)
-        pltpu.make_async_copy(x_ref, x_out, sem).start()
-
-    copy(e).wait()
-    plain = dot(held_ref[e], x_ref[e], NT)
-    g, u = g_ref[0], u_ref[0]
-    silu_v, slope = gated(g)
-    shares_ref[pl.ds(e, 1), :] = jnp.sum(silu_v * u * plain, axis=0, keepdims=True)
-    scaled = plain * prob_ref[e]
-    dg = scaled * u * slope
-    du = scaled * silu_v
-    dgt_ref[0] = dg.astype(jnp.bfloat16)
-    dut_ref[0] = du.astype(jnp.bfloat16)
-    dg_ref[0] = dg.T.astype(jnp.bfloat16)
-    du_ref[0] = du.T.astype(jnp.bfloat16)
+    experts, both = shares_ref.shape
+    places = both // 2
+    _, hidden, width = down_ref.shape
+    product = dot(
+        down_ref[...].reshape(PAIR * hidden, width), x_ref[...].reshape(PAIR * both, width), NT
+    )
+    for i in range(PAIR):
+        plain = product[hidden * i : hidden * (i + 1), both * i : both * (i + 1)]
+        g, u = g_ref[i], u_ref[i]
+        silu_v, slope = gated(g)
+        shares_ref[pl.ds(PAIR * e + i, 1), :] = jnp.sum(silu_v * u * plain, axis=0, keepdims=True)
+        scaled = plain * prob_ref[i]
+        dg = scaled * u * slope
+        du = scaled * silu_v
+        dt_ref[i, :hidden] = dg.astype(jnp.bfloat16)
+        dt_ref[i, hidden:] = du.astype(jnp.bfloat16)
+        dg_ref[i] = dg.T.astype(jnp.bfloat16)
+        du_ref[i] = du.T.astype(jnp.bfloat16)
 
     @pl.when(e == pl.num_programs(0) - 1)
     def _():
@@ -181,7 +186,6 @@
                 share = (share * mine_ref[i].astype(jnp.float32)).astype(jnp.bfloat16)
                 terms_ref[i * places : (i + 1) * places] = share
             share_ref[half] = dot(put_ref[half], terms_ref[...]).astype(jnp.bfloat16)
-        pltpu.make_async_copy(x_ref, x_out, sem).wait()
 
 
 def back_kernel(terms, start, steps, put_ref, *refs):
@@ -224,9 +228,12 @@
             other_ref[:, :columns] = extra_ref[1]
 
 
-def grad_kernel(x_ref, left, out):
+def grad_kernel(x_ref, left, *outs):
+    hidden = outs[0].shape[1]
     for at in range(0, x_ref.shape[2], WIDE):
-        out[0, :, at : at + WIDE] = dot(left[0], x_ref[0, :, at : at + WIDE]).astype(jnp.bfloat16)
+        product = dot(left[0], x_ref[0, :, at : at + WIDE]).astype(jnp.bfloat16)
+        for i, out in enumerate(outs):
+            out[0, :, at : at + WIDE] = product[hidden * i : hidden * (i + 1)]
 
 
 def whole(a):
@@ -239,9 +246,9 @@
     return pl.BlockSpec(shape, lambda i: (0,) * len(shape))
 
 
-def each(a):
+def each(a, size=1):
     shape = a.shape
-    return pl.BlockSpec((1, *shape[1:]), lambda i: (i,) + (0,) * (len(shape) - 1))
+    return pl.BlockSpec((size, *shape[1:]), lambda i: (i,) + (0,) * (len(shape) - 1))
 
 
 def bf16(*shape):
@@ -285,7 +292,7 @@
     ]
     ins = [whole(a) for a in args[:-2]] + [pl.BlockSpec(memory_space=pl.ANY)] * 2
     outs = [pl.BlockSpec(memory_space=pl.ANY)]
-    outs += [kept(s) for s in shapes[1:4]] + [each(s) for s in shapes[4:]]
+    outs += [kept(s) for s in shapes[1:4]] + [each(s, PAIR) for s in shapes[4:]]
     scratch = [
         pltpu.VMEM((2, count, held), jnp.bfloat16),
         pltpu.VMEM((experts, rows, width), jnp.bfloat16),
@@ -295,37 +302,39 @@
     ]
     flops = 4 * experts * rows * hidden * width + 2 * experts * rows * count * width
     return call(
-        functools.partial(up_kernel, tok_count), experts, ins, args, outs, shapes, scratch, flops
-    )
-
-
-def slope_call(own, other, pick, put, prob, mine, w_down, g, u):
+        functools.partial(up_kernel, tok_count), experts // PAIR, ins, args, outs, shapes, scratch, flops
+    )
+
+
+def place_call(pieces, pick, experts):
+    _, rows, count = pick.shape
+    size, width = pieces[0].shape
+    shape = bf16(experts, 2 * rows // experts, width)
+    ins = [pl.BlockSpec((size, WIDE), lambda i: (0, i))] * len(pieces) + [whole(pick)]
+    outs = [pl.BlockSpec((*shape.shape[:2], WIDE), lambda i: (0, 0, i))]
+    flops = 4 * rows * count * width
+    return call(place_kernel, width // WIDE, ins, (*pieces, pick), outs, [shape], flops=flops)[0]
+
+
+def slope_call(x, put, prob, mine, w_down, g, u):
     experts, hidden, width = w_down.shape
-    count, rows, columns = pick.shape[2], prob.shape[2], mine.shape[2]
-    places = rows // 2
-    args = (*own, *other, pick, put, prob, mine, w_down, g, u)
+    rows, count, columns = x.shape[1], put.shape[1], mine.shape[2]
+    args = (x, put, prob, mine, w_down, g, u)
     shapes = [
-        bf16(experts, rows, width),
         bf16(experts, rows, hidden),
         bf16(experts, rows, hidden),
-        bf16(experts, hidden, rows),
-        bf16(experts, hidden, rows),
+        bf16(experts, 2 * hidden, rows),
         bf16(2, count, columns),
     ]
-    ins = [whole(a) for a in args[:-3]] + [pl.BlockSpec(memory_space=pl.ANY), each(g), each(u)]
-    outs = [pl.BlockSpec(memory_space=pl.ANY)]
-    outs += [each(s) for s in shapes[1:5]] + [kept(shapes[5])]
+    ins = [each(x, PAIR), whole(put), each(prob, PAIR), whole(mine)]
+    ins += [each(a, PAIR) for a in (w_down, g, u)]
+    outs = [each(s, PAIR) for s in shapes[:3]] + [kept(shapes[3])]
     scratch = [
-        pltpu.VMEM((2, count, width), jnp.bfloat16),
-        pltpu.VMEM((experts, rows, width), jnp.bfloat16),
         pltpu.VMEM((experts, rows), jnp.float32),
-        pltpu.VMEM((experts * places, columns), jnp.bfloat16),
-        pltpu.VMEM(w_down.shape, jnp.bfloat16),
-        pltpu.SemaphoreType.DMA((experts,)),
-        pltpu.SemaphoreType.DMA,
+        pltpu.VMEM((put.shape[2], columns), jnp.bfloat16),
     ]
-    flops = 2 * experts * rows * hidden * width + 2 * experts * rows * count * width
-    return call(slope_kernel, experts, ins, args, outs, shapes, scratch, flops)
+    flops = 2 * experts * rows * hidden * width
+    return call(slope_kernel, experts // PAIR, ins, args, outs, shapes, scratch, flops)
 
 
 def back_call(put, lefts, rights, start, stop, extra=None):
@@ -352,13 +361,12 @@
     return call(kernel, grid, ins, args, outs, shapes, scratch, flops)
 
 
-def grad_call(x, left):
+def grad_call(x, left, hidden):
     experts, rows, width = x.shape
-    hidden = left.shape[1]
-    shape = bf16(experts, hidden, width)
-    flops = 2 * experts * rows * hidden * width
-    ins, outs = [each(x), each(left)], [each(shape)]
-    return call(grad_kernel, experts, ins, (x, left), outs, [shape], flops=flops)[0]
+    shapes = [bf16(experts, hidden, width)] * (left.shape[1] // hidden)
+    flops = 2 * experts * rows * left.shape[1] * width
+    ins, outs = [each(x), each(left)], [each(s) for s in shapes]
+    return call(grad_kernel, experts, ins, (x, left), outs, shapes, flops=flops)
 
 
 def dense_body(
@@ -436,17 +444,7 @@
     mixed_other, far_grads_other = together(mixed_other, far_grads_other)
     mixed = [mixed, swap(mixed_other, CORE)]
 
-    c, dg, du, dgt, dut, share = slope_call(
-        (grads, far_grads),
-        (grads_other, far_grads_other),
-        pick,
-        put,
-        prob_rows,
-        mine.reshape(local, places, -1),
-        down_weight,
-        g,
-        u,
-    )
+    c = place_call((grads, far_grads, grads_other, far_grads_other), pick, local)
 
     def leaving(parts, start, stop):
         return add(*(part[start:stop] for part in parts))
@@ -464,37 +462,34 @@
         return parts + [swap(leaving(parts, tok_count, 2 * tok_count), Z1)]
 
     weights = [gate_weight, up_weight]
-    mixed[1], dg, du = together(mixed[1], dg, du)
+    mixed[1], c = together(mixed[1], c)
     mixed = by_second(mixed)
+    dg, du, dt, share = slope_call(
+        c, put, prob_rows, mine.reshape(local, places, -1), down_weight, g, u
+    )
     left, left_other = back_call(put, [dg, du], weights, 0, middle)
     left = [left, swap(left_other, CORE)]
-    left[0], dg, du = together(left[0], dg, du)
+    left[0], mixed[2], dg, du = together(left[0], mixed[2], dg, du)
+    mixed = by_first(mixed)
     right, right_other = back_call(put, [dg, du], weights, middle, width, share)
     right = [right, swap(right_other, CORE)]
 
-    right[0], left[1] = together(right[0], left[1])
-    left = by_second(left)
-    mixed[2], ht = together(mixed[2], ht)
-    mixed = by_first(mixed)
-    down_weight_grad = grad_call(c, ht)
-
-    right[1], left[2], mixed[3], down_weight_grad = together(
-        right[1], left[2], mixed[3], down_weight_grad
-    )
-    right, left, mixed = by_second(right), by_first(left), by_far(mixed)
-    right[0], dgt = together(right[0], dgt)
-    gate_weight_grad = grad_call(x, dgt)
-
-    right[2], left[3], mixed[4], gate_weight_grad = together(
-        right[2], left[3], mixed[4], gate_weight_grad
-    )
-    right, left, mixed = by_first(right), by_far(left), by_near(mixed)
-    right[0], dut = together(right[0], dut)
-    up_weight_grad = grad_call(x, dut)
-
-    right[3], left[4], mixed[5], up_weight_grad = together(
-        right[3], left[4], mixed[5], up_weight_grad
-    )
+    right[0], left[1], mixed[3] = together(right[0], left[1], mixed[3])
+    left, mixed = by_second(left), by_far(mixed)
+    left[0], ht = together(left[0], ht)
+    (down_weight_grad,) = grad_call(c, ht, ht.shape[1])
+
+    right[1], left[2], mixed[4], down_weight_grad = together(
+        right[1], left[2], mixed[4], down_weight_grad
+    )
+    right, left, mixed = by_second(right), by_first(left), by_near(mixed)
+    right[0], dt = together(right[0], dt)
+    gate_weight_grad, up_weight_grad = grad_call(x, dt, ht.shape[1])
+
+    right[2], left[3], mixed[5], gate_weight_grad = together(
+        right[2], left[3], mixed[5], gate_weight_grad
+    )
+    right, left = by_first(right), by_far(left)
     right, left = by_far(right), by_near(left)
     right = by_near(right)
     mixed, left, right = (leaving(parts, 0, tok_count) for parts in (mixed, left, right))

time: 191 us -> 187 us (0.979)
  Pallas kernels: 91.1 us -> 86.2 us
  waiting for transfers between devices: 35 us -> 39.7 us
  other arithmetic: 22.2 us -> 18.8 us
    pallas_call x8, Pallas kernels: 91.1 us -> 86.2 us  [call(): pl.pallas_call(kernel, grid=(grid,), in_specs=ins, out_specs=outs, out_sh...]
    ppermute x37, waiting for transfers between devices: 35 us -> 39.7 us  [swap(): return lax.ppermute(values, AXES, pairs)]
    convert_element_type x15, other arithmetic: 16.6 us -> 13.2 us  [add(): return total.astype(jnp.bfloat16)]
  transfers between devices with their start and end apart: 37 -> 37, of which waited for: 12 -> 12; matrix products, arithmetic and copies ran while one was open for 10% -> 9% of each run, Pallas kernels for 48% -> 46%
where the time goes in v5:
time: 187 us; the launch traced here: 186 us
  Pallas kernels  86.2 us (46%)
  waiting for transfers between devices  39.7 us (21%)
  starting transfers between devices  35.8 us (19%)
  other arithmetic  18.8 us (10%)
  local copies, waits for them, and re-layouts  4.23 us (2%)
    pallas_call x8, Pallas kernels, call(): pl.pallas_call(kernel, grid=(grid,), in_specs=ins, out_specs=outs, out_sh...  86.2 us
    ppermute x37, waiting for transfers between devices, swap(): return lax.ppermute(values, AXES, pairs)  39.7 us
    ppermute x37, starting transfers between devices, swap(): return lax.ppermute(values, AXES, pairs)  35.8 us
    convert_element_type x15, other arithmetic, add(): return total.astype(jnp.bfloat16)  13.2 us
  transfers between devices with their start and end apart: 37, of which 12 were waited for; matrix products, arithmetic and copies ran while one was open for 9% of the time, Pallas kernels for 46%

profile of v5, /device:TPU:0, one launch (start us, length us, event | category | flops | bytes accessed | tf_op | source)
XLA Modules:
  0.0 185.9 jit_solution(12575054273155919014)
XLA Ops:
  0.6 3.1 %collective-permute-start.1 = (bf16[16,4096]{1,0:T(8,128)(2,1)}, bf16[16,4096]{1,0:T(8,128)(2,1)S(1)}, u32[]{:S(2)}, u32[]{:S(2)}) collective-permute-start(bf16[16,4096]{1,0:T(8,128)(2,1)} %param.8), channel_id=1, source_target_pairs={{0,2},{1,3},{2,0},{3,1},{4,6},{5,7},{6,4},{7,5},{8,10},{9,11},{10,... | collective-permute-start | bytes 393224 | tf_op jit(solution)/shard_map/ppermute | solution.py:32
  3.7 2.6 %collective-permute-start.2 = (bf16[16,4096]{1,0:T(8,128)(2,1)}, bf16[16,4096]{1,0:T(8,128)(2,1)S(1)}, u32[]{:S(2)}, u32[]{:S(2)}) collective-permute-start(bf16[16,4096]{1,0:T(8,128)(2,1)} %param.8), channel_id=1, source_target_pairs={{0,4},{1,5},{2,6},{3,7},{4,0},{5,1},{6,2},{7,3},{8,12},{9,13},{10,... | collective-permute-start | bytes 393224 | tf_op jit(solution)/shard_map/ppermute | solution.py:32
  10.6 1.8 collective-permute-start
  14.1 1.6 collective-permute-start.7
  15.7 1.8 collective-permute-start.8
  17.5 1.6 collective-permute-start.5
  19.6 3.3 %collective-permute-done.6 = bf16[16,128]{1,0:T(8,128)(2,1)S(1)} collective-permute-done((bf16[16,128]{1,0:T(8,128)(2,1)S(1)}, bf16[16,128]{1,0:T(8,128)(2,1)S(1)}, u32[]{:S(2)}, u32[]{:S(2)}) %collective-permute-start.6) | collective-permute-done | bytes 4128 | tf_op jit(solution)/shard_map/ppermute | solution.py:32
  22.9 2.0 %collective-permute-start.15 = (bf16[16,4096]{1,0:T(8,128)(2,1)S(1)}, bf16[16,4096]{1,0:T(8,128)(2,1)S(1)}, u32[]{:S(2)}, u32[]{:S(2)}) collective-permute-start(bf16[16,4096]{1,0:T(8,128)(2,1)S(1)} %copy-done.15), channel_id=1, source_target_pairs={{0,2},{1,3},{2,0},{3,1},{4,6},{5,7},{6,4},{7,5},{8,10},{9,11},{10,... | collective-permute-start | bytes 393224 | tf_op jit(solution)/shard_map/ppermute | solution.py:32
  24.9 4.1 %collective-permute-start.16 = (bf16[16,4096]{1,0:T(8,128)(2,1)S(1)}, bf16[16,4096]{1,0:T(8,128)(2,1)S(1)}, u32[]{:S(2)}, u32[]{:S(2)}) collective-permute-start(bf16[16,4096]{1,0:T(8,128)(2,1)S(1)} %copy-done.15), channel_id=1, source_target_pairs={{0,4},{1,5},{2,6},{3,7},{4,0},{5,1},{6,2},{7,3},{8,12},{9,13},{10,... | collective-permute-start | bytes 393224 | tf_op jit(solution)/shard_map/ppermute | solution.py:32
  29.0 2.2 %collective-permute-start.9 = (bf16[16,4224]{1,0:T(8,128)(2,1)S(1)}, bf16[16,4224]{1,0:T(8,128)(2,1)S(1)}, u32[]{:S(2)}, u32[]{:S(2)}) collective-permute-start(bf16[16,4224]{1,0:T(8,128)(2,1)S(1)} %constant_dynamic-update-slice_fusion), channel_id=1, source_target_pairs={{0,8},{1,17},{2,10},{3,19},{4,12},{5,21},{6,14},{7,23},{8,0},{9,25... | collective-permute-start | bytes 405512 | tf_op jit(solution)/shard_map/ppermute | solution.py:32
  31.4 2.8 %collective-permute-done.9 = bf16[16,4224]{1,0:T(8,128)(2,1)S(1)} collective-permute-done((bf16[16,4224]{1,0:T(8,128)(2,1)S(1)}, bf16[16,4224]{1,0:T(8,128)(2,1)S(1)}, u32[]{:S(2)}, u32[]{:S(2)}) %collective-permute-start.9) | collective-permute-done | bytes 135200 | tf_op jit(solution)/shard_map/ppermute | solution.py:32
  34.2 9.6 %collective-permute-done.10 = bf16[64,4224]{1,0:T(8,128)(2,1)S(1)} collective-permute-done((bf16[64,4224]{1,0:T(8,128)(2,1)S(1)}, bf16[64,4224]{1,0:T(8,128)(2,1)S(1)}, u32[]{:S(2)}, u32[]{:S(2)}) %collective-permute-start.10) | collective-permute-done | bytes 540704 | tf_op jit(solution)/shard_map/ppermute | solution.py:32
  44.3 6.2 %collective-permute-done.11 = bf16[32,4224]{1,0:T(8,128)(2,1)S(1)} collective-permute-done((bf16[32,4224]{1,0:T(8,128)(2,1)S(1)}, bf16[32,4224]{1,0:T(8,128)(2,1)S(1)}, u32[]{:S(2)}, u32[]{:S(2)}) %collective-permute-start.11) | collective-permute-done | bytes 270368 | tf_op jit(solution)/shard_map/ppermute | solution.py:32
  50.7 2.5 %collective-permute-done.18 = bf16[64,4096]{1,0:T(8,128)(2,1)S(1)} collective-permute-done((bf16[64,4096]{1,0:T(8,128)(2,1)S(1)}, bf16[64,4096]{1,0:T(8,128)(2,1)S(1)}, u32[]{:S(2)}, u32[]{:S(2)}) %collective-permute-start.18) | collective-permute-done | bytes 524320 | tf_op jit(solution)/shard_map/ppermute | solution.py:32
  56.0 17.9 %shard_map.127 = (bf16[8,96,4096]{2,1,0:T(8,128)(2,1)}, bf16[2,256,384]{2,1,0:T(8,128)(2,1)}, bf16[2,384,256]{2,1,0:T(8,128)(2,1)}, f32[8,1,96]{2,1,0:T(1,128)},...) custom-call(bf16[64,4224]{1,0:T(8,128)(2,1)} %copy-done.1, ...), custom_call_target="tpu_custom_call" | custom-call | flops 4026531840 | bytes 38636544 | tf_op jit(solution)/shard_map/pallas_call | solution.py:264
  74.0 10.0 %shard_map.128 = (bf16[256,4096]{1,0:T(8,128)(2,1)}, bf16[256,4096]{1,0:T(8,128)(2,1)}) custom-call(bf16[2,256,384]{2,1,0:T(8,128)(2,1)} %get-tuple-element.91.put_ref, bf16[8,96,192]{2,1,0:T(8,128)(2,1)} %get-tuple-element.94.refs_0_, bf16[8,192,4096]{2,1,0:T(8,128)(2,1)} %down_ref.1), custom_call_target="tpu_custom_call" | custom-call | flops 2818572288 | bytes 17465344 | tf_op jit(solution)/shard_map/pallas_call | solution.py:264
  85.0 6.6 %shard_map.129.x_ref = bf16[8,96,4096]{2,1,0:T(8,128)(2,1)} custom-call(bf16[128,4096]{1,0:T(8,128)(2,1)} %copy-done.4, bf16[128,4096]{1,0:T(8,128)(2,1)} %copy-done.9, bf16[128,4096]{1,0:T(8,128)(2,1)} %copy-done.10, bf16[128,4096]{1,0:T(8,128)(2,1)} %copy-done.11, bf16[2,384,256]{2,1,0:T(8,128)(2,1)} %get-tuple-element.101.pick_ref), custom_call_target="tpu_custom_call" | custom-call | flops 1610612736 | bytes 10878976 | tf_op jit(solution)/shard_map/pallas_call | solution.py:264
  93.6 11.1 %shard_map.130 = (bf16[8,96,192]{2,1,0:T(8,128)(2,1)}, bf16[8,96,192]{2,1,0:T(8,128)(2,1)}, bf16[8,384,96]{2,1,0:T(8,128)(2,1)}, bf16[2,256,128]{2,1,0:T(8,128)(2,1)}) custom-call(bf16[8,96,4096]{2,1,0:T(8,128)(2,1)} %shard_map.129.x_ref, bf16[2,256,384]{2,1,0:T(8,128)(2,1)} %get-tuple-element.91.put_ref, f32[8,1,96]{2,1,0:T(1,128)} %get-tuple-element.104.prob_ref, ...), custom_call_target="tpu_custom_call" | custom-call | flops 1207959552 | bytes 21859328 | tf_op jit(solution)/shard_map/pallas_call | solution.py:264
  104.6 8.1 %shard_map.131 = (bf16[256,2048]{1,0:T(8,128)(2,1)}, bf16[256,2048]{1,0:T(8,128)(2,1)}) custom-call(bf16[2,256,384]{2,1,0:T(8,128)(2,1)} %get-tuple-element.91.put_ref, bf16[8,96,192]{2,1,0:T(8,128)(2,1)} %get-tuple-element.111.refs_0_, bf16[8,96,192]{2,1,0:T(8,128)(2,1)} %get-tuple-element.112.refs_1_, bf16[8,192,4096]{2,1,0:T(8,128)(2,1)} %refs_2_.3, ...), custom_call_target="tpu_custom_call" | custom-call | flops 2013265920 | bytes 28246016 | tf_op jit(solution)/shard_map/pallas_call | solution.py:264
  114.5 8.3 %shard_map.132 = (bf16[256,2176]{1,0:T(8,128)(2,1)}, bf16[256,2176]{1,0:T(8,128)(2,1)}) custom-call(bf16[2,256,384]{2,1,0:T(8,128)(2,1)} %get-tuple-element.91.put_ref, bf16[8,96,192]{2,1,0:T(8,128)(2,1)} %get-tuple-element.111.refs_0_, bf16[8,96,192]{2,1,0:T(8,128)(2,1)} %get-tuple-element.112.refs_1_, bf16[8,192,4096]{2,1,0:T(8,128)(2,1)} %refs_2_.3, ...), custom_call_target="tpu_custom_call" | custom-call | flops 2013265920 | bytes 28508160 | tf_op jit(solution)/shard_map/pallas_call | solution.py:264
  126.6 10.7 %shard_map.133 = bf16[8,192,4096]{2,1,0:T(8,128)(2,1)} custom-call(bf16[8,96,4096]{2,1,0:T(8,128)(2,1)} %shard_map.129.x_ref, bf16[8,192,96]{2,1,0:T(8,128)(2,1)} %get-tuple-element.121.left), custom_call_target="tpu_custom_call" | custom-call | flops 1207959552 | bytes 19169280 | tf_op jit(solution)/shard_map/pallas_call | solution.py:264
  137.2 4.0 %collective-permute-done.28 = bf16[32,4096]{1,0:T(8,128)(2,1)} collective-permute-done((bf16[32,4096]{1,0:T(8,128)(2,1)S(1)}, bf16[32,4096]{1,0:T(8,128)(2,1)}, u32[]{:S(2)}, u32[]{:S(2)}) %collective-permute-start.28) | collective-permute-done | bytes 262176 | tf_op jit(solution)/shard_map/ppermute | solution.py:32
  141.3 1.9 %add_convert_fusion.5 = bf16[64,2048]{1,0:T(8,128)(2,1)} fusion(bf16[128,2048]{1,0:T(8,128)(2,1)} %collective-permute-done.27, bf16[256,2048]{1,0:T(8,128)(2,1)} %collective-permute-done.24, bf16[256,2048]{1,0:T(8,128)(2,1)S(1)} %copy-done.7), kind=kLoop, calls=%fused_computation.10 | loop fusion | flops 786432 | bytes 1048576 | tf_op jit(solution)/shard_map/convert_element_type | solution.py:39
  146.3 1.8 add_convert_fusion.10
  148.1 13.6 %shard_map.134 = (bf16[8,192,4096]{2,1,0:T(8,128)(2,1)}, bf16[8,192,4096]{2,1,0:T(8,128)(2,1)}) custom-call(bf16[8,96,4096]{2,1,0:T(8,128)(2,1)} %get-tuple-element.127.x_ref, bf16[8,384,96]{2,1,0:T(8,128)(2,1)} %get-tuple-element.129.left), custom_call_target="tpu_custom_call" | custom-call | flops 2415919104 | bytes 32047104 | tf_op jit(solution)/shard_map/pallas_call | solution.py:264
  162.8 1.8 collective-permute-start.32
  166.1 1.9 %add_convert_fusion.9 = bf16[16,4096]{1,0:T(8,128)(2,1)} fusion(bf16[16,4096]{1,0:T(8,128)(2,1)} %collective-permute-done.31, bf16[32,4096]{1,0:T(8,128)(2,1)} %collective-permute-done.28, bf16[64,4096]{1,0:T(8,128)(2,1)} %copy-done.14, bf16[128,4096]{1,0:T(8,128)(2,1)} %copy-done.8, bf16[256,4096]{1,0:T(8,128)(2,1)S(1)} %collective-permute-done.22, ...), kind=kLoop, calls=%fused_computation.17 | loop fusion | flops 786432 | bytes 917504 | tf_op jit(solution)/shard_map/convert_element_type | solution.py:39
  168.0 3.4 %collective-permute-done.34 = bf16[64,2176]{1,0:T(8,128)(2,1)S(1)} collective-permute-done((bf16[64,2176]{1,0:T(8,128)(2,1)S(1)}, bf16[64,2176]{1,0:T(8,128)(2,1)S(1)}, u32[]{:S(2)}, u32[]{:S(2)}) %collective-permute-start.34) | collective-permute-done | bytes 278560 | tf_op jit(solution)/shard_map/ppermute | solution.py:32
  173.6 2.1 %collective-permute-start.33 = (bf16[16,2048]{1,0:T(8,128)(2,1)S(1)}, bf16[16,2048]{1,0:T(8,128)(2,1)S(1)}, u32[]{:S(2)}, u32[]{:S(2)}) collective-permute-start(bf16[16,2048]{1,0:T(8,128)(2,1)S(1)} %add_convert_fusion.14), channel_id=1, source_target_pairs={{0,2},{1,3},{2,0},{3,1},{4,6},{5,7},{6,4},{7,5},{8,10},{9,11},{10,... | collective-permute-start | bytes 196616 | tf_op jit(solution)/shard_map/ppermute | solution.py:32
  175.7 3.4 %collective-permute-done.35 = bf16[32,2176]{1,0:T(8,128)(2,1)S(1)} collective-permute-done((bf16[32,2176]{1,0:T(8,128)(2,1)S(1)}, bf16[32,2176]{1,0:T(8,128)(2,1)S(1)}, u32[]{:S(2)}, u32[]{:S(2)}) %collective-permute-start.35) | collective-permute-done | bytes 139296 | tf_op jit(solution)/shard_map/ppermute | solution.py:32
  179.5 1.6 add_convert_fusion.13
  181.0 2.5 %collective-permute-done.36 = bf16[16,2176]{1,0:T(8,128)(2,1)S(1)} collective-permute-done((bf16[16,2176]{1,0:T(8,128)(2,1)S(1)}, bf16[16,2176]{1,0:T(8,128)(2,1)S(1)}, u32[]{:S(2)}, u32[]{:S(2)}) %collective-permute-start.36) | collective-permute-done | bytes 69664 | tf_op jit(solution)/shard_map/ppermute | solution.py:32
  (130 shorter events, 29.1 us)
Async XLA Ops:
  0.6 13.4 %collective-permute-start.1 = (bf16[16,4096]{1,0:T(8,128)(2,1)}, bf16[16,4096]{1,0:T(8,128)(2,1)S(1)}, u32[]{:S(2)}, u32[]{:S(2)}) collective-permute-start(bf16[16,4096]{1,0:T(8,128)(2,1)} %param.8), channel_id=1, source_target_pairs={{0,2},{1,3},{2,0},{3,1},{4,6},{5,7},{6,4},{7,5},{8,10},{9,11},{10,... | collective-permute-start | bytes 393224 | tf_op jit(solution)/shard_map/ppermute | solution.py:32
  3.7 10.4 %collective-permute-start.2 = (bf16[16,4096]{1,0:T(8,128)(2,1)}, bf16[16,4096]{1,0:T(8,128)(2,1)S(1)}, u32[]{:S(2)}, u32[]{:S(2)}) collective-permute-start(bf16[16,4096]{1,0:T(8,128)(2,1)} %param.8), channel_id=1, source_target_pairs={{0,4},{1,5},{2,6},{3,7},{4,0},{5,1},{6,2},{7,3},{8,12},{9,13},{10,... | collective-permute-start | bytes 393224 | tf_op jit(solution)/shard_map/ppermute | solution.py:32
  10.6 5.1 %collective-permute-start = (bf16[16,4224]{1,0:T(8,128)(2,1)S(1)}, bf16[16,4224]{1,0:T(8,128)(2,1)S(1)}, u32[]{:S(2)}, u32[]{:S(2)}) collective-permute-start(bf16[16,4224]{1,0:T(8,128)(2,1)S(1)} %concatenate.50), channel_id=1, source_target_pairs={{0,8},{1,17},{2,10},{3,19},{4,12},{5,21},{6,14},{7,23},{8,0},{9,25... | collective-permute-start | bytes 405512 | tf_op jit(solution)/shard_map/ppermute | solution.py:32
  14.1 14.9 %collective-permute-start.7 = (bf16[32,4224]{1,0:T(8,128)(2,1)S(1)}, bf16[32,4224]{1,0:T(8,128)(2,1)S(1)}, u32[]{:S(2)}, u32[]{:S(2)}) collective-permute-start(bf16[32,4224]{1,0:T(8,128)(2,1)S(1)} %maximum_maximum_fusion), channel_id=1, source_target_pairs={{0,8},{1,17},{2,10},{3,19},{4,12},{5,21},{6,14},{7,23},{8,0},{9,25... | collective-permute-start | bytes 811016 | tf_op jit(solution)/shard_map/ppermute | solution.py:32
  15.7 13.3 %collective-permute-start.8 = (bf16[32,4224]{1,0:T(8,128)(2,1)S(1)}, bf16[32,4224]{1,0:T(8,128)(2,1)S(1)}, u32[]{:S(2)}, u32[]{:S(2)}) collective-permute-start(bf16[32,4224]{1,0:T(8,128)(2,1)S(1)} %pad_maximum_fusion.5), channel_id=1, source_target_pairs={{0,16},{1,9},{2,18},{3,11},{4,20},{5,13},{6,22},{7,15},{8,24},{9,1... | collective-permute-start | bytes 811016 | tf_op jit(solution)/shard_map/ppermute | solution.py:32
  17.5 11.4 %collective-permute-start.5 = (bf16[16,4096]{1,0:T(8,128)(2,1)S(1)}, bf16[16,4096]{1,0:T(8,128)(2,1)S(1)}, u32[]{:S(2)}, u32[]{:S(2)}) collective-permute-start(bf16[16,4096]{1,0:T(8,128)(2,1)S(1)} %collective-permute-done.2), channel_id=1, source_target_pairs={{0,2},{1,3},{2,0},{3,1},{4,6},{5,7},{6,4},{7,5},{8,10},{9,11},{10,... | collective-permute-start | bytes 393224 | tf_op jit(solution)/shard_map/ppermute | solution.py:32
  22.9 21.0 %collective-permute-start.15 = (bf16[16,4096]{1,0:T(8,128)(2,1)S(1)}, bf16[16,4096]{1,0:T(8,128)(2,1)S(1)}, u32[]{:S(2)}, u32[]{:S(2)}) collective-permute-start(bf16[16,4096]{1,0:T(8,128)(2,1)S(1)} %copy-done.15), channel_id=1, source_target_pairs={{0,2},{1,3},{2,0},{3,1},{4,6},{5,7},{6,4},{7,5},{8,10},{9,11},{10,... | collective-permute-start | bytes 393224 | tf_op jit(solution)/shard_map/ppermute | solution.py:32
  24.9 19.0 %collective-permute-start.16 = (bf16[16,4096]{1,0:T(8,128)(2,1)S(1)}, bf16[16,4096]{1,0:T(8,128)(2,1)S(1)}, u32[]{:S(2)}, u32[]{:S(2)}) collective-permute-start(bf16[16,4096]{1,0:T(8,128)(2,1)S(1)} %copy-done.15), channel_id=1, source_target_pairs={{0,4},{1,5},{2,6},{3,7},{4,0},{5,1},{6,2},{7,3},{8,12},{9,13},{10,... | collective-permute-start | bytes 393224 | tf_op jit(solution)/shard_map/ppermute | solution.py:32
  29.0 14.9 %collective-permute-start.17 = (bf16[16,4096]{1,0:T(8,128)(2,1)S(1)}, bf16[16,4096]{1,0:T(8,128)(2,1)S(1)}, u32[]{:S(2)}, u32[]{:S(2)}) collective-permute-start(bf16[16,4096]{1,0:T(8,128)(2,1)S(1)} %copy-done.15), channel_id=1, source_target_pairs={{0,6},{1,7},{2,4},{3,5},{4,2},{5,3},{6,0},{7,1},{8,14},{9,15},{10,... | collective-permute-start | bytes 393224 | tf_op jit(solution)/shard_map/ppermute | solution.py:32
  29.0 5.2 %collective-permute-start.9 = (bf16[16,4224]{1,0:T(8,128)(2,1)S(1)}, bf16[16,4224]{1,0:T(8,128)(2,1)S(1)}, u32[]{:S(2)}, u32[]{:S(2)}) collective-permute-start(bf16[16,4224]{1,0:T(8,128)(2,1)S(1)} %constant_dynamic-update-slice_fusion), channel_id=1, source_target_pairs={{0,8},{1,17},{2,10},{3,19},{4,12},{5,21},{6,14},{7,23},{8,0},{9,25... | collective-permute-start | bytes 405512 | tf_op jit(solution)/shard_map/ppermute | solution.py:32
  31.3 12.6 %collective-permute-start.10 = (bf16[64,4224]{1,0:T(8,128)(2,1)S(1)}, bf16[64,4224]{1,0:T(8,128)(2,1)S(1)}, u32[]{:S(2)}, u32[]{:S(2)}) collective-permute-start(bf16[64,4224]{1,0:T(8,128)(2,1)S(1)} %pad_maximum_fusion.2), channel_id=1, source_target_pairs={{0,16},{1,9},{2,18},{3,11},{4,20},{5,13},{6,22},{7,15},{8,24},{9,1... | collective-permute-start | bytes 1622024 | tf_op jit(solution)/shard_map/ppermute | solution.py:32
  34.2 19.0 %collective-permute-start.12 = (bf16[64,4224]{1,0:T(8,128)(2,1)S(1)}, bf16[64,4224]{1,0:T(8,128)(2,1)S(1)}, u32[]{:S(2)}, u32[]{:S(2)}) collective-permute-start(bf16[64,4224]{1,0:T(8,128)(2,1)S(1)} %pad_maximum_fusion.1.own0), channel_id=1, source_target_pairs={{0,1},{1,0},{2,3},{3,2},{4,5},{5,4},{6,7},{7,6},{8,9},{9,8},{10,11... | collective-permute-start | bytes 1622024 | tf_op jit(solution)/shard_map/ppermute | solution.py:32
  43.9 9.2 %collective-permute-start.18 = (bf16[64,4096]{1,0:T(8,128)(2,1)S(1)}, bf16[64,4096]{1,0:T(8,128)(2,1)S(1)}, u32[]{:S(2)}, u32[]{:S(2)}) collective-permute-start(bf16[64,4096]{1,0:T(8,128)(2,1)S(1)} %pad_maximum_fusion.4), channel_id=1, source_target_pairs={{0,8},{1,17},{2,10},{3,19},{4,12},{5,21},{6,14},{7,23},{8,0},{9,25... | collective-permute-start | bytes 1572872 | tf_op jit(solution)/shard_map/ppermute | solution.py:32
  44.0 6.5 %collective-permute-start.11 = (bf16[32,4224]{1,0:T(8,128)(2,1)S(1)}, bf16[32,4224]{1,0:T(8,128)(2,1)S(1)}, u32[]{:S(2)}, u32[]{:S(2)}) collective-permute-start(bf16[32,4224]{1,0:T(8,128)(2,1)S(1)} %pad_maximum_fusion.6), channel_id=1, source_target_pairs={{0,16},{1,9},{2,18},{3,11},{4,20},{5,13},{6,22},{7,15},{8,24},{9,1... | collective-permute-start | bytes 811016 | tf_op jit(solution)/shard_map/ppermute | solution.py:32
  44.2 9.0 %collective-permute-start.13 = (bf16[128,4224]{1,0:T(8,128)(2,1)S(1)}, bf16[128,4224]{1,0:T(8,128)(2,1)S(1)}, u32[]{:S(2)}, u32[]{:S(2)}) collective-permute-start(bf16[128,4224]{1,0:T(8,128)(2,1)S(1)} %pad_maximum_fusion.own1), channel_id=1, source_target_pairs={{0,1},{1,0},{2,3},{3,2},{4,5},{5,4},{6,7},{7,6},{8,9},{9,8},{10,11... | collective-permute-start | bytes 3244040 | tf_op jit(solution)/shard_map/ppermute | solution.py:32
  53.3 20.6 %collective-permute-start.19 = (bf16[128,4096]{1,0:T(8,128)(2,1)S(1)}, bf16[128,4096]{1,0:T(8,128)(2,1)S(1)}, u32[]{:S(2)}, u32[]{:S(2)}) collective-permute-start(bf16[128,4096]{1,0:T(8,128)(2,1)S(1)} %constant_dynamic-update-slice_fusion.2.own0), channel_id=1, source_target_pairs={{0,16},{1,9},{2,18},{3,11},{4,20},{5,13},{6,22},{7,15},{8,24},{9,1... | collective-permute-start | bytes 3145736 | tf_op jit(solution)/shard_map/ppermute | solution.py:32
  53.4 20.5 %collective-permute-start.20 = (bf16[128,4096]{1,0:T(8,128)(2,1)S(1)}, bf16[128,4096]{1,0:T(8,128)(2,1)S(1)}, u32[]{:S(2)}, u32[]{:S(2)}) collective-permute-start(bf16[128,4096]{1,0:T(8,128)(2,1)S(1)} %constant_dynamic-update-slice_fusion.2.own0), channel_id=1, source_target_pairs={{0,1},{1,0},{2,3},{3,2},{4,5},{5,4},{6,7},{7,6},{8,9},{9,8},{10,11... | collective-permute-start | bytes 3145736 | tf_op jit(solution)/shard_map/ppermute | solution.py:32
  73.9 10.1 %collective-permute-start.21 = (bf16[128,4096]{1,0:T(8,128)(2,1)S(1)}, bf16[128,4096]{1,0:T(8,128)(2,1)S(1)}, u32[]{:S(2)}, u32[]{:S(2)}) collective-permute-start(bf16[128,4096]{1,0:T(8,128)(2,1)S(1)} %collective-permute-done.19.own1), channel_id=1, source_target_pairs={{0,1},{1,0},{2,3},{3,2},{4,5},{5,4},{6,7},{7,6},{8,9},{9,8},{10,11... | collective-permute-start | bytes 3145736 | tf_op jit(solution)/shard_map/ppermute | solution.py:32
  84.0 7.5 %collective-permute-start.22 = (bf16[256,4096]{1,0:T(8,128)(2,1)}, bf16[256,4096]{1,0:T(8,128)(2,1)S(1)}, u32[]{:S(2)}, u32[]{:S(2)}) collective-permute-start(bf16[256,4096]{1,0:T(8,128)(2,1)} %get-tuple-element.98), channel_id=1, source_target_pairs={{0,1},{1,0},{2,3},{3,2},{4,5},{5,4},{6,7},{7,6},{8,9},{9,8},{10,11... | collective-permute-start | bytes 6291464 | tf_op jit(solution)/shard_map/ppermute | solution.py:32
  91.8 21.0 %collective-permute-start.23 = (bf16[128,4096]{1,0:T(8,128)(2,1)S(1)}, bf16[128,4096]{1,0:T(8,128)(2,1)S(1)}, u32[]{:S(2)}, u32[]{:S(2)}) collective-permute-start(bf16[128,4096]{1,0:T(8,128)(2,1)S(1)} %add_convert_fusion), channel_id=1, source_target_pairs={{0,16},{1,9},{2,18},{3,11},{4,20},{5,13},{6,22},{7,15},{8,24},{9,1... | collective-permute-start | bytes 3145736 | tf_op jit(solution)/shard_map/ppermute | solution.py:32
  112.8 10.1 %collective-permute-start.24 = (bf16[256,2048]{1,0:T(8,128)(2,1)}, bf16[256,2048]{1,0:T(8,128)(2,1)}, u32[]{:S(2)}, u32[]{:S(2)}) collective-permute-start(bf16[256,2048]{1,0:T(8,128)(2,1)} %get-tuple-element.115), channel_id=1, source_target_pairs={{0,1},{1,0},{2,3},{3,2},{4,5},{5,4},{6,7},{7,6},{8,9},{9,8},{10,11... | collective-permute-start | bytes 3145736 | tf_op jit(solution)/shard_map/ppermute | solution.py:32
  113.1 9.8 %collective-permute-start.25 = (bf16[64,4096]{1,0:T(8,128)(2,1)S(1)}, bf16[64,4096]{1,0:T(8,128)(2,1)S(1)}, u32[]{:S(2)}, u32[]{:S(2)}) collective-permute-start(bf16[64,4096]{1,0:T(8,128)(2,1)S(1)} %add_convert_fusion.3), channel_id=1, source_target_pairs={{0,8},{1,17},{2,10},{3,19},{4,12},{5,21},{6,14},{7,23},{8,0},{9,25... | collective-permute-start | bytes 1572872 | tf_op jit(solution)/shard_map/ppermute | solution.py:32
  122.8 18.5 %collective-permute-start.26 = (bf16[256,2176]{1,0:T(8,128)(2,1)}, bf16[256,2176]{1,0:T(8,128)(2,1)S(1)}, u32[]{:S(2)}, u32[]{:S(2)}) collective-permute-start(bf16[256,2176]{1,0:T(8,128)(2,1)} %get-tuple-element.117), channel_id=1, source_target_pairs={{0,1},{1,0},{2,3},{3,2},{4,5},{5,4},{6,7},{7,6},{8,9},{9,8},{10,11... | collective-permute-start | bytes 3342344 | tf_op jit(solution)/shard_map/ppermute | solution.py:32
  124.3 17.0 %collective-permute-start.27 = (bf16[128,2048]{1,0:T(8,128)(2,1)S(1)}, bf16[128,2048]{1,0:T(8,128)(2,1)}, u32[]{:S(2)}, u32[]{:S(2)}) collective-permute-start(bf16[128,2048]{1,0:T(8,128)(2,1)S(1)} %add_convert_fusion.2), channel_id=1, source_target_pairs={{0,16},{1,9},{2,18},{3,11},{4,20},{5,13},{6,22},{7,15},{8,24},{9,1... | collective-permute-start | bytes 1572872 | tf_op jit(solution)/shard_map/ppermute | solution.py:32
  126.4 14.8 %collective-permute-start.28 = (bf16[32,4096]{1,0:T(8,128)(2,1)S(1)}, bf16[32,4096]{1,0:T(8,128)(2,1)}, u32[]{:S(2)}, u32[]{:S(2)}) collective-permute-start(bf16[32,4096]{1,0:T(8,128)(2,1)S(1)} %add_convert_fusion.6), channel_id=1, source_target_pairs={{0,4},{1,5},{2,6},{3,7},{4,0},{5,1},{6,2},{7,3},{8,12},{9,13},{10,... | collective-permute-start | bytes 786440 | tf_op jit(solution)/shard_map/ppermute | solution.py:32
  143.2 18.6 %collective-permute-start.30 = (bf16[64,2048]{1,0:T(8,128)(2,1)}, bf16[64,2048]{1,0:T(8,128)(2,1)S(1)}, u32[]{:S(2)}, u32[]{:S(2)}) collective-permute-start(bf16[64,2048]{1,0:T(8,128)(2,1)} %add_convert_fusion.5), channel_id=1, source_target_pairs={{0,8},{1,17},{2,10},{3,19},{4,12},{5,21},{6,14},{7,23},{8,0},{9,25... | collective-permute-start | bytes 786440 | tf_op jit(solution)/shard_map/ppermute | solution.py:32
  145.4 16.3 %collective-permute-start.29 = (bf16[128,2176]{1,0:T(8,128)(2,1)}, bf16[128,2176]{1,0:T(8,128)(2,1)S(1)}, u32[]{:S(2)}, u32[]{:S(2)}) collective-permute-start(bf16[128,2176]{1,0:T(8,128)(2,1)} %add_convert_fusion.1), channel_id=1, source_target_pairs={{0,16},{1,9},{2,18},{3,11},{4,20},{5,13},{6,22},{7,15},{8,24},{9,1... | collective-permute-start | bytes 1671176 | tf_op jit(solution)/shard_map/ppermute | solution.py:32
  148.1 13.6 %collective-permute-start.31 = (bf16[16,4096]{1,0:T(8,128)(2,1)}, bf16[16,4096]{1,0:T(8,128)(2,1)}, u32[]{:S(2)}, u32[]{:S(2)}) collective-permute-start(bf16[16,4096]{1,0:T(8,128)(2,1)} %add_convert_fusion.10), channel_id=1, source_target_pairs={{0,2},{1,3},{2,0},{3,1},{4,6},{5,7},{6,4},{7,5},{8,10},{9,11},{10,... | collective-permute-start | bytes 393224 | tf_op jit(solution)/shard_map/ppermute | solution.py:32
  162.8 9.9 %collective-permute-start.32 = (bf16[32,2048]{1,0:T(8,128)(2,1)S(1)}, bf16[32,2048]{1,0:T(8,128)(2,1)S(1)}, u32[]{:S(2)}, u32[]{:S(2)}) collective-permute-start(bf16[32,2048]{1,0:T(8,128)(2,1)S(1)} %add_convert_fusion.8), channel_id=1, source_target_pairs={{0,4},{1,5},{2,6},{3,7},{4,0},{5,1},{6,2},{7,3},{8,12},{9,13},{10,... | collective-permute-start | bytes 393224 | tf_op jit(solution)/shard_map/ppermute | solution.py:32
  164.7 6.6 %collective-permute-start.34 = (bf16[64,2176]{1,0:T(8,128)(2,1)S(1)}, bf16[64,2176]{1,0:T(8,128)(2,1)S(1)}, u32[]{:S(2)}, u32[]{:S(2)}) collective-permute-start(bf16[64,2176]{1,0:T(8,128)(2,1)S(1)} %add_convert_fusion.4), channel_id=1, source_target_pairs={{0,8},{1,17},{2,10},{3,19},{4,12},{5,21},{6,14},{7,23},{8,0},{9,25... | collective-permute-start | bytes 835592 | tf_op jit(solution)/shard_map/ppermute | solution.py:32
  171.4 7.6 %collective-permute-start.35 = (bf16[32,2176]{1,0:T(8,128)(2,1)S(1)}, bf16[32,2176]{1,0:T(8,128)(2,1)S(1)}, u32[]{:S(2)}, u32[]{:S(2)}) collective-permute-start(bf16[32,2176]{1,0:T(8,128)(2,1)S(1)} %add_convert_fusion.7), channel_id=1, source_target_pairs={{0,4},{1,5},{2,6},{3,7},{4,0},{5,1},{6,2},{7,3},{8,12},{9,13},{10,... | collective-permute-start | bytes 417800 | tf_op jit(solution)/shard_map/ppermute | solution.py:32
  173.6 5.9 %collective-permute-start.33 = (bf16[16,2048]{1,0:T(8,128)(2,1)S(1)}, bf16[16,2048]{1,0:T(8,128)(2,1)S(1)}, u32[]{:S(2)}, u32[]{:S(2)}) collective-permute-start(bf16[16,2048]{1,0:T(8,128)(2,1)S(1)} %add_convert_fusion.14), channel_id=1, source_target_pairs={{0,2},{1,3},{2,0},{3,1},{4,6},{5,7},{6,4},{7,5},{8,10},{9,11},{10,... | collective-permute-start | bytes 196616 | tf_op jit(solution)/shard_map/ppermute | solution.py:32
  (21 other events, 164.7 us)

commit v6 on v5

--- a/solution.py
+++ b/solution.py
@@ -1,4 +1,5 @@
 import functools
+import math
 
 import jax
 import jax.numpy as jnp
@@ -57,47 +58,32 @@
     return lax.broadcasted_iota(jnp.int32, shape, axis)
 
 
-def dispatch(pick, rows_ref, half, x_ref):
-    experts, both, width = x_ref.shape
+def ordered(pieces, tok_count):
+    rows = []
+    for quarter in range(4):
+        for piece, group in zip(pieces, GROUPS):
+            size = len(group) * tok_count
+            rows.append(piece[quarter * size : (quarter + 1) * size])
+    return jnp.concatenate(rows, axis=0)
+
+
+def put_in_places(pick, rows, half, x_ref):
+    experts, both = x_ref.shape[:2]
     places = both // 2
-    for at in range(0, width, WIDE):
-        rows = dot(pick, rows_ref[half, :, at : at + WIDE]).astype(jnp.bfloat16)
-        for e in range(experts):
-            x_ref[e, half * places : (half + 1) * places, at : at + WIDE] = rows[
-                e * places : (e + 1) * places
-            ]
-
-
-def join_groups(pieces, rows_ref, half, tok_count):
-    for piece, group in zip(pieces, GROUPS):
-        size = len(group) * tok_count
-        for quarter in range(4):
-            at = (quarter * 4 + group[0]) * tok_count
-            rows_ref[half, at : at + size] = piece[quarter * size : (quarter + 1) * size]
-
-
-def up_kernel(tok_count, own0, own1, own2, other0, other1, other2, mine_ref, mine_t_ref, both_ref,
-              gate_ref, up_ref, x_out, put_ref, pick_ref, prob_ref, g_ref, u_ref, h_ref, ht_ref,
-              rows_ref, x_ref, held_ref, held_sems, sem):
-    e = pl.program_id(0)
-    experts, both, width = x_ref.shape
+    rows = dot(pick, rows).astype(jnp.bfloat16)
+    for e in range(experts):
+        x_ref[e, half * places : (half + 1) * places] = rows[e * places : (e + 1) * places]
+
+
+def route_kernel(tok_count, *refs):
+    rows_refs, part_refs, (mine_ref, mine_t_ref, both_ref) = refs[:6], refs[6:12], refs[12:15]
+    x_ref, put_ref, pick_ref, prob_ref = refs[16:]
+    experts, both = x_ref.shape[:2]
     places = both // 2
-    hidden = gate_ref.shape[1]
-    count = rows_ref.shape[1]
-
-    def copies(i):
-        return (
-            pltpu.make_async_copy(gate_ref.at[i], held_ref.at[i, :hidden], held_sems.at[0, i]),
-            pltpu.make_async_copy(up_ref.at[i], held_ref.at[i, hidden:], held_sems.at[1, i]),
-        )
-
-    @pl.when(e == 0)
+    count = pick_ref.shape[2]
+
+    @pl.when(pl.program_id(0) == 0)
     def _():
-        for i in range(experts):
-            for copy in copies(i):
-                copy.start()
-        join_groups((own0, own1, own2), rows_ref, 0, tok_count)
-        join_groups((other0, other1, other2), rows_ref, 1, tok_count)
         row, col = iota((count, count), 0), iota((count, count), 1)
         block = lax.div(row, tok_count)
         before = ((col < row) & (lax.div(col, tok_count) == block)).astype(jnp.bfloat16)
@@ -106,53 +92,67 @@
         spot = lax.rem(iota((count, experts * places), 1), places).astype(jnp.float32)
         spot_t = lax.rem(iota((experts * places, count), 0), places).astype(jnp.float32)
         for half in range(2):
-            prob = rows_ref[half, :, width:]
+            prob = ordered(part_refs[3 * half : 3 * half + 3], tok_count)
             taken = prob.astype(jnp.float32) > 0.0
             rank = dot(before, jnp.where(taken, 1.0, 0.0).astype(jnp.bfloat16))
             place = jnp.where(taken, rank + first, -1.0).astype(jnp.bfloat16)
             put = jnp.where(dot(place, mine_ref[...]) == spot, 1.0, 0.0)
             pick = dot(mine_t_ref[...], place, NT) == spot_t
-            pick = jnp.where(pick, 1.0, 0.0).astype(jnp.bfloat16)
             put_ref[half] = put.astype(jnp.bfloat16)
-            pick_ref[half] = pick
+            pick_ref[half] = jnp.where(pick, 1.0, 0.0).astype(jnp.bfloat16)
             weight = jnp.sum(put * dot(prob, both_ref[...]), axis=0, keepdims=True)
             for i in range(experts):
                 prob_ref[i, :, half * places : (half + 1) * places] = weight[
                     :, i * places : (i + 1) * places
                 ]
-            dispatch(pick, rows_ref, half, x_ref)
-        pltpu.make_async_copy(x_ref, x_out, sem).start()
-
-    pair = pl.ds(PAIR * e, PAIR)
-    for i in range(PAIR):
-        for copy in copies(PAIR * e + i):
-            copy.wait()
-    product = dot(
-        held_ref[pair].reshape(PAIR * 2 * hidden, width), x_ref[pair].reshape(PAIR * both, width), NT
-    )
+
+    for half in range(2):
+        rows = ordered(rows_refs[3 * half : 3 * half + 3], tok_count)
+        put_in_places(pick_ref[half], rows, half, x_ref)
+
+
+def up_kernel(x_ref, prob_ref, gate_ref, up_ref, g_ref, u_ref, h_ref, ht_ref, held_ref, sems):
+    step = pl.program_id(0)
+    both, width = x_ref.shape[1:]
+    hidden = gate_ref.shape[1]
+
+    def copies(at):
+        slot = lax.rem(at, 2)
+        for i in range(PAIR):
+            e = PAIR * at + i
+            for j, source in enumerate((gate_ref, up_ref)):
+                held = held_ref.at[slot, i, hidden * j : hidden * (j + 1)]
+                yield pltpu.make_async_copy(source.at[e], held, sems.at[slot, 2 * i + j])
+
+    @pl.when(step == 0)
+    def _():
+        for copy in copies(step):
+            copy.start()
+
+    @pl.when(step + 1 < pl.num_programs(0))
+    def _():
+        for copy in copies(step + 1):
+            copy.start()
+
+    for copy in copies(step):
+        copy.wait()
+    weights = held_ref[lax.rem(step, 2)].reshape(PAIR * 2 * hidden, width)
+    product = dot(weights, x_ref[...].reshape(PAIR * both, width), NT)
     for i in range(PAIR):
         own = product[2 * hidden * i : 2 * hidden * (i + 1), both * i : both * (i + 1)]
         g, u = own[:hidden], own[hidden:]
         g_ref[i] = g
         u_ref[i] = u
         silu_v, _ = gated(g)
-        scaled = silu_v * u * prob_ref[PAIR * e + i]
+        scaled = silu_v * u * prob_ref[i]
         ht_ref[i] = scaled.astype(jnp.bfloat16)
         h_ref[i] = scaled.T.astype(jnp.bfloat16)
 
-    @pl.when(e == pl.num_programs(0) - 1)
-    def _():
-        pltpu.make_async_copy(x_ref, x_out, sem).wait()
-
 
 def place_kernel(own0, own1, other0, other1, pick_ref, x_ref):
-    experts, both = x_ref.shape[:2]
-    places = both // 2
     for half, pieces in enumerate(((own0, own1), (other0, other1))):
         rows = jnp.concatenate([pieces[0][...], pieces[1][...]], axis=0)
-        rows = dot(pick_ref[half], rows).astype(jnp.bfloat16)
-        for e in range(experts):
-            x_ref[e, half * places : (half + 1) * places] = rows[e * places : (e + 1) * places]
+        put_in_places(pick_ref[half], rows, half, x_ref)
 
 
 def slope_kernel(x_ref, put_ref, prob_ref, mine_ref, down_ref, g_ref, u_ref,
@@ -251,6 +251,14 @@
     return pl.BlockSpec((size, *shape[1:]), lambda i: (i,) + (0,) * (len(shape) - 1))
 
 
+def near_core(a):
+    return pltpu.with_memory_space_constraint(a, pltpu.VMEM)
+
+
+def in_hbm(a):
+    return pltpu.with_memory_space_constraint(a, pltpu.HBM)
+
+
 def bf16(*shape):
     return jax.ShapeDtypeStruct(shape, jnp.bfloat16)
 
@@ -260,7 +268,7 @@
 
 
 def call(kernel, grid, ins, args, outs, shapes, scratch=(), flops=0):
-    moved = sum(a.size * a.dtype.itemsize for a in (*args, *shapes))
+    moved = sum(math.prod(a.shape) * a.dtype.itemsize for a in (*args, *shapes))
     return pl.pallas_call(
         kernel,
         grid=(grid,),
@@ -268,48 +276,77 @@
         out_specs=outs,
         out_shape=shapes,
         scratch_shapes=scratch,
-        compiler_params=pltpu.CompilerParams(vmem_limit_bytes=56 * MIB),
+        compiler_params=pltpu.CompilerParams(vmem_limit_bytes=24 * MIB),
         cost_estimate=pl.CostEstimate(flops=flops, bytes_accessed=moved, transcendentals=0),
     )(*args)
 
 
-def up_call(own, other, maps, w_gate, w_up, tok_count):
-    experts, hidden, width = w_gate.shape
-    held = own[0].shape[1]
+def fetch_kernel(source, after, held, mark, sem):
+    copy = pltpu.make_async_copy(source, held, sem)
+    copy.start()
+    mark[...] = jnp.zeros_like(mark)
+    copy.wait()
+
+
+def fetch_call(weight, after):
+    return pl.pallas_call(
+        fetch_kernel,
+        in_specs=[pl.BlockSpec(memory_space=pl.ANY)] * 2,
+        out_specs=[pl.BlockSpec(memory_space=pl.ANY), pl.BlockSpec(memory_space=pltpu.VMEM)],
+        out_shape=[pltpu.VMEM(weight.shape, weight.dtype), f32(8, 128)],
+        scratch_shapes=[pltpu.SemaphoreType.DMA],
+        compiler_params=pltpu.CompilerParams(vmem_limit_bytes=MIB),
+        cost_estimate=pl.CostEstimate(
+            flops=0, bytes_accessed=weight.size * weight.dtype.itemsize, transcendentals=0
+        ),
+    )(in_hbm(weight), after)
+
+
+def route_call(own, other, maps, mark, experts, width, tok_count):
     count = sum(piece.shape[0] for piece in own)
     places = count // tok_count * CAP
-    rows = 2 * places
-    args = (*own, *other, *maps, w_gate, w_up)
+    columns = own[0].shape[1] - width
+    pieces = (*own, *other)
     shapes = [
-        bf16(experts, rows, width),
+        pltpu.HBM((experts, 2 * places, width), jnp.bfloat16),
         bf16(2, count, experts * places),
         bf16(2, experts * places, count),
-        f32(experts, 1, rows),
+        f32(experts, 1, 2 * places),
+    ]
+    ins = [pl.BlockSpec((piece.shape[0], WIDE), lambda i: (0, i)) for piece in pieces]
+    ins += [pl.BlockSpec((piece.shape[0], columns), lambda i: (0, width // columns)) for piece in pieces]
+    ins += [whole(a) for a in (*maps, mark)]
+    outs = [pl.BlockSpec((experts, 2 * places, WIDE), lambda i: (0, 0, i))]
+    outs += [kept(s) for s in shapes[1:]]
+    flops = 4 * experts * places * count * width
+    kernel = functools.partial(route_kernel, tok_count)
+    return call(kernel, width // WIDE, ins, (*pieces, *pieces, *maps, mark), outs, shapes, flops=flops)
+
+
+def up_call(x, prob, w_gate, w_up):
+    experts, hidden, width = w_gate.shape
+    rows = x.shape[1]
+    args = (in_hbm(x), prob, near_core(w_gate), near_core(w_up))
+    shapes = [
         f32(experts, hidden, rows),
         f32(experts, hidden, rows),
         bf16(experts, rows, hidden),
         bf16(experts, hidden, rows),
     ]
-    ins = [whole(a) for a in args[:-2]] + [pl.BlockSpec(memory_space=pl.ANY)] * 2
-    outs = [pl.BlockSpec(memory_space=pl.ANY)]
-    outs += [kept(s) for s in shapes[1:4]] + [each(s, PAIR) for s in shapes[4:]]
+    ins = [each(x, PAIR), each(prob, PAIR)] + [pl.BlockSpec(memory_space=pl.ANY)] * 2
+    outs = [each(s, PAIR) for s in shapes]
     scratch = [
-        pltpu.VMEM((2, count, held), jnp.bfloat16),
-        pltpu.VMEM((experts, rows, width), jnp.bfloat16),
-        pltpu.VMEM((experts, 2 * hidden, width), jnp.bfloat16),
-        pltpu.SemaphoreType.DMA((2, experts)),
-        pltpu.SemaphoreType.DMA,
+        pltpu.VMEM((2, PAIR, 2 * hidden, width), jnp.bfloat16),
+        pltpu.SemaphoreType.DMA((2, 2 * PAIR)),
     ]
-    flops = 4 * experts * rows * hidden * width + 2 * experts * rows * count * width
-    return call(
-        functools.partial(up_kernel, tok_count), experts // PAIR, ins, args, outs, shapes, scratch, flops
-    )
+    flops = 4 * experts * rows * hidden * width
+    return call(up_kernel, experts // PAIR, ins, args, outs, shapes, scratch, flops)
 
 
 def place_call(pieces, pick, experts):
     _, rows, count = pick.shape
     size, width = pieces[0].shape
-    shape = bf16(experts, 2 * rows // experts, width)
+    shape = pltpu.HBM((experts, 2 * rows // experts, width), jnp.bfloat16)
     ins = [pl.BlockSpec((size, WIDE), lambda i: (0, i))] * len(pieces) + [whole(pick)]
     outs = [pl.BlockSpec((*shape.shape[:2], WIDE), lambda i: (0, 0, i))]
     flops = 4 * rows * count * width
@@ -319,7 +356,7 @@
 def slope_call(x, put, prob, mine, w_down, g, u):
     experts, hidden, width = w_down.shape
     rows, count, columns = x.shape[1], put.shape[1], mine.shape[2]
-    args = (x, put, prob, mine, w_down, g, u)
+    args = (in_hbm(x), put, prob, mine, in_hbm(w_down), g, u)
     shapes = [
         bf16(experts, rows, hidden),
         bf16(experts, rows, hidden),
@@ -366,7 +403,7 @@
     shapes = [bf16(experts, hidden, width)] * (left.shape[1] // hidden)
     flops = 2 * experts * rows * left.shape[1] * width
     ins, outs = [each(x), each(left)], [each(s) for s in shapes]
-    return call(grad_kernel, experts, ins, (x, left), outs, shapes, flops=flops)
+    return call(grad_kernel, experts, ins, (in_hbm(x), left), outs, shapes, flops=flops)
 
 
 def dense_body(
@@ -411,7 +448,10 @@
     second0 = swap(zero, Y, X)
     cotangent, last_parts = together(cotangent, last_parts)
     grads = [swap(cotangent, bit) for bit in (Z1, Z2, Z3)]
-    last, last_parts, first1, second0 = together(last, last_parts, first1, second0)
+    last, last_parts, first1, second0, gate_weight = together(
+        last, last_parts, first1, second0, gate_weight
+    )
+    gate_weight, mark = fetch_call(gate_weight, last_parts)
 
     last = wide(last, last_parts)
     first2 = swap(last, X, Y)
@@ -419,7 +459,10 @@
     second1 = swap(middle_rows, Y, X)
     zero = rows_of(zero, second0)
     zero_other = swap(zero, CORE)
-    first2, second1, cotangent = together(first2, second1, cotangent)
+    first2, second1, cotangent, mark, up_weight = together(
+        first2, second1, cotangent, mark, up_weight
+    )
+    up_weight, mark = fetch_call(up_weight, mark)
 
     last = rows_of(last, first2)
     second2 = swap(last, Y, X)
@@ -429,18 +472,24 @@
     grads = rows_of(grads, swap(grads, X, Y))
     last = rows_of(last, second2)
     last_other = swap(last, CORE)
-    *rows, grads = together(
-        zero, middle_rows, last, zero_other, middle_other, last_other, grads
-    )
+    last, last_other, mark = together(last, last_other, mark)
+    x, put, pick, prob_rows = route_call(
+        (zero, middle_rows, last),
+        (zero_other, middle_other, last_other),
+        maps,
+        mark,
+        local,
+        width,
+        tok_count,
+    )
+    x, grads = together(x, grads)
     far_grads = swap(grads, Y, X)
     grads_other = swap(grads, CORE)
 
-    x, put, pick, prob_rows, g, u, h, ht = up_call(
-        rows[:3], rows[3:], maps, gate_weight, up_weight, tok_count
-    )
+    g, u, h, ht = up_call(x, prob_rows, gate_weight, up_weight)
     h, far_grads, grads_other = together(h, far_grads, grads_other)
     far_grads_other = swap(far_grads, CORE)
-    mixed, mixed_other = back_call(put, [h], [down_weight], 0, width)
+    mixed, mixed_other = back_call(put, [h], [in_hbm(down_weight)], 0, width)
     mixed_other, far_grads_other = together(mixed_other, far_grads_other)
     mixed = [mixed, swap(mixed_other, CORE)]
 
@@ -461,7 +510,7 @@
     def by_near(parts):
         return parts + [swap(leaving(parts, tok_count, 2 * tok_count), Z1)]
 
-    weights = [gate_weight, up_weight]
+    weights = [near_core(gate_weight), near_core(up_weight)]
     mixed[1], c = together(mixed[1], c)
     mixed = by_second(mixed)
     dg, du, dt, share = slope_call(

time: 187 us -> 168 us (0.90)
  other arithmetic: 18.8 us -> 5.02 us
  waiting for transfers between devices: 39.7 us -> 36.7 us
  Pallas kernels: 86.2 us -> 84.2 us
    pallas_call x8 -> x9, Pallas kernels: 86.2 us -> 75 us  [call(): pl.pallas_call(kernel, grid=(grid,), in_specs=ins, out_specs=outs, out_sh...]
    convert_element_type x15, other arithmetic: 13.2 us -> 2.23 us  [add(): return total.astype(jnp.bfloat16)]
    pallas_call x0 -> x2, Pallas kernels: none -> 9.17 us  [fetch_call(): pl.pallas_call(fetch_kernel, in_specs=[pl.BlockSpec(memory_space=pl.ANY)]...]
    ppermute x37, waiting for transfers between devices: 39.7 us -> 36.7 us  [swap(): return lax.ppermute(values, AXES, pairs)]
  transfers between devices with their start and end apart: 37 -> 37, of which waited for: 12 -> 12; matrix products, arithmetic and copies ran while one was open for 9% -> 2% of each run, Pallas kernels for 46% -> 47%
where the time goes in v6:
time: 168 us; the launch traced here: 167 us
  Pallas kernels  84.2 us (50%)
  waiting for transfers between devices  36.7 us (22%)
  starting transfers between devices  36.6 us (22%)
  other arithmetic  5.02 us (3%)
  local copies, waits for them, and re-layouts  3.39 us (2%)
    pallas_call x9, Pallas kernels, call(): pl.pallas_call(kernel, grid=(grid,), in_specs=ins, out_specs=outs, out_sh...  75 us
    ppermute x37, waiting for transfers between devices, swap(): return lax.ppermute(values, AXES, pairs)  36.7 us
    ppermute x37, starting transfers between devices, swap(): return lax.ppermute(values, AXES, pairs)  36.6 us
    pallas_call x2, Pallas kernels, fetch_call(): pl.pallas_call(fetch_kernel, in_specs=[pl.BlockSpec(memory_space=pl.ANY)]...  9.17 us
  transfers between devices with their start and end apart: 37, of which 12 were waited for; matrix products, arithmetic and copies ran while one was open for 2% of the time, Pallas kernels for 47%

profile of v6, /device:TPU:0, one launch (start us, length us, event | category | flops | bytes accessed | tf_op | source)
XLA Modules:
  0.0 167.0 jit_solution(13141484008256290656)
XLA Ops:
  3.5 3.0 %collective-permute-start.3 = (bf16[16,128]{1,0:T(8,128)(2,1)S(1)}, bf16[16,128]{1,0:T(8,128)(2,1)S(1)}, u32[]{:S(2)}, u32[]{:S(2)}) collective-permute-start(bf16[16,128]{1,0:T(8,128)(2,1)S(1)} %pad_maximum_fusion.8), channel_id=1, source_target_pairs={{0,2},{1,3},{2,0},{3,1},{4,6},{5,7},{6,4},{7,5},{8,10},{9,11},{10,... | collective-permute-start | bytes 12296 | tf_op jit(solution)/shard_map/ppermute | solution.py:33
  6.5 2.6 %collective-permute-start.4 = (bf16[16,128]{1,0:T(8,128)(2,1)S(1)}, bf16[16,128]{1,0:T(8,128)(2,1)S(1)}, u32[]{:S(2)}, u32[]{:S(2)}) collective-permute-start(bf16[16,128]{1,0:T(8,128)(2,1)S(1)} %pad_maximum_fusion.8), channel_id=1, source_target_pairs={{0,4},{1,5},{2,6},{3,7},{4,0},{5,1},{6,2},{7,3},{8,12},{9,13},{10,... | collective-permute-start | bytes 12296 | tf_op jit(solution)/shard_map/ppermute | solution.py:33
  10.6 1.8 %collective-permute-start = (bf16[16,4224]{1,0:T(8,128)(2,1)S(1)}, bf16[16,4224]{1,0:T(8,128)(2,1)S(1)}, u32[]{:S(2)}, u32[]{:S(2)}) collective-permute-start(bf16[16,4224]{1,0:T(8,128)(2,1)S(1)} %concatenate.50), channel_id=1, source_target_pairs={{0,8},{1,17},{2,10},{3,19},{4,12},{5,21},{6,14},{7,23},{8,0},{9,25... | collective-permute-start | bytes 405512 | tf_op jit(solution)/shard_map/ppermute | solution.py:33
  12.4 3.3 %collective-permute-done.1 = bf16[16,4096]{1,0:T(8,128)(2,1)S(1)} collective-permute-done((bf16[16,4096]{1,0:T(8,128)(2,1)}, bf16[16,4096]{1,0:T(8,128)(2,1)S(1)}, u32[]{:S(2)}, u32[]{:S(2)}) %collective-permute-start.1) | collective-permute-done | bytes 131104 | tf_op jit(solution)/shard_map/ppermute | solution.py:33
  15.7 2.2 %collective-permute-done.2 = bf16[16,4096]{1,0:T(8,128)(2,1)S(1)} collective-permute-done((bf16[16,4096]{1,0:T(8,128)(2,1)}, bf16[16,4096]{1,0:T(8,128)(2,1)S(1)}, u32[]{:S(2)}, u32[]{:S(2)}) %collective-permute-start.2) | collective-permute-done | bytes 131104 | tf_op jit(solution)/shard_map/ppermute | solution.py:33
  17.9 1.6 collective-permute-start.7
  19.5 1.6 collective-permute-start.8
  21.3 2.0 %collective-permute-start.5 = (bf16[16,4096]{1,0:T(8,128)(2,1)S(1)}, bf16[16,4096]{1,0:T(8,128)(2,1)S(1)}, u32[]{:S(2)}, u32[]{:S(2)}) collective-permute-start(bf16[16,4096]{1,0:T(8,128)(2,1)S(1)} %collective-permute-done.2), channel_id=1, source_target_pairs={{0,2},{1,3},{2,0},{3,1},{4,6},{5,7},{6,4},{7,5},{8,10},{9,11},{10,... | collective-permute-start | bytes 393224 | tf_op jit(solution)/shard_map/ppermute | solution.py:33
  24.9 1.9 %collective-permute-start.16 = (bf16[16,4096]{1,0:T(8,128)(2,1)S(1)}, bf16[16,4096]{1,0:T(8,128)(2,1)S(1)}, u32[]{:S(2)}, u32[]{:S(2)}) collective-permute-start(bf16[16,4096]{1,0:T(8,128)(2,1)S(1)} %copy-done.2), channel_id=1, source_target_pairs={{0,4},{1,5},{2,6},{3,7},{4,0},{5,1},{6,2},{7,3},{8,12},{9,13},{10,... | collective-permute-start | bytes 393224 | tf_op jit(solution)/shard_map/ppermute | solution.py:33
  27.3 2.0 %collective-permute-start.17 = (bf16[16,4096]{1,0:T(8,128)(2,1)S(1)}, bf16[16,4096]{1,0:T(8,128)(2,1)S(1)}, u32[]{:S(2)}, u32[]{:S(2)}) collective-permute-start(bf16[16,4096]{1,0:T(8,128)(2,1)S(1)} %copy-done.2), channel_id=1, source_target_pairs={{0,6},{1,7},{2,4},{3,5},{4,2},{5,3},{6,0},{7,1},{8,14},{9,15},{10,... | collective-permute-start | bytes 393224 | tf_op jit(solution)/shard_map/ppermute | solution.py:33
  30.9 4.6 %shard_map.127 = (bf16[8,192,4096]{2,1,0:T(8,128)(2,1)S(1)}, f32[8,128]{1,0:T(8,128)S(1)}) custom-call(bf16[8,192,4096]{2,1,0:T(8,128)(2,1)} %source, bf16[16,128]{1,0:T(8,128)(2,1)S(1)} %collective-permute-done.6.after), custom_call_target="tpu_custom_call" | custom-call | bytes 12582912 | tf_op jit(solution)/shard_map/pallas_call | solution.py:292
  35.5 4.9 %collective-permute-done.10 = bf16[64,4224]{1,0:T(8,128)(2,1)S(1)} collective-permute-done((bf16[64,4224]{1,0:T(8,128)(2,1)S(1)}, bf16[64,4224]{1,0:T(8,128)(2,1)S(1)}, u32[]{:S(2)}, u32[]{:S(2)}) %collective-permute-start.10) | collective-permute-done | bytes 540704 | tf_op jit(solution)/shard_map/ppermute | solution.py:33
  42.2 6.0 %collective-permute-done.11 = bf16[32,4224]{1,0:T(8,128)(2,1)S(1)} collective-permute-done((bf16[32,4224]{1,0:T(8,128)(2,1)S(1)}, bf16[32,4224]{1,0:T(8,128)(2,1)S(1)}, u32[]{:S(2)}, u32[]{:S(2)}) %collective-permute-start.11) | collective-permute-done | bytes 270368 | tf_op jit(solution)/shard_map/ppermute | solution.py:33
  48.3 4.6 %shard_map.128 = (bf16[8,192,4096]{2,1,0:T(8,128)(2,1)S(1)}, f32[8,128]{1,0:T(8,128)S(1)}) custom-call(bf16[8,192,4096]{2,1,0:T(8,128)(2,1)} %source.1, f32[8,128]{1,0:T(8,128)S(1)} %get-tuple-element.92.after), custom_call_target="tpu_custom_call" | custom-call | bytes 12582912 | tf_op jit(solution)/shard_map/pallas_call | solution.py:292
  53.0 6.1 %shard_map.129 = (bf16[8,96,4096]{2,1,0:T(8,128)(2,1)}, bf16[2,256,384]{2,1,0:T(8,128)(2,1)S(1)}, bf16[2,384,256]{2,1,0:T(8,128)(2,1)S(1)}, f32[8,1,96]{2,1,0:T(1,128)S(1)}) custom-call(bf16[64,4224]{1,0:T(8,128)(2,1)S(1)} %pad_maximum_fusion.1.refs_0_.refs_6_, bf16[128,4224]{1,0:T(8,128)(2,1)S(1)} %pad_maximum_fusion.refs_1_.refs_7_, ...), custom_call_target="tpu_custom_call" | custom-call | flops 1610612736 | bytes 16030720 | tf_op jit(solution)/shard_map/pallas_call | solution.py:272
  60.6 11.4 %shard_map.130 = (f32[8,192,96]{2,1,0:T(8,128)S(1)}, f32[8,192,96]{2,1,0:T(8,128)S(1)}, bf16[8,96,192]{2,1,0:T(8,128)(2,1)S(1)}, bf16[8,192,96]{2,1,0:T(8,128)(2,1)S(1)}) custom-call(bf16[8,96,4096]{2,1,0:T(8,128)(2,1)} %get-tuple-element.100.x_ref, f32[8,1,96]{2,1,0:T(1,128)S(1)} %get-tuple-element.101.prob_ref, ...), custom_call_target="tpu_custom_call" | custom-call | flops 2415919104 | bytes 33229824 | tf_op jit(solution)/shard_map/pallas_call | solution.py:272
  72.0 1.9 %collective-permute-done.19.own1 = bf16[128,4096]{1,0:T(8,128)(2,1)S(1)} collective-permute-done((bf16[128,4096]{1,0:T(8,128)(2,1)S(1)}, bf16[128,4096]{1,0:T(8,128)(2,1)S(1)}, u32[]{:S(2)}, u32[]{:S(2)}) %collective-permute-start.19) | collective-permute-done | bytes 1048608 | tf_op jit(solution)/shard_map/ppermute | solution.py:33
  73.9 7.7 %shard_map.131 = (bf16[256,4096]{1,0:T(8,128)(2,1)S(1)}, bf16[256,4096]{1,0:T(8,128)(2,1)S(1)}) custom-call(bf16[2,256,384]{2,1,0:T(8,128)(2,1)S(1)} %get-tuple-element.97.put_ref, bf16[8,96,192]{2,1,0:T(8,128)(2,1)S(1)} %get-tuple-element.106.refs_0_, bf16[8,192,4096]{2,1,0:T(8,128)(2,1)} %down_ref.1), custom_call_target="tpu_custom_call" | custom-call | flops 2818572288 | bytes 17465344 | tf_op jit(solution)/shard_map/pallas_call | solution.py:272
  82.2 4.3 %shard_map.132.x_ref = bf16[8,96,4096]{2,1,0:T(8,128)(2,1)} custom-call(bf16[128,4096]{1,0:T(8,128)(2,1)S(1)} %constant_dynamic-update-slice_fusion.2.own0, bf16[128,4096]{1,0:T(8,128)(2,1)S(1)} %collective-permute-done.19.own1, bf16[128,4096]{1,0:T(8,128)(2,1)S(1)} %collective-permute-done.20.other0, bf16[128,4096]{1,0:T(8,128)(2,1)S(1)} %collective-permute-done.21.other1, ...), custom_call_target="tpu_custom_call" | custom-call | flops 1610612736 | bytes 10878976 | tf_op jit(solution)/shard_map/pallas_call | solution.py:272
  87.6 9.6 %shard_map.133 = (bf16[8,96,192]{2,1,0:T(8,128)(2,1)S(1)}, bf16[8,96,192]{2,1,0:T(8,128)(2,1)S(1)}, bf16[8,384,96]{2,1,0:T(8,128)(2,1)S(1)}, bf16[2,256,128]{2,1,0:T(8,128)(2,1)S(1)}) custom-call(bf16[8,96,4096]{2,1,0:T(8,128)(2,1)} %shard_map.132.x_ref, bf16[2,256,384]{2,1,0:T(8,128)(2,1)S(1)} %get-tuple-element.97.put_ref, ...), custom_call_target="tpu_custom_call" | custom-call | flops 1207959552 | bytes 21859328 | tf_op jit(solution)/shard_map/pallas_call | solution.py:272
  97.1 5.9 %shard_map.134 = (bf16[256,2048]{1,0:T(8,128)(2,1)S(1)}, bf16[256,2048]{1,0:T(8,128)(2,1)S(1)}) custom-call(bf16[2,256,384]{2,1,0:T(8,128)(2,1)S(1)} %get-tuple-element.97.put_ref, bf16[8,96,192]{2,1,0:T(8,128)(2,1)S(1)} %get-tuple-element.122.refs_0_, bf16[8,96,192]{2,1,0:T(8,128)(2,1)S(1)} %get-tuple-element.123.refs_1_, ...), custom_call_target="tpu_custom_call" | custom-call | flops 2013265920 | bytes 28246016 | tf_op jit(solution)/shard_map/pallas_call | solution.py:272
  104.8 6.2 %shard_map.135 = (bf16[256,2176]{1,0:T(8,128)(2,1)S(1)}, bf16[256,2176]{1,0:T(8,128)(2,1)S(1)}) custom-call(bf16[2,256,384]{2,1,0:T(8,128)(2,1)S(1)} %get-tuple-element.97.put_ref, bf16[8,96,192]{2,1,0:T(8,128)(2,1)S(1)} %get-tuple-element.122.refs_0_, bf16[8,96,192]{2,1,0:T(8,128)(2,1)S(1)} %get-tuple-element.123.refs_1_, ...), custom_call_target="tpu_custom_call" | custom-call | flops 2013265920 | bytes 28508160 | tf_op jit(solution)/shard_map/pallas_call | solution.py:272
  111.2 1.7 %collective-permute-done.25 = bf16[64,4096]{1,0:T(8,128)(2,1)S(1)} collective-permute-done((bf16[64,4096]{1,0:T(8,128)(2,1)S(1)}, bf16[64,4096]{1,0:T(8,128)(2,1)S(1)}, u32[]{:S(2)}, u32[]{:S(2)}) %collective-permute-start.25) | collective-permute-done | bytes 524320 | tf_op jit(solution)/shard_map/ppermute | solution.py:33
  114.3 2.3 %collective-permute-start.28 = (bf16[32,4096]{1,0:T(8,128)(2,1)S(1)}, bf16[32,4096]{1,0:T(8,128)(2,1)S(1)}, u32[]{:S(2)}, u32[]{:S(2)}) collective-permute-start(bf16[32,4096]{1,0:T(8,128)(2,1)S(1)} %add_convert_fusion.6), channel_id=1, source_target_pairs={{0,4},{1,5},{2,6},{3,7},{4,0},{5,1},{6,2},{7,3},{8,12},{9,13},{10,... | collective-permute-start | bytes 786440 | tf_op jit(solution)/shard_map/ppermute | solution.py:33
  116.6 10.5 %shard_map.136 = bf16[8,192,4096]{2,1,0:T(8,128)(2,1)} custom-call(bf16[8,96,4096]{2,1,0:T(8,128)(2,1)} %shard_map.132.x_ref, bf16[8,192,96]{2,1,0:T(8,128)(2,1)S(1)} %get-tuple-element.132.left), custom_call_target="tpu_custom_call" | custom-call | flops 1207959552 | bytes 19169280 | tf_op jit(solution)/shard_map/pallas_call | solution.py:272
  129.2 1.6 collective-permute-start.29
  131.0 13.3 %shard_map.137 = (bf16[8,192,4096]{2,1,0:T(8,128)(2,1)}, bf16[8,192,4096]{2,1,0:T(8,128)(2,1)}) custom-call(bf16[8,96,4096]{2,1,0:T(8,128)(2,1)} %get-tuple-element.100.x_ref, bf16[8,384,96]{2,1,0:T(8,128)(2,1)S(1)} %get-tuple-element.139.left), custom_call_target="tpu_custom_call" | custom-call | flops 2415919104 | bytes 32047104 | tf_op jit(solution)/shard_map/pallas_call | solution.py:272
  144.4 2.7 %collective-permute-start.32 = (bf16[32,2048]{1,0:T(8,128)(2,1)S(1)}, bf16[32,2048]{1,0:T(8,128)(2,1)S(1)}, u32[]{:S(2)}, u32[]{:S(2)}) collective-permute-start(bf16[32,2048]{1,0:T(8,128)(2,1)S(1)} %add_convert_fusion.8), channel_id=1, source_target_pairs={{0,4},{1,5},{2,6},{3,7},{4,0},{5,1},{6,2},{7,3},{8,12},{9,13},{10,... | collective-permute-start | bytes 393224 | tf_op jit(solution)/shard_map/ppermute | solution.py:33
  149.0 4.8 %collective-permute-done.34 = bf16[64,2176]{1,0:T(8,128)(2,1)S(1)} collective-permute-done((bf16[64,2176]{1,0:T(8,128)(2,1)S(1)}, bf16[64,2176]{1,0:T(8,128)(2,1)S(1)}, u32[]{:S(2)}, u32[]{:S(2)}) %collective-permute-start.34) | collective-permute-done | bytes 278560 | tf_op jit(solution)/shard_map/ppermute | solution.py:33
  154.3 2.1 %collective-permute-start.33 = (bf16[16,2048]{1,0:T(8,128)(2,1)S(1)}, bf16[16,2048]{1,0:T(8,128)(2,1)S(1)}, u32[]{:S(2)}, u32[]{:S(2)}) collective-permute-start(bf16[16,2048]{1,0:T(8,128)(2,1)S(1)} %add_convert_fusion.14), channel_id=1, source_target_pairs={{0,2},{1,3},{2,0},{3,1},{4,6},{5,7},{6,4},{7,5},{8,10},{9,11},{10,... | collective-permute-start | bytes 196616 | tf_op jit(solution)/shard_map/ppermute | solution.py:33
  156.4 4.6 %collective-permute-done.35 = bf16[32,2176]{1,0:T(8,128)(2,1)S(1)} collective-permute-done((bf16[32,2176]{1,0:T(8,128)(2,1)S(1)}, bf16[32,2176]{1,0:T(8,128)(2,1)S(1)}, u32[]{:S(2)}, u32[]{:S(2)}) %collective-permute-start.35) | collective-permute-done | bytes 139296 | tf_op jit(solution)/shard_map/ppermute | solution.py:33
  161.2 4.2 %collective-permute-done.36 = bf16[16,2176]{1,0:T(8,128)(2,1)S(1)} collective-permute-done((bf16[16,2176]{1,0:T(8,128)(2,1)S(1)}, bf16[16,2176]{1,0:T(8,128)(2,1)S(1)}, u32[]{:S(2)}, u32[]{:S(2)}) %collective-permute-start.36) | collective-permute-done | bytes 69664 | tf_op jit(solution)/shard_map/ppermute | solution.py:33
  (107 shorter events, 23.0 us)
Async XLA Ops:
  3.5 8.9 %collective-permute-start.3 = (bf16[16,128]{1,0:T(8,128)(2,1)S(1)}, bf16[16,128]{1,0:T(8,128)(2,1)S(1)}, u32[]{:S(2)}, u32[]{:S(2)}) collective-permute-start(bf16[16,128]{1,0:T(8,128)(2,1)S(1)} %pad_maximum_fusion.8), channel_id=1, source_target_pairs={{0,2},{1,3},{2,0},{3,1},{4,6},{5,7},{6,4},{7,5},{8,10},{9,11},{10,... | collective-permute-start | bytes 12296 | tf_op jit(solution)/shard_map/ppermute | solution.py:33
  9.1 6.6 %collective-permute-start.1 = (bf16[16,4096]{1,0:T(8,128)(2,1)}, bf16[16,4096]{1,0:T(8,128)(2,1)S(1)}, u32[]{:S(2)}, u32[]{:S(2)}) collective-permute-start(bf16[16,4096]{1,0:T(8,128)(2,1)} %param.8), channel_id=1, source_target_pairs={{0,2},{1,3},{2,0},{3,1},{4,6},{5,7},{6,4},{7,5},{8,10},{9,11},{10,... | collective-permute-start | bytes 393224 | tf_op jit(solution)/shard_map/ppermute | solution.py:33
  9.5 8.4 %collective-permute-start.2 = (bf16[16,4096]{1,0:T(8,128)(2,1)}, bf16[16,4096]{1,0:T(8,128)(2,1)S(1)}, u32[]{:S(2)}, u32[]{:S(2)}) collective-permute-start(bf16[16,4096]{1,0:T(8,128)(2,1)} %param.8), channel_id=1, source_target_pairs={{0,4},{1,5},{2,6},{3,7},{4,0},{5,1},{6,2},{7,3},{8,12},{9,13},{10,... | collective-permute-start | bytes 393224 | tf_op jit(solution)/shard_map/ppermute | solution.py:33
  10.6 8.9 %collective-permute-start = (bf16[16,4224]{1,0:T(8,128)(2,1)S(1)}, bf16[16,4224]{1,0:T(8,128)(2,1)S(1)}, u32[]{:S(2)}, u32[]{:S(2)}) collective-permute-start(bf16[16,4224]{1,0:T(8,128)(2,1)S(1)} %concatenate.50), channel_id=1, source_target_pairs={{0,8},{1,17},{2,10},{3,19},{4,12},{5,21},{6,14},{7,23},{8,0},{9,25... | collective-permute-start | bytes 405512 | tf_op jit(solution)/shard_map/ppermute | solution.py:33
  17.9 11.3 %collective-permute-start.7 = (bf16[32,4224]{1,0:T(8,128)(2,1)S(1)}, bf16[32,4224]{1,0:T(8,128)(2,1)S(1)}, u32[]{:S(2)}, u32[]{:S(2)}) collective-permute-start(bf16[32,4224]{1,0:T(8,128)(2,1)S(1)} %maximum_maximum_fusion), channel_id=1, source_target_pairs={{0,8},{1,17},{2,10},{3,19},{4,12},{5,21},{6,14},{7,23},{8,0},{9,25... | collective-permute-start | bytes 811016 | tf_op jit(solution)/shard_map/ppermute | solution.py:33
  19.5 9.8 %collective-permute-start.8 = (bf16[32,4224]{1,0:T(8,128)(2,1)S(1)}, bf16[32,4224]{1,0:T(8,128)(2,1)S(1)}, u32[]{:S(2)}, u32[]{:S(2)}) collective-permute-start(bf16[32,4224]{1,0:T(8,128)(2,1)S(1)} %pad_maximum_fusion.5), channel_id=1, source_target_pairs={{0,16},{1,9},{2,18},{3,11},{4,20},{5,13},{6,22},{7,15},{8,24},{9,1... | collective-permute-start | bytes 811016 | tf_op jit(solution)/shard_map/ppermute | solution.py:33
  21.3 6.0 %collective-permute-start.5 = (bf16[16,4096]{1,0:T(8,128)(2,1)S(1)}, bf16[16,4096]{1,0:T(8,128)(2,1)S(1)}, u32[]{:S(2)}, u32[]{:S(2)}) collective-permute-start(bf16[16,4096]{1,0:T(8,128)(2,1)S(1)} %collective-permute-done.2), channel_id=1, source_target_pairs={{0,2},{1,3},{2,0},{3,1},{4,6},{5,7},{6,4},{7,5},{8,10},{9,11},{10,... | collective-permute-start | bytes 393224 | tf_op jit(solution)/shard_map/ppermute | solution.py:33
  24.9 15.6 %collective-permute-start.15 = (bf16[16,4096]{1,0:T(8,128)(2,1)S(1)}, bf16[16,4096]{1,0:T(8,128)(2,1)S(1)}, u32[]{:S(2)}, u32[]{:S(2)}) collective-permute-start(bf16[16,4096]{1,0:T(8,128)(2,1)S(1)} %copy-done.2), channel_id=1, source_target_pairs={{0,2},{1,3},{2,0},{3,1},{4,6},{5,7},{6,4},{7,5},{8,10},{9,11},{10,... | collective-permute-start | bytes 393224 | tf_op jit(solution)/shard_map/ppermute | solution.py:33
  24.9 15.6 %collective-permute-start.16 = (bf16[16,4096]{1,0:T(8,128)(2,1)S(1)}, bf16[16,4096]{1,0:T(8,128)(2,1)S(1)}, u32[]{:S(2)}, u32[]{:S(2)}) collective-permute-start(bf16[16,4096]{1,0:T(8,128)(2,1)S(1)} %copy-done.2), channel_id=1, source_target_pairs={{0,4},{1,5},{2,6},{3,7},{4,0},{5,1},{6,2},{7,3},{8,12},{9,13},{10,... | collective-permute-start | bytes 393224 | tf_op jit(solution)/shard_map/ppermute | solution.py:33
  27.3 13.2 %collective-permute-start.17 = (bf16[16,4096]{1,0:T(8,128)(2,1)S(1)}, bf16[16,4096]{1,0:T(8,128)(2,1)S(1)}, u32[]{:S(2)}, u32[]{:S(2)}) collective-permute-start(bf16[16,4096]{1,0:T(8,128)(2,1)S(1)} %copy-done.2), channel_id=1, source_target_pairs={{0,6},{1,7},{2,4},{3,5},{4,2},{5,3},{6,0},{7,1},{8,14},{9,15},{10,... | collective-permute-start | bytes 393224 | tf_op jit(solution)/shard_map/ppermute | solution.py:33
  29.3 6.2 %collective-permute-start.9 = (bf16[16,4224]{1,0:T(8,128)(2,1)S(1)}, bf16[16,4224]{1,0:T(8,128)(2,1)S(1)}, u32[]{:S(2)}, u32[]{:S(2)}) collective-permute-start(bf16[16,4224]{1,0:T(8,128)(2,1)S(1)} %constant_dynamic-update-slice_fusion), channel_id=1, source_target_pairs={{0,8},{1,17},{2,10},{3,19},{4,12},{5,21},{6,14},{7,23},{8,0},{9,25... | collective-permute-start | bytes 405512 | tf_op jit(solution)/shard_map/ppermute | solution.py:33
  30.2 10.2 %collective-permute-start.10 = (bf16[64,4224]{1,0:T(8,128)(2,1)S(1)}, bf16[64,4224]{1,0:T(8,128)(2,1)S(1)}, u32[]{:S(2)}, u32[]{:S(2)}) collective-permute-start(bf16[64,4224]{1,0:T(8,128)(2,1)S(1)} %pad_maximum_fusion.2), channel_id=1, source_target_pairs={{0,16},{1,9},{2,18},{3,11},{4,20},{5,13},{6,22},{7,15},{8,24},{9,1... | collective-permute-start | bytes 1622024 | tf_op jit(solution)/shard_map/ppermute | solution.py:33
  35.5 17.5 %collective-permute-start.13 = (bf16[64,4224]{1,0:T(8,128)(2,1)S(1)}, bf16[64,4224]{1,0:T(8,128)(2,1)S(1)}, u32[]{:S(2)}, u32[]{:S(2)}) collective-permute-start(bf16[64,4224]{1,0:T(8,128)(2,1)S(1)} %pad_maximum_fusion.1.refs_0_.refs_6_), channel_id=1, source_target_pairs={{0,1},{1,0},{2,3},{3,2},{4,5},{5,4},{6,7},{7,6},{8,9},{9,8},{10,11... | collective-permute-start | bytes 1622024 | tf_op jit(solution)/shard_map/ppermute | solution.py:33
  40.5 12.4 %collective-permute-start.18 = (bf16[64,4096]{1,0:T(8,128)(2,1)S(1)}, bf16[64,4096]{1,0:T(8,128)(2,1)S(1)}, u32[]{:S(2)}, u32[]{:S(2)}) collective-permute-start(bf16[64,4096]{1,0:T(8,128)(2,1)S(1)} %pad_maximum_fusion.4), channel_id=1, source_target_pairs={{0,8},{1,17},{2,10},{3,19},{4,12},{5,21},{6,14},{7,23},{8,0},{9,25... | collective-permute-start | bytes 1572872 | tf_op jit(solution)/shard_map/ppermute | solution.py:33
  41.5 6.6 %collective-permute-start.11 = (bf16[32,4224]{1,0:T(8,128)(2,1)S(1)}, bf16[32,4224]{1,0:T(8,128)(2,1)S(1)}, u32[]{:S(2)}, u32[]{:S(2)}) collective-permute-start(bf16[32,4224]{1,0:T(8,128)(2,1)S(1)} %pad_maximum_fusion.6), channel_id=1, source_target_pairs={{0,16},{1,9},{2,18},{3,11},{4,20},{5,13},{6,22},{7,15},{8,24},{9,1... | collective-permute-start | bytes 811016 | tf_op jit(solution)/shard_map/ppermute | solution.py:33
  42.1 10.9 %collective-permute-start.14 = (bf16[128,4224]{1,0:T(8,128)(2,1)S(1)}, bf16[128,4224]{1,0:T(8,128)(2,1)S(1)}, u32[]{:S(2)}, u32[]{:S(2)}) collective-permute-start(bf16[128,4224]{1,0:T(8,128)(2,1)S(1)} %pad_maximum_fusion.refs_1_.refs_7_), channel_id=1, source_target_pairs={{0,1},{1,0},{2,3},{3,2},{4,5},{5,4},{6,7},{7,6},{8,9},{9,8},{10,11... | collective-permute-start | bytes 3244040 | tf_op jit(solution)/shard_map/ppermute | solution.py:33
  59.1 14.8 %collective-permute-start.19 = (bf16[128,4096]{1,0:T(8,128)(2,1)S(1)}, bf16[128,4096]{1,0:T(8,128)(2,1)S(1)}, u32[]{:S(2)}, u32[]{:S(2)}) collective-permute-start(bf16[128,4096]{1,0:T(8,128)(2,1)S(1)} %constant_dynamic-update-slice_fusion.2.own0), channel_id=1, source_target_pairs={{0,16},{1,9},{2,18},{3,11},{4,20},{5,13},{6,22},{7,15},{8,24},{9,1... | collective-permute-start | bytes 3145736 | tf_op jit(solution)/shard_map/ppermute | solution.py:33
  59.8 14.2 %collective-permute-start.20 = (bf16[128,4096]{1,0:T(8,128)(2,1)S(1)}, bf16[128,4096]{1,0:T(8,128)(2,1)S(1)}, u32[]{:S(2)}, u32[]{:S(2)}) collective-permute-start(bf16[128,4096]{1,0:T(8,128)(2,1)S(1)} %constant_dynamic-update-slice_fusion.2.own0), channel_id=1, source_target_pairs={{0,1},{1,0},{2,3},{3,2},{4,5},{5,4},{6,7},{7,6},{8,9},{9,8},{10,11... | collective-permute-start | bytes 3145736 | tf_op jit(solution)/shard_map/ppermute | solution.py:33
  73.9 7.7 %collective-permute-start.21 = (bf16[128,4096]{1,0:T(8,128)(2,1)S(1)}, bf16[128,4096]{1,0:T(8,128)(2,1)S(1)}, u32[]{:S(2)}, u32[]{:S(2)}) collective-permute-start(bf16[128,4096]{1,0:T(8,128)(2,1)S(1)} %collective-permute-done.19.own1), channel_id=1, source_target_pairs={{0,1},{1,0},{2,3},{3,2},{4,5},{5,4},{6,7},{7,6},{8,9},{9,8},{10,11... | collective-permute-start | bytes 3145736 | tf_op jit(solution)/shard_map/ppermute | solution.py:33
  86.7 16.8 %collective-permute-start.23 = (bf16[128,4096]{1,0:T(8,128)(2,1)S(1)}, bf16[128,4096]{1,0:T(8,128)(2,1)S(1)}, u32[]{:S(2)}, u32[]{:S(2)}) collective-permute-start(bf16[128,4096]{1,0:T(8,128)(2,1)S(1)} %add_convert_fusion), channel_id=1, source_target_pairs={{0,16},{1,9},{2,18},{3,11},{4,20},{5,13},{6,22},{7,15},{8,24},{9,1... | collective-permute-start | bytes 3145736 | tf_op jit(solution)/shard_map/ppermute | solution.py:33
  103.0 8.2 %collective-permute-start.24 = (bf16[256,2048]{1,0:T(8,128)(2,1)S(1)}, bf16[256,2048]{1,0:T(8,128)(2,1)S(1)}, u32[]{:S(2)}, u32[]{:S(2)}) collective-permute-start(bf16[256,2048]{1,0:T(8,128)(2,1)S(1)} %get-tuple-element.126), channel_id=1, source_target_pairs={{0,1},{1,0},{2,3},{3,2},{4,5},{5,4},{6,7},{7,6},{8,9},{9,8},{10,11... | collective-permute-start | bytes 3145736 | tf_op jit(solution)/shard_map/ppermute | solution.py:33
  103.7 9.2 %collective-permute-start.25 = (bf16[64,4096]{1,0:T(8,128)(2,1)S(1)}, bf16[64,4096]{1,0:T(8,128)(2,1)S(1)}, u32[]{:S(2)}, u32[]{:S(2)}) collective-permute-start(bf16[64,4096]{1,0:T(8,128)(2,1)S(1)} %add_convert_fusion.3), channel_id=1, source_target_pairs={{0,8},{1,17},{2,10},{3,19},{4,12},{5,21},{6,14},{7,23},{8,0},{9,25... | collective-permute-start | bytes 1572872 | tf_op jit(solution)/shard_map/ppermute | solution.py:33
  111.0 17.2 %collective-permute-start.26 = (bf16[256,2176]{1,0:T(8,128)(2,1)S(1)}, bf16[256,2176]{1,0:T(8,128)(2,1)S(1)}, u32[]{:S(2)}, u32[]{:S(2)}) collective-permute-start(bf16[256,2176]{1,0:T(8,128)(2,1)S(1)} %get-tuple-element.128), channel_id=1, source_target_pairs={{0,1},{1,0},{2,3},{3,2},{4,5},{5,4},{6,7},{7,6},{8,9},{9,8},{10,11... | collective-permute-start | bytes 3342344 | tf_op jit(solution)/shard_map/ppermute | solution.py:33
  113.1 15.2 %collective-permute-start.27 = (bf16[128,2048]{1,0:T(8,128)(2,1)S(1)}, bf16[128,2048]{1,0:T(8,128)(2,1)S(1)}, u32[]{:S(2)}, u32[]{:S(2)}) collective-permute-start(bf16[128,2048]{1,0:T(8,128)(2,1)S(1)} %add_convert_fusion.2), channel_id=1, source_target_pairs={{0,16},{1,9},{2,18},{3,11},{4,20},{5,13},{6,22},{7,15},{8,24},{9,1... | collective-permute-start | bytes 1572872 | tf_op jit(solution)/shard_map/ppermute | solution.py:33
  114.3 13.9 %collective-permute-start.28 = (bf16[32,4096]{1,0:T(8,128)(2,1)S(1)}, bf16[32,4096]{1,0:T(8,128)(2,1)S(1)}, u32[]{:S(2)}, u32[]{:S(2)}) collective-permute-start(bf16[32,4096]{1,0:T(8,128)(2,1)S(1)} %add_convert_fusion.6), channel_id=1, source_target_pairs={{0,4},{1,5},{2,6},{3,7},{4,0},{5,1},{6,2},{7,3},{8,12},{9,13},{10,... | collective-permute-start | bytes 786440 | tf_op jit(solution)/shard_map/ppermute | solution.py:33
  128.4 16.0 %collective-permute-start.30 = (bf16[64,2048]{1,0:T(8,128)(2,1)S(1)}, bf16[64,2048]{1,0:T(8,128)(2,1)S(1)}, u32[]{:S(2)}, u32[]{:S(2)}) collective-permute-start(bf16[64,2048]{1,0:T(8,128)(2,1)S(1)} %add_convert_fusion.5), channel_id=1, source_target_pairs={{0,8},{1,17},{2,10},{3,19},{4,12},{5,21},{6,14},{7,23},{8,0},{9,25... | collective-permute-start | bytes 786440 | tf_op jit(solution)/shard_map/ppermute | solution.py:33
  129.2 15.1 %collective-permute-start.29 = (bf16[128,2176]{1,0:T(8,128)(2,1)S(1)}, bf16[128,2176]{1,0:T(8,128)(2,1)S(1)}, u32[]{:S(2)}, u32[]{:S(2)}) collective-permute-start(bf16[128,2176]{1,0:T(8,128)(2,1)S(1)} %add_convert_fusion.1), channel_id=1, source_target_pairs={{0,16},{1,9},{2,18},{3,11},{4,20},{5,13},{6,22},{7,15},{8,24},{9,1... | collective-permute-start | bytes 1671176 | tf_op jit(solution)/shard_map/ppermute | solution.py:33
  130.9 13.4 %collective-permute-start.31 = (bf16[16,4096]{1,0:T(8,128)(2,1)S(1)}, bf16[16,4096]{1,0:T(8,128)(2,1)S(1)}, u32[]{:S(2)}, u32[]{:S(2)}) collective-permute-start(bf16[16,4096]{1,0:T(8,128)(2,1)S(1)} %add_convert_fusion.10), channel_id=1, source_target_pairs={{0,2},{1,3},{2,0},{3,1},{4,6},{5,7},{6,4},{7,5},{8,10},{9,11},{10,... | collective-permute-start | bytes 393224 | tf_op jit(solution)/shard_map/ppermute | solution.py:33
  144.4 9.9 %collective-permute-start.32 = (bf16[32,2048]{1,0:T(8,128)(2,1)S(1)}, bf16[32,2048]{1,0:T(8,128)(2,1)S(1)}, u32[]{:S(2)}, u32[]{:S(2)}) collective-permute-start(bf16[32,2048]{1,0:T(8,128)(2,1)S(1)} %add_convert_fusion.8), channel_id=1, source_target_pairs={{0,4},{1,5},{2,6},{3,7},{4,0},{5,1},{6,2},{7,3},{8,12},{9,13},{10,... | collective-permute-start | bytes 393224 | tf_op jit(solution)/shard_map/ppermute | solution.py:33
  147.2 6.6 %collective-permute-start.34 = (bf16[64,2176]{1,0:T(8,128)(2,1)S(1)}, bf16[64,2176]{1,0:T(8,128)(2,1)S(1)}, u32[]{:S(2)}, u32[]{:S(2)}) collective-permute-start(bf16[64,2176]{1,0:T(8,128)(2,1)S(1)} %add_convert_fusion.4), channel_id=1, source_target_pairs={{0,8},{1,17},{2,10},{3,19},{4,12},{5,21},{6,14},{7,23},{8,0},{9,25... | collective-permute-start | bytes 835592 | tf_op jit(solution)/shard_map/ppermute | solution.py:33
  153.9 7.1 %collective-permute-start.35 = (bf16[32,2176]{1,0:T(8,128)(2,1)S(1)}, bf16[32,2176]{1,0:T(8,128)(2,1)S(1)}, u32[]{:S(2)}, u32[]{:S(2)}) collective-permute-start(bf16[32,2176]{1,0:T(8,128)(2,1)S(1)} %add_convert_fusion.7), channel_id=1, source_target_pairs={{0,4},{1,5},{2,6},{3,7},{4,0},{5,1},{6,2},{7,3},{8,12},{9,13},{10,... | collective-permute-start | bytes 417800 | tf_op jit(solution)/shard_map/ppermute | solution.py:33
  154.3 6.8 %collective-permute-start.33 = (bf16[16,2048]{1,0:T(8,128)(2,1)S(1)}, bf16[16,2048]{1,0:T(8,128)(2,1)S(1)}, u32[]{:S(2)}, u32[]{:S(2)}) collective-permute-start(bf16[16,2048]{1,0:T(8,128)(2,1)S(1)} %add_convert_fusion.14), channel_id=1, source_target_pairs={{0,2},{1,3},{2,0},{3,1},{4,6},{5,7},{6,4},{7,5},{8,10},{9,11},{10,... | collective-permute-start | bytes 196616 | tf_op jit(solution)/shard_map/ppermute | solution.py:33
  (8 other events, 52.3 us)

commit v7 on v6

--- a/solution.py
+++ b/solution.py
@@ -113,16 +113,13 @@
 
 def up_kernel(x_ref, prob_ref, gate_ref, up_ref, g_ref, u_ref, h_ref, ht_ref, held_ref, sems):
     step = pl.program_id(0)
-    both, width = x_ref.shape[1:]
     hidden = gate_ref.shape[1]
 
-    def copies(at):
-        slot = lax.rem(at, 2)
-        for i in range(PAIR):
-            e = PAIR * at + i
-            for j, source in enumerate((gate_ref, up_ref)):
-                held = held_ref.at[slot, i, hidden * j : hidden * (j + 1)]
-                yield pltpu.make_async_copy(source.at[e], held, sems.at[slot, 2 * i + j])
+    def copies(e):
+        slot = lax.rem(e, 2)
+        for j, source in enumerate((gate_ref, up_ref)):
+            held = held_ref.at[slot, hidden * j : hidden * (j + 1)]
+            yield pltpu.make_async_copy(source.at[e], held, sems.at[slot, j])
 
     @pl.when(step == 0)
     def _():
@@ -136,27 +133,25 @@
 
     for copy in copies(step):
         copy.wait()
-    weights = held_ref[lax.rem(step, 2)].reshape(PAIR * 2 * hidden, width)
-    product = dot(weights, x_ref[...].reshape(PAIR * both, width), NT)
-    for i in range(PAIR):
-        own = product[2 * hidden * i : 2 * hidden * (i + 1), both * i : both * (i + 1)]
-        g, u = own[:hidden], own[hidden:]
-        g_ref[i] = g
-        u_ref[i] = u
-        silu_v, _ = gated(g)
-        scaled = silu_v * u * prob_ref[i]
-        ht_ref[i] = scaled.astype(jnp.bfloat16)
-        h_ref[i] = scaled.T.astype(jnp.bfloat16)
-
-
-def place_kernel(own0, own1, other0, other1, pick_ref, x_ref):
+    product = dot(held_ref[lax.rem(step, 2)], x_ref[0], NT)
+    g, u = product[:hidden], product[hidden:]
+    g_ref[0] = g
+    u_ref[0] = u
+    silu_v, _ = gated(g)
+    scaled = silu_v * u * prob_ref[0]
+    ht_ref[0] = scaled.astype(jnp.bfloat16)
+    h_ref[0] = scaled.T.astype(jnp.bfloat16)
+
+
+def place_kernel(own0, own1, other0, other1, pick_ref, x_ref, kept_ref):
     for half, pieces in enumerate(((own0, own1), (other0, other1))):
         rows = jnp.concatenate([pieces[0][...], pieces[1][...]], axis=0)
         put_in_places(pick_ref[half], rows, half, x_ref)
+    kept_ref[...] = x_ref[...]
 
 
 def slope_kernel(x_ref, put_ref, prob_ref, mine_ref, down_ref, g_ref, u_ref,
-                 dg_ref, du_ref, dt_ref, share_ref, shares_ref, terms_ref):
+                 dg_ref, du_ref, dgt_ref, dut_ref, share_ref, shares_ref, terms_ref):
     e = pl.program_id(0)
     experts, both = shares_ref.shape
     places = both // 2
@@ -172,8 +167,8 @@
         scaled = plain * prob_ref[i]
         dg = scaled * u * slope
         du = scaled * silu_v
-        dt_ref[i, :hidden] = dg.astype(jnp.bfloat16)
-        dt_ref[i, hidden:] = du.astype(jnp.bfloat16)
+        dgt_ref[i] = dg.astype(jnp.bfloat16)
+        dut_ref[i] = du.astype(jnp.bfloat16)
         dg_ref[i] = dg.T.astype(jnp.bfloat16)
         du_ref[i] = du.T.astype(jnp.bfloat16)
 
@@ -188,31 +183,18 @@
             share_ref[half] = dot(put_ref[half], terms_ref[...]).astype(jnp.bfloat16)
 
 
-def back_kernel(terms, start, steps, put_ref, *refs):
+def back_kernel(terms, steps, put_ref, *refs):
     lefts, rights = refs[:terms], refs[terms : 2 * terms]
-    extra_ref = refs[2 * terms] if len(refs) > 2 * terms + 5 else None
-    own_ref, other_ref, rows_ref, held_ref, sems = refs[-5:]
+    extra_ref = refs[2 * terms] if len(refs) > 2 * terms + 3 else None
+    own_ref, other_ref, rows_ref = refs[-3:]
     experts, places = rights[0].shape[0], put_ref.shape[2] // rights[0].shape[0]
-    step = pl.program_id(0)
-
-    def copy(i, at):
-        columns = pl.ds(pl.multiple_of(start + at * CHUNK, CHUNK), CHUNK)
-        return pltpu.make_async_copy(rights[i].at[:, :, columns], held_ref.at[i, at], sems.at[i, at])
-
-    @pl.when(step == 0)
+
+    @pl.when(pl.program_id(0) < steps)
     def _():
-        for at in range(steps):
-            for i in range(terms):
-                copy(i, at).start()
-
-    @pl.when(step < steps)
-    def _():
-        for i in range(terms):
-            copy(i, step).wait()
         for e in range(experts):
-            rows = dot(lefts[0][e], held_ref[0, step, e])
-            for i in range(1, terms):
-                rows = rows + dot(lefts[i][e], held_ref[i, step, e])
+            rows = dot(lefts[0][e], rights[0][e])
+            for left, right in zip(lefts[1:], rights[1:]):
+                rows = rows + dot(left[e], right[e])
             rows = rows.astype(jnp.bfloat16)
             for half in range(2):
                 rows_ref[half, e * places : (e + 1) * places] = rows[half * places : (half + 1) * places]
@@ -221,7 +203,7 @@
 
     if extra_ref is not None:
 
-        @pl.when(step == steps)
+        @pl.when(pl.program_id(0) == steps)
         def _():
             columns = extra_ref.shape[2]
             own_ref[:, :columns] = extra_ref[0]
@@ -276,7 +258,7 @@
         out_specs=outs,
         out_shape=shapes,
         scratch_shapes=scratch,
-        compiler_params=pltpu.CompilerParams(vmem_limit_bytes=24 * MIB),
+        compiler_params=pltpu.CompilerParams(vmem_limit_bytes=14 * MIB),
         cost_estimate=pl.CostEstimate(flops=flops, bytes_accessed=moved, transcendentals=0),
     )(*args)
 
@@ -308,7 +290,7 @@
     columns = own[0].shape[1] - width
     pieces = (*own, *other)
     shapes = [
-        pltpu.HBM((experts, 2 * places, width), jnp.bfloat16),
+        pltpu.VMEM((experts, 2 * places, width), jnp.bfloat16),
         bf16(2, count, experts * places),
         bf16(2, experts * places, count),
         f32(experts, 1, 2 * places),
@@ -326,46 +308,48 @@
 def up_call(x, prob, w_gate, w_up):
     experts, hidden, width = w_gate.shape
     rows = x.shape[1]
-    args = (in_hbm(x), prob, near_core(w_gate), near_core(w_up))
+    args = (near_core(x), prob, near_core(w_gate), near_core(w_up))
     shapes = [
         f32(experts, hidden, rows),
         f32(experts, hidden, rows),
         bf16(experts, rows, hidden),
         bf16(experts, hidden, rows),
     ]
-    ins = [each(x, PAIR), each(prob, PAIR)] + [pl.BlockSpec(memory_space=pl.ANY)] * 2
-    outs = [each(s, PAIR) for s in shapes]
+    ins = [each(x), each(prob)] + [pl.BlockSpec(memory_space=pl.ANY)] * 2
+    outs = [each(s) for s in shapes]
     scratch = [
-        pltpu.VMEM((2, PAIR, 2 * hidden, width), jnp.bfloat16),
-        pltpu.SemaphoreType.DMA((2, 2 * PAIR)),
+        pltpu.VMEM((2, 2 * hidden, width), jnp.bfloat16),
+        pltpu.SemaphoreType.DMA((2, 2)),
     ]
     flops = 4 * experts * rows * hidden * width
-    return call(up_kernel, experts // PAIR, ins, args, outs, shapes, scratch, flops)
+    return call(up_kernel, experts, ins, args, outs, shapes, scratch, flops)
 
 
 def place_call(pieces, pick, experts):
     _, rows, count = pick.shape
     size, width = pieces[0].shape
-    shape = pltpu.HBM((experts, 2 * rows // experts, width), jnp.bfloat16)
+    shape = (experts, 2 * rows // experts, width)
+    shapes = [pltpu.VMEM(shape, jnp.bfloat16), pltpu.HBM(shape, jnp.bfloat16)]
     ins = [pl.BlockSpec((size, WIDE), lambda i: (0, i))] * len(pieces) + [whole(pick)]
-    outs = [pl.BlockSpec((*shape.shape[:2], WIDE), lambda i: (0, 0, i))]
+    outs = [pl.BlockSpec((*shape[:2], WIDE), lambda i: (0, 0, i))] * 2
     flops = 4 * rows * count * width
-    return call(place_kernel, width // WIDE, ins, (*pieces, pick), outs, [shape], flops=flops)[0]
+    return call(place_kernel, width // WIDE, ins, (*pieces, pick), outs, shapes, flops=flops)
 
 
 def slope_call(x, put, prob, mine, w_down, g, u):
     experts, hidden, width = w_down.shape
     rows, count, columns = x.shape[1], put.shape[1], mine.shape[2]
-    args = (in_hbm(x), put, prob, mine, in_hbm(w_down), g, u)
+    args = (near_core(x), put, prob, mine, in_hbm(w_down), g, u)
     shapes = [
         bf16(experts, rows, hidden),
         bf16(experts, rows, hidden),
-        bf16(experts, 2 * hidden, rows),
+        bf16(experts, hidden, rows),
+        bf16(experts, hidden, rows),
         bf16(2, count, columns),
     ]
     ins = [each(x, PAIR), whole(put), each(prob, PAIR), whole(mine)]
     ins += [each(a, PAIR) for a in (w_down, g, u)]
-    outs = [each(s, PAIR) for s in shapes[:3]] + [kept(shapes[3])]
+    outs = [each(s, PAIR) for s in shapes[:4]] + [kept(shapes[4])]
     scratch = [
         pltpu.VMEM((experts, rows), jnp.float32),
         pltpu.VMEM((put.shape[2], columns), jnp.bfloat16),
@@ -384,16 +368,17 @@
     args = (put, *lefts, *rights) + (() if extra is None else (extra,))
     shapes = [bf16(count, columns)] * 2
     ins = [whole(put)] + [whole(a) for a in lefts]
-    ins += [pl.BlockSpec(memory_space=pl.ANY)] * terms
+    first, last = start // CHUNK, stop // CHUNK - 1
+    ins += [
+        pl.BlockSpec((experts, hidden, CHUNK), lambda i: (0, 0, jnp.minimum(first + i, last)))
+    ] * terms
     ins += [] if extra is None else [whole(extra)]
     outs = [pl.BlockSpec((count, CHUNK), lambda i: (0, i))] * 2
     scratch = [
         pltpu.VMEM((2, put.shape[2], CHUNK), jnp.bfloat16),
-        pltpu.VMEM((terms, steps, experts, hidden, CHUNK), jnp.bfloat16),
-        pltpu.SemaphoreType.DMA((terms, steps)),
     ]
     flops = 2 * experts * rows * (stop - start) * (hidden * terms + count)
-    kernel = functools.partial(back_kernel, terms, start, steps)
+    kernel = functools.partial(back_kernel, terms, steps)
     grid = steps + (0 if extra is None else 1)
     return call(kernel, grid, ins, args, outs, shapes, scratch, flops)
 
@@ -403,14 +388,14 @@
     shapes = [bf16(experts, hidden, width)] * (left.shape[1] // hidden)
     flops = 2 * experts * rows * left.shape[1] * width
     ins, outs = [each(x), each(left)], [each(s) for s in shapes]
-    return call(grad_kernel, experts, ins, (in_hbm(x), left), outs, shapes, flops=flops)
+    return call(grad_kernel, experts, ins, (x, left), outs, shapes, flops=flops)
 
 
 def dense_body(
     tokens, cotangent, gate_prob, expert_ids, placement, gate_weight, up_weight, down_weight
 ):
     tok_count, width = tokens.shape
-    local = gate_weight.shape[0]
+    local, hidden, _ = gate_weight.shape
     total_experts = placement.shape[0]
     devices = lax.axis_size("dp") * lax.axis_size("expert")
     places = devices // 2 * CAP
@@ -439,7 +424,7 @@
     near_parts, far_parts = swap(parts, Z1), swap(parts, Z2)
     zero = wide(tokens, parts)
     first0 = swap(zero, X, Y)
-    near, far, near_parts, far_parts = together(near, far, near_parts, far_parts)
+    near, far = together(near, far)
 
     last, last_parts = swap(far, Z1), swap(far_parts, Z1)
     middle_rows = wide(rows_of(near, far), rows_of(near_parts, far_parts))
@@ -451,7 +436,7 @@
     last, last_parts, first1, second0, gate_weight = together(
         last, last_parts, first1, second0, gate_weight
     )
-    gate_weight, mark = fetch_call(gate_weight, last_parts)
+    gate_weight, mark = fetch_call(gate_weight, gate_prob)
 
     last = wide(last, last_parts)
     first2 = swap(last, X, Y)
@@ -466,13 +451,13 @@
 
     last = rows_of(last, first2)
     second2 = swap(last, Y, X)
+    second2, mark = together(second2, mark)
     middle_rows = rows_of(middle_rows, second1)
     middle_other = swap(middle_rows, CORE)
     grads = rows_of(cotangent, *grads)
     grads = rows_of(grads, swap(grads, X, Y))
     last = rows_of(last, second2)
     last_other = swap(last, CORE)
-    last, last_other, mark = together(last, last_other, mark)
     x, put, pick, prob_rows = route_call(
         (zero, middle_rows, last),
         (zero_other, middle_other, last_other),
@@ -493,7 +478,7 @@
     mixed_other, far_grads_other = together(mixed_other, far_grads_other)
     mixed = [mixed, swap(mixed_other, CORE)]
 
-    c = place_call((grads, far_grads, grads_other, far_grads_other), pick, local)
+    near_c, c = place_call((grads, far_grads, grads_other, far_grads_other), pick, local)
 
     def leaving(parts, start, stop):
         return add(*(part[start:stop] for part in parts))
@@ -511,10 +496,11 @@
         return parts + [swap(leaving(parts, tok_count, 2 * tok_count), Z1)]
 
     weights = [near_core(gate_weight), near_core(up_weight)]
-    mixed[1], c = together(mixed[1], c)
-    mixed = by_second(mixed)
-    dg, du, dt, share = slope_call(
-        c, put, prob_rows, mine.reshape(local, places, -1), down_weight, g, u
+    mixed[1], far_c = together(mixed[1], c)
+    rows, g = together(leaving(mixed, 2 * quarter, 4 * quarter), g)
+    mixed.append(swap(rows, Y, X))
+    dg, du, dgt, dut, share = slope_call(
+        near_c, put, prob_rows, mine.reshape(local, places, -1), down_weight, g, u
     )
     left, left_other = back_call(put, [dg, du], weights, 0, middle)
     left = [left, swap(left_other, CORE)]
@@ -524,26 +510,39 @@
     right = [right, swap(right_other, CORE)]
 
     right[0], left[1], mixed[3] = together(right[0], left[1], mixed[3])
-    left, mixed = by_second(left), by_far(mixed)
-    left[0], ht = together(left[0], ht)
-    (down_weight_grad,) = grad_call(c, ht, ht.shape[1])
-
-    right[1], left[2], mixed[4], down_weight_grad = together(
-        right[1], left[2], mixed[4], down_weight_grad
-    )
-    right, left, mixed = by_second(right), by_first(left), by_near(mixed)
-    right[0], dt = together(right[0], dt)
-    gate_weight_grad, up_weight_grad = grad_call(x, dt, ht.shape[1])
-
-    right[2], left[3], mixed[5], gate_weight_grad = together(
-        right[2], left[3], mixed[5], gate_weight_grad
-    )
-    right, left = by_first(right), by_far(left)
-    right, left = by_far(right), by_near(left)
-    right = by_near(right)
-    mixed, left, right = (leaving(parts, 0, tok_count) for parts in (mixed, left, right))
-    token_grad = jnp.concatenate([left, right[:, : width - middle]], axis=1)
-    share = right[:, width - middle : width - middle + total_experts].astype(jnp.float32)
+    rows, ht = together(leaving(left, 2 * quarter, 4 * quarter), ht)
+    left.append(swap(rows, Y, X))
+    mixed = by_far(mixed)
+    (down_weight_grad,) = grad_call(far_c, ht, hidden)
+
+    right[1], mixed[4], down_weight_grad = together(right[1], mixed[4], down_weight_grad)
+    rows, dgt = together(leaving(right, 2 * quarter, 4 * quarter), dgt)
+    right.append(swap(rows, Y, X))
+    mixed = by_near(mixed)
+    (gate_weight_grad,) = grad_call(x, dgt, hidden)
+
+    def joined(parts, start, stop):
+        halves = [
+            sum(part[start:stop].astype(jnp.float32) for part in half) for half in (left, right)
+        ]
+        total = jnp.concatenate(halves, axis=1)
+        return sum((part[start:stop].astype(jnp.float32) for part in parts), total)
+
+    def sent(parts, start, stop):
+        return joined(parts, start, stop).astype(jnp.bfloat16)
+
+    right[2], left[2], gate_weight_grad = together(right[2], left[2], gate_weight_grad)
+    rows, dut = together(sent([], quarter, 2 * quarter), dut)
+    parts = [swap(rows, X, Y)]
+    (up_weight_grad,) = grad_call(x, dut, hidden)
+
+    parts[0], mixed[5], up_weight_grad = together(parts[0], mixed[5], up_weight_grad)
+    parts.append(swap(sent(parts, 2 * tok_count, 4 * tok_count), Z2))
+    mixed = leaving(mixed, 0, tok_count)
+    parts.append(swap(sent(parts, tok_count, 2 * tok_count), Z1))
+    total = sent(parts, 0, tok_count)
+    token_grad = total[:, :width]
+    share = total[:, width : width + total_experts].astype(jnp.float32)
     gate_grad = jnp.sum(jnp.where(used, share[:, None, :], 0.0), axis=2)
     return (mixed, token_grad, gate_grad, gate_weight_grad, up_weight_grad, down_weight_grad)
 

time: 168 us -> 164 us (0.976)
  waiting for transfers between devices: 36.7 us -> 45.9 us
  starting transfers between devices: 36.6 us -> 28.9 us
  Pallas kernels: 84.2 us -> 79.3 us
    ppermute x37 -> x34, waiting for transfers between devices: 36.7 us -> 45.9 us  [swap(): return lax.ppermute(values, AXES, pairs)]
    ppermute x37 -> x34, starting transfers between devices: 36.6 us -> 28.9 us  [swap(): return lax.ppermute(values, AXES, pairs)]
    pallas_call x9 -> x10, Pallas kernels: 75 us -> 70.1 us  [call(): pl.pallas_call(kernel, grid=(grid,), in_specs=ins, out_specs=outs, out_sh...]
  transfers between devices with their start and end apart: 37 -> 34, of which waited for: 12 -> 16; matrix products, arithmetic and copies ran while one was open for 2% -> 2% of each run, Pallas kernels for 47% -> 46%
where the time goes in v7:
time: 164 us
  Pallas kernels  79.3 us (48%)
  waiting for transfers between devices  45.9 us (28%)
  starting transfers between devices  28.9 us (18%)
  other arithmetic  4.43 us (3%)
  local copies, waits for them, and re-layouts  4.03 us (2%)
    pallas_call x10, Pallas kernels, call(): pl.pallas_call(kernel, grid=(grid,), in_specs=ins, out_specs=outs, out_sh...  70.1 us
    ppermute x34, waiting for transfers between devices, swap(): return lax.ppermute(values, AXES, pairs)  45.9 us
    ppermute x34, starting transfers between devices, swap(): return lax.ppermute(values, AXES, pairs)  28.9 us
    pallas_call x2, Pallas kernels, fetch_call(): pl.pallas_call(fetch_kernel, in_specs=[pl.BlockSpec(memory_space=pl.ANY)]...  9.17 us
  transfers between devices with their start and end apart: 34, of which 16 were waited for; matrix products, arithmetic and copies ran while one was open for 2% of the time, Pallas kernels for 46%

profile of v7, /device:TPU:0, one launch (start us, length us, event | category | flops | bytes accessed | tf_op | source)
XLA Modules:
  0.0 163.6 jit_solution(17727721040581099814)
XLA Ops:
  3.5 3.0 %collective-permute-start.6 = (bf16[16,128]{1,0:T(8,128)(2,1)S(1)}, bf16[16,128]{1,0:T(8,128)(2,1)S(1)}, u32[]{:S(2)}, u32[]{:S(2)}) collective-permute-start(bf16[16,128]{1,0:T(8,128)(2,1)S(1)} %pad_maximum_fusion.8), channel_id=1, source_target_pairs={{0,2},{1,3},{2,0},{3,1},{4,6},{5,7},{6,4},{7,5},{8,10},{9,11},{10,... | collective-permute-start | bytes 12296 | tf_op jit(solution)/shard_map/ppermute | solution.py:33
  6.5 2.6 %collective-permute-start.4 = (bf16[16,128]{1,0:T(8,128)(2,1)S(1)}, bf16[16,128]{1,0:T(8,128)(2,1)S(1)}, u32[]{:S(2)}, u32[]{:S(2)}) collective-permute-start(bf16[16,128]{1,0:T(8,128)(2,1)S(1)} %pad_maximum_fusion.8), channel_id=1, source_target_pairs={{0,4},{1,5},{2,6},{3,7},{4,0},{5,1},{6,2},{7,3},{8,12},{9,13},{10,... | collective-permute-start | bytes 12296 | tf_op jit(solution)/shard_map/ppermute | solution.py:33
  10.6 1.8 %collective-permute-start = (bf16[16,4224]{1,0:T(8,128)(2,1)S(1)}, bf16[16,4224]{1,0:T(8,128)(2,1)S(1)}, u32[]{:S(2)}, u32[]{:S(2)}) collective-permute-start(bf16[16,4224]{1,0:T(8,128)(2,1)S(1)} %concatenate.60), channel_id=1, source_target_pairs={{0,8},{1,17},{2,10},{3,19},{4,12},{5,21},{6,14},{7,23},{8,0},{9,25... | collective-permute-start | bytes 405512 | tf_op jit(solution)/shard_map/ppermute | solution.py:33
  12.4 5.2 %collective-permute-done.2 = bf16[16,4096]{1,0:T(8,128)(2,1)S(1)} collective-permute-done((bf16[16,4096]{1,0:T(8,128)(2,1)}, bf16[16,4096]{1,0:T(8,128)(2,1)S(1)}, u32[]{:S(2)}, u32[]{:S(2)}) %collective-permute-start.2) | collective-permute-done | bytes 131104 | tf_op jit(solution)/shard_map/ppermute | solution.py:33
  17.6 1.6 collective-permute-start.7
  19.2 1.6 collective-permute-start.8
  21.0 2.0 %collective-permute-start.3 = (bf16[16,4096]{1,0:T(8,128)(2,1)S(1)}, bf16[16,4096]{1,0:T(8,128)(2,1)S(1)}, u32[]{:S(2)}, u32[]{:S(2)}) collective-permute-start(bf16[16,4096]{1,0:T(8,128)(2,1)S(1)} %collective-permute-done.2), channel_id=1, source_target_pairs={{0,2},{1,3},{2,0},{3,1},{4,6},{5,7},{6,4},{7,5},{8,10},{9,11},{10,... | collective-permute-start | bytes 393224 | tf_op jit(solution)/shard_map/ppermute | solution.py:33
  23.1 1.5 collective-permute-done.5
  26.9 2.5 %collective-permute-start.15 = (bf16[16,4096]{1,0:T(8,128)(2,1)S(1)}, bf16[16,4096]{1,0:T(8,128)(2,1)S(1)}, u32[]{:S(2)}, u32[]{:S(2)}) collective-permute-start(bf16[16,4096]{1,0:T(8,128)(2,1)S(1)} %copy-done.1), channel_id=1, source_target_pairs={{0,2},{1,3},{2,0},{3,1},{4,6},{5,7},{6,4},{7,5},{8,10},{9,11},{10,... | collective-permute-start | bytes 393224 | tf_op jit(solution)/shard_map/ppermute | solution.py:33
  30.7 4.6 %shard_map.127 = (bf16[8,192,4096]{2,1,0:T(8,128)(2,1)S(1)}, f32[8,128]{1,0:T(8,128)S(1)}) custom-call(bf16[8,192,4096]{2,1,0:T(8,128)(2,1)} %source, f32[16,8]{1,0:T(8,128)S(1)} %copy.18.after), custom_call_target="tpu_custom_call" | custom-call | bytes 12582912 | tf_op jit(solution)/shard_map/pallas_call | solution.py:274
  36.0 3.5 %collective-permute-done.10 = bf16[64,4224]{1,0:T(8,128)(2,1)S(1)} collective-permute-done((bf16[64,4224]{1,0:T(8,128)(2,1)S(1)}, bf16[64,4224]{1,0:T(8,128)(2,1)S(1)}, u32[]{:S(2)}, u32[]{:S(2)}) %collective-permute-start.10) | collective-permute-done | bytes 540704 | tf_op jit(solution)/shard_map/ppermute | solution.py:33
  40.2 1.5 collective-permute-start.18
  41.9 4.6 %shard_map.128 = (bf16[8,192,4096]{2,1,0:T(8,128)(2,1)S(1)}, f32[8,128]{1,0:T(8,128)S(1)}) custom-call(bf16[8,192,4096]{2,1,0:T(8,128)(2,1)} %source.1, f32[8,128]{1,0:T(8,128)S(1)} %get-tuple-element.93.after), custom_call_target="tpu_custom_call" | custom-call | bytes 12582912 | tf_op jit(solution)/shard_map/pallas_call | solution.py:274
  46.6 2.4 %collective-permute-done.11 = bf16[32,4224]{1,0:T(8,128)(2,1)S(1)} collective-permute-done((bf16[32,4224]{1,0:T(8,128)(2,1)S(1)}, bf16[32,4224]{1,0:T(8,128)(2,1)S(1)}, u32[]{:S(2)}, u32[]{:S(2)}) %collective-permute-start.11) | collective-permute-done | bytes 270368 | tf_op jit(solution)/shard_map/ppermute | solution.py:33
  49.5 1.6 collective-permute-done.14.refs_5_.refs_11_
  51.1 4.8 %shard_map.129 = (bf16[8,96,4096]{2,1,0:T(8,128)(2,1)S(1)}, bf16[2,256,384]{2,1,0:T(8,128)(2,1)S(1)}, bf16[2,384,256]{2,1,0:T(8,128)(2,1)S(1)}, f32[8,1,96]{2,1,0:T(1,128)S(1)}) custom-call(bf16[64,4224]{1,0:T(8,128)(2,1)S(1)} %pad_maximum_fusion.1.refs_0_.refs_6_, bf16[128,4224]{1,0:T(8,128)(2,1)S(1)} %pad_maximum_fusion.refs_1_.refs_7_, ...), custom_call_target="tpu_custom_call" | custom-call | flops 1610612736 | bytes 16030720 | tf_op jit(solution)/shard_map/pallas_call | solution.py:254
  56.6 10.3 %shard_map.130 = (f32[8,192,96]{2,1,0:T(8,128)S(1)}, f32[8,192,96]{2,1,0:T(8,128)S(1)}, bf16[8,96,192]{2,1,0:T(8,128)(2,1)S(1)}, bf16[8,192,96]{2,1,0:T(8,128)(2,1)S(1)}) custom-call(bf16[8,96,4096]{2,1,0:T(8,128)(2,1)S(1)} %get-tuple-element.100.x_ref, f32[8,1,96]{2,1,0:T(1,128)S(1)} %get-tuple-element.101.prob_ref, ...), custom_call_target="tpu_custom_call" | custom-call | flops 2415919104 | bytes 33229824 | tf_op jit(solution)/shard_map/pallas_call | solution.py:254
  66.9 4.0 %collective-permute-done.19.own1 = bf16[128,4096]{1,0:T(8,128)(2,1)S(1)} collective-permute-done((bf16[128,4096]{1,0:T(8,128)(2,1)S(1)}, bf16[128,4096]{1,0:T(8,128)(2,1)S(1)}, u32[]{:S(2)}, u32[]{:S(2)}) %collective-permute-start.19) | collective-permute-done | bytes 1048608 | tf_op jit(solution)/shard_map/ppermute | solution.py:33
  70.9 9.8 %shard_map.131 = (bf16[256,4096]{1,0:T(8,128)(2,1)S(1)}, bf16[256,4096]{1,0:T(8,128)(2,1)S(1)}) custom-call(bf16[2,256,384]{2,1,0:T(8,128)(2,1)S(1)} %get-tuple-element.97.put_ref, bf16[8,96,192]{2,1,0:T(8,128)(2,1)S(1)} %get-tuple-element.106.refs_0_, bf16[8,192,4096]{2,1,0:T(8,128)(2,1)} %down_ref.1), custom_call_target="tpu_custom_call" | custom-call | flops 2818572288 | bytes 17465344 | tf_op jit(solution)/shard_map/pallas_call | solution.py:254
  81.3 4.6 %shard_map.132 = (bf16[8,96,4096]{2,1,0:T(8,128)(2,1)S(1)}, bf16[8,96,4096]{2,1,0:T(8,128)(2,1)}) custom-call(bf16[128,4096]{1,0:T(8,128)(2,1)S(1)} %constant_dynamic-update-slice_fusion.2.own0, bf16[128,4096]{1,0:T(8,128)(2,1)S(1)} %collective-permute-done.19.own1, bf16[128,4096]{1,0:T(8,128)(2,1)S(1)} %collective-permute-done.20.other0, ...), custom_call_target="tpu_custom_call" | custom-call | flops 1610612736 | bytes 17170432 | tf_op jit(solution)/shard_map/pallas_call | solution.py:254
  86.8 8.5 %shard_map.133 = (bf16[8,96,192]{2,1,0:T(8,128)(2,1)S(1)}, bf16[8,96,192]{2,1,0:T(8,128)(2,1)S(1)}, bf16[8,192,96]{2,1,0:T(8,128)(2,1)S(1)}, bf16[8,192,96]{2,1,0:T(8,128)(2,1)S(1)}, bf16[2,256,128]{2,1,0:T(8,128)(2,1)S(1)}) custom-call(bf16[8,96,4096]{2,1,0:T(8,128)(2,1)S(1)} %get-tuple-element.116.x_ref, ...), custom_call_target="tpu_custom_call" | custom-call | flops 1207959552 | bytes 21859328 | tf_op jit(solution)/shard_map/pallas_call | solution.py:254
  95.3 4.8 %shard_map.134 = (bf16[256,2048]{1,0:T(8,128)(2,1)S(1)}, bf16[256,2048]{1,0:T(8,128)(2,1)S(1)}) custom-call(bf16[2,256,384]{2,1,0:T(8,128)(2,1)S(1)} %get-tuple-element.97.put_ref, bf16[8,96,192]{2,1,0:T(8,128)(2,1)S(1)} %get-tuple-element.125.refs_0_, bf16[8,96,192]{2,1,0:T(8,128)(2,1)S(1)} %get-tuple-element.126.refs_1_, ...), custom_call_target="tpu_custom_call" | custom-call | flops 2013265920 | bytes 28246016 | tf_op jit(solution)/shard_map/pallas_call | solution.py:254
  101.2 1.4 collective-permute-start.25
  102.6 5.1 %shard_map.135 = (bf16[256,2176]{1,0:T(8,128)(2,1)S(1)}, bf16[256,2176]{1,0:T(8,128)(2,1)S(1)}) custom-call(bf16[2,256,384]{2,1,0:T(8,128)(2,1)S(1)} %get-tuple-element.97.put_ref, bf16[8,96,192]{2,1,0:T(8,128)(2,1)S(1)} %get-tuple-element.125.refs_0_, bf16[8,96,192]{2,1,0:T(8,128)(2,1)S(1)} %get-tuple-element.126.refs_1_, ...), custom_call_target="tpu_custom_call" | custom-call | flops 2013265920 | bytes 28508160 | tf_op jit(solution)/shard_map/pallas_call | solution.py:254
  107.9 2.6 %collective-permute-done.25 = bf16[64,4096]{1,0:T(8,128)(2,1)S(1)} collective-permute-done((bf16[64,4096]{1,0:T(8,128)(2,1)S(1)}, bf16[64,4096]{1,0:T(8,128)(2,1)S(1)}, u32[]{:S(2)}, u32[]{:S(2)}) %collective-permute-start.25) | collective-permute-done | bytes 524320 | tf_op jit(solution)/shard_map/ppermute | solution.py:33
  111.7 7.4 %shard_map.136 = bf16[8,192,4096]{2,1,0:T(8,128)(2,1)} custom-call(bf16[8,96,4096]{2,1,0:T(8,128)(2,1)S(1)} %bitcast.3, bf16[8,192,96]{2,1,0:T(8,128)(2,1)S(1)} %get-tuple-element.136.left), custom_call_target="tpu_custom_call" | custom-call | flops 1207959552 | bytes 19169280 | tf_op jit(solution)/shard_map/pallas_call | solution.py:254
  119.1 4.6 %collective-permute-done.27 = bf16[32,4096]{1,0:T(8,128)(2,1)S(1)} collective-permute-done((bf16[32,4096]{1,0:T(8,128)(2,1)S(1)}, bf16[32,4096]{1,0:T(8,128)(2,1)S(1)}, u32[]{:S(2)}, u32[]{:S(2)}) %collective-permute-start.27) | collective-permute-done | bytes 262176 | tf_op jit(solution)/shard_map/ppermute | solution.py:33
  125.1 7.4 %shard_map.137 = bf16[8,192,4096]{2,1,0:T(8,128)(2,1)} custom-call(bf16[8,96,4096]{2,1,0:T(8,128)(2,1)S(1)} %bitcast.1, bf16[8,192,96]{2,1,0:T(8,128)(2,1)S(1)} %get-tuple-element.143.left), custom_call_target="tpu_custom_call" | custom-call | flops 1207959552 | bytes 19169280 | tf_op jit(solution)/shard_map/pallas_call | solution.py:254
  133.8 1.6 collective-permute-start.30
  135.4 7.4 %shard_map.138 = bf16[8,192,4096]{2,1,0:T(8,128)(2,1)} custom-call(bf16[8,96,4096]{2,1,0:T(8,128)(2,1)S(1)} %bitcast.1, bf16[8,192,96]{2,1,0:T(8,128)(2,1)S(1)} %get-tuple-element.148.left), custom_call_target="tpu_custom_call" | custom-call | flops 1207959552 | bytes 19169280 | tf_op jit(solution)/shard_map/pallas_call | solution.py:254
  143.9 13.0 %collective-permute-done.32 = bf16[32,4224]{1,0:T(8,128)(2,1)S(1)} collective-permute-done((bf16[32,4224]{1,0:T(8,128)(2,1)S(1)}, bf16[32,4224]{1,0:T(8,128)(2,1)S(1)}, u32[]{:S(2)}, u32[]{:S(2)}) %collective-permute-start.32) | collective-permute-done | bytes 270368 | tf_op jit(solution)/shard_map/ppermute | solution.py:33
  157.8 4.2 %collective-permute-done.33 = bf16[16,4224]{1,0:T(8,128)(2,1)S(1)} collective-permute-done((bf16[16,4224]{1,0:T(8,128)(2,1)S(1)}, bf16[16,4224]{1,0:T(8,128)(2,1)S(1)}, u32[]{:S(2)}, u32[]{:S(2)}) %collective-permute-start.33) | collective-permute-done | bytes 135200 | tf_op jit(solution)/shard_map/ppermute | solution.py:33
  (111 shorter events, 21.1 us)
Async XLA Ops:
  3.5 14.1 %collective-permute-start.6 = (bf16[16,128]{1,0:T(8,128)(2,1)S(1)}, bf16[16,128]{1,0:T(8,128)(2,1)S(1)}, u32[]{:S(2)}, u32[]{:S(2)}) collective-permute-start(bf16[16,128]{1,0:T(8,128)(2,1)S(1)} %pad_maximum_fusion.8), channel_id=1, source_target_pairs={{0,2},{1,3},{2,0},{3,1},{4,6},{5,7},{6,4},{7,5},{8,10},{9,11},{10,... | collective-permute-start | bytes 12296 | tf_op jit(solution)/shard_map/ppermute | solution.py:33
  6.5 11.1 %collective-permute-start.4 = (bf16[16,128]{1,0:T(8,128)(2,1)S(1)}, bf16[16,128]{1,0:T(8,128)(2,1)S(1)}, u32[]{:S(2)}, u32[]{:S(2)}) collective-permute-start(bf16[16,128]{1,0:T(8,128)(2,1)S(1)} %pad_maximum_fusion.8), channel_id=1, source_target_pairs={{0,4},{1,5},{2,6},{3,7},{4,0},{5,1},{6,2},{7,3},{8,12},{9,13},{10,... | collective-permute-start | bytes 12296 | tf_op jit(solution)/shard_map/ppermute | solution.py:33
  9.1 8.5 %collective-permute-start.2 = (bf16[16,4096]{1,0:T(8,128)(2,1)}, bf16[16,4096]{1,0:T(8,128)(2,1)S(1)}, u32[]{:S(2)}, u32[]{:S(2)}) collective-permute-start(bf16[16,4096]{1,0:T(8,128)(2,1)} %param.8), channel_id=1, source_target_pairs={{0,4},{1,5},{2,6},{3,7},{4,0},{5,1},{6,2},{7,3},{8,12},{9,13},{10,... | collective-permute-start | bytes 393224 | tf_op jit(solution)/shard_map/ppermute | solution.py:33
  9.4 8.1 %collective-permute-start.1 = (bf16[16,4096]{1,0:T(8,128)(2,1)}, bf16[16,4096]{1,0:T(8,128)(2,1)S(1)}, u32[]{:S(2)}, u32[]{:S(2)}) collective-permute-start(bf16[16,4096]{1,0:T(8,128)(2,1)} %param.8), channel_id=1, source_target_pairs={{0,2},{1,3},{2,0},{3,1},{4,6},{5,7},{6,4},{7,5},{8,10},{9,11},{10,... | collective-permute-start | bytes 393224 | tf_op jit(solution)/shard_map/ppermute | solution.py:33
  10.6 8.6 %collective-permute-start = (bf16[16,4224]{1,0:T(8,128)(2,1)S(1)}, bf16[16,4224]{1,0:T(8,128)(2,1)S(1)}, u32[]{:S(2)}, u32[]{:S(2)}) collective-permute-start(bf16[16,4224]{1,0:T(8,128)(2,1)S(1)} %concatenate.60), channel_id=1, source_target_pairs={{0,8},{1,17},{2,10},{3,19},{4,12},{5,21},{6,14},{7,23},{8,0},{9,25... | collective-permute-start | bytes 405512 | tf_op jit(solution)/shard_map/ppermute | solution.py:33
  17.6 11.8 %collective-permute-start.7 = (bf16[32,4224]{1,0:T(8,128)(2,1)S(1)}, bf16[32,4224]{1,0:T(8,128)(2,1)S(1)}, u32[]{:S(2)}, u32[]{:S(2)}) collective-permute-start(bf16[32,4224]{1,0:T(8,128)(2,1)S(1)} %maximum_maximum_fusion), channel_id=1, source_target_pairs={{0,8},{1,17},{2,10},{3,19},{4,12},{5,21},{6,14},{7,23},{8,0},{9,25... | collective-permute-start | bytes 811016 | tf_op jit(solution)/shard_map/ppermute | solution.py:33
  19.2 10.2 %collective-permute-start.8 = (bf16[32,4224]{1,0:T(8,128)(2,1)S(1)}, bf16[32,4224]{1,0:T(8,128)(2,1)S(1)}, u32[]{:S(2)}, u32[]{:S(2)}) collective-permute-start(bf16[32,4224]{1,0:T(8,128)(2,1)S(1)} %pad_maximum_fusion.6), channel_id=1, source_target_pairs={{0,16},{1,9},{2,18},{3,11},{4,20},{5,13},{6,22},{7,15},{8,24},{9,1... | collective-permute-start | bytes 811016 | tf_op jit(solution)/shard_map/ppermute | solution.py:33
  21.0 6.0 %collective-permute-start.3 = (bf16[16,4096]{1,0:T(8,128)(2,1)S(1)}, bf16[16,4096]{1,0:T(8,128)(2,1)S(1)}, u32[]{:S(2)}, u32[]{:S(2)}) collective-permute-start(bf16[16,4096]{1,0:T(8,128)(2,1)S(1)} %collective-permute-done.2), channel_id=1, source_target_pairs={{0,2},{1,3},{2,0},{3,1},{4,6},{5,7},{6,4},{7,5},{8,10},{9,11},{10,... | collective-permute-start | bytes 393224 | tf_op jit(solution)/shard_map/ppermute | solution.py:33
  24.6 15.6 %collective-permute-start.17 = (bf16[16,4096]{1,0:T(8,128)(2,1)S(1)}, bf16[16,4096]{1,0:T(8,128)(2,1)S(1)}, u32[]{:S(2)}, u32[]{:S(2)}) collective-permute-start(bf16[16,4096]{1,0:T(8,128)(2,1)S(1)} %copy-done.1), channel_id=1, source_target_pairs={{0,6},{1,7},{2,4},{3,5},{4,2},{5,3},{6,0},{7,1},{8,14},{9,15},{10,... | collective-permute-start | bytes 393224 | tf_op jit(solution)/shard_map/ppermute | solution.py:33
  25.4 14.8 %collective-permute-start.16 = (bf16[16,4096]{1,0:T(8,128)(2,1)S(1)}, bf16[16,4096]{1,0:T(8,128)(2,1)S(1)}, u32[]{:S(2)}, u32[]{:S(2)}) collective-permute-start(bf16[16,4096]{1,0:T(8,128)(2,1)S(1)} %copy-done.1), channel_id=1, source_target_pairs={{0,4},{1,5},{2,6},{3,7},{4,0},{5,1},{6,2},{7,3},{8,12},{9,13},{10,... | collective-permute-start | bytes 393224 | tf_op jit(solution)/shard_map/ppermute | solution.py:33
  26.9 13.2 %collective-permute-start.15 = (bf16[16,4096]{1,0:T(8,128)(2,1)S(1)}, bf16[16,4096]{1,0:T(8,128)(2,1)S(1)}, u32[]{:S(2)}, u32[]{:S(2)}) collective-permute-start(bf16[16,4096]{1,0:T(8,128)(2,1)S(1)} %copy-done.1), channel_id=1, source_target_pairs={{0,2},{1,3},{2,0},{3,1},{4,6},{5,7},{6,4},{7,5},{8,10},{9,11},{10,... | collective-permute-start | bytes 393224 | tf_op jit(solution)/shard_map/ppermute | solution.py:33
  29.4 6.6 %collective-permute-start.9 = (bf16[16,4224]{1,0:T(8,128)(2,1)S(1)}, bf16[16,4224]{1,0:T(8,128)(2,1)S(1)}, u32[]{:S(2)}, u32[]{:S(2)}) collective-permute-start(bf16[16,4224]{1,0:T(8,128)(2,1)S(1)} %constant_dynamic-update-slice_fusion), channel_id=1, source_target_pairs={{0,8},{1,17},{2,10},{3,19},{4,12},{5,21},{6,14},{7,23},{8,0},{9,25... | collective-permute-start | bytes 405512 | tf_op jit(solution)/shard_map/ppermute | solution.py:33
  30.1 9.4 %collective-permute-start.10 = (bf16[64,4224]{1,0:T(8,128)(2,1)S(1)}, bf16[64,4224]{1,0:T(8,128)(2,1)S(1)}, u32[]{:S(2)}, u32[]{:S(2)}) collective-permute-start(bf16[64,4224]{1,0:T(8,128)(2,1)S(1)} %pad_maximum_fusion.2), channel_id=1, source_target_pairs={{0,16},{1,9},{2,18},{3,11},{4,20},{5,13},{6,22},{7,15},{8,24},{9,1... | collective-permute-start | bytes 1622024 | tf_op jit(solution)/shard_map/ppermute | solution.py:33
  36.0 13.5 %collective-permute-start.12 = (bf16[64,4224]{1,0:T(8,128)(2,1)S(1)}, bf16[64,4224]{1,0:T(8,128)(2,1)S(1)}, u32[]{:S(2)}, u32[]{:S(2)}) collective-permute-start(bf16[64,4224]{1,0:T(8,128)(2,1)S(1)} %pad_maximum_fusion.1.refs_0_.refs_6_), channel_id=1, source_target_pairs={{0,1},{1,0},{2,3},{3,2},{4,5},{5,4},{6,7},{7,6},{8,9},{9,8},{10,11... | collective-permute-start | bytes 1622024 | tf_op jit(solution)/shard_map/ppermute | solution.py:33
  39.5 9.5 %collective-permute-start.11 = (bf16[32,4224]{1,0:T(8,128)(2,1)S(1)}, bf16[32,4224]{1,0:T(8,128)(2,1)S(1)}, u32[]{:S(2)}, u32[]{:S(2)}) collective-permute-start(bf16[32,4224]{1,0:T(8,128)(2,1)S(1)} %pad_maximum_fusion.7), channel_id=1, source_target_pairs={{0,16},{1,9},{2,18},{3,11},{4,20},{5,13},{6,22},{7,15},{8,24},{9,1... | collective-permute-start | bytes 811016 | tf_op jit(solution)/shard_map/ppermute | solution.py:33
  40.2 9.2 %collective-permute-start.18 = (bf16[64,4096]{1,0:T(8,128)(2,1)S(1)}, bf16[64,4096]{1,0:T(8,128)(2,1)S(1)}, u32[]{:S(2)}, u32[]{:S(2)}) collective-permute-start(bf16[64,4096]{1,0:T(8,128)(2,1)S(1)} %pad_maximum_fusion.5), channel_id=1, source_target_pairs={{0,8},{1,17},{2,10},{3,19},{4,12},{5,21},{6,14},{7,23},{8,0},{9,25... | collective-permute-start | bytes 1572872 | tf_op jit(solution)/shard_map/ppermute | solution.py:33
  41.9 9.2 %collective-permute-start.13 = (bf16[128,4224]{1,0:T(8,128)(2,1)S(1)}, bf16[128,4224]{1,0:T(8,128)(2,1)S(1)}, u32[]{:S(2)}, u32[]{:S(2)}) collective-permute-start(bf16[128,4224]{1,0:T(8,128)(2,1)S(1)} %pad_maximum_fusion.refs_1_.refs_7_), channel_id=1, source_target_pairs={{0,1},{1,0},{2,3},{3,2},{4,5},{5,4},{6,7},{7,6},{8,9},{9,8},{10,11... | collective-permute-start | bytes 3244040 | tf_op jit(solution)/shard_map/ppermute | solution.py:33
  55.9 11.0 %collective-permute-start.20 = (bf16[128,4096]{1,0:T(8,128)(2,1)S(1)}, bf16[128,4096]{1,0:T(8,128)(2,1)S(1)}, u32[]{:S(2)}, u32[]{:S(2)}) collective-permute-start(bf16[128,4096]{1,0:T(8,128)(2,1)S(1)} %constant_dynamic-update-slice_fusion.2.own0), channel_id=1, source_target_pairs={{0,1},{1,0},{2,3},{3,2},{4,5},{5,4},{6,7},{7,6},{8,9},{9,8},{10,11... | collective-permute-start | bytes 3145736 | tf_op jit(solution)/shard_map/ppermute | solution.py:33
  56.1 14.8 %collective-permute-start.19 = (bf16[128,4096]{1,0:T(8,128)(2,1)S(1)}, bf16[128,4096]{1,0:T(8,128)(2,1)S(1)}, u32[]{:S(2)}, u32[]{:S(2)}) collective-permute-start(bf16[128,4096]{1,0:T(8,128)(2,1)S(1)} %constant_dynamic-update-slice_fusion.2.own0), channel_id=1, source_target_pairs={{0,16},{1,9},{2,18},{3,11},{4,20},{5,13},{6,22},{7,15},{8,24},{9,1... | collective-permute-start | bytes 3145736 | tf_op jit(solution)/shard_map/ppermute | solution.py:33
  70.9 9.8 %collective-permute-start.21 = (bf16[128,4096]{1,0:T(8,128)(2,1)S(1)}, bf16[128,4096]{1,0:T(8,128)(2,1)S(1)}, u32[]{:S(2)}, u32[]{:S(2)}) collective-permute-start(bf16[128,4096]{1,0:T(8,128)(2,1)S(1)} %collective-permute-done.19.own1), channel_id=1, source_target_pairs={{0,1},{1,0},{2,3},{3,2},{4,5},{5,4},{6,7},{7,6},{8,9},{9,8},{10,11... | collective-permute-start | bytes 3145736 | tf_op jit(solution)/shard_map/ppermute | solution.py:33
  80.7 5.1 %collective-permute-start.22 = (bf16[256,4096]{1,0:T(8,128)(2,1)S(1)}, bf16[256,4096]{1,0:T(8,128)(2,1)S(1)}, u32[]{:S(2)}, u32[]{:S(2)}) collective-permute-start(bf16[256,4096]{1,0:T(8,128)(2,1)S(1)} %get-tuple-element.110), channel_id=1, source_target_pairs={{0,1},{1,0},{2,3},{3,2},{4,5},{5,4},{6,7},{7,6},{8,9},{9,8},{10,11... | collective-permute-start | bytes 6291464 | tf_op jit(solution)/shard_map/ppermute | solution.py:33
  86.1 14.9 %collective-permute-start.23 = (bf16[128,4096]{1,0:T(8,128)(2,1)S(1)}, bf16[128,4096]{1,0:T(8,128)(2,1)S(1)}, u32[]{:S(2)}, u32[]{:S(2)}) collective-permute-start(bf16[128,4096]{1,0:T(8,128)(2,1)S(1)} %add_convert_fusion), channel_id=1, source_target_pairs={{0,16},{1,9},{2,18},{3,11},{4,20},{5,13},{6,22},{7,15},{8,24},{9,1... | collective-permute-start | bytes 3145736 | tf_op jit(solution)/shard_map/ppermute | solution.py:33
  100.2 7.7 %collective-permute-start.24 = (bf16[256,2048]{1,0:T(8,128)(2,1)S(1)}, bf16[256,2048]{1,0:T(8,128)(2,1)S(1)}, u32[]{:S(2)}, u32[]{:S(2)}) collective-permute-start(bf16[256,2048]{1,0:T(8,128)(2,1)S(1)} %get-tuple-element.129), channel_id=1, source_target_pairs={{0,1},{1,0},{2,3},{3,2},{4,5},{5,4},{6,7},{7,6},{8,9},{9,8},{10,11... | collective-permute-start | bytes 3145736 | tf_op jit(solution)/shard_map/ppermute | solution.py:33
  101.2 9.2 %collective-permute-start.25 = (bf16[64,4096]{1,0:T(8,128)(2,1)S(1)}, bf16[64,4096]{1,0:T(8,128)(2,1)S(1)}, u32[]{:S(2)}, u32[]{:S(2)}) collective-permute-start(bf16[64,4096]{1,0:T(8,128)(2,1)S(1)} %add_convert_fusion.3), channel_id=1, source_target_pairs={{0,8},{1,17},{2,10},{3,19},{4,12},{5,21},{6,14},{7,23},{8,0},{9,25... | collective-permute-start | bytes 1572872 | tf_op jit(solution)/shard_map/ppermute | solution.py:33
  107.8 15.9 %collective-permute-start.26 = (bf16[256,2176]{1,0:T(8,128)(2,1)S(1)}, bf16[256,2176]{1,0:T(8,128)(2,1)S(1)}, u32[]{:S(2)}, u32[]{:S(2)}) collective-permute-start(bf16[256,2176]{1,0:T(8,128)(2,1)S(1)} %get-tuple-element.131), channel_id=1, source_target_pairs={{0,1},{1,0},{2,3},{3,2},{4,5},{5,4},{6,7},{7,6},{8,9},{9,8},{10,11... | collective-permute-start | bytes 3342344 | tf_op jit(solution)/shard_map/ppermute | solution.py:33
  110.6 13.1 %collective-permute-start.27 = (bf16[32,4096]{1,0:T(8,128)(2,1)S(1)}, bf16[32,4096]{1,0:T(8,128)(2,1)S(1)}, u32[]{:S(2)}, u32[]{:S(2)}) collective-permute-start(bf16[32,4096]{1,0:T(8,128)(2,1)S(1)} %add_convert_fusion.6), channel_id=1, source_target_pairs={{0,4},{1,5},{2,6},{3,7},{4,0},{5,1},{6,2},{7,3},{8,12},{9,13},{10,... | collective-permute-start | bytes 786440 | tf_op jit(solution)/shard_map/ppermute | solution.py:33
  110.8 21.7 %collective-permute-start.29 = (bf16[128,2048]{1,0:T(8,128)(2,1)S(1)}, bf16[128,2048]{1,0:T(8,128)(2,1)S(1)}, u32[]{:S(2)}, u32[]{:S(2)}) collective-permute-start(bf16[128,2048]{1,0:T(8,128)(2,1)S(1)} %add_convert_fusion.2), channel_id=1, source_target_pairs={{0,16},{1,9},{2,18},{3,11},{4,20},{5,13},{6,22},{7,15},{8,24},{9,1... | collective-permute-start | bytes 1572872 | tf_op jit(solution)/shard_map/ppermute | solution.py:33
  123.8 9.6 %collective-permute-start.28 = (bf16[128,2176]{1,0:T(8,128)(2,1)S(1)}, bf16[128,2176]{1,0:T(8,128)(2,1)S(1)}, u32[]{:S(2)}, u32[]{:S(2)}) collective-permute-start(bf16[128,2176]{1,0:T(8,128)(2,1)S(1)} %add_convert_fusion.1), channel_id=1, source_target_pairs={{0,16},{1,9},{2,18},{3,11},{4,20},{5,13},{6,22},{7,15},{8,24},{9,1... | collective-permute-start | bytes 1671176 | tf_op jit(solution)/shard_map/ppermute | solution.py:33
  125.0 17.9 %collective-permute-start.31 = (bf16[16,4096]{1,0:T(8,128)(2,1)S(1)}, bf16[16,4096]{1,0:T(8,128)(2,1)S(1)}, u32[]{:S(2)}, u32[]{:S(2)}) collective-permute-start(bf16[16,4096]{1,0:T(8,128)(2,1)S(1)} %add_convert_fusion.8), channel_id=1, source_target_pairs={{0,2},{1,3},{2,0},{3,1},{4,6},{5,7},{6,4},{7,5},{8,10},{9,11},{10,... | collective-permute-start | bytes 393224 | tf_op jit(solution)/shard_map/ppermute | solution.py:33
  133.8 9.4 %collective-permute-start.30 = (bf16[64,4224]{1,0:T(8,128)(2,1)S(1)}, bf16[64,4224]{1,0:T(8,128)(2,1)S(1)}, u32[]{:S(2)}, u32[]{:S(2)}) collective-permute-start(bf16[64,4224]{1,0:T(8,128)(2,1)S(1)} %pad_maximum_fusion.4), channel_id=1, source_target_pairs={{0,8},{1,17},{2,10},{3,19},{4,12},{5,21},{6,14},{7,23},{8,0},{9,25... | collective-permute-start | bytes 1622024 | tf_op jit(solution)/shard_map/ppermute | solution.py:33
  143.3 13.6 %collective-permute-start.32 = (bf16[32,4224]{1,0:T(8,128)(2,1)S(1)}, bf16[32,4224]{1,0:T(8,128)(2,1)S(1)}, u32[]{:S(2)}, u32[]{:S(2)}) collective-permute-start(bf16[32,4224]{1,0:T(8,128)(2,1)S(1)} %fusion), channel_id=1, source_target_pairs={{0,4},{1,5},{2,6},{3,7},{4,0},{5,1},{6,2},{7,3},{8,12},{9,13},{10,... | collective-permute-start | bytes 811016 | tf_op jit(solution)/shard_map/ppermute | solution.py:33
  157.0 5.1 %collective-permute-start.33 = (bf16[16,4224]{1,0:T(8,128)(2,1)S(1)}, bf16[16,4224]{1,0:T(8,128)(2,1)S(1)}, u32[]{:S(2)}, u32[]{:S(2)}) collective-permute-start(bf16[16,4224]{1,0:T(8,128)(2,1)S(1)} %fusion.5), channel_id=1, source_target_pairs={{0,2},{1,3},{2,0},{3,1},{4,6},{5,7},{6,4},{7,5},{8,10},{9,11},{10,... | collective-permute-start | bytes 405512 | tf_op jit(solution)/shard_map/ppermute | solution.py:33
  (8 other events, 88.9 us)

commit v8 on v7

--- a/solution.py
+++ b/solution.py
@@ -76,8 +76,8 @@
 
 
 def route_kernel(tok_count, *refs):
-    rows_refs, part_refs, (mine_ref, mine_t_ref, both_ref) = refs[:6], refs[6:12], refs[12:15]
-    x_ref, put_ref, pick_ref, prob_ref = refs[16:]
+    rows_refs, part_refs, (mine_ref, mine_t_ref, both_ref) = refs[:6], refs[6:8], refs[8:11]
+    x_ref, put_ref, pick_ref, prob_ref = refs[12:]
     experts, both = x_ref.shape[:2]
     places = both // 2
     count = pick_ref.shape[2]
@@ -92,7 +92,7 @@
         spot = lax.rem(iota((count, experts * places), 1), places).astype(jnp.float32)
         spot_t = lax.rem(iota((experts * places, count), 0), places).astype(jnp.float32)
         for half in range(2):
-            prob = ordered(part_refs[3 * half : 3 * half + 3], tok_count)
+            prob = part_refs[half][...]
             taken = prob.astype(jnp.float32) > 0.0
             rank = dot(before, jnp.where(taken, 1.0, 0.0).astype(jnp.bfloat16))
             place = jnp.where(taken, rank + first, -1.0).astype(jnp.bfloat16)
@@ -284,10 +284,10 @@
     )(in_hbm(weight), after)
 
 
-def route_call(own, other, maps, mark, experts, width, tok_count):
+def route_call(own, other, parts, maps, mark, experts, tok_count):
     count = sum(piece.shape[0] for piece in own)
     places = count // tok_count * CAP
-    columns = own[0].shape[1] - width
+    width = own[0].shape[1]
     pieces = (*own, *other)
     shapes = [
         pltpu.VMEM((experts, 2 * places, width), jnp.bfloat16),
@@ -296,13 +296,12 @@
         f32(experts, 1, 2 * places),
     ]
     ins = [pl.BlockSpec((piece.shape[0], WIDE), lambda i: (0, i)) for piece in pieces]
-    ins += [pl.BlockSpec((piece.shape[0], columns), lambda i: (0, width // columns)) for piece in pieces]
-    ins += [whole(a) for a in (*maps, mark)]
+    ins += [whole(a) for a in (*parts, *maps, mark)]
     outs = [pl.BlockSpec((experts, 2 * places, WIDE), lambda i: (0, 0, i))]
     outs += [kept(s) for s in shapes[1:]]
     flops = 4 * experts * places * count * width
     kernel = functools.partial(route_kernel, tok_count)
-    return call(kernel, width // WIDE, ins, (*pieces, *pieces, *maps, mark), outs, shapes, flops=flops)
+    return call(kernel, width // WIDE, ins, (*pieces, *parts, *maps, mark), outs, shapes, flops=flops)
 
 
 def up_call(x, prob, w_gate, w_up):
@@ -363,19 +362,20 @@
     rows = lefts[0].shape[1]
     count = put.shape[1]
     terms = len(lefts)
-    steps = (stop - start) // CHUNK
+    chunk = CHUNK * 2 // terms
+    steps = (stop - start) // chunk
     columns = stop - start + (0 if extra is None else extra.shape[2])
     args = (put, *lefts, *rights) + (() if extra is None else (extra,))
     shapes = [bf16(count, columns)] * 2
     ins = [whole(put)] + [whole(a) for a in lefts]
-    first, last = start // CHUNK, stop // CHUNK - 1
+    first, last = start // chunk, stop // chunk - 1
     ins += [
-        pl.BlockSpec((experts, hidden, CHUNK), lambda i: (0, 0, jnp.minimum(first + i, last)))
+        pl.BlockSpec((experts, hidden, chunk), lambda i: (0, 0, jnp.minimum(first + i, last)))
     ] * terms
     ins += [] if extra is None else [whole(extra)]
-    outs = [pl.BlockSpec((count, CHUNK), lambda i: (0, i))] * 2
+    outs = [pl.BlockSpec((count, chunk), lambda i: (0, i))] * 2
     scratch = [
-        pltpu.VMEM((2, put.shape[2], CHUNK), jnp.bfloat16),
+        pltpu.VMEM((2, put.shape[2], chunk), jnp.bfloat16),
     ]
     flops = 2 * experts * rows * (stop - start) * (hidden * terms + count)
     kernel = functools.partial(back_kernel, terms, steps)
@@ -417,28 +417,20 @@
     def rows_of(*blocks):
         return jnp.concatenate(blocks)
 
-    def wide(values, extra):
-        return jnp.concatenate([values, extra], axis=1)
-
     near, far = swap(tokens, Z1), swap(tokens, Z2)
-    near_parts, far_parts = swap(parts, Z1), swap(parts, Z2)
-    zero = wide(tokens, parts)
-    first0 = swap(zero, X, Y)
+    first0 = swap(tokens, X, Y)
     near, far = together(near, far)
 
-    last, last_parts = swap(far, Z1), swap(far_parts, Z1)
-    middle_rows = wide(rows_of(near, far), rows_of(near_parts, far_parts))
+    last = swap(far, Z1)
+    middle_rows = rows_of(far, near)
     first1 = swap(middle_rows, X, Y)
-    zero = rows_of(zero, first0)
+    zero = rows_of(tokens, first0)
     second0 = swap(zero, Y, X)
-    cotangent, last_parts = together(cotangent, last_parts)
-    grads = [swap(cotangent, bit) for bit in (Z1, Z2, Z3)]
-    last, last_parts, first1, second0, gate_weight = together(
-        last, last_parts, first1, second0, gate_weight
-    )
-    gate_weight, mark = fetch_call(gate_weight, gate_prob)
-
-    last = wide(last, last_parts)
+    last, cotangent = together(last, cotangent)
+    grads = [swap(cotangent, bit) for bit in (Z2, Z1, Z3)]
+    last, first1, second0, gate_weight = together(last, first1, second0, gate_weight)
+    gate_weight, mark = fetch_call(gate_weight, last)
+
     first2 = swap(last, X, Y)
     middle_rows = rows_of(middle_rows, first1)
     second1 = swap(middle_rows, Y, X)
@@ -449,11 +441,17 @@
     )
     up_weight, mark = fetch_call(up_weight, mark)
 
+    parts = rows_of(parts, *(swap(parts, bit) for bit in (Z2, Z1, Z3)))
+    parts = rows_of(parts, swap(parts, X, Y))
+    parts = rows_of(parts, swap(parts, Y, X))
+    parts = (parts, swap(parts, CORE))
+
     last = rows_of(last, first2)
     second2 = swap(last, Y, X)
     second2, mark = together(second2, mark)
     middle_rows = rows_of(middle_rows, second1)
     middle_other = swap(middle_rows, CORE)
+    second2, cotangent = together(second2, cotangent)
     grads = rows_of(cotangent, *grads)
     grads = rows_of(grads, swap(grads, X, Y))
     last = rows_of(last, second2)
@@ -461,10 +459,10 @@
     x, put, pick, prob_rows = route_call(
         (zero, middle_rows, last),
         (zero_other, middle_other, last_other),
+        parts,
         maps,
         mark,
         local,
-        width,
         tok_count,
     )
     x, grads = together(x, grads)
@@ -489,11 +487,11 @@
     def by_first(parts):
         return parts + [swap(leaving(parts, quarter, 2 * quarter), X, Y)]
 
+    def by_near(parts):
+        return parts + [swap(leaving(parts, 2 * tok_count, 4 * tok_count), Z1)]
+
     def by_far(parts):
-        return parts + [swap(leaving(parts, 2 * tok_count, 4 * tok_count), Z2)]
-
-    def by_near(parts):
-        return parts + [swap(leaving(parts, tok_count, 2 * tok_count), Z1)]
+        return parts + [swap(leaving(parts, tok_count, 2 * tok_count), Z2)]
 
     weights = [near_core(gate_weight), near_core(up_weight)]
     mixed[1], far_c = together(mixed[1], c)
@@ -509,40 +507,45 @@
     right, right_other = back_call(put, [dg, du], weights, middle, width, share)
     right = [right, swap(right_other, CORE)]
 
-    right[0], left[1], mixed[3] = together(right[0], left[1], mixed[3])
+    right[0], left[1] = together(right[0], left[1])
     rows, ht = together(leaving(left, 2 * quarter, 4 * quarter), ht)
     left.append(swap(rows, Y, X))
-    mixed = by_far(mixed)
     (down_weight_grad,) = grad_call(far_c, ht, hidden)
 
-    right[1], mixed[4], down_weight_grad = together(right[1], mixed[4], down_weight_grad)
-    rows, dgt = together(leaving(right, 2 * quarter, 4 * quarter), dgt)
+    right[1], left[2], mixed[3], down_weight_grad = together(
+        right[1], left[2], mixed[3], down_weight_grad
+    )
+    rows, left_rows, mixed_rows, dgt = together(
+        leaving(right, 2 * quarter, 4 * quarter),
+        leaving(left, quarter, 2 * quarter),
+        leaving(mixed, 2 * tok_count, 4 * tok_count),
+        dgt,
+    )
     right.append(swap(rows, Y, X))
-    mixed = by_near(mixed)
+    left.append(swap(left_rows, X, Y))
+    mixed.append(swap(mixed_rows, Z1))
     (gate_weight_grad,) = grad_call(x, dgt, hidden)
 
-    def joined(parts, start, stop):
-        halves = [
-            sum(part[start:stop].astype(jnp.float32) for part in half) for half in (left, right)
-        ]
-        total = jnp.concatenate(halves, axis=1)
-        return sum((part[start:stop].astype(jnp.float32) for part in parts), total)
-
-    def sent(parts, start, stop):
-        return joined(parts, start, stop).astype(jnp.bfloat16)
-
-    right[2], left[2], gate_weight_grad = together(right[2], left[2], gate_weight_grad)
-    rows, dut = together(sent([], quarter, 2 * quarter), dut)
-    parts = [swap(rows, X, Y)]
+    right[2], left[3], mixed[4], gate_weight_grad = together(
+        right[2], left[3], mixed[4], gate_weight_grad
+    )
+    rows, left_rows, mixed_rows, dut = together(
+        leaving(right, quarter, 2 * quarter),
+        leaving(left, 2 * tok_count, 4 * tok_count),
+        leaving(mixed, tok_count, 2 * tok_count),
+        dut,
+    )
+    right.append(swap(rows, X, Y))
+    left.append(swap(left_rows, Z1))
+    mixed.append(swap(mixed_rows, Z2))
     (up_weight_grad,) = grad_call(x, dut, hidden)
 
-    parts[0], mixed[5], up_weight_grad = together(parts[0], mixed[5], up_weight_grad)
-    parts.append(swap(sent(parts, 2 * tok_count, 4 * tok_count), Z2))
-    mixed = leaving(mixed, 0, tok_count)
-    parts.append(swap(sent(parts, tok_count, 2 * tok_count), Z1))
-    total = sent(parts, 0, tok_count)
-    token_grad = total[:, :width]
-    share = total[:, width : width + total_experts].astype(jnp.float32)
+    right[3], left[4], up_weight_grad = together(right[3], left[4], up_weight_grad)
+    right, left = by_near(right), by_far(left)
+    right = by_far(right)
+    mixed, left, right = (leaving(parts, 0, tok_count) for parts in (mixed, left, right))
+    token_grad = jnp.concatenate([left, right[:, : width - middle]], axis=1)
+    share = right[:, width - middle : width - middle + total_experts].astype(jnp.float32)
     gate_grad = jnp.sum(jnp.where(used, share[:, None, :], 0.0), axis=2)
     return (mixed, token_grad, gate_grad, gate_weight_grad, up_weight_grad, down_weight_grad)
 

time: 164 us -> 166 us (1.012)
  starting transfers between devices: 28.9 us -> 43.4 us
  waiting for transfers between devices: 45.9 us -> 32.2 us
  Pallas kernels: 79.3 us -> 76.5 us
  local copies, waits for them, and re-layouts: 4.03 us -> 6.73 us
    ppermute x34 -> x40, starting transfers between devices: 28.9 us -> 43.4 us  [swap(): return lax.ppermute(values, AXES, pairs)]
    ppermute x34 -> x40, waiting for transfers between devices: 45.9 us -> 32.2 us  [swap(): return lax.ppermute(values, AXES, pairs)]
    unnamed x20 -> x28, local copies, waits for them, and re-layouts: 2.3 us -> 6.6 us
    pallas_call x10, Pallas kernels: 70.1 us -> 67.4 us  [call(): pl.pallas_call(kernel, grid=(grid,), in_specs=ins, out_specs=outs, out_sh...]
  transfers between devices with their start and end apart: 34 -> 40, of which waited for: 16 -> 14; matrix products, arithmetic and copies ran while one was open for 2% -> 4% of each run, Pallas kernels for 46% -> 44%
where the time goes in v8:
time: 166 us
  Pallas kernels  76.5 us (46%)
  starting transfers between devices  43.4 us (26%)
  waiting for transfers between devices  32.2 us (19%)
  local copies, waits for them, and re-layouts  6.73 us (4%)
  other arithmetic  5.83 us (4%)
    pallas_call x10, Pallas kernels, call(): pl.pallas_call(kernel, grid=(grid,), in_specs=ins, out_specs=outs, out_sh...  67.4 us
    ppermute x40, starting transfers between devices, swap(): return lax.ppermute(values, AXES, pairs)  43.4 us
    ppermute x40, waiting for transfers between devices, swap(): return lax.ppermute(values, AXES, pairs)  32.2 us
    pallas_call x2, Pallas kernels, fetch_call(): pl.pallas_call(fetch_kernel, in_specs=[pl.BlockSpec(memory_space=pl.ANY)]...  9.17 us
    unnamed x28, local copies, waits for them, and re-layouts  6.6 us
  transfers between devices with their start and end apart: 40, of which 14 were waited for; matrix products, arithmetic and copies ran while one was open for 4% of the time, Pallas kernels for 44%

profile of v8, /device:TPU:0, one launch (start us, length us, event | category | flops | bytes accessed | tf_op | source)
XLA Modules:
  0.0 165.9 jit_solution(15103186022918484433)
XLA Ops:
  0.6 3.0 %collective-permute-start = (bf16[16,4096]{1,0:T(8,128)(2,1)}, bf16[16,4096]{1,0:T(8,128)(2,1)S(1)}, u32[]{:S(2)}, u32[]{:S(2)}) collective-permute-start(bf16[16,4096]{1,0:T(8,128)(2,1)} %param.8), channel_id=1, source_target_pairs={{0,8},{1,17},{2,10},{3,19},{4,12},{5,21},{6,14},{7,23},{8,0},{9,25... | collective-permute-start | bytes 393224 | tf_op jit(solution)/shard_map/ppermute | solution.py:33
  8.0 2.6 %collective-permute-start.12 = (bf16[16,128]{1,0:T(8,128)(2,1)S(1)}, bf16[16,128]{1,0:T(8,128)(2,1)S(1)}, u32[]{:S(2)}, u32[]{:S(2)}) collective-permute-start(bf16[16,128]{1,0:T(8,128)(2,1)S(1)} %get-tuple-element.173), channel_id=1, source_target_pairs={{0,4},{1,5},{2,6},{3,7},{4,0},{5,1},{6,2},{7,3},{8,12},{9,13},{10,... | collective-permute-start | bytes 12296 | tf_op jit(solution)/shard_map/ppermute | solution.py:33
  13.5 1.8 %collective-permute-start.2 = (bf16[16,4096]{1,0:T(8,128)(2,1)}, bf16[16,4096]{1,0:T(8,128)(2,1)S(1)}, u32[]{:S(2)}, u32[]{:S(2)}) collective-permute-start(bf16[16,4096]{1,0:T(8,128)(2,1)} %param.8), channel_id=1, source_target_pairs={{0,4},{1,5},{2,6},{3,7},{4,0},{5,1},{6,2},{7,3},{8,12},{9,13},{10,... | collective-permute-start | bytes 393224 | tf_op jit(solution)/shard_map/ppermute | solution.py:33
  17.1 3.3 %collective-permute-done.15 = bf16[64,128]{1,0:T(8,128)(2,1)S(1)} collective-permute-done((bf16[64,128]{1,0:T(8,128)(2,1)S(1)}, bf16[64,128]{1,0:T(8,128)(2,1)S(1)}, u32[]{:S(2)}, u32[]{:S(2)}) %collective-permute-start.15) | collective-permute-done | bytes 16416 | tf_op jit(solution)/shard_map/ppermute | solution.py:33
  22.0 2.4 %collective-permute-done.16 = bf16[128,128]{1,0:T(8,128)(2,1)S(1)} collective-permute-done((bf16[128,128]{1,0:T(8,128)(2,1)S(1)}, bf16[128,128]{1,0:T(8,128)(2,1)S(1)}, u32[]{:S(2)}, u32[]{:S(2)}) %collective-permute-start.16) | collective-permute-done | bytes 32800 | tf_op jit(solution)/shard_map/ppermute | solution.py:33
  26.1 2.0 %collective-permute-start.5 = (bf16[32,4096]{1,0:T(8,128)(2,1)S(1)}, bf16[32,4096]{1,0:T(8,128)(2,1)S(1)}, u32[]{:S(2)}, u32[]{:S(2)}) collective-permute-start(bf16[32,4096]{1,0:T(8,128)(2,1)S(1)} %pad_maximum_fusion.3), channel_id=1, source_target_pairs={{0,16},{1,9},{2,18},{3,11},{4,20},{5,13},{6,22},{7,15},{8,24},{9,1... | collective-permute-start | bytes 786440 | tf_op jit(solution)/shard_map/ppermute | solution.py:33
  28.1 2.2 %collective-permute-done.3.after = bf16[16,4096]{1,0:T(8,128)(2,1)S(1)} collective-permute-done((bf16[16,4096]{1,0:T(8,128)(2,1)S(1)}, bf16[16,4096]{1,0:T(8,128)(2,1)S(1)}, u32[]{:S(2)}, u32[]{:S(2)}) %collective-permute-start.3) | collective-permute-done | bytes 131104 | tf_op jit(solution)/shard_map/ppermute | solution.py:33
  30.4 1.7 %collective-permute-start.19 = (bf16[16,4096]{1,0:T(8,128)(2,1)S(1)}, bf16[16,4096]{1,0:T(8,128)(2,1)S(1)}, u32[]{:S(2)}, u32[]{:S(2)}) collective-permute-start(bf16[16,4096]{1,0:T(8,128)(2,1)S(1)} %copy-done.2), channel_id=1, source_target_pairs={{0,2},{1,3},{2,0},{3,1},{4,6},{5,7},{6,4},{7,5},{8,10},{9,11},{10,... | collective-permute-start | bytes 393224 | tf_op jit(solution)/shard_map/ppermute | solution.py:33
  34.3 1.9 %collective-permute-start.7 = (bf16[64,4096]{1,0:T(8,128)(2,1)S(1)}, bf16[64,4096]{1,0:T(8,128)(2,1)S(1)}, u32[]{:S(2)}, u32[]{:S(2)}) collective-permute-start(bf16[64,4096]{1,0:T(8,128)(2,1)S(1)} %pad_maximum_fusion), channel_id=1, source_target_pairs={{0,16},{1,9},{2,18},{3,11},{4,20},{5,13},{6,22},{7,15},{8,24},{9,1... | collective-permute-start | bytes 1572872 | tf_op jit(solution)/shard_map/ppermute | solution.py:33
  36.2 4.6 %shard_map.127 = (bf16[8,192,4096]{2,1,0:T(8,128)(2,1)S(1)}, f32[8,128]{1,0:T(8,128)S(1)}) custom-call(bf16[8,192,4096]{2,1,0:T(8,128)(2,1)} %source, bf16[16,4096]{1,0:T(8,128)(2,1)S(1)} %collective-permute-done.3.after), custom_call_target="tpu_custom_call" | custom-call | bytes 12582912 | tf_op jit(solution)/shard_map/pallas_call | solution.py:274
  43.5 1.9 %collective-permute-start.8 = (bf16[32,4096]{1,0:T(8,128)(2,1)S(1)}, bf16[32,4096]{1,0:T(8,128)(2,1)S(1)}, u32[]{:S(2)}, u32[]{:S(2)}) collective-permute-start(bf16[32,4096]{1,0:T(8,128)(2,1)S(1)} %pad_maximum_fusion.4), channel_id=1, source_target_pairs={{0,16},{1,9},{2,18},{3,11},{4,20},{5,13},{6,22},{7,15},{8,24},{9,1... | collective-permute-start | bytes 786440 | tf_op jit(solution)/shard_map/ppermute | solution.py:33
  45.5 4.6 %shard_map.128 = (bf16[8,192,4096]{2,1,0:T(8,128)(2,1)S(1)}, f32[8,128]{1,0:T(8,128)S(1)}) custom-call(bf16[8,192,4096]{2,1,0:T(8,128)(2,1)} %source.1, f32[8,128]{1,0:T(8,128)S(1)} %get-tuple-element.98.after), custom_call_target="tpu_custom_call" | custom-call | bytes 12582912 | tf_op jit(solution)/shard_map/pallas_call | solution.py:274
  52.1 8.1 %collective-permute-done.21 = bf16[64,4096]{1,0:T(8,128)(2,1)S(1)} collective-permute-done((bf16[64,4096]{1,0:T(8,128)(2,1)S(1)}, bf16[64,4096]{1,0:T(8,128)(2,1)S(1)}, u32[]{:S(2)}, u32[]{:S(2)}) %collective-permute-start.21) | collective-permute-done | bytes 524320 | tf_op jit(solution)/shard_map/ppermute | solution.py:33
  60.3 4.2 %shard_map.129 = (bf16[8,96,4096]{2,1,0:T(8,128)(2,1)S(1)}, bf16[2,256,384]{2,1,0:T(8,128)(2,1)S(1)}, bf16[2,384,256]{2,1,0:T(8,128)(2,1)S(1)}, f32[8,1,96]{2,1,0:T(1,128)S(1)}) custom-call(bf16[64,4096]{1,0:T(8,128)(2,1)S(1)} %constant_dynamic-update-slice_fusion.refs_0_, bf16[128,4096]{1,0:T(8,128)(2,1)S(1)} %constant_dynamic-update-slice_fusion.3.refs_1_, ...), custom_call_target="tpu_custom_call" | custom-call | flops 1610612736 | bytes 11705344 | tf_op jit(solution)/shard_map/pallas_call | solution.py:254
  64.5 1.7 %collective-permute-start.22 = (bf16[128,4096]{1,0:T(8,128)(2,1)S(1)}, bf16[128,4096]{1,0:T(8,128)(2,1)S(1)}, u32[]{:S(2)}, u32[]{:S(2)}) collective-permute-start(bf16[128,4096]{1,0:T(8,128)(2,1)S(1)} %constant_dynamic-update-slice_fusion.21.own0), channel_id=1, source_target_pairs={{0,16},{1,9},{2,18},{3,11},{4,20},{5,13},{6,22},{7,15},{8,24},{9,1... | collective-permute-start | bytes 3145736 | tf_op jit(solution)/shard_map/ppermute | solution.py:33
  66.2 10.3 %shard_map.130 = (f32[8,192,96]{2,1,0:T(8,128)S(1)}, f32[8,192,96]{2,1,0:T(8,128)S(1)}, bf16[8,96,192]{2,1,0:T(8,128)(2,1)S(1)}, bf16[8,192,96]{2,1,0:T(8,128)(2,1)S(1)}) custom-call(bf16[8,96,4096]{2,1,0:T(8,128)(2,1)S(1)} %get-tuple-element.107.x_ref, f32[8,1,96]{2,1,0:T(1,128)S(1)} %get-tuple-element.108.prob_ref, ...), custom_call_target="tpu_custom_call" | custom-call | flops 2415919104 | bytes 33229824 | tf_op jit(solution)/shard_map/pallas_call | solution.py:254
  76.5 2.9 %collective-permute-done.22.own1 = bf16[128,4096]{1,0:T(8,128)(2,1)S(1)} collective-permute-done((bf16[128,4096]{1,0:T(8,128)(2,1)S(1)}, bf16[128,4096]{1,0:T(8,128)(2,1)S(1)}, u32[]{:S(2)}, u32[]{:S(2)}) %collective-permute-start.22) | collective-permute-done | bytes 1048608 | tf_op jit(solution)/shard_map/ppermute | solution.py:33
  79.4 7.8 %shard_map.131 = (bf16[256,4096]{1,0:T(8,128)(2,1)S(1)}, bf16[256,4096]{1,0:T(8,128)(2,1)S(1)}) custom-call(bf16[2,256,384]{2,1,0:T(8,128)(2,1)S(1)} %get-tuple-element.104.put_ref, bf16[8,96,192]{2,1,0:T(8,128)(2,1)S(1)} %get-tuple-element.113.refs_0_, bf16[8,192,4096]{2,1,0:T(8,128)(2,1)} %down_ref.1), custom_call_target="tpu_custom_call" | custom-call | flops 2818572288 | bytes 17465344 | tf_op jit(solution)/shard_map/pallas_call | solution.py:254
  87.9 4.6 %shard_map.132 = (bf16[8,96,4096]{2,1,0:T(8,128)(2,1)S(1)}, bf16[8,96,4096]{2,1,0:T(8,128)(2,1)}) custom-call(bf16[128,4096]{1,0:T(8,128)(2,1)S(1)} %constant_dynamic-update-slice_fusion.21.own0, bf16[128,4096]{1,0:T(8,128)(2,1)S(1)} %collective-permute-done.22.own1, bf16[128,4096]{1,0:T(8,128)(2,1)S(1)} %collective-permute-done.23.other0, ...), custom_call_target="tpu_custom_call" | custom-call | flops 1610612736 | bytes 17170432 | tf_op jit(solution)/shard_map/pallas_call | solution.py:254
  92.7 1.7 %collective-permute-start.26 = (bf16[128,4096]{1,0:T(8,128)(2,1)S(1)}, bf16[128,4096]{1,0:T(8,128)(2,1)S(1)}, u32[]{:S(2)}, u32[]{:S(2)}) collective-permute-start(bf16[128,4096]{1,0:T(8,128)(2,1)S(1)} %add_convert_fusion), channel_id=1, source_target_pairs={{0,16},{1,9},{2,18},{3,11},{4,20},{5,13},{6,22},{7,15},{8,24},{9,1... | collective-permute-start | bytes 3145736 | tf_op jit(solution)/shard_map/ppermute | solution.py:33
  94.4 8.5 %shard_map.133 = (bf16[8,96,192]{2,1,0:T(8,128)(2,1)S(1)}, bf16[8,96,192]{2,1,0:T(8,128)(2,1)S(1)}, bf16[8,192,96]{2,1,0:T(8,128)(2,1)S(1)}, bf16[8,192,96]{2,1,0:T(8,128)(2,1)S(1)}, bf16[2,256,128]{2,1,0:T(8,128)(2,1)S(1)}) custom-call(bf16[8,96,4096]{2,1,0:T(8,128)(2,1)S(1)} %get-tuple-element.123.x_ref, ...), custom_call_target="tpu_custom_call" | custom-call | flops 1207959552 | bytes 21859328 | tf_op jit(solution)/shard_map/pallas_call | solution.py:254
  102.9 4.8 %shard_map.134 = (bf16[256,2048]{1,0:T(8,128)(2,1)S(1)}, bf16[256,2048]{1,0:T(8,128)(2,1)S(1)}) custom-call(bf16[2,256,384]{2,1,0:T(8,128)(2,1)S(1)} %get-tuple-element.104.put_ref, bf16[8,96,192]{2,1,0:T(8,128)(2,1)S(1)} %get-tuple-element.132.refs_0_, bf16[8,96,192]{2,1,0:T(8,128)(2,1)S(1)} %get-tuple-element.133.refs_1_, ...), custom_call_target="tpu_custom_call" | custom-call | flops 2013265920 | bytes 28246016 | tf_op jit(solution)/shard_map/pallas_call | solution.py:254
  107.8 5.2 %shard_map.135 = (bf16[256,2176]{1,0:T(8,128)(2,1)S(1)}, bf16[256,2176]{1,0:T(8,128)(2,1)S(1)}) custom-call(bf16[2,256,384]{2,1,0:T(8,128)(2,1)S(1)} %get-tuple-element.104.put_ref, bf16[8,96,192]{2,1,0:T(8,128)(2,1)S(1)} %get-tuple-element.132.refs_0_, bf16[8,96,192]{2,1,0:T(8,128)(2,1)S(1)} %get-tuple-element.133.refs_1_, ...), custom_call_target="tpu_custom_call" | custom-call | flops 2013265920 | bytes 28508160 | tf_op jit(solution)/shard_map/pallas_call | solution.py:254
  115.9 3.3 %copy-done.1 = bf16[8,96,4096]{2,1,0:T(8,128)(2,1)S(1)} copy-done((bf16[8,96,4096]{2,1,0:T(8,128)(2,1)S(1)}, bf16[8,96,4096]{2,1,0:T(8,128)(2,1)}, u32[]{:S(2)}) %copy-start.1) | copy-done | bytes 6291480
  119.3 7.4 %shard_map.136 = bf16[8,192,4096]{2,1,0:T(8,128)(2,1)} custom-call(bf16[8,96,4096]{2,1,0:T(8,128)(2,1)S(1)} %copy-done.1, bf16[8,192,96]{2,1,0:T(8,128)(2,1)S(1)} %get-tuple-element.143.left), custom_call_target="tpu_custom_call" | custom-call | flops 1207959552 | bytes 19169280 | tf_op jit(solution)/shard_map/pallas_call | solution.py:254
  126.7 1.7 %collective-permute-done.29 = bf16[128,2048]{1,0:T(8,128)(2,1)S(1)} collective-permute-done((bf16[128,2048]{1,0:T(8,128)(2,1)S(1)}, bf16[128,2048]{1,0:T(8,128)(2,1)S(1)}, u32[]{:S(2)}, u32[]{:S(2)}) %collective-permute-start.29) | collective-permute-done | bytes 524320 | tf_op jit(solution)/shard_map/ppermute | solution.py:33
  132.2 7.4 %shard_map.137 = bf16[8,192,4096]{2,1,0:T(8,128)(2,1)} custom-call(bf16[8,96,4096]{2,1,0:T(8,128)(2,1)S(1)} %bitcast.1, bf16[8,192,96]{2,1,0:T(8,128)(2,1)S(1)} %get-tuple-element.152.left), custom_call_target="tpu_custom_call" | custom-call | flops 1207959552 | bytes 19169280 | tf_op jit(solution)/shard_map/pallas_call | solution.py:254
  144.2 7.4 %shard_map.138 = bf16[8,192,4096]{2,1,0:T(8,128)(2,1)} custom-call(bf16[8,96,4096]{2,1,0:T(8,128)(2,1)S(1)} %bitcast.1, bf16[8,192,96]{2,1,0:T(8,128)(2,1)S(1)} %get-tuple-element.160.left), custom_call_target="tpu_custom_call" | custom-call | flops 1207959552 | bytes 19169280 | tf_op jit(solution)/shard_map/pallas_call | solution.py:254
  152.4 1.8 %collective-permute-start.38 = (bf16[32,2176]{1,0:T(8,128)(2,1)S(1)}, bf16[32,2176]{1,0:T(8,128)(2,1)S(1)}, u32[]{:S(2)}, u32[]{:S(2)}) collective-permute-start(bf16[32,2176]{1,0:T(8,128)(2,1)S(1)} %add_convert_fusion.7), channel_id=1, source_target_pairs={{0,2},{1,3},{2,0},{3,1},{4,6},{5,7},{6,4},{7,5},{8,10},{9,11},{10,... | collective-permute-start | bytes 417800 | tf_op jit(solution)/shard_map/ppermute | solution.py:33
  155.8 2.4 %collective-permute-done.38 = bf16[32,2176]{1,0:T(8,128)(2,1)S(1)} collective-permute-done((bf16[32,2176]{1,0:T(8,128)(2,1)S(1)}, bf16[32,2176]{1,0:T(8,128)(2,1)S(1)}, u32[]{:S(2)}, u32[]{:S(2)}) %collective-permute-start.38) | collective-permute-done | bytes 139296 | tf_op jit(solution)/shard_map/ppermute | solution.py:33
  158.3 2.4 %collective-permute-start.39 = (bf16[16,2176]{1,0:T(8,128)(2,1)S(1)}, bf16[16,2176]{1,0:T(8,128)(2,1)S(1)}, u32[]{:S(2)}, u32[]{:S(2)}) collective-permute-start(bf16[16,2176]{1,0:T(8,128)(2,1)S(1)} %add_convert_fusion.12), channel_id=1, source_target_pairs={{0,4},{1,5},{2,6},{3,7},{4,0},{5,1},{6,2},{7,3},{8,12},{9,13},{10,... | collective-permute-start | bytes 208904 | tf_op jit(solution)/shard_map/ppermute | solution.py:33
  161.5 2.8 %collective-permute-done.39 = bf16[16,2176]{1,0:T(8,128)(2,1)S(1)} collective-permute-done((bf16[16,2176]{1,0:T(8,128)(2,1)S(1)}, bf16[16,2176]{1,0:T(8,128)(2,1)S(1)}, u32[]{:S(2)}, u32[]{:S(2)}) %collective-permute-start.39) | collective-permute-done | bytes 69664 | tf_op jit(solution)/shard_map/ppermute | solution.py:33
  (130 shorter events, 36.5 us)
Async XLA Ops:
  0.6 24.5 %collective-permute-start = (bf16[16,4096]{1,0:T(8,128)(2,1)}, bf16[16,4096]{1,0:T(8,128)(2,1)S(1)}, u32[]{:S(2)}, u32[]{:S(2)}) collective-permute-start(bf16[16,4096]{1,0:T(8,128)(2,1)} %param.8), channel_id=1, source_target_pairs={{0,8},{1,17},{2,10},{3,19},{4,12},{5,21},{6,14},{7,23},{8,0},{9,25... | collective-permute-start | bytes 393224 | tf_op jit(solution)/shard_map/ppermute | solution.py:33
  3.6 20.8 %collective-permute-start.1 = (bf16[16,4096]{1,0:T(8,128)(2,1)}, bf16[16,4096]{1,0:T(8,128)(2,1)S(1)}, u32[]{:S(2)}, u32[]{:S(2)}) collective-permute-start(bf16[16,4096]{1,0:T(8,128)(2,1)} %param.8), channel_id=1, source_target_pairs={{0,2},{1,3},{2,0},{3,1},{4,6},{5,7},{6,4},{7,5},{8,10},{9,11},{10,... | collective-permute-start | bytes 393224 | tf_op jit(solution)/shard_map/ppermute | solution.py:33
  13.5 10.9 %collective-permute-start.2 = (bf16[16,4096]{1,0:T(8,128)(2,1)}, bf16[16,4096]{1,0:T(8,128)(2,1)S(1)}, u32[]{:S(2)}, u32[]{:S(2)}) collective-permute-start(bf16[16,4096]{1,0:T(8,128)(2,1)} %param.8), channel_id=1, source_target_pairs={{0,4},{1,5},{2,6},{3,7},{4,0},{5,1},{6,2},{7,3},{8,12},{9,13},{10,... | collective-permute-start | bytes 393224 | tf_op jit(solution)/shard_map/ppermute | solution.py:33
  24.4 35.9 %collective-permute-start.17 = (bf16[256,128]{1,0:T(8,128)(2,1)S(1)}, bf16[256,128]{1,0:T(8,128)(2,1)S(1)}, u32[]{:S(2)}, u32[]{:S(2)}) collective-permute-start(bf16[256,128]{1,0:T(8,128)(2,1)S(1)} %constant_dynamic-update-slice_fusion.15.refs_6_), channel_id=1, source_target_pairs={{0,1},{1,0},{2,3},{3,2},{4,5},{5,4},{6,7},{7,6},{8,9},{9,8},{10,11... | collective-permute-start | bytes 196616 | tf_op jit(solution)/shard_map/ppermute | solution.py:33
  24.4 5.9 %collective-permute-start.3 = (bf16[16,4096]{1,0:T(8,128)(2,1)S(1)}, bf16[16,4096]{1,0:T(8,128)(2,1)S(1)}, u32[]{:S(2)}, u32[]{:S(2)}) collective-permute-start(bf16[16,4096]{1,0:T(8,128)(2,1)S(1)} %collective-permute-done.2), channel_id=1, source_target_pairs={{0,2},{1,3},{2,0},{3,1},{4,6},{5,7},{6,4},{7,5},{8,10},{9,11},{10,... | collective-permute-start | bytes 393224 | tf_op jit(solution)/shard_map/ppermute | solution.py:33
  24.7 7.7 %collective-permute-start.4 = (bf16[32,4096]{1,0:T(8,128)(2,1)S(1)}, bf16[32,4096]{1,0:T(8,128)(2,1)S(1)}, u32[]{:S(2)}, u32[]{:S(2)}) collective-permute-start(bf16[32,4096]{1,0:T(8,128)(2,1)S(1)} %pad_maximum_fusion.2), channel_id=1, source_target_pairs={{0,8},{1,17},{2,10},{3,19},{4,12},{5,21},{6,14},{7,23},{8,0},{9,25... | collective-permute-start | bytes 786440 | tf_op jit(solution)/shard_map/ppermute | solution.py:33
  26.1 7.2 %collective-permute-start.5 = (bf16[32,4096]{1,0:T(8,128)(2,1)S(1)}, bf16[32,4096]{1,0:T(8,128)(2,1)S(1)}, u32[]{:S(2)}, u32[]{:S(2)}) collective-permute-start(bf16[32,4096]{1,0:T(8,128)(2,1)S(1)} %pad_maximum_fusion.3), channel_id=1, source_target_pairs={{0,16},{1,9},{2,18},{3,11},{4,20},{5,13},{6,22},{7,15},{8,24},{9,1... | collective-permute-start | bytes 786440 | tf_op jit(solution)/shard_map/ppermute | solution.py:33
  30.3 19.9 %collective-permute-start.18 = (bf16[16,4096]{1,0:T(8,128)(2,1)S(1)}, bf16[16,4096]{1,0:T(8,128)(2,1)S(1)}, u32[]{:S(2)}, u32[]{:S(2)}) collective-permute-start(bf16[16,4096]{1,0:T(8,128)(2,1)S(1)} %copy-done.2), channel_id=1, source_target_pairs={{0,4},{1,5},{2,6},{3,7},{4,0},{5,1},{6,2},{7,3},{8,12},{9,13},{10,... | collective-permute-start | bytes 393224 | tf_op jit(solution)/shard_map/ppermute | solution.py:33
  30.4 20.4 %collective-permute-start.19 = (bf16[16,4096]{1,0:T(8,128)(2,1)S(1)}, bf16[16,4096]{1,0:T(8,128)(2,1)S(1)}, u32[]{:S(2)}, u32[]{:S(2)}) collective-permute-start(bf16[16,4096]{1,0:T(8,128)(2,1)S(1)} %copy-done.2), channel_id=1, source_target_pairs={{0,2},{1,3},{2,0},{3,1},{4,6},{5,7},{6,4},{7,5},{8,10},{9,11},{10,... | collective-permute-start | bytes 393224 | tf_op jit(solution)/shard_map/ppermute | solution.py:33
  33.3 7.5 %collective-permute-start.6 = (bf16[16,4096]{1,0:T(8,128)(2,1)S(1)}, bf16[16,4096]{1,0:T(8,128)(2,1)S(1)}, u32[]{:S(2)}, u32[]{:S(2)}) collective-permute-start(bf16[16,4096]{1,0:T(8,128)(2,1)S(1)} %collective-permute-done.3.after), channel_id=1, source_target_pairs={{0,8},{1,17},{2,10},{3,19},{4,12},{5,21},{6,14},{7,23},{8,0},{9,25... | collective-permute-start | bytes 393224 | tf_op jit(solution)/shard_map/ppermute | solution.py:33
  34.3 9.2 %collective-permute-start.7 = (bf16[64,4096]{1,0:T(8,128)(2,1)S(1)}, bf16[64,4096]{1,0:T(8,128)(2,1)S(1)}, u32[]{:S(2)}, u32[]{:S(2)}) collective-permute-start(bf16[64,4096]{1,0:T(8,128)(2,1)S(1)} %pad_maximum_fusion), channel_id=1, source_target_pairs={{0,16},{1,9},{2,18},{3,11},{4,20},{5,13},{6,22},{7,15},{8,24},{9,1... | collective-permute-start | bytes 1572872 | tf_op jit(solution)/shard_map/ppermute | solution.py:33
  40.9 10.1 %collective-permute-start.20 = (bf16[16,4096]{1,0:T(8,128)(2,1)S(1)}, bf16[16,4096]{1,0:T(8,128)(2,1)S(1)}, u32[]{:S(2)}, u32[]{:S(2)}) collective-permute-start(bf16[16,4096]{1,0:T(8,128)(2,1)S(1)} %copy-done.2), channel_id=1, source_target_pairs={{0,6},{1,7},{2,4},{3,5},{4,2},{5,3},{6,0},{7,1},{8,14},{9,15},{10,... | collective-permute-start | bytes 393224 | tf_op jit(solution)/shard_map/ppermute | solution.py:33
  43.5 6.6 %collective-permute-start.8 = (bf16[32,4096]{1,0:T(8,128)(2,1)S(1)}, bf16[32,4096]{1,0:T(8,128)(2,1)S(1)}, u32[]{:S(2)}, u32[]{:S(2)}) collective-permute-start(bf16[32,4096]{1,0:T(8,128)(2,1)S(1)} %pad_maximum_fusion.4), channel_id=1, source_target_pairs={{0,16},{1,9},{2,18},{3,11},{4,20},{5,13},{6,22},{7,15},{8,24},{9,1... | collective-permute-start | bytes 786440 | tf_op jit(solution)/shard_map/ppermute | solution.py:33
  50.1 10.1 %collective-permute-start.9 = (bf16[64,4096]{1,0:T(8,128)(2,1)S(1)}, bf16[64,4096]{1,0:T(8,128)(2,1)S(1)}, u32[]{:S(2)}, u32[]{:S(2)}) collective-permute-start(bf16[64,4096]{1,0:T(8,128)(2,1)S(1)} %constant_dynamic-update-slice_fusion.refs_0_), channel_id=1, source_target_pairs={{0,1},{1,0},{2,3},{3,2},{4,5},{5,4},{6,7},{7,6},{8,9},{9,8},{10,11... | collective-permute-start | bytes 1572872 | tf_op jit(solution)/shard_map/ppermute | solution.py:33
  50.3 10.0 %collective-permute-start.10 = (bf16[128,4096]{1,0:T(8,128)(2,1)S(1)}, bf16[128,4096]{1,0:T(8,128)(2,1)S(1)}, u32[]{:S(2)}, u32[]{:S(2)}) collective-permute-start(bf16[128,4096]{1,0:T(8,128)(2,1)S(1)} %constant_dynamic-update-slice_fusion.3.refs_1_), channel_id=1, source_target_pairs={{0,1},{1,0},{2,3},{3,2},{4,5},{5,4},{6,7},{7,6},{8,9},{9,8},{10,11... | collective-permute-start | bytes 3145736 | tf_op jit(solution)/shard_map/ppermute | solution.py:33
  50.8 9.4 %collective-permute-start.11 = (bf16[64,4096]{1,0:T(8,128)(2,1)S(1)}, bf16[64,4096]{1,0:T(8,128)(2,1)S(1)}, u32[]{:S(2)}, u32[]{:S(2)}) collective-permute-start(bf16[64,4096]{1,0:T(8,128)(2,1)S(1)} %constant_dynamic-update-slice_fusion.7.refs_2_), channel_id=1, source_target_pairs={{0,1},{1,0},{2,3},{3,2},{4,5},{5,4},{6,7},{7,6},{8,9},{9,8},{10,11... | collective-permute-start | bytes 1572872 | tf_op jit(solution)/shard_map/ppermute | solution.py:33
  51.0 9.2 %collective-permute-start.21 = (bf16[64,4096]{1,0:T(8,128)(2,1)S(1)}, bf16[64,4096]{1,0:T(8,128)(2,1)S(1)}, u32[]{:S(2)}, u32[]{:S(2)}) collective-permute-start(bf16[64,4096]{1,0:T(8,128)(2,1)S(1)} %pad_maximum_fusion.1), channel_id=1, source_target_pairs={{0,8},{1,17},{2,10},{3,19},{4,12},{5,21},{6,14},{7,23},{8,0},{9,25... | collective-permute-start | bytes 1572872 | tf_op jit(solution)/shard_map/ppermute | solution.py:33
  64.5 14.9 %collective-permute-start.22 = (bf16[128,4096]{1,0:T(8,128)(2,1)S(1)}, bf16[128,4096]{1,0:T(8,128)(2,1)S(1)}, u32[]{:S(2)}, u32[]{:S(2)}) collective-permute-start(bf16[128,4096]{1,0:T(8,128)(2,1)S(1)} %constant_dynamic-update-slice_fusion.21.own0), channel_id=1, source_target_pairs={{0,16},{1,9},{2,18},{3,11},{4,20},{5,13},{6,22},{7,15},{8,24},{9,1... | collective-permute-start | bytes 3145736 | tf_op jit(solution)/shard_map/ppermute | solution.py:33
  66.2 13.2 %collective-permute-start.23 = (bf16[128,4096]{1,0:T(8,128)(2,1)S(1)}, bf16[128,4096]{1,0:T(8,128)(2,1)S(1)}, u32[]{:S(2)}, u32[]{:S(2)}) collective-permute-start(bf16[128,4096]{1,0:T(8,128)(2,1)S(1)} %constant_dynamic-update-slice_fusion.21.own0), channel_id=1, source_target_pairs={{0,1},{1,0},{2,3},{3,2},{4,5},{5,4},{6,7},{7,6},{8,9},{9,8},{10,11... | collective-permute-start | bytes 3145736 | tf_op jit(solution)/shard_map/ppermute | solution.py:33
  79.4 7.8 %collective-permute-start.24 = (bf16[128,4096]{1,0:T(8,128)(2,1)S(1)}, bf16[128,4096]{1,0:T(8,128)(2,1)S(1)}, u32[]{:S(2)}, u32[]{:S(2)}) collective-permute-start(bf16[128,4096]{1,0:T(8,128)(2,1)S(1)} %collective-permute-done.22.own1), channel_id=1, source_target_pairs={{0,1},{1,0},{2,3},{3,2},{4,5},{5,4},{6,7},{7,6},{8,9},{9,8},{10,11... | collective-permute-start | bytes 3145736 | tf_op jit(solution)/shard_map/ppermute | solution.py:33
  92.7 15.1 %collective-permute-start.26 = (bf16[128,4096]{1,0:T(8,128)(2,1)S(1)}, bf16[128,4096]{1,0:T(8,128)(2,1)S(1)}, u32[]{:S(2)}, u32[]{:S(2)}) collective-permute-start(bf16[128,4096]{1,0:T(8,128)(2,1)S(1)} %add_convert_fusion), channel_id=1, source_target_pairs={{0,16},{1,9},{2,18},{3,11},{4,20},{5,13},{6,22},{7,15},{8,24},{9,1... | collective-permute-start | bytes 3145736 | tf_op jit(solution)/shard_map/ppermute | solution.py:33
  113.0 15.4 %collective-permute-start.27 = (bf16[256,2176]{1,0:T(8,128)(2,1)S(1)}, bf16[256,2176]{1,0:T(8,128)(2,1)S(1)}, u32[]{:S(2)}, u32[]{:S(2)}) collective-permute-start(bf16[256,2176]{1,0:T(8,128)(2,1)S(1)} %get-tuple-element.135), channel_id=1, source_target_pairs={{0,1},{1,0},{2,3},{3,2},{4,5},{5,4},{6,7},{7,6},{8,9},{9,8},{10,11... | collective-permute-start | bytes 3342344 | tf_op jit(solution)/shard_map/ppermute | solution.py:33
  113.6 14.7 %collective-permute-start.29 = (bf16[128,2048]{1,0:T(8,128)(2,1)S(1)}, bf16[128,2048]{1,0:T(8,128)(2,1)S(1)}, u32[]{:S(2)}, u32[]{:S(2)}) collective-permute-start(bf16[128,2048]{1,0:T(8,128)(2,1)S(1)} %add_convert_fusion.3), channel_id=1, source_target_pairs={{0,16},{1,9},{2,18},{3,11},{4,20},{5,13},{6,22},{7,15},{8,24},{9,1... | collective-permute-start | bytes 1572872 | tf_op jit(solution)/shard_map/ppermute | solution.py:33
  114.9 13.5 %collective-permute-start.30 = (bf16[64,4096]{1,0:T(8,128)(2,1)S(1)}, bf16[64,4096]{1,0:T(8,128)(2,1)S(1)}, u32[]{:S(2)}, u32[]{:S(2)}) collective-permute-start(bf16[64,4096]{1,0:T(8,128)(2,1)S(1)} %add_convert_fusion.2), channel_id=1, source_target_pairs={{0,8},{1,17},{2,10},{3,19},{4,12},{5,21},{6,14},{7,23},{8,0},{9,25... | collective-permute-start | bytes 1572872 | tf_op jit(solution)/shard_map/ppermute | solution.py:33
  128.8 12.3 %collective-permute-start.31 = (bf16[128,2176]{1,0:T(8,128)(2,1)S(1)}, bf16[128,2176]{1,0:T(8,128)(2,1)S(1)}, u32[]{:S(2)}, u32[]{:S(2)}) collective-permute-start(bf16[128,2176]{1,0:T(8,128)(2,1)S(1)} %add_convert_fusion.1), channel_id=1, source_target_pairs={{0,16},{1,9},{2,18},{3,11},{4,20},{5,13},{6,22},{7,15},{8,24},{9,1... | collective-permute-start | bytes 1671176 | tf_op jit(solution)/shard_map/ppermute | solution.py:33
  129.4 10.1 %collective-permute-start.32 = (bf16[64,2048]{1,0:T(8,128)(2,1)S(1)}, bf16[64,2048]{1,0:T(8,128)(2,1)S(1)}, u32[]{:S(2)}, u32[]{:S(2)}) collective-permute-start(bf16[64,2048]{1,0:T(8,128)(2,1)S(1)} %add_convert_fusion.6), channel_id=1, source_target_pairs={{0,8},{1,17},{2,10},{3,19},{4,12},{5,21},{6,14},{7,23},{8,0},{9,25... | collective-permute-start | bytes 786440 | tf_op jit(solution)/shard_map/ppermute | solution.py:33
  130.5 9.1 %collective-permute-start.33 = (bf16[32,4096]{1,0:T(8,128)(2,1)S(1)}, bf16[32,4096]{1,0:T(8,128)(2,1)S(1)}, u32[]{:S(2)}, u32[]{:S(2)}) collective-permute-start(bf16[32,4096]{1,0:T(8,128)(2,1)S(1)} %add_convert_fusion.5), channel_id=1, source_target_pairs={{0,2},{1,3},{2,0},{3,1},{4,6},{5,7},{6,4},{7,5},{8,10},{9,11},{10,... | collective-permute-start | bytes 786440 | tf_op jit(solution)/shard_map/ppermute | solution.py:33
  141.4 10.2 %collective-permute-start.34 = (bf16[16,4096]{1,0:T(8,128)(2,1)S(1)}, bf16[16,4096]{1,0:T(8,128)(2,1)S(1)}, u32[]{:S(2)}, u32[]{:S(2)}) collective-permute-start(bf16[16,4096]{1,0:T(8,128)(2,1)S(1)} %add_convert_fusion.9), channel_id=1, source_target_pairs={{0,4},{1,5},{2,6},{3,7},{4,0},{5,1},{6,2},{7,3},{8,12},{9,13},{10,... | collective-permute-start | bytes 393224 | tf_op jit(solution)/shard_map/ppermute | solution.py:33
  143.0 9.3 %collective-permute-start.35 = (bf16[64,2176]{1,0:T(8,128)(2,1)S(1)}, bf16[64,2176]{1,0:T(8,128)(2,1)S(1)}, u32[]{:S(2)}, u32[]{:S(2)}) collective-permute-start(bf16[64,2176]{1,0:T(8,128)(2,1)S(1)} %add_convert_fusion.4), channel_id=1, source_target_pairs={{0,8},{1,17},{2,10},{3,19},{4,12},{5,21},{6,14},{7,23},{8,0},{9,25... | collective-permute-start | bytes 835592 | tf_op jit(solution)/shard_map/ppermute | solution.py:33
  143.9 8.4 %collective-permute-start.36 = (bf16[32,2048]{1,0:T(8,128)(2,1)S(1)}, bf16[32,2048]{1,0:T(8,128)(2,1)S(1)}, u32[]{:S(2)}, u32[]{:S(2)}) collective-permute-start(bf16[32,2048]{1,0:T(8,128)(2,1)S(1)} %add_convert_fusion.10), channel_id=1, source_target_pairs={{0,2},{1,3},{2,0},{3,1},{4,6},{5,7},{6,4},{7,5},{8,10},{9,11},{10,... | collective-permute-start | bytes 393224 | tf_op jit(solution)/shard_map/ppermute | solution.py:33
  154.3 7.2 %collective-permute-start.37 = (bf16[16,2048]{1,0:T(8,128)(2,1)S(1)}, bf16[16,2048]{1,0:T(8,128)(2,1)S(1)}, u32[]{:S(2)}, u32[]{:S(2)}) collective-permute-start(bf16[16,2048]{1,0:T(8,128)(2,1)S(1)} %add_convert_fusion.14), channel_id=1, source_target_pairs={{0,4},{1,5},{2,6},{3,7},{4,0},{5,1},{6,2},{7,3},{8,12},{9,13},{10,... | collective-permute-start | bytes 196616 | tf_op jit(solution)/shard_map/ppermute | solution.py:33
  158.3 6.0 %collective-permute-start.39 = (bf16[16,2176]{1,0:T(8,128)(2,1)S(1)}, bf16[16,2176]{1,0:T(8,128)(2,1)S(1)}, u32[]{:S(2)}, u32[]{:S(2)}) collective-permute-start(bf16[16,2176]{1,0:T(8,128)(2,1)S(1)} %add_convert_fusion.12), channel_id=1, source_target_pairs={{0,4},{1,5},{2,6},{3,7},{4,0},{5,1},{6,2},{7,3},{8,12},{9,13},{10,... | collective-permute-start | bytes 208904 | tf_op jit(solution)/shard_map/ppermute | solution.py:33
  (13 other events, 120.0 us)

commit v9 on v8

--- a/solution.py
+++ b/solution.py
@@ -388,7 +388,7 @@
     shapes = [bf16(experts, hidden, width)] * (left.shape[1] // hidden)
     flops = 2 * experts * rows * left.shape[1] * width
     ins, outs = [each(x), each(left)], [each(s) for s in shapes]
-    return call(grad_kernel, experts, ins, (x, left), outs, shapes, flops=flops)
+    return call(grad_kernel, experts, ins, (in_hbm(x), left), outs, shapes, flops=flops)
 
 
 def dense_body(
@@ -419,6 +419,7 @@
 
     near, far = swap(tokens, Z1), swap(tokens, Z2)
     first0 = swap(tokens, X, Y)
+    far_parts, near_parts, last_parts = (swap(parts, bit) for bit in (Z2, Z1, Z3))
     near, far = together(near, far)
 
     last = swap(far, Z1)
@@ -428,7 +429,9 @@
     second0 = swap(zero, Y, X)
     last, cotangent = together(last, cotangent)
     grads = [swap(cotangent, bit) for bit in (Z2, Z1, Z3)]
-    last, first1, second0, gate_weight = together(last, first1, second0, gate_weight)
+    last, first1, second0, gate_weight, far_parts, near_parts, last_parts = together(
+        last, first1, second0, gate_weight, far_parts, near_parts, last_parts
+    )
     gate_weight, mark = fetch_call(gate_weight, last)
 
     first2 = swap(last, X, Y)
@@ -436,22 +439,22 @@
     second1 = swap(middle_rows, Y, X)
     zero = rows_of(zero, second0)
     zero_other = swap(zero, CORE)
-    first2, second1, cotangent, mark, up_weight = together(
-        first2, second1, cotangent, mark, up_weight
+    parts = rows_of(parts, far_parts, near_parts, last_parts)
+    first_parts = swap(parts, X, Y)
+    first2, second1, cotangent, mark, up_weight, first_parts = together(
+        first2, second1, cotangent, mark, up_weight, first_parts
     )
     up_weight, mark = fetch_call(up_weight, mark)
-
-    parts = rows_of(parts, *(swap(parts, bit) for bit in (Z2, Z1, Z3)))
-    parts = rows_of(parts, swap(parts, X, Y))
-    parts = rows_of(parts, swap(parts, Y, X))
-    parts = (parts, swap(parts, CORE))
 
     last = rows_of(last, first2)
     second2 = swap(last, Y, X)
-    second2, mark = together(second2, mark)
+    parts = rows_of(parts, first_parts)
+    second_parts = swap(parts, Y, X)
+    second2, mark, second_parts = together(second2, mark, second_parts)
+    parts = rows_of(parts, second_parts)
+    parts = (parts, swap(parts, CORE))
     middle_rows = rows_of(middle_rows, second1)
     middle_other = swap(middle_rows, CORE)
-    second2, cotangent = together(second2, cotangent)
     grads = rows_of(cotangent, *grads)
     grads = rows_of(grads, swap(grads, X, Y))
     last = rows_of(last, second2)

time: 166 us -> 161 us (0.970)
  Pallas kernels: 76.5 us -> 86 us
  starting transfers between devices: 43.4 us -> 37 us
  waiting for transfers between devices: 32.2 us -> 27 us
  local copies, waits for them, and re-layouts: 6.73 us -> 3.38 us
    pallas_call x10, Pallas kernels: 67.4 us -> 76.9 us  [call(): pl.pallas_call(kernel, grid=(grid,), in_specs=ins, out_specs=outs, out_sh...]
    ppermute x40, starting transfers between devices: 43.4 us -> 37 us  [swap(): return lax.ppermute(values, AXES, pairs)]
    ppermute x40, waiting for transfers between devices: 32.2 us -> 27 us  [swap(): return lax.ppermute(values, AXES, pairs)]
    unnamed x28 -> x23, local copies, waits for them, and re-layouts: 6.6 us -> 3.26 us
  transfers between devices with their start and end apart: 40 -> 40, of which waited for: 14 -> 11; matrix products, arithmetic and copies ran while one was open for 4% -> 4% of each run, Pallas kernels for 44% -> 51%
where the time goes in v9:
time: 161 us; the launch traced here: 160 us
  Pallas kernels  86 us (53%)
  starting transfers between devices  37 us (23%)
  waiting for transfers between devices  27 us (17%)
  other arithmetic  5.82 us (4%)
  local copies, waits for them, and re-layouts  3.38 us (2%)
    pallas_call x10, Pallas kernels, call(): pl.pallas_call(kernel, grid=(grid,), in_specs=ins, out_specs=outs, out_sh...  76.9 us
    ppermute x40, starting transfers between devices, swap(): return lax.ppermute(values, AXES, pairs)  37 us
    ppermute x40, waiting for transfers between devices, swap(): return lax.ppermute(values, AXES, pairs)  27 us
    pallas_call x2, Pallas kernels, fetch_call(): pl.pallas_call(fetch_kernel, in_specs=[pl.BlockSpec(memory_space=pl.ANY)]...  9.17 us
    unnamed x23, local copies, waits for them, and re-layouts  3.26 us
  transfers between devices with their start and end apart: 40, of which 11 were waited for; matrix products, arithmetic and copies ran while one was open for 4% of the time, Pallas kernels for 51%

profile of v9, /device:TPU:0, one launch (start us, length us, event | category | flops | bytes accessed | tf_op | source)
XLA Modules:
  0.0 160.4 jit_solution(7417084057866410075)
XLA Ops:
  0.6 3.0 %collective-permute-start = (bf16[16,4096]{1,0:T(8,128)(2,1)}, bf16[16,4096]{1,0:T(8,128)(2,1)S(1)}, u32[]{:S(2)}, u32[]{:S(2)}) collective-permute-start(bf16[16,4096]{1,0:T(8,128)(2,1)} %param.8), channel_id=1, source_target_pairs={{0,8},{1,17},{2,10},{3,19},{4,12},{5,21},{6,14},{7,23},{8,0},{9,25... | collective-permute-start | bytes 393224 | tf_op jit(solution)/shard_map/ppermute | solution.py:33
  3.6 1.6 collective-permute-start.1
  5.2 2.6 %collective-permute-start.2 = (bf16[16,4096]{1,0:T(8,128)(2,1)}, bf16[16,4096]{1,0:T(8,128)(2,1)S(1)}, u32[]{:S(2)}, u32[]{:S(2)}) collective-permute-start(bf16[16,4096]{1,0:T(8,128)(2,1)} %param.8), channel_id=1, source_target_pairs={{0,4},{1,5},{2,6},{3,7},{4,0},{5,1},{6,2},{7,3},{8,12},{9,13},{10,... | collective-permute-start | bytes 393224 | tf_op jit(solution)/shard_map/ppermute | solution.py:33
  12.6 3.7 %collective-permute-start.8 = (bf16[16,128]{1,0:T(8,128)(2,1)S(1)}, bf16[16,128]{1,0:T(8,128)(2,1)S(1)}, u32[]{:S(2)}, u32[]{:S(2)}) collective-permute-start(bf16[16,128]{1,0:T(8,128)(2,1)S(1)} %get-tuple-element.179), channel_id=1, source_target_pairs={{0,6},{1,7},{2,4},{3,5},{4,2},{5,3},{6,0},{7,1},{8,14},{9,15},{10,... | collective-permute-start | bytes 12296 | tf_op jit(solution)/shard_map/ppermute | solution.py:33
  17.9 3.4 %collective-permute-done.3.after = bf16[16,4096]{1,0:T(8,128)(2,1)S(1)} collective-permute-done((bf16[16,4096]{1,0:T(8,128)(2,1)S(1)}, bf16[16,4096]{1,0:T(8,128)(2,1)S(1)}, u32[]{:S(2)}, u32[]{:S(2)}) %collective-permute-start.3) | collective-permute-done | bytes 131104 | tf_op jit(solution)/shard_map/ppermute | solution.py:33
  21.2 1.5 collective-permute-start.5
  24.6 3.0 %collective-permute-done.5 = bf16[32,4096]{1,0:T(8,128)(2,1)S(1)} collective-permute-done((bf16[32,4096]{1,0:T(8,128)(2,1)S(1)}, bf16[32,4096]{1,0:T(8,128)(2,1)S(1)}, u32[]{:S(2)}, u32[]{:S(2)}) %collective-permute-start.5) | collective-permute-done | bytes 262176 | tf_op jit(solution)/shard_map/ppermute | solution.py:33
  28.3 1.5 collective-permute-start.10
  29.9 1.5 collective-permute-start.11
  31.4 4.6 %shard_map.127 = (bf16[8,192,4096]{2,1,0:T(8,128)(2,1)S(1)}, f32[8,128]{1,0:T(8,128)S(1)}) custom-call(bf16[8,192,4096]{2,1,0:T(8,128)(2,1)} %source, bf16[16,4096]{1,0:T(8,128)(2,1)S(1)} %collective-permute-done.3.after), custom_call_target="tpu_custom_call" | custom-call | bytes 12582912 | tf_op jit(solution)/shard_map/pallas_call | solution.py:274
  37.5 1.6 collective-permute-start.12
  39.7 3.1 %collective-permute-done.20 = bf16[16,4096]{1,0:T(8,128)(2,1)S(1)} collective-permute-done((bf16[16,4096]{1,0:T(8,128)(2,1)S(1)}, bf16[16,4096]{1,0:T(8,128)(2,1)S(1)}, u32[]{:S(2)}, u32[]{:S(2)}) %collective-permute-start.20) | collective-permute-done | bytes 131104 | tf_op jit(solution)/shard_map/ppermute | solution.py:33
  43.6 4.6 %shard_map.128 = (bf16[8,192,4096]{2,1,0:T(8,128)(2,1)S(1)}, f32[8,128]{1,0:T(8,128)S(1)}) custom-call(bf16[8,192,4096]{2,1,0:T(8,128)(2,1)} %source.1, f32[8,128]{1,0:T(8,128)S(1)} %get-tuple-element.104.after), custom_call_target="tpu_custom_call" | custom-call | bytes 12582912 | tf_op jit(solution)/shard_map/pallas_call | solution.py:274
  48.8 3.4 %collective-permute-done.21 = bf16[64,4096]{1,0:T(8,128)(2,1)S(1)} collective-permute-done((bf16[64,4096]{1,0:T(8,128)(2,1)S(1)}, bf16[64,4096]{1,0:T(8,128)(2,1)S(1)}, u32[]{:S(2)}, u32[]{:S(2)}) %collective-permute-start.21) | collective-permute-done | bytes 524320 | tf_op jit(solution)/shard_map/ppermute | solution.py:33
  52.2 4.2 %shard_map.129 = (bf16[8,96,4096]{2,1,0:T(8,128)(2,1)S(1)}, bf16[2,256,384]{2,1,0:T(8,128)(2,1)S(1)}, bf16[2,384,256]{2,1,0:T(8,128)(2,1)S(1)}, f32[8,1,96]{2,1,0:T(1,128)S(1)}) custom-call(bf16[64,4096]{1,0:T(8,128)(2,1)S(1)} %constant_dynamic-update-slice_fusion.refs_0_, bf16[128,4096]{1,0:T(8,128)(2,1)S(1)} %constant_dynamic-update-slice_fusion.3.refs_1_, ...), custom_call_target="tpu_custom_call" | custom-call | flops 1610612736 | bytes 11705344 | tf_op jit(solution)/shard_map/pallas_call | solution.py:254
  57.0 10.3 %shard_map.130 = (f32[8,192,96]{2,1,0:T(8,128)S(1)}, f32[8,192,96]{2,1,0:T(8,128)S(1)}, bf16[8,96,192]{2,1,0:T(8,128)(2,1)S(1)}, bf16[8,192,96]{2,1,0:T(8,128)(2,1)S(1)}) custom-call(bf16[8,96,4096]{2,1,0:T(8,128)(2,1)S(1)} %get-tuple-element.113.x_ref, f32[8,1,96]{2,1,0:T(1,128)S(1)} %get-tuple-element.114.prob_ref, ...), custom_call_target="tpu_custom_call" | custom-call | flops 2415919104 | bytes 33229824 | tf_op jit(solution)/shard_map/pallas_call | solution.py:254
  67.3 4.0 %collective-permute-done.22.own1 = bf16[128,4096]{1,0:T(8,128)(2,1)S(1)} collective-permute-done((bf16[128,4096]{1,0:T(8,128)(2,1)S(1)}, bf16[128,4096]{1,0:T(8,128)(2,1)S(1)}, u32[]{:S(2)}, u32[]{:S(2)}) %collective-permute-start.22) | collective-permute-done | bytes 1048608 | tf_op jit(solution)/shard_map/ppermute | solution.py:33
  71.3 7.8 %shard_map.131 = (bf16[256,4096]{1,0:T(8,128)(2,1)S(1)}, bf16[256,4096]{1,0:T(8,128)(2,1)S(1)}) custom-call(bf16[2,256,384]{2,1,0:T(8,128)(2,1)S(1)} %get-tuple-element.110.put_ref, bf16[8,96,192]{2,1,0:T(8,128)(2,1)S(1)} %get-tuple-element.119.refs_0_, bf16[8,192,4096]{2,1,0:T(8,128)(2,1)} %down_ref.1), custom_call_target="tpu_custom_call" | custom-call | flops 2818572288 | bytes 17465344 | tf_op jit(solution)/shard_map/pallas_call | solution.py:254
  79.8 4.6 %shard_map.132 = (bf16[8,96,4096]{2,1,0:T(8,128)(2,1)S(1)}, bf16[8,96,4096]{2,1,0:T(8,128)(2,1)}) custom-call(bf16[128,4096]{1,0:T(8,128)(2,1)S(1)} %constant_dynamic-update-slice_fusion.21.own0, bf16[128,4096]{1,0:T(8,128)(2,1)S(1)} %collective-permute-done.22.own1, bf16[128,4096]{1,0:T(8,128)(2,1)S(1)} %collective-permute-done.23.other0, ...), custom_call_target="tpu_custom_call" | custom-call | flops 1610612736 | bytes 17170432 | tf_op jit(solution)/shard_map/pallas_call | solution.py:254
  85.2 8.5 %shard_map.133 = (bf16[8,96,192]{2,1,0:T(8,128)(2,1)S(1)}, bf16[8,96,192]{2,1,0:T(8,128)(2,1)S(1)}, bf16[8,192,96]{2,1,0:T(8,128)(2,1)S(1)}, bf16[8,192,96]{2,1,0:T(8,128)(2,1)S(1)}, bf16[2,256,128]{2,1,0:T(8,128)(2,1)S(1)}) custom-call(bf16[8,96,4096]{2,1,0:T(8,128)(2,1)S(1)} %get-tuple-element.129.x_ref, ...), custom_call_target="tpu_custom_call" | custom-call | flops 1207959552 | bytes 21859328 | tf_op jit(solution)/shard_map/pallas_call | solution.py:254
  93.7 4.8 %shard_map.134 = (bf16[256,2048]{1,0:T(8,128)(2,1)S(1)}, bf16[256,2048]{1,0:T(8,128)(2,1)S(1)}) custom-call(bf16[2,256,384]{2,1,0:T(8,128)(2,1)S(1)} %get-tuple-element.110.put_ref, bf16[8,96,192]{2,1,0:T(8,128)(2,1)S(1)} %get-tuple-element.138.refs_0_, bf16[8,96,192]{2,1,0:T(8,128)(2,1)S(1)} %get-tuple-element.139.refs_1_, ...), custom_call_target="tpu_custom_call" | custom-call | flops 2013265920 | bytes 28246016 | tf_op jit(solution)/shard_map/pallas_call | solution.py:254
  99.5 5.2 %shard_map.135 = (bf16[256,2176]{1,0:T(8,128)(2,1)S(1)}, bf16[256,2176]{1,0:T(8,128)(2,1)S(1)}) custom-call(bf16[2,256,384]{2,1,0:T(8,128)(2,1)S(1)} %get-tuple-element.110.put_ref, bf16[8,96,192]{2,1,0:T(8,128)(2,1)S(1)} %get-tuple-element.138.refs_0_, bf16[8,96,192]{2,1,0:T(8,128)(2,1)S(1)} %get-tuple-element.139.refs_1_, ...), custom_call_target="tpu_custom_call" | custom-call | flops 2013265920 | bytes 28508160 | tf_op jit(solution)/shard_map/pallas_call | solution.py:254
  106.8 10.5 %shard_map.136 = bf16[8,192,4096]{2,1,0:T(8,128)(2,1)} custom-call(bf16[8,96,4096]{2,1,0:T(8,128)(2,1)} %get-tuple-element.148.x_ref, bf16[8,192,96]{2,1,0:T(8,128)(2,1)S(1)} %get-tuple-element.149.left), custom_call_target="tpu_custom_call" | custom-call | flops 1207959552 | bytes 19169280 | tf_op jit(solution)/shard_map/pallas_call | solution.py:254
  117.4 2.4 %collective-permute-done.29 = bf16[128,2048]{1,0:T(8,128)(2,1)S(1)} collective-permute-done((bf16[128,2048]{1,0:T(8,128)(2,1)S(1)}, bf16[128,2048]{1,0:T(8,128)(2,1)S(1)}, u32[]{:S(2)}, u32[]{:S(2)}) %collective-permute-start.29) | collective-permute-done | bytes 524320 | tf_op jit(solution)/shard_map/ppermute | solution.py:33
  121.3 10.5 %shard_map.137 = bf16[8,192,4096]{2,1,0:T(8,128)(2,1)} custom-call(bf16[8,96,4096]{2,1,0:T(8,128)(2,1)} %copy-done, bf16[8,192,96]{2,1,0:T(8,128)(2,1)S(1)} %get-tuple-element.158.left), custom_call_target="tpu_custom_call" | custom-call | flops 1207959552 | bytes 19169280 | tf_op jit(solution)/shard_map/pallas_call | solution.py:254
  132.2 1.7 %collective-permute-start.34 = (bf16[16,4096]{1,0:T(8,128)(2,1)S(1)}, bf16[16,4096]{1,0:T(8,128)(2,1)S(1)}, u32[]{:S(2)}, u32[]{:S(2)}) collective-permute-start(bf16[16,4096]{1,0:T(8,128)(2,1)S(1)} %add_convert_fusion.9), channel_id=1, source_target_pairs={{0,4},{1,5},{2,6},{3,7},{4,0},{5,1},{6,2},{7,3},{8,12},{9,13},{10,... | collective-permute-start | bytes 393224 | tf_op jit(solution)/shard_map/ppermute | solution.py:33
  134.8 1.2 collective-permute-start.36
  135.9 10.6 %shard_map.138 = bf16[8,192,4096]{2,1,0:T(8,128)(2,1)} custom-call(bf16[8,96,4096]{2,1,0:T(8,128)(2,1)} %copy-done, bf16[8,192,96]{2,1,0:T(8,128)(2,1)S(1)} %get-tuple-element.166.left), custom_call_target="tpu_custom_call" | custom-call | flops 1207959552 | bytes 19169280 | tf_op jit(solution)/shard_map/pallas_call | solution.py:254
  148.3 2.1 %collective-permute-start.37 = (bf16[16,2048]{1,0:T(8,128)(2,1)S(1)}, bf16[16,2048]{1,0:T(8,128)(2,1)S(1)}, u32[]{:S(2)}, u32[]{:S(2)}) collective-permute-start(bf16[16,2048]{1,0:T(8,128)(2,1)S(1)} %add_convert_fusion.14), channel_id=1, source_target_pairs={{0,4},{1,5},{2,6},{3,7},{4,0},{5,1},{6,2},{7,3},{8,12},{9,13},{10,... | collective-permute-start | bytes 196616 | tf_op jit(solution)/shard_map/ppermute | solution.py:33
  150.4 2.1 %collective-permute-done.38 = bf16[32,2176]{1,0:T(8,128)(2,1)S(1)} collective-permute-done((bf16[32,2176]{1,0:T(8,128)(2,1)S(1)}, bf16[32,2176]{1,0:T(8,128)(2,1)S(1)}, u32[]{:S(2)}, u32[]{:S(2)}) %collective-permute-start.38) | collective-permute-done | bytes 139296 | tf_op jit(solution)/shard_map/ppermute | solution.py:33
  152.5 3.7 %collective-permute-start.39 = (bf16[16,2176]{1,0:T(8,128)(2,1)S(1)}, bf16[16,2176]{1,0:T(8,128)(2,1)S(1)}, u32[]{:S(2)}, u32[]{:S(2)}) collective-permute-start(bf16[16,2176]{1,0:T(8,128)(2,1)S(1)} %add_convert_fusion.12), channel_id=1, source_target_pairs={{0,4},{1,5},{2,6},{3,7},{4,0},{5,1},{6,2},{7,3},{8,12},{9,13},{10,... | collective-permute-start | bytes 208904 | tf_op jit(solution)/shard_map/ppermute | solution.py:33
  156.2 2.6 %collective-permute-done.39 = bf16[16,2176]{1,0:T(8,128)(2,1)S(1)} collective-permute-done((bf16[16,2176]{1,0:T(8,128)(2,1)S(1)}, bf16[16,2176]{1,0:T(8,128)(2,1)S(1)}, u32[]{:S(2)}, u32[]{:S(2)}) %collective-permute-start.39) | collective-permute-done | bytes 69664 | tf_op jit(solution)/shard_map/ppermute | solution.py:33
  (123 shorter events, 23.8 us)
Async XLA Ops:
  0.6 15.7 %collective-permute-start = (bf16[16,4096]{1,0:T(8,128)(2,1)}, bf16[16,4096]{1,0:T(8,128)(2,1)S(1)}, u32[]{:S(2)}, u32[]{:S(2)}) collective-permute-start(bf16[16,4096]{1,0:T(8,128)(2,1)} %param.8), channel_id=1, source_target_pairs={{0,8},{1,17},{2,10},{3,19},{4,12},{5,21},{6,14},{7,23},{8,0},{9,25... | collective-permute-start | bytes 393224 | tf_op jit(solution)/shard_map/ppermute | solution.py:33
  3.6 8.9 %collective-permute-start.1 = (bf16[16,4096]{1,0:T(8,128)(2,1)}, bf16[16,4096]{1,0:T(8,128)(2,1)S(1)}, u32[]{:S(2)}, u32[]{:S(2)}) collective-permute-start(bf16[16,4096]{1,0:T(8,128)(2,1)} %param.8), channel_id=1, source_target_pairs={{0,2},{1,3},{2,0},{3,1},{4,6},{5,7},{6,4},{7,5},{8,10},{9,11},{10,... | collective-permute-start | bytes 393224 | tf_op jit(solution)/shard_map/ppermute | solution.py:33
  5.2 11.0 %collective-permute-start.2 = (bf16[16,4096]{1,0:T(8,128)(2,1)}, bf16[16,4096]{1,0:T(8,128)(2,1)S(1)}, u32[]{:S(2)}, u32[]{:S(2)}) collective-permute-start(bf16[16,4096]{1,0:T(8,128)(2,1)} %param.8), channel_id=1, source_target_pairs={{0,4},{1,5},{2,6},{3,7},{4,0},{5,1},{6,2},{7,3},{8,12},{9,13},{10,... | collective-permute-start | bytes 393224 | tf_op jit(solution)/shard_map/ppermute | solution.py:33
  10.6 12.2 %collective-permute-start.6 = (bf16[16,128]{1,0:T(8,128)(2,1)S(1)}, bf16[16,128]{1,0:T(8,128)(2,1)S(1)}, u32[]{:S(2)}, u32[]{:S(2)}) collective-permute-start(bf16[16,128]{1,0:T(8,128)(2,1)S(1)} %get-tuple-element.179), channel_id=1, source_target_pairs={{0,4},{1,5},{2,6},{3,7},{4,0},{5,1},{6,2},{7,3},{8,12},{9,13},{10,... | collective-permute-start | bytes 12296 | tf_op jit(solution)/shard_map/ppermute | solution.py:33
  10.9 11.9 %collective-permute-start.7 = (bf16[16,128]{1,0:T(8,128)(2,1)S(1)}, bf16[16,128]{1,0:T(8,128)(2,1)S(1)}, u32[]{:S(2)}, u32[]{:S(2)}) collective-permute-start(bf16[16,128]{1,0:T(8,128)(2,1)S(1)} %get-tuple-element.179), channel_id=1, source_target_pairs={{0,2},{1,3},{2,0},{3,1},{4,6},{5,7},{6,4},{7,5},{8,10},{9,11},{10,... | collective-permute-start | bytes 12296 | tf_op jit(solution)/shard_map/ppermute | solution.py:33
  12.6 11.1 %collective-permute-start.8 = (bf16[16,128]{1,0:T(8,128)(2,1)S(1)}, bf16[16,128]{1,0:T(8,128)(2,1)S(1)}, u32[]{:S(2)}, u32[]{:S(2)}) collective-permute-start(bf16[16,128]{1,0:T(8,128)(2,1)S(1)} %get-tuple-element.179), channel_id=1, source_target_pairs={{0,6},{1,7},{2,4},{3,5},{4,2},{5,3},{6,0},{7,1},{8,14},{9,15},{10,... | collective-permute-start | bytes 12296 | tf_op jit(solution)/shard_map/ppermute | solution.py:33
  16.3 8.3 %collective-permute-start.4 = (bf16[32,4096]{1,0:T(8,128)(2,1)S(1)}, bf16[32,4096]{1,0:T(8,128)(2,1)S(1)}, u32[]{:S(2)}, u32[]{:S(2)}) collective-permute-start(bf16[32,4096]{1,0:T(8,128)(2,1)S(1)} %pad_maximum_fusion.2), channel_id=1, source_target_pairs={{0,8},{1,17},{2,10},{3,19},{4,12},{5,21},{6,14},{7,23},{8,0},{9,25... | collective-permute-start | bytes 786440 | tf_op jit(solution)/shard_map/ppermute | solution.py:33
  21.2 6.4 %collective-permute-start.5 = (bf16[32,4096]{1,0:T(8,128)(2,1)S(1)}, bf16[32,4096]{1,0:T(8,128)(2,1)S(1)}, u32[]{:S(2)}, u32[]{:S(2)}) collective-permute-start(bf16[32,4096]{1,0:T(8,128)(2,1)S(1)} %pad_maximum_fusion.3), channel_id=1, source_target_pairs={{0,16},{1,9},{2,18},{3,11},{4,20},{5,13},{6,22},{7,15},{8,24},{9,1... | collective-permute-start | bytes 786440 | tf_op jit(solution)/shard_map/ppermute | solution.py:33
  22.8 16.4 %collective-permute-start.18 = (bf16[16,4096]{1,0:T(8,128)(2,1)S(1)}, bf16[16,4096]{1,0:T(8,128)(2,1)S(1)}, u32[]{:S(2)}, u32[]{:S(2)}) collective-permute-start(bf16[16,4096]{1,0:T(8,128)(2,1)S(1)} %copy-done.1), channel_id=1, source_target_pairs={{0,4},{1,5},{2,6},{3,7},{4,0},{5,1},{6,2},{7,3},{8,12},{9,13},{10,... | collective-permute-start | bytes 393224 | tf_op jit(solution)/shard_map/ppermute | solution.py:33
  22.9 16.9 %collective-permute-start.19 = (bf16[16,4096]{1,0:T(8,128)(2,1)S(1)}, bf16[16,4096]{1,0:T(8,128)(2,1)S(1)}, u32[]{:S(2)}, u32[]{:S(2)}) collective-permute-start(bf16[16,4096]{1,0:T(8,128)(2,1)S(1)} %copy-done.1), channel_id=1, source_target_pairs={{0,2},{1,3},{2,0},{3,1},{4,6},{5,7},{6,4},{7,5},{8,10},{9,11},{10,... | collective-permute-start | bytes 393224 | tf_op jit(solution)/shard_map/ppermute | solution.py:33
  27.7 8.7 %collective-permute-start.9 = (bf16[16,4096]{1,0:T(8,128)(2,1)S(1)}, bf16[16,4096]{1,0:T(8,128)(2,1)S(1)}, u32[]{:S(2)}, u32[]{:S(2)}) collective-permute-start(bf16[16,4096]{1,0:T(8,128)(2,1)S(1)} %collective-permute-done.3.after), channel_id=1, source_target_pairs={{0,8},{1,17},{2,10},{3,19},{4,12},{5,21},{6,14},{7,23},{8,0},{9,25... | collective-permute-start | bytes 393224 | tf_op jit(solution)/shard_map/ppermute | solution.py:33
  28.3 9.2 %collective-permute-start.10 = (bf16[64,4096]{1,0:T(8,128)(2,1)S(1)}, bf16[64,4096]{1,0:T(8,128)(2,1)S(1)}, u32[]{:S(2)}, u32[]{:S(2)}) collective-permute-start(bf16[64,4096]{1,0:T(8,128)(2,1)S(1)} %pad_maximum_fusion), channel_id=1, source_target_pairs={{0,16},{1,9},{2,18},{3,11},{4,20},{5,13},{6,22},{7,15},{8,24},{9,1... | collective-permute-start | bytes 1572872 | tf_op jit(solution)/shard_map/ppermute | solution.py:33
  36.0 6.8 %collective-permute-start.20 = (bf16[16,4096]{1,0:T(8,128)(2,1)S(1)}, bf16[16,4096]{1,0:T(8,128)(2,1)S(1)}, u32[]{:S(2)}, u32[]{:S(2)}) collective-permute-start(bf16[16,4096]{1,0:T(8,128)(2,1)S(1)} %copy-done.1), channel_id=1, source_target_pairs={{0,6},{1,7},{2,4},{3,5},{4,2},{5,3},{6,0},{7,1},{8,14},{9,15},{10,... | collective-permute-start | bytes 393224 | tf_op jit(solution)/shard_map/ppermute | solution.py:33
  36.3 15.9 %collective-permute-start.14 = (bf16[64,4096]{1,0:T(8,128)(2,1)S(1)}, bf16[64,4096]{1,0:T(8,128)(2,1)S(1)}, u32[]{:S(2)}, u32[]{:S(2)}) collective-permute-start(bf16[64,4096]{1,0:T(8,128)(2,1)S(1)} %constant_dynamic-update-slice_fusion.refs_0_), channel_id=1, source_target_pairs={{0,1},{1,0},{2,3},{3,2},{4,5},{5,4},{6,7},{7,6},{8,9},{9,8},{10,11... | collective-permute-start | bytes 1572872 | tf_op jit(solution)/shard_map/ppermute | solution.py:33
  37.5 10.7 %collective-permute-start.12 = (bf16[32,4096]{1,0:T(8,128)(2,1)S(1)}, bf16[32,4096]{1,0:T(8,128)(2,1)S(1)}, u32[]{:S(2)}, u32[]{:S(2)}) collective-permute-start(bf16[32,4096]{1,0:T(8,128)(2,1)S(1)} %pad_maximum_fusion.4), channel_id=1, source_target_pairs={{0,16},{1,9},{2,18},{3,11},{4,20},{5,13},{6,22},{7,15},{8,24},{9,1... | collective-permute-start | bytes 786440 | tf_op jit(solution)/shard_map/ppermute | solution.py:33
  39.2 9.0 %collective-permute-start.13 = (bf16[128,128]{1,0:T(8,128)(2,1)S(1)}, bf16[128,128]{1,0:T(8,128)(2,1)S(1)}, u32[]{:S(2)}, u32[]{:S(2)}) collective-permute-start(bf16[128,128]{1,0:T(8,128)(2,1)S(1)} %get-tuple-element.181), channel_id=1, source_target_pairs={{0,16},{1,9},{2,18},{3,11},{4,20},{5,13},{6,22},{7,15},{8,24},{9,1... | collective-permute-start | bytes 98312 | tf_op jit(solution)/shard_map/ppermute | solution.py:33
  39.7 12.5 %collective-permute-start.15 = (bf16[128,4096]{1,0:T(8,128)(2,1)S(1)}, bf16[128,4096]{1,0:T(8,128)(2,1)S(1)}, u32[]{:S(2)}, u32[]{:S(2)}) collective-permute-start(bf16[128,4096]{1,0:T(8,128)(2,1)S(1)} %constant_dynamic-update-slice_fusion.3.refs_1_), channel_id=1, source_target_pairs={{0,1},{1,0},{2,3},{3,2},{4,5},{5,4},{6,7},{7,6},{8,9},{9,8},{10,11... | collective-permute-start | bytes 3145736 | tf_op jit(solution)/shard_map/ppermute | solution.py:33
  42.9 9.2 %collective-permute-start.21 = (bf16[64,4096]{1,0:T(8,128)(2,1)S(1)}, bf16[64,4096]{1,0:T(8,128)(2,1)S(1)}, u32[]{:S(2)}, u32[]{:S(2)}) collective-permute-start(bf16[64,4096]{1,0:T(8,128)(2,1)S(1)} %pad_maximum_fusion.1), channel_id=1, source_target_pairs={{0,8},{1,17},{2,10},{3,19},{4,12},{5,21},{6,14},{7,23},{8,0},{9,25... | collective-permute-start | bytes 1572872 | tf_op jit(solution)/shard_map/ppermute | solution.py:33
  56.4 14.9 %collective-permute-start.22 = (bf16[128,4096]{1,0:T(8,128)(2,1)S(1)}, bf16[128,4096]{1,0:T(8,128)(2,1)S(1)}, u32[]{:S(2)}, u32[]{:S(2)}) collective-permute-start(bf16[128,4096]{1,0:T(8,128)(2,1)S(1)} %constant_dynamic-update-slice_fusion.21.own0), channel_id=1, source_target_pairs={{0,16},{1,9},{2,18},{3,11},{4,20},{5,13},{6,22},{7,15},{8,24},{9,1... | collective-permute-start | bytes 3145736 | tf_op jit(solution)/shard_map/ppermute | solution.py:33
  57.0 14.3 %collective-permute-start.23 = (bf16[128,4096]{1,0:T(8,128)(2,1)S(1)}, bf16[128,4096]{1,0:T(8,128)(2,1)S(1)}, u32[]{:S(2)}, u32[]{:S(2)}) collective-permute-start(bf16[128,4096]{1,0:T(8,128)(2,1)S(1)} %constant_dynamic-update-slice_fusion.21.own0), channel_id=1, source_target_pairs={{0,1},{1,0},{2,3},{3,2},{4,5},{5,4},{6,7},{7,6},{8,9},{9,8},{10,11... | collective-permute-start | bytes 3145736 | tf_op jit(solution)/shard_map/ppermute | solution.py:33
  71.3 7.8 %collective-permute-start.24 = (bf16[128,4096]{1,0:T(8,128)(2,1)S(1)}, bf16[128,4096]{1,0:T(8,128)(2,1)S(1)}, u32[]{:S(2)}, u32[]{:S(2)}) collective-permute-start(bf16[128,4096]{1,0:T(8,128)(2,1)S(1)} %collective-permute-done.22.own1), channel_id=1, source_target_pairs={{0,1},{1,0},{2,3},{3,2},{4,5},{5,4},{6,7},{7,6},{8,9},{9,8},{10,11... | collective-permute-start | bytes 3145736 | tf_op jit(solution)/shard_map/ppermute | solution.py:33
  84.6 14.9 %collective-permute-start.26 = (bf16[128,4096]{1,0:T(8,128)(2,1)S(1)}, bf16[128,4096]{1,0:T(8,128)(2,1)S(1)}, u32[]{:S(2)}, u32[]{:S(2)}) collective-permute-start(bf16[128,4096]{1,0:T(8,128)(2,1)S(1)} %add_convert_fusion), channel_id=1, source_target_pairs={{0,16},{1,9},{2,18},{3,11},{4,20},{5,13},{6,22},{7,15},{8,24},{9,1... | collective-permute-start | bytes 3145736 | tf_op jit(solution)/shard_map/ppermute | solution.py:33
  104.7 15.1 %collective-permute-start.27 = (bf16[256,2176]{1,0:T(8,128)(2,1)S(1)}, bf16[256,2176]{1,0:T(8,128)(2,1)S(1)}, u32[]{:S(2)}, u32[]{:S(2)}) collective-permute-start(bf16[256,2176]{1,0:T(8,128)(2,1)S(1)} %get-tuple-element.141), channel_id=1, source_target_pairs={{0,1},{1,0},{2,3},{3,2},{4,5},{5,4},{6,7},{7,6},{8,9},{9,8},{10,11... | collective-permute-start | bytes 3342344 | tf_op jit(solution)/shard_map/ppermute | solution.py:33
  104.9 14.8 %collective-permute-start.29 = (bf16[128,2048]{1,0:T(8,128)(2,1)S(1)}, bf16[128,2048]{1,0:T(8,128)(2,1)S(1)}, u32[]{:S(2)}, u32[]{:S(2)}) collective-permute-start(bf16[128,2048]{1,0:T(8,128)(2,1)S(1)} %add_convert_fusion.3), channel_id=1, source_target_pairs={{0,16},{1,9},{2,18},{3,11},{4,20},{5,13},{6,22},{7,15},{8,24},{9,1... | collective-permute-start | bytes 1572872 | tf_op jit(solution)/shard_map/ppermute | solution.py:33
  106.2 13.5 %collective-permute-start.30 = (bf16[64,4096]{1,0:T(8,128)(2,1)S(1)}, bf16[64,4096]{1,0:T(8,128)(2,1)S(1)}, u32[]{:S(2)}, u32[]{:S(2)}) collective-permute-start(bf16[64,4096]{1,0:T(8,128)(2,1)S(1)} %add_convert_fusion.2), channel_id=1, source_target_pairs={{0,8},{1,17},{2,10},{3,19},{4,12},{5,21},{6,14},{7,23},{8,0},{9,25... | collective-permute-start | bytes 1572872 | tf_op jit(solution)/shard_map/ppermute | solution.py:33
  120.1 11.8 %collective-permute-start.31 = (bf16[128,2176]{1,0:T(8,128)(2,1)S(1)}, bf16[128,2176]{1,0:T(8,128)(2,1)S(1)}, u32[]{:S(2)}, u32[]{:S(2)}) collective-permute-start(bf16[128,2176]{1,0:T(8,128)(2,1)S(1)} %add_convert_fusion.1), channel_id=1, source_target_pairs={{0,16},{1,9},{2,18},{3,11},{4,20},{5,13},{6,22},{7,15},{8,24},{9,1... | collective-permute-start | bytes 1671176 | tf_op jit(solution)/shard_map/ppermute | solution.py:33
  120.9 11.0 %collective-permute-start.32 = (bf16[64,2048]{1,0:T(8,128)(2,1)S(1)}, bf16[64,2048]{1,0:T(8,128)(2,1)S(1)}, u32[]{:S(2)}, u32[]{:S(2)}) collective-permute-start(bf16[64,2048]{1,0:T(8,128)(2,1)S(1)} %add_convert_fusion.6), channel_id=1, source_target_pairs={{0,8},{1,17},{2,10},{3,19},{4,12},{5,21},{6,14},{7,23},{8,0},{9,25... | collective-permute-start | bytes 786440 | tf_op jit(solution)/shard_map/ppermute | solution.py:33
  121.3 10.6 %collective-permute-start.33 = (bf16[32,4096]{1,0:T(8,128)(2,1)S(1)}, bf16[32,4096]{1,0:T(8,128)(2,1)S(1)}, u32[]{:S(2)}, u32[]{:S(2)}) collective-permute-start(bf16[32,4096]{1,0:T(8,128)(2,1)S(1)} %add_convert_fusion.5), channel_id=1, source_target_pairs={{0,2},{1,3},{2,0},{3,1},{4,6},{5,7},{6,4},{7,5},{8,10},{9,11},{10,... | collective-permute-start | bytes 786440 | tf_op jit(solution)/shard_map/ppermute | solution.py:33
  132.2 14.3 %collective-permute-start.34 = (bf16[16,4096]{1,0:T(8,128)(2,1)S(1)}, bf16[16,4096]{1,0:T(8,128)(2,1)S(1)}, u32[]{:S(2)}, u32[]{:S(2)}) collective-permute-start(bf16[16,4096]{1,0:T(8,128)(2,1)S(1)} %add_convert_fusion.9), channel_id=1, source_target_pairs={{0,4},{1,5},{2,6},{3,7},{4,0},{5,1},{6,2},{7,3},{8,12},{9,13},{10,... | collective-permute-start | bytes 393224 | tf_op jit(solution)/shard_map/ppermute | solution.py:33
  133.8 13.4 %collective-permute-start.35 = (bf16[64,2176]{1,0:T(8,128)(2,1)S(1)}, bf16[64,2176]{1,0:T(8,128)(2,1)S(1)}, u32[]{:S(2)}, u32[]{:S(2)}) collective-permute-start(bf16[64,2176]{1,0:T(8,128)(2,1)S(1)} %add_convert_fusion.4), channel_id=1, source_target_pairs={{0,8},{1,17},{2,10},{3,19},{4,12},{5,21},{6,14},{7,23},{8,0},{9,25... | collective-permute-start | bytes 835592 | tf_op jit(solution)/shard_map/ppermute | solution.py:33
  134.8 12.5 %collective-permute-start.36 = (bf16[32,2048]{1,0:T(8,128)(2,1)S(1)}, bf16[32,2048]{1,0:T(8,128)(2,1)S(1)}, u32[]{:S(2)}, u32[]{:S(2)}) collective-permute-start(bf16[32,2048]{1,0:T(8,128)(2,1)S(1)} %add_convert_fusion.10), channel_id=1, source_target_pairs={{0,2},{1,3},{2,0},{3,1},{4,6},{5,7},{6,4},{7,5},{8,10},{9,11},{10,... | collective-permute-start | bytes 393224 | tf_op jit(solution)/shard_map/ppermute | solution.py:33
  148.3 7.9 %collective-permute-start.37 = (bf16[16,2048]{1,0:T(8,128)(2,1)S(1)}, bf16[16,2048]{1,0:T(8,128)(2,1)S(1)}, u32[]{:S(2)}, u32[]{:S(2)}) collective-permute-start(bf16[16,2048]{1,0:T(8,128)(2,1)S(1)} %add_convert_fusion.14), channel_id=1, source_target_pairs={{0,4},{1,5},{2,6},{3,7},{4,0},{5,1},{6,2},{7,3},{8,12},{9,13},{10,... | collective-permute-start | bytes 196616 | tf_op jit(solution)/shard_map/ppermute | solution.py:33
  (10 other events, 75.0 us)

commit v10 on v9

--- a/solution.py
+++ b/solution.py
@@ -258,7 +258,7 @@
         out_specs=outs,
         out_shape=shapes,
         scratch_shapes=scratch,
-        compiler_params=pltpu.CompilerParams(vmem_limit_bytes=14 * MIB),
+        compiler_params=pltpu.CompilerParams(vmem_limit_bytes=12 * MIB),
         cost_estimate=pl.CostEstimate(flops=flops, bytes_accessed=moved, transcendentals=0),
     )(*args)
 
@@ -388,7 +388,7 @@
     shapes = [bf16(experts, hidden, width)] * (left.shape[1] // hidden)
     flops = 2 * experts * rows * left.shape[1] * width
     ins, outs = [each(x), each(left)], [each(s) for s in shapes]
-    return call(grad_kernel, experts, ins, (in_hbm(x), left), outs, shapes, flops=flops)
+    return call(grad_kernel, experts, ins, (near_core(x), left), outs, shapes, flops=flops)
 
 
 def dense_body(
@@ -456,7 +456,7 @@
     middle_rows = rows_of(middle_rows, second1)
     middle_other = swap(middle_rows, CORE)
     grads = rows_of(cotangent, *grads)
-    grads = rows_of(grads, swap(grads, X, Y))
+    first_grads = swap(grads, X, Y)
     last = rows_of(last, second2)
     last_other = swap(last, CORE)
     x, put, pick, prob_rows = route_call(
@@ -468,7 +468,8 @@
         local,
         tok_count,
     )
-    x, grads = together(x, grads)
+    x, first_grads = together(x, first_grads)
+    grads = rows_of(grads, first_grads)
     far_grads = swap(grads, Y, X)
     grads_other = swap(grads, CORE)
 

time: 161 us -> 158 us (0.981)
  Pallas kernels: 86 us -> 76.2 us
  other arithmetic: 5.82 us -> 10.8 us
    pallas_call x10, Pallas kernels: 76.9 us -> 67.1 us  [call(): pl.pallas_call(kernel, grid=(grid,), in_specs=ins, out_specs=outs, out_sh...]
    convert_element_type x15, other arithmetic: 2.26 us -> 7.29 us  [add(): return total.astype(jnp.bfloat16)]
    unnamed x23 -> x25, local copies, waits for them, and re-layouts: 3.26 us -> 3.26 us
  transfers between devices with their start and end apart: 40 -> 40, of which waited for: 11 -> 15; matrix products, arithmetic and copies ran while one was open for 4% -> 5% of each run, Pallas kernels for 51% -> 49%
where the time goes in v10:
time: 158 us; the launch traced here: 157 us
  Pallas kernels  76.2 us (48%)
  starting transfers between devices  38.4 us (24%)
  waiting for transfers between devices  26.9 us (17%)
  other arithmetic  10.8 us (7%)
  local copies, waits for them, and re-layouts  3.38 us (2%)
    pallas_call x10, Pallas kernels, call(): pl.pallas_call(kernel, grid=(grid,), in_specs=ins, out_specs=outs, out_sh...  67.1 us
    ppermute x40, starting transfers between devices, swap(): return lax.ppermute(values, AXES, pairs)  38.4 us
    ppermute x40, waiting for transfers between devices, swap(): return lax.ppermute(values, AXES, pairs)  26.9 us
    pallas_call x2, Pallas kernels, fetch_call(): pl.pallas_call(fetch_kernel, in_specs=[pl.BlockSpec(memory_space=pl.ANY)]...  9.17 us
    convert_element_type x15, other arithmetic, add(): return total.astype(jnp.bfloat16)  7.29 us
    unnamed x25, local copies, waits for them, and re-layouts  3.26 us
  transfers between devices with their start and end apart: 40, of which 15 were waited for; matrix products, arithmetic and copies ran while one was open for 5% of the time, Pallas kernels for 49%

profile of v10, /device:TPU:0, one launch (start us, length us, event | category | flops | bytes accessed | tf_op | source)
XLA Modules:
  0.0 157.0 jit_solution(8465271314854217802)
XLA Ops:
  0.6 3.0 %collective-permute-start = (bf16[16,4096]{1,0:T(8,128)(2,1)}, bf16[16,4096]{1,0:T(8,128)(2,1)S(1)}, u32[]{:S(2)}, u32[]{:S(2)}) collective-permute-start(bf16[16,4096]{1,0:T(8,128)(2,1)} %param.8), channel_id=1, source_target_pairs={{0,8},{1,17},{2,10},{3,19},{4,12},{5,21},{6,14},{7,23},{8,0},{9,25... | collective-permute-start | bytes 393224 | tf_op jit(solution)/shard_map/ppermute | solution.py:33
  3.6 1.6 %collective-permute-start.1 = (bf16[16,4096]{1,0:T(8,128)(2,1)}, bf16[16,4096]{1,0:T(8,128)(2,1)S(1)}, u32[]{:S(2)}, u32[]{:S(2)}) collective-permute-start(bf16[16,4096]{1,0:T(8,128)(2,1)} %param.8), channel_id=1, source_target_pairs={{0,2},{1,3},{2,0},{3,1},{4,6},{5,7},{6,4},{7,5},{8,10},{9,11},{10,... | collective-permute-start | bytes 393224 | tf_op jit(solution)/shard_map/ppermute | solution.py:33
  5.2 2.6 %collective-permute-start.2 = (bf16[16,4096]{1,0:T(8,128)(2,1)}, bf16[16,4096]{1,0:T(8,128)(2,1)S(1)}, u32[]{:S(2)}, u32[]{:S(2)}) collective-permute-start(bf16[16,4096]{1,0:T(8,128)(2,1)} %param.8), channel_id=1, source_target_pairs={{0,4},{1,5},{2,6},{3,7},{4,0},{5,1},{6,2},{7,3},{8,12},{9,13},{10,... | collective-permute-start | bytes 393224 | tf_op jit(solution)/shard_map/ppermute | solution.py:33
  12.6 3.7 %collective-permute-start.8 = (bf16[16,128]{1,0:T(8,128)(2,1)S(1)}, bf16[16,128]{1,0:T(8,128)(2,1)S(1)}, u32[]{:S(2)}, u32[]{:S(2)}) collective-permute-start(bf16[16,128]{1,0:T(8,128)(2,1)S(1)} %get-tuple-element.179), channel_id=1, source_target_pairs={{0,6},{1,7},{2,4},{3,5},{4,2},{5,3},{6,0},{7,1},{8,14},{9,15},{10,... | collective-permute-start | bytes 12296 | tf_op jit(solution)/shard_map/ppermute | solution.py:33
  17.9 3.4 %collective-permute-done.3.after = bf16[16,4096]{1,0:T(8,128)(2,1)S(1)} collective-permute-done((bf16[16,4096]{1,0:T(8,128)(2,1)S(1)}, bf16[16,4096]{1,0:T(8,128)(2,1)S(1)}, u32[]{:S(2)}, u32[]{:S(2)}) %collective-permute-start.3) | collective-permute-done | bytes 131104 | tf_op jit(solution)/shard_map/ppermute | solution.py:33
  21.2 1.5 collective-permute-start.5
  24.6 3.0 %collective-permute-done.5 = bf16[32,4096]{1,0:T(8,128)(2,1)S(1)} collective-permute-done((bf16[32,4096]{1,0:T(8,128)(2,1)S(1)}, bf16[32,4096]{1,0:T(8,128)(2,1)S(1)}, u32[]{:S(2)}, u32[]{:S(2)}) %collective-permute-start.5) | collective-permute-done | bytes 262176 | tf_op jit(solution)/shard_map/ppermute | solution.py:33
  28.3 1.5 collective-permute-start.10
  29.9 1.5 collective-permute-start.11
  31.4 4.6 %shard_map.127 = (bf16[8,192,4096]{2,1,0:T(8,128)(2,1)S(1)}, f32[8,128]{1,0:T(8,128)S(1)}) custom-call(bf16[8,192,4096]{2,1,0:T(8,128)(2,1)} %source, bf16[16,4096]{1,0:T(8,128)(2,1)S(1)} %collective-permute-done.3.after), custom_call_target="tpu_custom_call" | custom-call | bytes 12582912 | tf_op jit(solution)/shard_map/pallas_call | solution.py:274
  37.5 1.6 %collective-permute-start.12 = (bf16[32,4096]{1,0:T(8,128)(2,1)S(1)}, bf16[32,4096]{1,0:T(8,128)(2,1)S(1)}, u32[]{:S(2)}, u32[]{:S(2)}) collective-permute-start(bf16[32,4096]{1,0:T(8,128)(2,1)S(1)} %pad_maximum_fusion.4), channel_id=1, source_target_pairs={{0,16},{1,9},{2,18},{3,11},{4,20},{5,13},{6,22},{7,15},{8,24},{9,1... | collective-permute-start | bytes 786440 | tf_op jit(solution)/shard_map/ppermute | solution.py:33
  39.7 3.1 %collective-permute-done.20 = bf16[16,4096]{1,0:T(8,128)(2,1)S(1)} collective-permute-done((bf16[16,4096]{1,0:T(8,128)(2,1)S(1)}, bf16[16,4096]{1,0:T(8,128)(2,1)S(1)}, u32[]{:S(2)}, u32[]{:S(2)}) %collective-permute-start.20) | collective-permute-done | bytes 131104 | tf_op jit(solution)/shard_map/ppermute | solution.py:33
  43.5 4.6 %shard_map.128 = (bf16[8,192,4096]{2,1,0:T(8,128)(2,1)S(1)}, f32[8,128]{1,0:T(8,128)S(1)}) custom-call(bf16[8,192,4096]{2,1,0:T(8,128)(2,1)} %source.1, f32[8,128]{1,0:T(8,128)S(1)} %get-tuple-element.104.after), custom_call_target="tpu_custom_call" | custom-call | bytes 12582912 | tf_op jit(solution)/shard_map/pallas_call | solution.py:274
  50.3 4.0 %shard_map.129 = (bf16[8,96,4096]{2,1,0:T(8,128)(2,1)S(1)}, bf16[2,256,384]{2,1,0:T(8,128)(2,1)S(1)}, bf16[2,384,256]{2,1,0:T(8,128)(2,1)S(1)}, f32[8,1,96]{2,1,0:T(1,128)S(1)}) custom-call(bf16[64,4096]{1,0:T(8,128)(2,1)S(1)} %constant_dynamic-update-slice_fusion.refs_0_, bf16[128,4096]{1,0:T(8,128)(2,1)S(1)} %constant_dynamic-update-slice_fusion.3.refs_1_, ...), custom_call_target="tpu_custom_call" | custom-call | flops 1610612736 | bytes 11705344 | tf_op jit(solution)/shard_map/pallas_call | solution.py:254
  55.7 10.3 %shard_map.130 = (f32[8,192,96]{2,1,0:T(8,128)S(1)}, f32[8,192,96]{2,1,0:T(8,128)S(1)}, bf16[8,96,192]{2,1,0:T(8,128)(2,1)S(1)}, bf16[8,192,96]{2,1,0:T(8,128)(2,1)S(1)}) custom-call(bf16[8,96,4096]{2,1,0:T(8,128)(2,1)S(1)} %get-tuple-element.113.x_ref, f32[8,1,96]{2,1,0:T(1,128)S(1)} %get-tuple-element.114.prob_ref, ...), custom_call_target="tpu_custom_call" | custom-call | flops 2415919104 | bytes 33229824 | tf_op jit(solution)/shard_map/pallas_call | solution.py:254
  66.0 3.2 %collective-permute-done.22.own1 = bf16[128,4096]{1,0:T(8,128)(2,1)S(1)} collective-permute-done((bf16[128,4096]{1,0:T(8,128)(2,1)S(1)}, bf16[128,4096]{1,0:T(8,128)(2,1)S(1)}, u32[]{:S(2)}, u32[]{:S(2)}) %collective-permute-start.22) | collective-permute-done | bytes 1048608 | tf_op jit(solution)/shard_map/ppermute | solution.py:33
  69.2 7.7 %shard_map.131 = (bf16[256,4096]{1,0:T(8,128)(2,1)S(1)}, bf16[256,4096]{1,0:T(8,128)(2,1)S(1)}) custom-call(bf16[2,256,384]{2,1,0:T(8,128)(2,1)S(1)} %get-tuple-element.110.put_ref, bf16[8,96,192]{2,1,0:T(8,128)(2,1)S(1)} %get-tuple-element.119.refs_0_, bf16[8,192,4096]{2,1,0:T(8,128)(2,1)} %down_ref.1), custom_call_target="tpu_custom_call" | custom-call | flops 2818572288 | bytes 17465344 | tf_op jit(solution)/shard_map/pallas_call | solution.py:254
  77.6 4.6 %shard_map.132 = (bf16[8,96,4096]{2,1,0:T(8,128)(2,1)S(1)}, bf16[8,96,4096]{2,1,0:T(8,128)(2,1)}) custom-call(bf16[128,4096]{1,0:T(8,128)(2,1)S(1)} %constant_dynamic-update-slice_fusion.21.own0, bf16[128,4096]{1,0:T(8,128)(2,1)S(1)} %collective-permute-done.22.own1, bf16[128,4096]{1,0:T(8,128)(2,1)S(1)} %collective-permute-done.23.other0, ...), custom_call_target="tpu_custom_call" | custom-call | flops 1610612736 | bytes 17170432 | tf_op jit(solution)/shard_map/pallas_call | solution.py:254
  84.3 8.5 %shard_map.133 = (bf16[8,96,192]{2,1,0:T(8,128)(2,1)S(1)}, bf16[8,96,192]{2,1,0:T(8,128)(2,1)S(1)}, bf16[8,192,96]{2,1,0:T(8,128)(2,1)S(1)}, bf16[8,192,96]{2,1,0:T(8,128)(2,1)S(1)}, bf16[2,256,128]{2,1,0:T(8,128)(2,1)S(1)}) custom-call(bf16[8,96,4096]{2,1,0:T(8,128)(2,1)S(1)} %get-tuple-element.129.x_ref, ...), custom_call_target="tpu_custom_call" | custom-call | flops 1207959552 | bytes 21859328 | tf_op jit(solution)/shard_map/pallas_call | solution.py:254
  92.8 4.8 %shard_map.134 = (bf16[256,2048]{1,0:T(8,128)(2,1)S(1)}, bf16[256,2048]{1,0:T(8,128)(2,1)S(1)}) custom-call(bf16[2,256,384]{2,1,0:T(8,128)(2,1)S(1)} %get-tuple-element.110.put_ref, bf16[8,96,192]{2,1,0:T(8,128)(2,1)S(1)} %get-tuple-element.138.refs_0_, bf16[8,96,192]{2,1,0:T(8,128)(2,1)S(1)} %get-tuple-element.139.refs_1_, ...), custom_call_target="tpu_custom_call" | custom-call | flops 2013265920 | bytes 28246016 | tf_op jit(solution)/shard_map/pallas_call | solution.py:254
  98.6 5.1 %shard_map.135 = (bf16[256,2176]{1,0:T(8,128)(2,1)S(1)}, bf16[256,2176]{1,0:T(8,128)(2,1)S(1)}) custom-call(bf16[2,256,384]{2,1,0:T(8,128)(2,1)S(1)} %get-tuple-element.110.put_ref, bf16[8,96,192]{2,1,0:T(8,128)(2,1)S(1)} %get-tuple-element.138.refs_0_, bf16[8,96,192]{2,1,0:T(8,128)(2,1)S(1)} %get-tuple-element.139.refs_1_, ...), custom_call_target="tpu_custom_call" | custom-call | flops 2013265920 | bytes 28508160 | tf_op jit(solution)/shard_map/pallas_call | solution.py:254
  106.3 1.6 collective-permute-start.30
  107.9 7.4 %shard_map.136 = bf16[8,192,4096]{2,1,0:T(8,128)(2,1)} custom-call(bf16[8,96,4096]{2,1,0:T(8,128)(2,1)S(1)} %bitcast.1, bf16[8,192,96]{2,1,0:T(8,128)(2,1)S(1)} %get-tuple-element.149.left), custom_call_target="tpu_custom_call" | custom-call | flops 1207959552 | bytes 19169280 | tf_op jit(solution)/shard_map/pallas_call | solution.py:254
  116.7 1.6 %collective-permute-done.30 = bf16[64,4096]{1,0:T(8,128)(2,1)S(1)} collective-permute-done((bf16[64,4096]{1,0:T(8,128)(2,1)S(1)}, bf16[64,4096]{1,0:T(8,128)(2,1)S(1)}, u32[]{:S(2)}, u32[]{:S(2)}) %collective-permute-start.30) | collective-permute-done | bytes 524320 | tf_op jit(solution)/shard_map/ppermute | solution.py:33
  120.4 1.8 %collective-permute-start.32 = (bf16[64,2048]{1,0:T(8,128)(2,1)S(1)}, bf16[64,2048]{1,0:T(8,128)(2,1)S(1)}, u32[]{:S(2)}, u32[]{:S(2)}) collective-permute-start(bf16[64,2048]{1,0:T(8,128)(2,1)S(1)} %add_convert_fusion.6), channel_id=1, source_target_pairs={{0,8},{1,17},{2,10},{3,19},{4,12},{5,21},{6,14},{7,23},{8,0},{9,25... | collective-permute-start | bytes 786440 | tf_op jit(solution)/shard_map/ppermute | solution.py:33
  122.2 7.3 %shard_map.137 = bf16[8,192,4096]{2,1,0:T(8,128)(2,1)} custom-call(bf16[8,96,4096]{2,1,0:T(8,128)(2,1)S(1)} %get-tuple-element.113.x_ref, bf16[8,192,96]{2,1,0:T(8,128)(2,1)S(1)} %get-tuple-element.158.left), custom_call_target="tpu_custom_call" | custom-call | flops 1207959552 | bytes 19169280 | tf_op jit(solution)/shard_map/pallas_call | solution.py:254
  130.3 1.8 %collective-permute-done.31 = bf16[128,2176]{1,0:T(8,128)(2,1)S(1)} collective-permute-done((bf16[128,2176]{1,0:T(8,128)(2,1)S(1)}, bf16[128,2176]{1,0:T(8,128)(2,1)S(1)}, u32[]{:S(2)}, u32[]{:S(2)}) %collective-permute-start.31) | collective-permute-done | bytes 557088 | tf_op jit(solution)/shard_map/ppermute | solution.py:33
  135.7 7.4 %shard_map.138 = bf16[8,192,4096]{2,1,0:T(8,128)(2,1)} custom-call(bf16[8,96,4096]{2,1,0:T(8,128)(2,1)S(1)} %get-tuple-element.113.x_ref, bf16[8,192,96]{2,1,0:T(8,128)(2,1)S(1)} %get-tuple-element.166.left), custom_call_target="tpu_custom_call" | custom-call | flops 1207959552 | bytes 19169280 | tf_op jit(solution)/shard_map/pallas_call | solution.py:254
  143.1 1.7 %add_convert_fusion.8 = bf16[16,4096]{1,0:T(8,128)(2,1)} fusion(bf16[16,4096]{1,0:T(8,128)(2,1)S(1)} %collective-permute-done.34, bf16[32,4096]{1,0:T(8,128)(2,1)S(1)} %collective-permute-done.33, bf16[64,4096]{1,0:T(8,128)(2,1)S(1)} %collective-permute-done.30, bf16[128,4096]{1,0:T(8,128)(2,1)S(1)} %collective-permute-done.26, ...), kind=kLoop, calls=%fused_computation.13 | loop fusion | flops 786432 | bytes 917504 | tf_op jit(solution)/shard_map/convert_element_type | solution.py:40
  145.7 2.9 %collective-permute-start.37 = (bf16[16,2048]{1,0:T(8,128)(2,1)S(1)}, bf16[16,2048]{1,0:T(8,128)(2,1)S(1)}, u32[]{:S(2)}, u32[]{:S(2)}) collective-permute-start(bf16[16,2048]{1,0:T(8,128)(2,1)S(1)} %add_convert_fusion.14), channel_id=1, source_target_pairs={{0,4},{1,5},{2,6},{3,7},{4,0},{5,1},{6,2},{7,3},{8,12},{9,13},{10,... | collective-permute-start | bytes 196616 | tf_op jit(solution)/shard_map/ppermute | solution.py:33
  150.1 1.8 %collective-permute-start.39 = (bf16[16,2176]{1,0:T(8,128)(2,1)S(1)}, bf16[16,2176]{1,0:T(8,128)(2,1)S(1)}, u32[]{:S(2)}, u32[]{:S(2)}) collective-permute-start(bf16[16,2176]{1,0:T(8,128)(2,1)S(1)} %add_convert_fusion.12), channel_id=1, source_target_pairs={{0,4},{1,5},{2,6},{3,7},{4,0},{5,1},{6,2},{7,3},{8,12},{9,13},{10,... | collective-permute-start | bytes 208904 | tf_op jit(solution)/shard_map/ppermute | solution.py:33
  152.0 3.4 %collective-permute-done.39 = bf16[16,2176]{1,0:T(8,128)(2,1)S(1)} collective-permute-done((bf16[16,2176]{1,0:T(8,128)(2,1)S(1)}, bf16[16,2176]{1,0:T(8,128)(2,1)S(1)}, u32[]{:S(2)}, u32[]{:S(2)}) %collective-permute-start.39) | collective-permute-done | bytes 69664 | tf_op jit(solution)/shard_map/ppermute | solution.py:33
  (126 shorter events, 33.4 us)
Async XLA Ops:
  0.6 15.7 %collective-permute-start = (bf16[16,4096]{1,0:T(8,128)(2,1)}, bf16[16,4096]{1,0:T(8,128)(2,1)S(1)}, u32[]{:S(2)}, u32[]{:S(2)}) collective-permute-start(bf16[16,4096]{1,0:T(8,128)(2,1)} %param.8), channel_id=1, source_target_pairs={{0,8},{1,17},{2,10},{3,19},{4,12},{5,21},{6,14},{7,23},{8,0},{9,25... | collective-permute-start | bytes 393224 | tf_op jit(solution)/shard_map/ppermute | solution.py:33
  3.6 8.9 %collective-permute-start.1 = (bf16[16,4096]{1,0:T(8,128)(2,1)}, bf16[16,4096]{1,0:T(8,128)(2,1)S(1)}, u32[]{:S(2)}, u32[]{:S(2)}) collective-permute-start(bf16[16,4096]{1,0:T(8,128)(2,1)} %param.8), channel_id=1, source_target_pairs={{0,2},{1,3},{2,0},{3,1},{4,6},{5,7},{6,4},{7,5},{8,10},{9,11},{10,... | collective-permute-start | bytes 393224 | tf_op jit(solution)/shard_map/ppermute | solution.py:33
  5.2 11.0 %collective-permute-start.2 = (bf16[16,4096]{1,0:T(8,128)(2,1)}, bf16[16,4096]{1,0:T(8,128)(2,1)S(1)}, u32[]{:S(2)}, u32[]{:S(2)}) collective-permute-start(bf16[16,4096]{1,0:T(8,128)(2,1)} %param.8), channel_id=1, source_target_pairs={{0,4},{1,5},{2,6},{3,7},{4,0},{5,1},{6,2},{7,3},{8,12},{9,13},{10,... | collective-permute-start | bytes 393224 | tf_op jit(solution)/shard_map/ppermute | solution.py:33
  10.6 12.2 %collective-permute-start.6 = (bf16[16,128]{1,0:T(8,128)(2,1)S(1)}, bf16[16,128]{1,0:T(8,128)(2,1)S(1)}, u32[]{:S(2)}, u32[]{:S(2)}) collective-permute-start(bf16[16,128]{1,0:T(8,128)(2,1)S(1)} %get-tuple-element.179), channel_id=1, source_target_pairs={{0,4},{1,5},{2,6},{3,7},{4,0},{5,1},{6,2},{7,3},{8,12},{9,13},{10,... | collective-permute-start | bytes 12296 | tf_op jit(solution)/shard_map/ppermute | solution.py:33
  10.9 11.9 %collective-permute-start.7 = (bf16[16,128]{1,0:T(8,128)(2,1)S(1)}, bf16[16,128]{1,0:T(8,128)(2,1)S(1)}, u32[]{:S(2)}, u32[]{:S(2)}) collective-permute-start(bf16[16,128]{1,0:T(8,128)(2,1)S(1)} %get-tuple-element.179), channel_id=1, source_target_pairs={{0,2},{1,3},{2,0},{3,1},{4,6},{5,7},{6,4},{7,5},{8,10},{9,11},{10,... | collective-permute-start | bytes 12296 | tf_op jit(solution)/shard_map/ppermute | solution.py:33
  12.6 11.1 %collective-permute-start.8 = (bf16[16,128]{1,0:T(8,128)(2,1)S(1)}, bf16[16,128]{1,0:T(8,128)(2,1)S(1)}, u32[]{:S(2)}, u32[]{:S(2)}) collective-permute-start(bf16[16,128]{1,0:T(8,128)(2,1)S(1)} %get-tuple-element.179), channel_id=1, source_target_pairs={{0,6},{1,7},{2,4},{3,5},{4,2},{5,3},{6,0},{7,1},{8,14},{9,15},{10,... | collective-permute-start | bytes 12296 | tf_op jit(solution)/shard_map/ppermute | solution.py:33
  16.3 8.3 %collective-permute-start.4 = (bf16[32,4096]{1,0:T(8,128)(2,1)S(1)}, bf16[32,4096]{1,0:T(8,128)(2,1)S(1)}, u32[]{:S(2)}, u32[]{:S(2)}) collective-permute-start(bf16[32,4096]{1,0:T(8,128)(2,1)S(1)} %pad_maximum_fusion.2), channel_id=1, source_target_pairs={{0,8},{1,17},{2,10},{3,19},{4,12},{5,21},{6,14},{7,23},{8,0},{9,25... | collective-permute-start | bytes 786440 | tf_op jit(solution)/shard_map/ppermute | solution.py:33
  21.2 6.4 %collective-permute-start.5 = (bf16[32,4096]{1,0:T(8,128)(2,1)S(1)}, bf16[32,4096]{1,0:T(8,128)(2,1)S(1)}, u32[]{:S(2)}, u32[]{:S(2)}) collective-permute-start(bf16[32,4096]{1,0:T(8,128)(2,1)S(1)} %pad_maximum_fusion.3), channel_id=1, source_target_pairs={{0,16},{1,9},{2,18},{3,11},{4,20},{5,13},{6,22},{7,15},{8,24},{9,1... | collective-permute-start | bytes 786440 | tf_op jit(solution)/shard_map/ppermute | solution.py:33
  22.8 16.4 %collective-permute-start.18 = (bf16[16,4096]{1,0:T(8,128)(2,1)S(1)}, bf16[16,4096]{1,0:T(8,128)(2,1)S(1)}, u32[]{:S(2)}, u32[]{:S(2)}) collective-permute-start(bf16[16,4096]{1,0:T(8,128)(2,1)S(1)} %copy-done), channel_id=1, source_target_pairs={{0,4},{1,5},{2,6},{3,7},{4,0},{5,1},{6,2},{7,3},{8,12},{9,13},{10,... | collective-permute-start | bytes 393224 | tf_op jit(solution)/shard_map/ppermute | solution.py:33
  22.9 16.9 %collective-permute-start.19 = (bf16[16,4096]{1,0:T(8,128)(2,1)S(1)}, bf16[16,4096]{1,0:T(8,128)(2,1)S(1)}, u32[]{:S(2)}, u32[]{:S(2)}) collective-permute-start(bf16[16,4096]{1,0:T(8,128)(2,1)S(1)} %copy-done), channel_id=1, source_target_pairs={{0,2},{1,3},{2,0},{3,1},{4,6},{5,7},{6,4},{7,5},{8,10},{9,11},{10,... | collective-permute-start | bytes 393224 | tf_op jit(solution)/shard_map/ppermute | solution.py:33
  27.7 8.7 %collective-permute-start.9 = (bf16[16,4096]{1,0:T(8,128)(2,1)S(1)}, bf16[16,4096]{1,0:T(8,128)(2,1)S(1)}, u32[]{:S(2)}, u32[]{:S(2)}) collective-permute-start(bf16[16,4096]{1,0:T(8,128)(2,1)S(1)} %collective-permute-done.3.after), channel_id=1, source_target_pairs={{0,8},{1,17},{2,10},{3,19},{4,12},{5,21},{6,14},{7,23},{8,0},{9,25... | collective-permute-start | bytes 393224 | tf_op jit(solution)/shard_map/ppermute | solution.py:33
  28.3 9.2 %collective-permute-start.10 = (bf16[64,4096]{1,0:T(8,128)(2,1)S(1)}, bf16[64,4096]{1,0:T(8,128)(2,1)S(1)}, u32[]{:S(2)}, u32[]{:S(2)}) collective-permute-start(bf16[64,4096]{1,0:T(8,128)(2,1)S(1)} %pad_maximum_fusion), channel_id=1, source_target_pairs={{0,16},{1,9},{2,18},{3,11},{4,20},{5,13},{6,22},{7,15},{8,24},{9,1... | collective-permute-start | bytes 1572872 | tf_op jit(solution)/shard_map/ppermute | solution.py:33
  36.0 6.8 %collective-permute-start.20 = (bf16[16,4096]{1,0:T(8,128)(2,1)S(1)}, bf16[16,4096]{1,0:T(8,128)(2,1)S(1)}, u32[]{:S(2)}, u32[]{:S(2)}) collective-permute-start(bf16[16,4096]{1,0:T(8,128)(2,1)S(1)} %copy-done), channel_id=1, source_target_pairs={{0,6},{1,7},{2,4},{3,5},{4,2},{5,3},{6,0},{7,1},{8,14},{9,15},{10,... | collective-permute-start | bytes 393224 | tf_op jit(solution)/shard_map/ppermute | solution.py:33
  36.3 12.5 %collective-permute-start.14 = (bf16[64,4096]{1,0:T(8,128)(2,1)S(1)}, bf16[64,4096]{1,0:T(8,128)(2,1)S(1)}, u32[]{:S(2)}, u32[]{:S(2)}) collective-permute-start(bf16[64,4096]{1,0:T(8,128)(2,1)S(1)} %constant_dynamic-update-slice_fusion.refs_0_), channel_id=1, source_target_pairs={{0,1},{1,0},{2,3},{3,2},{4,5},{5,4},{6,7},{7,6},{8,9},{9,8},{10,11... | collective-permute-start | bytes 1572872 | tf_op jit(solution)/shard_map/ppermute | solution.py:33
  37.5 10.7 %collective-permute-start.12 = (bf16[32,4096]{1,0:T(8,128)(2,1)S(1)}, bf16[32,4096]{1,0:T(8,128)(2,1)S(1)}, u32[]{:S(2)}, u32[]{:S(2)}) collective-permute-start(bf16[32,4096]{1,0:T(8,128)(2,1)S(1)} %pad_maximum_fusion.4), channel_id=1, source_target_pairs={{0,16},{1,9},{2,18},{3,11},{4,20},{5,13},{6,22},{7,15},{8,24},{9,1... | collective-permute-start | bytes 786440 | tf_op jit(solution)/shard_map/ppermute | solution.py:33
  39.2 9.0 %collective-permute-start.13 = (bf16[128,128]{1,0:T(8,128)(2,1)S(1)}, bf16[128,128]{1,0:T(8,128)(2,1)S(1)}, u32[]{:S(2)}, u32[]{:S(2)}) collective-permute-start(bf16[128,128]{1,0:T(8,128)(2,1)S(1)} %get-tuple-element.181), channel_id=1, source_target_pairs={{0,16},{1,9},{2,18},{3,11},{4,20},{5,13},{6,22},{7,15},{8,24},{9,1... | collective-permute-start | bytes 98312 | tf_op jit(solution)/shard_map/ppermute | solution.py:33
  39.7 10.5 %collective-permute-start.15 = (bf16[128,4096]{1,0:T(8,128)(2,1)S(1)}, bf16[128,4096]{1,0:T(8,128)(2,1)S(1)}, u32[]{:S(2)}, u32[]{:S(2)}) collective-permute-start(bf16[128,4096]{1,0:T(8,128)(2,1)S(1)} %constant_dynamic-update-slice_fusion.3.refs_1_), channel_id=1, source_target_pairs={{0,1},{1,0},{2,3},{3,2},{4,5},{5,4},{6,7},{7,6},{8,9},{9,8},{10,11... | collective-permute-start | bytes 3145736 | tf_op jit(solution)/shard_map/ppermute | solution.py:33
  42.9 11.3 %collective-permute-start.21 = (bf16[64,4096]{1,0:T(8,128)(2,1)S(1)}, bf16[64,4096]{1,0:T(8,128)(2,1)S(1)}, u32[]{:S(2)}, u32[]{:S(2)}) collective-permute-start(bf16[64,4096]{1,0:T(8,128)(2,1)S(1)} %pad_maximum_fusion.1), channel_id=1, source_target_pairs={{0,8},{1,17},{2,10},{3,19},{4,12},{5,21},{6,14},{7,23},{8,0},{9,25... | collective-permute-start | bytes 1572872 | tf_op jit(solution)/shard_map/ppermute | solution.py:33
  54.3 14.9 %collective-permute-start.22 = (bf16[128,4096]{1,0:T(8,128)(2,1)S(1)}, bf16[128,4096]{1,0:T(8,128)(2,1)S(1)}, u32[]{:S(2)}, u32[]{:S(2)}) collective-permute-start(bf16[128,4096]{1,0:T(8,128)(2,1)S(1)} %constant_dynamic-update-slice_fusion.21.own0), channel_id=1, source_target_pairs={{0,16},{1,9},{2,18},{3,11},{4,20},{5,13},{6,22},{7,15},{8,24},{9,1... | collective-permute-start | bytes 3145736 | tf_op jit(solution)/shard_map/ppermute | solution.py:33
  54.9 14.2 %collective-permute-start.23 = (bf16[128,4096]{1,0:T(8,128)(2,1)S(1)}, bf16[128,4096]{1,0:T(8,128)(2,1)S(1)}, u32[]{:S(2)}, u32[]{:S(2)}) collective-permute-start(bf16[128,4096]{1,0:T(8,128)(2,1)S(1)} %constant_dynamic-update-slice_fusion.21.own0), channel_id=1, source_target_pairs={{0,1},{1,0},{2,3},{3,2},{4,5},{5,4},{6,7},{7,6},{8,9},{9,8},{10,11... | collective-permute-start | bytes 3145736 | tf_op jit(solution)/shard_map/ppermute | solution.py:33
  69.2 7.8 %collective-permute-start.24 = (bf16[128,4096]{1,0:T(8,128)(2,1)S(1)}, bf16[128,4096]{1,0:T(8,128)(2,1)S(1)}, u32[]{:S(2)}, u32[]{:S(2)}) collective-permute-start(bf16[128,4096]{1,0:T(8,128)(2,1)S(1)} %collective-permute-done.22.own1), channel_id=1, source_target_pairs={{0,1},{1,0},{2,3},{3,2},{4,5},{5,4},{6,7},{7,6},{8,9},{9,8},{10,11... | collective-permute-start | bytes 3145736 | tf_op jit(solution)/shard_map/ppermute | solution.py:33
  83.7 14.9 %collective-permute-start.26 = (bf16[128,4096]{1,0:T(8,128)(2,1)S(1)}, bf16[128,4096]{1,0:T(8,128)(2,1)S(1)}, u32[]{:S(2)}, u32[]{:S(2)}) collective-permute-start(bf16[128,4096]{1,0:T(8,128)(2,1)S(1)} %add_convert_fusion), channel_id=1, source_target_pairs={{0,16},{1,9},{2,18},{3,11},{4,20},{5,13},{6,22},{7,15},{8,24},{9,1... | collective-permute-start | bytes 3145736 | tf_op jit(solution)/shard_map/ppermute | solution.py:33
  103.7 14.6 %collective-permute-start.27 = (bf16[256,2176]{1,0:T(8,128)(2,1)S(1)}, bf16[256,2176]{1,0:T(8,128)(2,1)S(1)}, u32[]{:S(2)}, u32[]{:S(2)}) collective-permute-start(bf16[256,2176]{1,0:T(8,128)(2,1)S(1)} %get-tuple-element.141), channel_id=1, source_target_pairs={{0,1},{1,0},{2,3},{3,2},{4,5},{5,4},{6,7},{7,6},{8,9},{9,8},{10,11... | collective-permute-start | bytes 3342344 | tf_op jit(solution)/shard_map/ppermute | solution.py:33
  103.9 12.8 %collective-permute-start.29 = (bf16[128,2048]{1,0:T(8,128)(2,1)S(1)}, bf16[128,2048]{1,0:T(8,128)(2,1)S(1)}, u32[]{:S(2)}, u32[]{:S(2)}) collective-permute-start(bf16[128,2048]{1,0:T(8,128)(2,1)S(1)} %add_convert_fusion.3), channel_id=1, source_target_pairs={{0,16},{1,9},{2,18},{3,11},{4,20},{5,13},{6,22},{7,15},{8,24},{9,1... | collective-permute-start | bytes 1572872 | tf_op jit(solution)/shard_map/ppermute | solution.py:33
  106.3 12.0 %collective-permute-start.30 = (bf16[64,4096]{1,0:T(8,128)(2,1)S(1)}, bf16[64,4096]{1,0:T(8,128)(2,1)S(1)}, u32[]{:S(2)}, u32[]{:S(2)}) collective-permute-start(bf16[64,4096]{1,0:T(8,128)(2,1)S(1)} %add_convert_fusion.2), channel_id=1, source_target_pairs={{0,8},{1,17},{2,10},{3,19},{4,12},{5,21},{6,14},{7,23},{8,0},{9,25... | collective-permute-start | bytes 1572872 | tf_op jit(solution)/shard_map/ppermute | solution.py:33
  119.7 12.4 %collective-permute-start.31 = (bf16[128,2176]{1,0:T(8,128)(2,1)S(1)}, bf16[128,2176]{1,0:T(8,128)(2,1)S(1)}, u32[]{:S(2)}, u32[]{:S(2)}) collective-permute-start(bf16[128,2176]{1,0:T(8,128)(2,1)S(1)} %add_convert_fusion.1), channel_id=1, source_target_pairs={{0,16},{1,9},{2,18},{3,11},{4,20},{5,13},{6,22},{7,15},{8,24},{9,1... | collective-permute-start | bytes 1671176 | tf_op jit(solution)/shard_map/ppermute | solution.py:33
  120.4 9.2 %collective-permute-start.32 = (bf16[64,2048]{1,0:T(8,128)(2,1)S(1)}, bf16[64,2048]{1,0:T(8,128)(2,1)S(1)}, u32[]{:S(2)}, u32[]{:S(2)}) collective-permute-start(bf16[64,2048]{1,0:T(8,128)(2,1)S(1)} %add_convert_fusion.6), channel_id=1, source_target_pairs={{0,8},{1,17},{2,10},{3,19},{4,12},{5,21},{6,14},{7,23},{8,0},{9,25... | collective-permute-start | bytes 786440 | tf_op jit(solution)/shard_map/ppermute | solution.py:33
  122.2 8.1 %collective-permute-start.33 = (bf16[32,4096]{1,0:T(8,128)(2,1)S(1)}, bf16[32,4096]{1,0:T(8,128)(2,1)S(1)}, u32[]{:S(2)}, u32[]{:S(2)}) collective-permute-start(bf16[32,4096]{1,0:T(8,128)(2,1)S(1)} %add_convert_fusion.5), channel_id=1, source_target_pairs={{0,2},{1,3},{2,0},{3,1},{4,6},{5,7},{6,4},{7,5},{8,10},{9,11},{10,... | collective-permute-start | bytes 786440 | tf_op jit(solution)/shard_map/ppermute | solution.py:33
  133.2 9.8 %collective-permute-start.34 = (bf16[16,4096]{1,0:T(8,128)(2,1)S(1)}, bf16[16,4096]{1,0:T(8,128)(2,1)S(1)}, u32[]{:S(2)}, u32[]{:S(2)}) collective-permute-start(bf16[16,4096]{1,0:T(8,128)(2,1)S(1)} %add_convert_fusion.9), channel_id=1, source_target_pairs={{0,4},{1,5},{2,6},{3,7},{4,0},{5,1},{6,2},{7,3},{8,12},{9,13},{10,... | collective-permute-start | bytes 393224 | tf_op jit(solution)/shard_map/ppermute | solution.py:33
  133.3 11.4 %collective-permute-start.35 = (bf16[64,2176]{1,0:T(8,128)(2,1)S(1)}, bf16[64,2176]{1,0:T(8,128)(2,1)S(1)}, u32[]{:S(2)}, u32[]{:S(2)}) collective-permute-start(bf16[64,2176]{1,0:T(8,128)(2,1)S(1)} %add_convert_fusion.4), channel_id=1, source_target_pairs={{0,8},{1,17},{2,10},{3,19},{4,12},{5,21},{6,14},{7,23},{8,0},{9,25... | collective-permute-start | bytes 835592 | tf_op jit(solution)/shard_map/ppermute | solution.py:33
  134.5 10.3 %collective-permute-start.36 = (bf16[32,2048]{1,0:T(8,128)(2,1)S(1)}, bf16[32,2048]{1,0:T(8,128)(2,1)S(1)}, u32[]{:S(2)}, u32[]{:S(2)}) collective-permute-start(bf16[32,2048]{1,0:T(8,128)(2,1)S(1)} %add_convert_fusion.10), channel_id=1, source_target_pairs={{0,2},{1,3},{2,0},{3,1},{4,6},{5,7},{6,4},{7,5},{8,10},{9,11},{10,... | collective-permute-start | bytes 393224 | tf_op jit(solution)/shard_map/ppermute | solution.py:33
  145.7 6.2 %collective-permute-start.37 = (bf16[16,2048]{1,0:T(8,128)(2,1)S(1)}, bf16[16,2048]{1,0:T(8,128)(2,1)S(1)}, u32[]{:S(2)}, u32[]{:S(2)}) collective-permute-start(bf16[16,2048]{1,0:T(8,128)(2,1)S(1)} %add_convert_fusion.14), channel_id=1, source_target_pairs={{0,4},{1,5},{2,6},{3,7},{4,0},{5,1},{6,2},{7,3},{8,12},{9,13},{10,... | collective-permute-start | bytes 196616 | tf_op jit(solution)/shard_map/ppermute | solution.py:33
  (11 other events, 77.9 us)

commit v11 on v10

--- a/solution.py
+++ b/solution.py
@@ -210,12 +210,10 @@
             other_ref[:, :columns] = extra_ref[1]
 
 
-def grad_kernel(x_ref, left, *outs):
-    hidden = outs[0].shape[1]
+def grad_kernel(x_ref, left, *refs):
+    out = refs[-1]
     for at in range(0, x_ref.shape[2], WIDE):
-        product = dot(left[0], x_ref[0, :, at : at + WIDE]).astype(jnp.bfloat16)
-        for i, out in enumerate(outs):
-            out[0, :, at : at + WIDE] = product[hidden * i : hidden * (i + 1)]
+        out[0, :, at : at + WIDE] = dot(left[0], x_ref[0, :, at : at + WIDE]).astype(jnp.bfloat16)
 
 
 def whole(a):
@@ -383,19 +381,37 @@
     return call(kernel, grid, ins, args, outs, shapes, scratch, flops)
 
 
-def grad_call(x, left, hidden):
+def grad_call(x, left, first=0, last=None, into=None):
     experts, rows, width = x.shape
-    shapes = [bf16(experts, hidden, width)] * (left.shape[1] // hidden)
-    flops = 2 * experts * rows * left.shape[1] * width
-    ins, outs = [each(x), each(left)], [each(s) for s in shapes]
-    return call(grad_kernel, experts, ins, (near_core(x), left), outs, shapes, flops=flops)
+    hidden = left.shape[1]
+    count = (experts if last is None else last) - first
+    args = (near_core(x), left) + (() if into is None else (into,))
+
+    def own(a):
+        return pl.BlockSpec((1, *a.shape[1:]), lambda i: (first + i, 0, 0))
+
+    shape = bf16(experts, hidden, width)
+    ins = [own(x), own(left)] + ([] if into is None else [pl.BlockSpec(memory_space=pl.ANY)])
+    moved = 2 * count * (rows * width + rows * hidden + hidden * width)
+    return pl.pallas_call(
+        grad_kernel,
+        grid=(count,),
+        in_specs=ins,
+        out_specs=own(shape),
+        out_shape=shape,
+        input_output_aliases={} if into is None else {2: 0},
+        compiler_params=pltpu.CompilerParams(vmem_limit_bytes=12 * MIB),
+        cost_estimate=pl.CostEstimate(
+            flops=2 * count * rows * hidden * width, bytes_accessed=moved, transcendentals=0
+        ),
+    )(*args)
 
 
 def dense_body(
     tokens, cotangent, gate_prob, expert_ids, placement, gate_weight, up_weight, down_weight
 ):
     tok_count, width = tokens.shape
-    local, hidden, _ = gate_weight.shape
+    local = gate_weight.shape[0]
     total_experts = placement.shape[0]
     devices = lax.axis_size("dp") * lax.axis_size("expert")
     places = devices // 2 * CAP
@@ -419,8 +435,8 @@
 
     near, far = swap(tokens, Z1), swap(tokens, Z2)
     first0 = swap(tokens, X, Y)
+    near, far, parts = together(near, far, parts)
     far_parts, near_parts, last_parts = (swap(parts, bit) for bit in (Z2, Z1, Z3))
-    near, far = together(near, far)
 
     last = swap(far, Z1)
     middle_rows = rows_of(far, near)
@@ -514,7 +530,7 @@
     right[0], left[1] = together(right[0], left[1])
     rows, ht = together(leaving(left, 2 * quarter, 4 * quarter), ht)
     left.append(swap(rows, Y, X))
-    (down_weight_grad,) = grad_call(far_c, ht, hidden)
+    down_weight_grad = grad_call(far_c, ht)
 
     right[1], left[2], mixed[3], down_weight_grad = together(
         right[1], left[2], mixed[3], down_weight_grad
@@ -528,7 +544,7 @@
     right.append(swap(rows, Y, X))
     left.append(swap(left_rows, X, Y))
     mixed.append(swap(mixed_rows, Z1))
-    (gate_weight_grad,) = grad_call(x, dgt, hidden)
+    gate_weight_grad = grad_call(x, dgt)
 
     right[2], left[3], mixed[4], gate_weight_grad = together(
         right[2], left[3], mixed[4], gate_weight_grad
@@ -542,10 +558,18 @@
     right.append(swap(rows, X, Y))
     left.append(swap(left_rows, Z1))
     mixed.append(swap(mixed_rows, Z2))
-    (up_weight_grad,) = grad_call(x, dut, hidden)
+    up_weight_grad = grad_call(x, dut, 0, local // 2)
 
     right[3], left[4], up_weight_grad = together(right[3], left[4], up_weight_grad)
-    right, left = by_near(right), by_far(left)
+    rows, left_rows, dut = together(
+        leaving(right, 2 * tok_count, 4 * tok_count),
+        leaving(left, tok_count, 2 * tok_count),
+        dut,
+    )
+    right.append(swap(rows, Z1))
+    left.append(swap(left_rows, Z2))
+    up_weight_grad = grad_call(x, dut, local // 2, local, up_weight_grad)
+    right[4], up_weight_grad = together(right[4], up_weight_grad)
     right = by_far(right)
     mixed, left, right = (leaving(parts, 0, tok_count) for parts in (mixed, left, right))
     token_grad = jnp.concatenate([left, right[:, : width - middle]], axis=1)

time: 158 us -> 159 us (level)
  starting transfers between devices: 38.4 us -> 41.4 us
  waiting for transfers between devices: 26.9 us -> 24.7 us
    pallas_call x0 -> x4, Pallas kernels: none -> 22.7 us  [grad_call(): pl.pallas_call(grad_kernel, grid=(count,), in_specs=ins, out_specs=own(sh...]
    pallas_call x10 -> x7, Pallas kernels: 67.1 us -> 45 us  [call(): pl.pallas_call(kernel, grid=(grid,), in_specs=ins, out_specs=outs, out_sh...]
    ppermute x40, starting transfers between devices: 38.4 us -> 41.4 us  [swap(): return lax.ppermute(values, AXES, pairs)]
    ppermute x40, waiting for transfers between devices: 26.9 us -> 24.7 us  [swap(): return lax.ppermute(values, AXES, pairs)]
  transfers between devices with their start and end apart: 40 -> 40, of which waited for: 15 -> 10; matrix products, arithmetic and copies ran while one was open for 5% -> 5% of each run, Pallas kernels for 49% -> 49%
where the time goes in v11:
time: 159 us; the launch traced here: 158 us
  Pallas kernels  76.8 us (48%)
  starting transfers between devices  41.4 us (26%)
  waiting for transfers between devices  24.7 us (16%)
  other arithmetic  10.8 us (7%)
  local copies, waits for them, and re-layouts  3.42 us (2%)
    pallas_call x7, Pallas kernels, call(): pl.pallas_call(kernel, grid=(grid,), in_specs=ins, out_specs=outs, out_sh...  45 us
    ppermute x40, starting transfers between devices, swap(): return lax.ppermute(values, AXES, pairs)  41.4 us
    ppermute x40, waiting for transfers between devices, swap(): return lax.ppermute(values, AXES, pairs)  24.7 us
    pallas_call x4, Pallas kernels, grad_call(): pl.pallas_call(grad_kernel, grid=(count,), in_specs=ins, out_specs=own(sh...  22.7 us
    pallas_call x2, Pallas kernels, fetch_call(): pl.pallas_call(fetch_kernel, in_specs=[pl.BlockSpec(memory_space=pl.ANY)]...  9.17 us
    convert_element_type x15, other arithmetic, add(): return total.astype(jnp.bfloat16)  7.28 us
    unnamed x25, local copies, waits for them, and re-layouts  3.29 us
  transfers between devices with their start and end apart: 40, of which 10 were waited for; matrix products, arithmetic and copies ran while one was open for 5% of the time, Pallas kernels for 49%

profile of v11, /device:TPU:0, one launch (start us, length us, event | category | flops | bytes accessed | tf_op | source)
XLA Modules:
  0.0 158.2 jit_solution(650617205916458378)
XLA Ops:
  0.6 4.1 %collective-permute-start.2 = (bf16[16,4096]{1,0:T(8,128)(2,1)}, bf16[16,4096]{1,0:T(8,128)(2,1)S(1)}, u32[]{:S(2)}, u32[]{:S(2)}) collective-permute-start(bf16[16,4096]{1,0:T(8,128)(2,1)} %param.8), channel_id=1, source_target_pairs={{0,4},{1,5},{2,6},{3,7},{4,0},{5,1},{6,2},{7,3},{8,12},{9,13},{10,... | collective-permute-start | bytes 393224 | tf_op jit(solution)/shard_map/ppermute | solution.py:33
  4.7 1.6 collective-permute-start.1
  11.8 3.0 %collective-permute-start.8 = (bf16[16,128]{1,0:T(8,128)(2,1)S(1)}, bf16[16,128]{1,0:T(8,128)(2,1)S(1)}, u32[]{:S(2)}, u32[]{:S(2)}) collective-permute-start(bf16[16,128]{1,0:T(8,128)(2,1)S(1)} %pad_maximum_fusion.7), channel_id=1, source_target_pairs={{0,6},{1,7},{2,4},{3,5},{4,2},{5,3},{6,0},{7,1},{8,14},{9,15},{10,... | collective-permute-start | bytes 12296 | tf_op jit(solution)/shard_map/ppermute | solution.py:33
  14.8 2.0 %collective-permute-start.3 = (bf16[16,4096]{1,0:T(8,128)(2,1)S(1)}, bf16[16,4096]{1,0:T(8,128)(2,1)S(1)}, u32[]{:S(2)}, u32[]{:S(2)}) collective-permute-start(bf16[16,4096]{1,0:T(8,128)(2,1)S(1)} %collective-permute-done.2), channel_id=1, source_target_pairs={{0,2},{1,3},{2,0},{3,1},{4,6},{5,7},{6,4},{7,5},{8,10},{9,11},{10,... | collective-permute-start | bytes 393224 | tf_op jit(solution)/shard_map/ppermute | solution.py:33
  16.9 1.6 collective-permute-start.4
  19.4 1.6 %collective-permute-start.5 = (bf16[32,4096]{1,0:T(8,128)(2,1)S(1)}, bf16[32,4096]{1,0:T(8,128)(2,1)S(1)}, u32[]{:S(2)}, u32[]{:S(2)}) collective-permute-start(bf16[32,4096]{1,0:T(8,128)(2,1)S(1)} %pad_maximum_fusion.3), channel_id=1, source_target_pairs={{0,16},{1,9},{2,18},{3,11},{4,20},{5,13},{6,22},{7,15},{8,24},{9,1... | collective-permute-start | bytes 786440 | tf_op jit(solution)/shard_map/ppermute | solution.py:33
  21.2 3.0 %collective-permute-start.20 = (bf16[16,4096]{1,0:T(8,128)(2,1)S(1)}, bf16[16,4096]{1,0:T(8,128)(2,1)S(1)}, u32[]{:S(2)}, u32[]{:S(2)}) collective-permute-start(bf16[16,4096]{1,0:T(8,128)(2,1)S(1)} %copy-done), channel_id=1, source_target_pairs={{0,6},{1,7},{2,4},{3,5},{4,2},{5,3},{6,0},{7,1},{8,14},{9,15},{10,... | collective-permute-start | bytes 393224 | tf_op jit(solution)/shard_map/ppermute | solution.py:33
  29.6 4.6 %shard_map.127 = (bf16[8,192,4096]{2,1,0:T(8,128)(2,1)S(1)}, f32[8,128]{1,0:T(8,128)S(1)}) custom-call(bf16[8,192,4096]{2,1,0:T(8,128)(2,1)} %source, bf16[16,4096]{1,0:T(8,128)(2,1)S(1)} %collective-permute-done.3.after), custom_call_target="tpu_custom_call" | custom-call | bytes 12582912 | tf_op jit(solution)/shard_map/pallas_call | solution.py:272
  34.3 2.9 %collective-permute-done.10 = bf16[64,4096]{1,0:T(8,128)(2,1)S(1)} collective-permute-done((bf16[64,4096]{1,0:T(8,128)(2,1)S(1)}, bf16[64,4096]{1,0:T(8,128)(2,1)S(1)}, u32[]{:S(2)}, u32[]{:S(2)}) %collective-permute-start.10) | collective-permute-done | bytes 524320 | tf_op jit(solution)/shard_map/ppermute | solution.py:33
  39.5 2.9 %collective-permute-done.18 = bf16[16,4096]{1,0:T(8,128)(2,1)S(1)} collective-permute-done((bf16[16,4096]{1,0:T(8,128)(2,1)S(1)}, bf16[16,4096]{1,0:T(8,128)(2,1)S(1)}, u32[]{:S(2)}, u32[]{:S(2)}) %collective-permute-start.18) | collective-permute-done | bytes 131104 | tf_op jit(solution)/shard_map/ppermute | solution.py:33
  43.2 4.6 %shard_map.128 = (bf16[8,192,4096]{2,1,0:T(8,128)(2,1)S(1)}, f32[8,128]{1,0:T(8,128)S(1)}) custom-call(bf16[8,192,4096]{2,1,0:T(8,128)(2,1)} %source.1, f32[8,128]{1,0:T(8,128)S(1)} %get-tuple-element.111.after), custom_call_target="tpu_custom_call" | custom-call | bytes 12582912 | tf_op jit(solution)/shard_map/pallas_call | solution.py:272
  48.5 1.5 collective-permute-done.17.refs_7_
  50.0 4.0 %shard_map.129 = (bf16[8,96,4096]{2,1,0:T(8,128)(2,1)S(1)}, bf16[2,256,384]{2,1,0:T(8,128)(2,1)S(1)}, bf16[2,384,256]{2,1,0:T(8,128)(2,1)S(1)}, f32[8,1,96]{2,1,0:T(1,128)S(1)}) custom-call(bf16[64,4096]{1,0:T(8,128)(2,1)S(1)} %constant_dynamic-update-slice_fusion.refs_0_, bf16[128,4096]{1,0:T(8,128)(2,1)S(1)} %constant_dynamic-update-slice_fusion.3.refs_1_, ...), custom_call_target="tpu_custom_call" | custom-call | flops 1610612736 | bytes 11705344 | tf_op jit(solution)/shard_map/pallas_call | solution.py:252
  55.4 10.3 %shard_map.130 = (f32[8,192,96]{2,1,0:T(8,128)S(1)}, f32[8,192,96]{2,1,0:T(8,128)S(1)}, bf16[8,96,192]{2,1,0:T(8,128)(2,1)S(1)}, bf16[8,192,96]{2,1,0:T(8,128)(2,1)S(1)}) custom-call(bf16[8,96,4096]{2,1,0:T(8,128)(2,1)S(1)} %get-tuple-element.120.x_ref, f32[8,1,96]{2,1,0:T(1,128)S(1)} %get-tuple-element.121.prob_ref, ...), custom_call_target="tpu_custom_call" | custom-call | flops 2415919104 | bytes 33229824 | tf_op jit(solution)/shard_map/pallas_call | solution.py:252
  65.7 3.6 %collective-permute-done.22.own1 = bf16[128,4096]{1,0:T(8,128)(2,1)S(1)} collective-permute-done((bf16[128,4096]{1,0:T(8,128)(2,1)S(1)}, bf16[128,4096]{1,0:T(8,128)(2,1)S(1)}, u32[]{:S(2)}, u32[]{:S(2)}) %collective-permute-start.22) | collective-permute-done | bytes 1048608 | tf_op jit(solution)/shard_map/ppermute | solution.py:33
  69.3 7.7 %shard_map.131 = (bf16[256,4096]{1,0:T(8,128)(2,1)S(1)}, bf16[256,4096]{1,0:T(8,128)(2,1)S(1)}) custom-call(bf16[2,256,384]{2,1,0:T(8,128)(2,1)S(1)} %get-tuple-element.117.put_ref, bf16[8,96,192]{2,1,0:T(8,128)(2,1)S(1)} %get-tuple-element.126.refs_0_, bf16[8,192,4096]{2,1,0:T(8,128)(2,1)} %down_ref.1), custom_call_target="tpu_custom_call" | custom-call | flops 2818572288 | bytes 17465344 | tf_op jit(solution)/shard_map/pallas_call | solution.py:252
  77.6 4.6 %shard_map.132 = (bf16[8,96,4096]{2,1,0:T(8,128)(2,1)S(1)}, bf16[8,96,4096]{2,1,0:T(8,128)(2,1)}) custom-call(bf16[128,4096]{1,0:T(8,128)(2,1)S(1)} %constant_dynamic-update-slice_fusion.21.own0, bf16[128,4096]{1,0:T(8,128)(2,1)S(1)} %collective-permute-done.22.own1, bf16[128,4096]{1,0:T(8,128)(2,1)S(1)} %collective-permute-done.23.other0, ...), custom_call_target="tpu_custom_call" | custom-call | flops 1610612736 | bytes 17170432 | tf_op jit(solution)/shard_map/pallas_call | solution.py:252
  84.8 8.5 %shard_map.133 = (bf16[8,96,192]{2,1,0:T(8,128)(2,1)S(1)}, bf16[8,96,192]{2,1,0:T(8,128)(2,1)S(1)}, bf16[8,192,96]{2,1,0:T(8,128)(2,1)S(1)}, bf16[8,192,96]{2,1,0:T(8,128)(2,1)S(1)}, bf16[2,256,128]{2,1,0:T(8,128)(2,1)S(1)}) custom-call(bf16[8,96,4096]{2,1,0:T(8,128)(2,1)S(1)} %get-tuple-element.136.x_ref, ...), custom_call_target="tpu_custom_call" | custom-call | flops 1207959552 | bytes 21859328 | tf_op jit(solution)/shard_map/pallas_call | solution.py:252
  93.3 4.8 %shard_map.134 = (bf16[256,2048]{1,0:T(8,128)(2,1)S(1)}, bf16[256,2048]{1,0:T(8,128)(2,1)S(1)}) custom-call(bf16[2,256,384]{2,1,0:T(8,128)(2,1)S(1)} %get-tuple-element.117.put_ref, bf16[8,96,192]{2,1,0:T(8,128)(2,1)S(1)} %get-tuple-element.145.refs_0_, bf16[8,96,192]{2,1,0:T(8,128)(2,1)S(1)} %get-tuple-element.146.refs_1_, ...), custom_call_target="tpu_custom_call" | custom-call | flops 2013265920 | bytes 28246016 | tf_op jit(solution)/shard_map/pallas_call | solution.py:252
  98.5 5.1 %shard_map.135 = (bf16[256,2176]{1,0:T(8,128)(2,1)S(1)}, bf16[256,2176]{1,0:T(8,128)(2,1)S(1)}) custom-call(bf16[2,256,384]{2,1,0:T(8,128)(2,1)S(1)} %get-tuple-element.117.put_ref, bf16[8,96,192]{2,1,0:T(8,128)(2,1)S(1)} %get-tuple-element.145.refs_0_, bf16[8,96,192]{2,1,0:T(8,128)(2,1)S(1)} %get-tuple-element.146.refs_1_, ...), custom_call_target="tpu_custom_call" | custom-call | flops 2013265920 | bytes 28508160 | tf_op jit(solution)/shard_map/pallas_call | solution.py:252
  105.2 1.6 collective-permute-start.30
  108.0 7.4 %shard_map.136 = bf16[8,192,4096]{2,1,0:T(8,128)(2,1)} custom-call(bf16[8,96,4096]{2,1,0:T(8,128)(2,1)S(1)} %bitcast.1, bf16[8,192,96]{2,1,0:T(8,128)(2,1)S(1)} %get-tuple-element.156.left), custom_call_target="tpu_custom_call" | custom-call | flops 1207959552 | bytes 19169280 | tf_op jit(solution)/shard_map/pallas_call | solution.py:396
  115.4 4.4 %collective-permute-done.30 = bf16[64,4096]{1,0:T(8,128)(2,1)S(1)} collective-permute-done((bf16[64,4096]{1,0:T(8,128)(2,1)S(1)}, bf16[64,4096]{1,0:T(8,128)(2,1)S(1)}, u32[]{:S(2)}, u32[]{:S(2)}) %collective-permute-start.30) | collective-permute-done | bytes 524320 | tf_op jit(solution)/shard_map/ppermute | solution.py:33
  122.3 1.5 collective-permute-start.32
  124.4 7.3 %shard_map.137 = bf16[8,192,4096]{2,1,0:T(8,128)(2,1)} custom-call(bf16[8,96,4096]{2,1,0:T(8,128)(2,1)S(1)} %get-tuple-element.120.x_ref, bf16[8,192,96]{2,1,0:T(8,128)(2,1)S(1)} %get-tuple-element.165.left), custom_call_target="tpu_custom_call" | custom-call | flops 1207959552 | bytes 19169280 | tf_op jit(solution)/shard_map/pallas_call | solution.py:396
  131.7 1.8 %collective-permute-done.31 = bf16[128,2176]{1,0:T(8,128)(2,1)S(1)} collective-permute-done((bf16[128,2176]{1,0:T(8,128)(2,1)S(1)}, bf16[128,2176]{1,0:T(8,128)(2,1)S(1)}, u32[]{:S(2)}, u32[]{:S(2)}) %collective-permute-start.31) | collective-permute-done | bytes 557088 | tf_op jit(solution)/shard_map/ppermute | solution.py:33
  137.2 4.0 %shard_map.138.refs_0_ = bf16[8,192,4096]{2,1,0:T(8,128)(2,1)} custom-call(bf16[8,96,4096]{2,1,0:T(8,128)(2,1)S(1)} %get-tuple-element.120.x_ref, bf16[8,192,96]{2,1,0:T(8,128)(2,1)S(1)} %get-tuple-element.178.left), custom_call_target="tpu_custom_call" | custom-call | flops 603979776 | bytes 9584640 | tf_op jit(solution)/shard_map/pallas_call | solution.py:396
  142.5 1.9 %collective-permute-done.34 = bf16[16,4096]{1,0:T(8,128)(2,1)S(1)} collective-permute-done((bf16[16,4096]{1,0:T(8,128)(2,1)S(1)}, bf16[16,4096]{1,0:T(8,128)(2,1)S(1)}, u32[]{:S(2)}, u32[]{:S(2)}) %collective-permute-start.34) | collective-permute-done | bytes 131104 | tf_op jit(solution)/shard_map/ppermute | solution.py:33
  144.4 1.7 %add_convert_fusion.8 = bf16[16,4096]{1,0:T(8,128)(2,1)} fusion(bf16[16,4096]{1,0:T(8,128)(2,1)S(1)} %collective-permute-done.34, bf16[32,4096]{1,0:T(8,128)(2,1)S(1)} %collective-permute-done.33, bf16[64,4096]{1,0:T(8,128)(2,1)S(1)} %collective-permute-done.30, bf16[128,4096]{1,0:T(8,128)(2,1)S(1)} %collective-permute-done.26, ...), kind=kLoop, calls=%fused_computation.13 | loop fusion | flops 786432 | bytes 917504 | tf_op jit(solution)/shard_map/convert_element_type | solution.py:40
  146.6 4.0 %shard_map.139 = bf16[8,192,4096]{2,1,0:T(8,128)(2,1)} custom-call(bf16[8,96,4096]{2,1,0:T(8,128)(2,1)S(1)} %get-tuple-element.120.x_ref, bf16[8,192,96]{2,1,0:T(8,128)(2,1)S(1)} %get-tuple-element.178.left, bf16[8,192,4096]{2,1,0:T(8,128)(2,1)} %shard_map.138.refs_0_), custom_call_target="tpu_custom_call", output_to_operand_aliasing={{}: (2, {})} | custom-call | flops 603979776 | bytes 9584640 | tf_op jit(solution)/shard_map/pallas_call | solution.py:396
  150.6 2.5 %collective-permute-start.39 = (bf16[16,2176]{1,0:T(8,128)(2,1)S(1)}, bf16[16,2176]{1,0:T(8,128)(2,1)S(1)}, u32[]{:S(2)}, u32[]{:S(2)}) collective-permute-start(bf16[16,2176]{1,0:T(8,128)(2,1)S(1)} %add_convert_fusion.12), channel_id=1, source_target_pairs={{0,4},{1,5},{2,6},{3,7},{4,0},{5,1},{6,2},{7,3},{8,12},{9,13},{10,... | collective-permute-start | bytes 208904 | tf_op jit(solution)/shard_map/ppermute | solution.py:33
  153.1 3.5 %collective-permute-done.39 = bf16[16,2176]{1,0:T(8,128)(2,1)S(1)} collective-permute-done((bf16[16,2176]{1,0:T(8,128)(2,1)S(1)}, bf16[16,2176]{1,0:T(8,128)(2,1)S(1)}, u32[]{:S(2)}, u32[]{:S(2)}) %collective-permute-start.39) | collective-permute-done | bytes 69664 | tf_op jit(solution)/shard_map/ppermute | solution.py:33
  (127 shorter events, 33.7 us)
Async XLA Ops:
  0.6 11.2 %collective-permute-start.2 = (bf16[16,4096]{1,0:T(8,128)(2,1)}, bf16[16,4096]{1,0:T(8,128)(2,1)S(1)}, u32[]{:S(2)}, u32[]{:S(2)}) collective-permute-start(bf16[16,4096]{1,0:T(8,128)(2,1)} %param.8), channel_id=1, source_target_pairs={{0,4},{1,5},{2,6},{3,7},{4,0},{5,1},{6,2},{7,3},{8,12},{9,13},{10,... | collective-permute-start | bytes 393224 | tf_op jit(solution)/shard_map/ppermute | solution.py:33
  4.7 7.1 %collective-permute-start.1 = (bf16[16,4096]{1,0:T(8,128)(2,1)}, bf16[16,4096]{1,0:T(8,128)(2,1)S(1)}, u32[]{:S(2)}, u32[]{:S(2)}) collective-permute-start(bf16[16,4096]{1,0:T(8,128)(2,1)} %param.8), channel_id=1, source_target_pairs={{0,2},{1,3},{2,0},{3,1},{4,6},{5,7},{6,4},{7,5},{8,10},{9,11},{10,... | collective-permute-start | bytes 393224 | tf_op jit(solution)/shard_map/ppermute | solution.py:33
  6.3 12.1 %collective-permute-start = (bf16[16,4096]{1,0:T(8,128)(2,1)}, bf16[16,4096]{1,0:T(8,128)(2,1)S(1)}, u32[]{:S(2)}, u32[]{:S(2)}) collective-permute-start(bf16[16,4096]{1,0:T(8,128)(2,1)} %param.8), channel_id=1, source_target_pairs={{0,8},{1,17},{2,10},{3,19},{4,12},{5,21},{6,14},{7,23},{8,0},{9,25... | collective-permute-start | bytes 393224 | tf_op jit(solution)/shard_map/ppermute | solution.py:33
  11.8 9.4 %collective-permute-start.8 = (bf16[16,128]{1,0:T(8,128)(2,1)S(1)}, bf16[16,128]{1,0:T(8,128)(2,1)S(1)}, u32[]{:S(2)}, u32[]{:S(2)}) collective-permute-start(bf16[16,128]{1,0:T(8,128)(2,1)S(1)} %pad_maximum_fusion.7), channel_id=1, source_target_pairs={{0,6},{1,7},{2,4},{3,5},{4,2},{5,3},{6,0},{7,1},{8,14},{9,15},{10,... | collective-permute-start | bytes 12296 | tf_op jit(solution)/shard_map/ppermute | solution.py:33
  14.8 9.4 %collective-permute-start.7 = (bf16[16,128]{1,0:T(8,128)(2,1)S(1)}, bf16[16,128]{1,0:T(8,128)(2,1)S(1)}, u32[]{:S(2)}, u32[]{:S(2)}) collective-permute-start(bf16[16,128]{1,0:T(8,128)(2,1)S(1)} %pad_maximum_fusion.7), channel_id=1, source_target_pairs={{0,2},{1,3},{2,0},{3,1},{4,6},{5,7},{6,4},{7,5},{8,10},{9,11},{10,... | collective-permute-start | bytes 12296 | tf_op jit(solution)/shard_map/ppermute | solution.py:33
  16.9 9.0 %collective-permute-start.4 = (bf16[32,4096]{1,0:T(8,128)(2,1)S(1)}, bf16[32,4096]{1,0:T(8,128)(2,1)S(1)}, u32[]{:S(2)}, u32[]{:S(2)}) collective-permute-start(bf16[32,4096]{1,0:T(8,128)(2,1)S(1)} %pad_maximum_fusion.2), channel_id=1, source_target_pairs={{0,8},{1,17},{2,10},{3,19},{4,12},{5,21},{6,14},{7,23},{8,0},{9,25... | collective-permute-start | bytes 786440 | tf_op jit(solution)/shard_map/ppermute | solution.py:33
  21.2 17.5 %collective-permute-start.20 = (bf16[16,4096]{1,0:T(8,128)(2,1)S(1)}, bf16[16,4096]{1,0:T(8,128)(2,1)S(1)}, u32[]{:S(2)}, u32[]{:S(2)}) collective-permute-start(bf16[16,4096]{1,0:T(8,128)(2,1)S(1)} %copy-done), channel_id=1, source_target_pairs={{0,6},{1,7},{2,4},{3,5},{4,2},{5,3},{6,0},{7,1},{8,14},{9,15},{10,... | collective-permute-start | bytes 393224 | tf_op jit(solution)/shard_map/ppermute | solution.py:33
  24.2 15.3 %collective-permute-start.19 = (bf16[16,4096]{1,0:T(8,128)(2,1)S(1)}, bf16[16,4096]{1,0:T(8,128)(2,1)S(1)}, u32[]{:S(2)}, u32[]{:S(2)}) collective-permute-start(bf16[16,4096]{1,0:T(8,128)(2,1)S(1)} %copy-done), channel_id=1, source_target_pairs={{0,2},{1,3},{2,0},{3,1},{4,6},{5,7},{6,4},{7,5},{8,10},{9,11},{10,... | collective-permute-start | bytes 393224 | tf_op jit(solution)/shard_map/ppermute | solution.py:33
  25.9 8.3 %collective-permute-start.11 = (bf16[64,128]{1,0:T(8,128)(2,1)S(1)}, bf16[64,128]{1,0:T(8,128)(2,1)S(1)}, u32[]{:S(2)}, u32[]{:S(2)}) collective-permute-start(bf16[64,128]{1,0:T(8,128)(2,1)S(1)} %pad_maximum_fusion.6), channel_id=1, source_target_pairs={{0,8},{1,17},{2,10},{3,19},{4,12},{5,21},{6,14},{7,23},{8,0},{9,25... | collective-permute-start | bytes 49160 | tf_op jit(solution)/shard_map/ppermute | solution.py:33
  27.3 7.0 %collective-permute-start.9 = (bf16[16,4096]{1,0:T(8,128)(2,1)S(1)}, bf16[16,4096]{1,0:T(8,128)(2,1)S(1)}, u32[]{:S(2)}, u32[]{:S(2)}) collective-permute-start(bf16[16,4096]{1,0:T(8,128)(2,1)S(1)} %collective-permute-done.3.after), channel_id=1, source_target_pairs={{0,8},{1,17},{2,10},{3,19},{4,12},{5,21},{6,14},{7,23},{8,0},{9,25... | collective-permute-start | bytes 393224 | tf_op jit(solution)/shard_map/ppermute | solution.py:33
  28.0 9.2 %collective-permute-start.10 = (bf16[64,4096]{1,0:T(8,128)(2,1)S(1)}, bf16[64,4096]{1,0:T(8,128)(2,1)S(1)}, u32[]{:S(2)}, u32[]{:S(2)}) collective-permute-start(bf16[64,4096]{1,0:T(8,128)(2,1)S(1)} %pad_maximum_fusion), channel_id=1, source_target_pairs={{0,16},{1,9},{2,18},{3,11},{4,20},{5,13},{6,22},{7,15},{8,24},{9,1... | collective-permute-start | bytes 1572872 | tf_op jit(solution)/shard_map/ppermute | solution.py:33
  34.2 8.2 %collective-permute-start.18 = (bf16[16,4096]{1,0:T(8,128)(2,1)S(1)}, bf16[16,4096]{1,0:T(8,128)(2,1)S(1)}, u32[]{:S(2)}, u32[]{:S(2)}) collective-permute-start(bf16[16,4096]{1,0:T(8,128)(2,1)S(1)} %copy-done), channel_id=1, source_target_pairs={{0,4},{1,5},{2,6},{3,7},{4,0},{5,1},{6,2},{7,3},{8,12},{9,13},{10,... | collective-permute-start | bytes 393224 | tf_op jit(solution)/shard_map/ppermute | solution.py:33
  34.3 14.2 %collective-permute-start.14 = (bf16[64,4096]{1,0:T(8,128)(2,1)S(1)}, bf16[64,4096]{1,0:T(8,128)(2,1)S(1)}, u32[]{:S(2)}, u32[]{:S(2)}) collective-permute-start(bf16[64,4096]{1,0:T(8,128)(2,1)S(1)} %constant_dynamic-update-slice_fusion.refs_0_), channel_id=1, source_target_pairs={{0,1},{1,0},{2,3},{3,2},{4,5},{5,4},{6,7},{7,6},{8,9},{9,8},{10,11... | collective-permute-start | bytes 1572872 | tf_op jit(solution)/shard_map/ppermute | solution.py:33
  37.3 10.5 %collective-permute-start.13 = (bf16[128,128]{1,0:T(8,128)(2,1)S(1)}, bf16[128,128]{1,0:T(8,128)(2,1)S(1)}, u32[]{:S(2)}, u32[]{:S(2)}) collective-permute-start(bf16[128,128]{1,0:T(8,128)(2,1)S(1)} %get-tuple-element.191), channel_id=1, source_target_pairs={{0,16},{1,9},{2,18},{3,11},{4,20},{5,13},{6,22},{7,15},{8,24},{9,1... | collective-permute-start | bytes 98312 | tf_op jit(solution)/shard_map/ppermute | solution.py:33
  38.8 9.0 %collective-permute-start.12 = (bf16[32,4096]{1,0:T(8,128)(2,1)S(1)}, bf16[32,4096]{1,0:T(8,128)(2,1)S(1)}, u32[]{:S(2)}, u32[]{:S(2)}) collective-permute-start(bf16[32,4096]{1,0:T(8,128)(2,1)S(1)} %pad_maximum_fusion.4), channel_id=1, source_target_pairs={{0,16},{1,9},{2,18},{3,11},{4,20},{5,13},{6,22},{7,15},{8,24},{9,1... | collective-permute-start | bytes 786440 | tf_op jit(solution)/shard_map/ppermute | solution.py:33
  42.4 11.6 %collective-permute-start.21 = (bf16[64,4096]{1,0:T(8,128)(2,1)S(1)}, bf16[64,4096]{1,0:T(8,128)(2,1)S(1)}, u32[]{:S(2)}, u32[]{:S(2)}) collective-permute-start(bf16[64,4096]{1,0:T(8,128)(2,1)S(1)} %pad_maximum_fusion.1), channel_id=1, source_target_pairs={{0,8},{1,17},{2,10},{3,19},{4,12},{5,21},{6,14},{7,23},{8,0},{9,25... | collective-permute-start | bytes 1572872 | tf_op jit(solution)/shard_map/ppermute | solution.py:33
  43.1 7.0 %collective-permute-start.15 = (bf16[128,4096]{1,0:T(8,128)(2,1)S(1)}, bf16[128,4096]{1,0:T(8,128)(2,1)S(1)}, u32[]{:S(2)}, u32[]{:S(2)}) collective-permute-start(bf16[128,4096]{1,0:T(8,128)(2,1)S(1)} %constant_dynamic-update-slice_fusion.3.refs_1_), channel_id=1, source_target_pairs={{0,1},{1,0},{2,3},{3,2},{4,5},{5,4},{6,7},{7,6},{8,9},{9,8},{10,11... | collective-permute-start | bytes 3145736 | tf_op jit(solution)/shard_map/ppermute | solution.py:33
  54.0 11.6 %collective-permute-start.23 = (bf16[128,4096]{1,0:T(8,128)(2,1)S(1)}, bf16[128,4096]{1,0:T(8,128)(2,1)S(1)}, u32[]{:S(2)}, u32[]{:S(2)}) collective-permute-start(bf16[128,4096]{1,0:T(8,128)(2,1)S(1)} %constant_dynamic-update-slice_fusion.21.own0), channel_id=1, source_target_pairs={{0,1},{1,0},{2,3},{3,2},{4,5},{5,4},{6,7},{7,6},{8,9},{9,8},{10,11... | collective-permute-start | bytes 3145736 | tf_op jit(solution)/shard_map/ppermute | solution.py:33
  54.5 14.8 %collective-permute-start.22 = (bf16[128,4096]{1,0:T(8,128)(2,1)S(1)}, bf16[128,4096]{1,0:T(8,128)(2,1)S(1)}, u32[]{:S(2)}, u32[]{:S(2)}) collective-permute-start(bf16[128,4096]{1,0:T(8,128)(2,1)S(1)} %constant_dynamic-update-slice_fusion.21.own0), channel_id=1, source_target_pairs={{0,16},{1,9},{2,18},{3,11},{4,20},{5,13},{6,22},{7,15},{8,24},{9,1... | collective-permute-start | bytes 3145736 | tf_op jit(solution)/shard_map/ppermute | solution.py:33
  69.3 7.8 %collective-permute-start.24 = (bf16[128,4096]{1,0:T(8,128)(2,1)S(1)}, bf16[128,4096]{1,0:T(8,128)(2,1)S(1)}, u32[]{:S(2)}, u32[]{:S(2)}) collective-permute-start(bf16[128,4096]{1,0:T(8,128)(2,1)S(1)} %collective-permute-done.22.own1), channel_id=1, source_target_pairs={{0,1},{1,0},{2,3},{3,2},{4,5},{5,4},{6,7},{7,6},{8,9},{9,8},{10,11... | collective-permute-start | bytes 3145736 | tf_op jit(solution)/shard_map/ppermute | solution.py:33
  83.7 14.9 %collective-permute-start.26 = (bf16[128,4096]{1,0:T(8,128)(2,1)S(1)}, bf16[128,4096]{1,0:T(8,128)(2,1)S(1)}, u32[]{:S(2)}, u32[]{:S(2)}) collective-permute-start(bf16[128,4096]{1,0:T(8,128)(2,1)S(1)} %add_convert_fusion), channel_id=1, source_target_pairs={{0,16},{1,9},{2,18},{3,11},{4,20},{5,13},{6,22},{7,15},{8,24},{9,1... | collective-permute-start | bytes 3145736 | tf_op jit(solution)/shard_map/ppermute | solution.py:33
  98.1 8.6 %collective-permute-start.28 = (bf16[256,2048]{1,0:T(8,128)(2,1)S(1)}, bf16[256,2048]{1,0:T(8,128)(2,1)S(1)}, u32[]{:S(2)}, u32[]{:S(2)}) collective-permute-start(bf16[256,2048]{1,0:T(8,128)(2,1)S(1)} %get-tuple-element.151), channel_id=1, source_target_pairs={{0,1},{1,0},{2,3},{3,2},{4,5},{5,4},{6,7},{7,6},{8,9},{9,8},{10,11... | collective-permute-start | bytes 3145736 | tf_op jit(solution)/shard_map/ppermute | solution.py:33
  103.7 16.1 %collective-permute-start.27 = (bf16[256,2176]{1,0:T(8,128)(2,1)S(1)}, bf16[256,2176]{1,0:T(8,128)(2,1)S(1)}, u32[]{:S(2)}, u32[]{:S(2)}) collective-permute-start(bf16[256,2176]{1,0:T(8,128)(2,1)S(1)} %get-tuple-element.148), channel_id=1, source_target_pairs={{0,1},{1,0},{2,3},{3,2},{4,5},{5,4},{6,7},{7,6},{8,9},{9,8},{10,11... | collective-permute-start | bytes 3342344 | tf_op jit(solution)/shard_map/ppermute | solution.py:33
  105.2 14.7 %collective-permute-start.30 = (bf16[64,4096]{1,0:T(8,128)(2,1)S(1)}, bf16[64,4096]{1,0:T(8,128)(2,1)S(1)}, u32[]{:S(2)}, u32[]{:S(2)}) collective-permute-start(bf16[64,4096]{1,0:T(8,128)(2,1)S(1)} %add_convert_fusion.2), channel_id=1, source_target_pairs={{0,8},{1,17},{2,10},{3,19},{4,12},{5,21},{6,14},{7,23},{8,0},{9,25... | collective-permute-start | bytes 1572872 | tf_op jit(solution)/shard_map/ppermute | solution.py:33
  106.9 13.0 %collective-permute-start.29 = (bf16[128,2048]{1,0:T(8,128)(2,1)S(1)}, bf16[128,2048]{1,0:T(8,128)(2,1)S(1)}, u32[]{:S(2)}, u32[]{:S(2)}) collective-permute-start(bf16[128,2048]{1,0:T(8,128)(2,1)S(1)} %add_convert_fusion.3), channel_id=1, source_target_pairs={{0,16},{1,9},{2,18},{3,11},{4,20},{5,13},{6,22},{7,15},{8,24},{9,1... | collective-permute-start | bytes 1572872 | tf_op jit(solution)/shard_map/ppermute | solution.py:33
  121.2 12.4 %collective-permute-start.31 = (bf16[128,2176]{1,0:T(8,128)(2,1)S(1)}, bf16[128,2176]{1,0:T(8,128)(2,1)S(1)}, u32[]{:S(2)}, u32[]{:S(2)}) collective-permute-start(bf16[128,2176]{1,0:T(8,128)(2,1)S(1)} %add_convert_fusion.1), channel_id=1, source_target_pairs={{0,16},{1,9},{2,18},{3,11},{4,20},{5,13},{6,22},{7,15},{8,24},{9,1... | collective-permute-start | bytes 1671176 | tf_op jit(solution)/shard_map/ppermute | solution.py:33
  122.3 9.4 %collective-permute-start.32 = (bf16[64,2048]{1,0:T(8,128)(2,1)S(1)}, bf16[64,2048]{1,0:T(8,128)(2,1)S(1)}, u32[]{:S(2)}, u32[]{:S(2)}) collective-permute-start(bf16[64,2048]{1,0:T(8,128)(2,1)S(1)} %add_convert_fusion.6), channel_id=1, source_target_pairs={{0,8},{1,17},{2,10},{3,19},{4,12},{5,21},{6,14},{7,23},{8,0},{9,25... | collective-permute-start | bytes 786440 | tf_op jit(solution)/shard_map/ppermute | solution.py:33
  123.8 7.9 %collective-permute-start.33 = (bf16[32,4096]{1,0:T(8,128)(2,1)S(1)}, bf16[32,4096]{1,0:T(8,128)(2,1)S(1)}, u32[]{:S(2)}, u32[]{:S(2)}) collective-permute-start(bf16[32,4096]{1,0:T(8,128)(2,1)S(1)} %add_convert_fusion.5), channel_id=1, source_target_pairs={{0,2},{1,3},{2,0},{3,1},{4,6},{5,7},{6,4},{7,5},{8,10},{9,11},{10,... | collective-permute-start | bytes 786440 | tf_op jit(solution)/shard_map/ppermute | solution.py:33
  134.7 7.2 %collective-permute-start.35 = (bf16[64,2176]{1,0:T(8,128)(2,1)S(1)}, bf16[64,2176]{1,0:T(8,128)(2,1)S(1)}, u32[]{:S(2)}, u32[]{:S(2)}) collective-permute-start(bf16[64,2176]{1,0:T(8,128)(2,1)S(1)} %add_convert_fusion.4), channel_id=1, source_target_pairs={{0,8},{1,17},{2,10},{3,19},{4,12},{5,21},{6,14},{7,23},{8,0},{9,25... | collective-permute-start | bytes 835592 | tf_op jit(solution)/shard_map/ppermute | solution.py:33
  136.1 8.3 %collective-permute-start.34 = (bf16[16,4096]{1,0:T(8,128)(2,1)S(1)}, bf16[16,4096]{1,0:T(8,128)(2,1)S(1)}, u32[]{:S(2)}, u32[]{:S(2)}) collective-permute-start(bf16[16,4096]{1,0:T(8,128)(2,1)S(1)} %add_convert_fusion.9), channel_id=1, source_target_pairs={{0,4},{1,5},{2,6},{3,7},{4,0},{5,1},{6,2},{7,3},{8,12},{9,13},{10,... | collective-permute-start | bytes 393224 | tf_op jit(solution)/shard_map/ppermute | solution.py:33
  142.1 8.5 %collective-permute-start.38 = (bf16[32,2176]{1,0:T(8,128)(2,1)S(1)}, bf16[32,2176]{1,0:T(8,128)(2,1)S(1)}, u32[]{:S(2)}, u32[]{:S(2)}) collective-permute-start(bf16[32,2176]{1,0:T(8,128)(2,1)S(1)} %add_convert_fusion.7), channel_id=1, source_target_pairs={{0,2},{1,3},{2,0},{3,1},{4,6},{5,7},{6,4},{7,5},{8,10},{9,11},{10,... | collective-permute-start | bytes 417800 | tf_op jit(solution)/shard_map/ppermute | solution.py:33
  146.1 7.0 %collective-permute-start.37 = (bf16[16,2048]{1,0:T(8,128)(2,1)S(1)}, bf16[16,2048]{1,0:T(8,128)(2,1)S(1)}, u32[]{:S(2)}, u32[]{:S(2)}) collective-permute-start(bf16[16,2048]{1,0:T(8,128)(2,1)S(1)} %add_convert_fusion.14), channel_id=1, source_target_pairs={{0,4},{1,5},{2,6},{3,7},{4,0},{5,1},{6,2},{7,3},{8,12},{9,13},{10,... | collective-permute-start | bytes 196616 | tf_op jit(solution)/shard_map/ppermute | solution.py:33
  (11 other events, 78.3 us)

commit v12 on v11

--- a/solution.py
+++ b/solution.py
@@ -501,12 +501,6 @@
     def leaving(parts, start, stop):
         return add(*(part[start:stop] for part in parts))
 
-    def by_second(parts):
-        return parts + [swap(leaving(parts, 2 * quarter, 4 * quarter), Y, X)]
-
-    def by_first(parts):
-        return parts + [swap(leaving(parts, quarter, 2 * quarter), X, Y)]
-
     def by_near(parts):
         return parts + [swap(leaving(parts, 2 * tok_count, 4 * tok_count), Z1)]
 
@@ -522,42 +516,41 @@
     )
     left, left_other = back_call(put, [dg, du], weights, 0, middle)
     left = [left, swap(left_other, CORE)]
-    left[0], mixed[2], dg, du = together(left[0], mixed[2], dg, du)
-    mixed = by_first(mixed)
+    left[0], mixed[2] = together(left[0], mixed[2])
+    rows, dg, du = together(leaving(mixed, quarter, 2 * quarter), dg, du)
+    mixed.append(swap(rows, X, Y))
     right, right_other = back_call(put, [dg, du], weights, middle, width, share)
     right = [right, swap(right_other, CORE)]
 
     right[0], left[1] = together(right[0], left[1])
     rows, ht = together(leaving(left, 2 * quarter, 4 * quarter), ht)
     left.append(swap(rows, Y, X))
+    mixed_rows, ht = together(leaving(mixed, 2 * tok_count, 4 * tok_count), ht)
+    mixed.append(swap(mixed_rows, Z1))
     down_weight_grad = grad_call(far_c, ht)
 
-    right[1], left[2], mixed[3], down_weight_grad = together(
-        right[1], left[2], mixed[3], down_weight_grad
+    right[1], left[2], mixed[4], down_weight_grad = together(
+        right[1], left[2], mixed[4], down_weight_grad
     )
     rows, left_rows, mixed_rows, dgt = together(
         leaving(right, 2 * quarter, 4 * quarter),
         leaving(left, quarter, 2 * quarter),
-        leaving(mixed, 2 * tok_count, 4 * tok_count),
+        leaving(mixed, tok_count, 2 * tok_count),
         dgt,
     )
     right.append(swap(rows, Y, X))
     left.append(swap(left_rows, X, Y))
-    mixed.append(swap(mixed_rows, Z1))
+    mixed.append(swap(mixed_rows, Z2))
     gate_weight_grad = grad_call(x, dgt)
 
-    right[2], left[3], mixed[4], gate_weight_grad = together(
-        right[2], left[3], mixed[4], gate_weight_grad
-    )
-    rows, left_rows, mixed_rows, dut = together(
+    right[2], left[3], gate_weight_grad = together(right[2], left[3], gate_weight_grad)
+    rows, left_rows, dut = together(
         leaving(right, quarter, 2 * quarter),
         leaving(left, 2 * tok_count, 4 * tok_count),
-        leaving(mixed, tok_count, 2 * tok_count),
         dut,
     )
     right.append(swap(rows, X, Y))
     left.append(swap(left_rows, Z1))
-    mixed.append(swap(mixed_rows, Z2))
     up_weight_grad = grad_call(x, dut, 0, local // 2)
 
     right[3], left[4], up_weight_grad = together(right[3], left[4], up_weight_grad)

time: 159 us -> 156 us (0.981)
  waiting for transfers between devices: 24.7 us -> 20.8 us
    ppermute x40, waiting for transfers between devices: 24.7 us -> 20.8 us  [swap(): return lax.ppermute(values, AXES, pairs)]
  transfers between devices with their start and end apart: 40 -> 40, of which waited for: 10 -> 12; matrix products, arithmetic and copies ran while one was open for 5% -> 6% of each run, Pallas kernels for 49% -> 49%
where the time goes in v12:
time: 156 us; the launch traced here: 155 us
  Pallas kernels  76.8 us (49%)
  starting transfers between devices  42.2 us (27%)
  waiting for transfers between devices  20.8 us (13%)
  other arithmetic  10.8 us (7%)
  local copies, waits for them, and re-layouts  3.42 us (2%)
    pallas_call x7, Pallas kernels, call(): pl.pallas_call(kernel, grid=(grid,), in_specs=ins, out_specs=outs, out_sh...  45 us
    ppermute x40, starting transfers between devices, swap(): return lax.ppermute(values, AXES, pairs)  42.2 us
    pallas_call x4, Pallas kernels, grad_call(): pl.pallas_call(grad_kernel, grid=(count,), in_specs=ins, out_specs=own(sh...  22.6 us
    ppermute x40, waiting for transfers between devices, swap(): return lax.ppermute(values, AXES, pairs)  20.8 us
    pallas_call x2, Pallas kernels, fetch_call(): pl.pallas_call(fetch_kernel, in_specs=[pl.BlockSpec(memory_space=pl.ANY)]...  9.17 us
    convert_element_type x15, other arithmetic, add(): return total.astype(jnp.bfloat16)  7.29 us
    unnamed x25, local copies, waits for them, and re-layouts  3.29 us
  transfers between devices with their start and end apart: 40, of which 12 were waited for; matrix products, arithmetic and copies ran while one was open for 6% of the time, Pallas kernels for 49%

profile of v12, /device:TPU:0, one launch (start us, length us, event | category | flops | bytes accessed | tf_op | source)
XLA Modules:
  0.0 155.1 jit_solution(11415310375186950906)
XLA Ops:
  0.6 4.1 %collective-permute-start.2 = (bf16[16,4096]{1,0:T(8,128)(2,1)}, bf16[16,4096]{1,0:T(8,128)(2,1)S(1)}, u32[]{:S(2)}, u32[]{:S(2)}) collective-permute-start(bf16[16,4096]{1,0:T(8,128)(2,1)} %param.8), channel_id=1, source_target_pairs={{0,4},{1,5},{2,6},{3,7},{4,0},{5,1},{6,2},{7,3},{8,12},{9,13},{10,... | collective-permute-start | bytes 393224 | tf_op jit(solution)/shard_map/ppermute | solution.py:33
  4.7 1.6 %collective-permute-start.1 = (bf16[16,4096]{1,0:T(8,128)(2,1)}, bf16[16,4096]{1,0:T(8,128)(2,1)S(1)}, u32[]{:S(2)}, u32[]{:S(2)}) collective-permute-start(bf16[16,4096]{1,0:T(8,128)(2,1)} %param.8), channel_id=1, source_target_pairs={{0,2},{1,3},{2,0},{3,1},{4,6},{5,7},{6,4},{7,5},{8,10},{9,11},{10,... | collective-permute-start | bytes 393224 | tf_op jit(solution)/shard_map/ppermute | solution.py:33
  11.8 3.0 %collective-permute-start.8 = (bf16[16,128]{1,0:T(8,128)(2,1)S(1)}, bf16[16,128]{1,0:T(8,128)(2,1)S(1)}, u32[]{:S(2)}, u32[]{:S(2)}) collective-permute-start(bf16[16,128]{1,0:T(8,128)(2,1)S(1)} %pad_maximum_fusion.7), channel_id=1, source_target_pairs={{0,6},{1,7},{2,4},{3,5},{4,2},{5,3},{6,0},{7,1},{8,14},{9,15},{10,... | collective-permute-start | bytes 12296 | tf_op jit(solution)/shard_map/ppermute | solution.py:33
  14.8 2.0 %collective-permute-start.3 = (bf16[16,4096]{1,0:T(8,128)(2,1)S(1)}, bf16[16,4096]{1,0:T(8,128)(2,1)S(1)}, u32[]{:S(2)}, u32[]{:S(2)}) collective-permute-start(bf16[16,4096]{1,0:T(8,128)(2,1)S(1)} %collective-permute-done.2), channel_id=1, source_target_pairs={{0,2},{1,3},{2,0},{3,1},{4,6},{5,7},{6,4},{7,5},{8,10},{9,11},{10,... | collective-permute-start | bytes 393224 | tf_op jit(solution)/shard_map/ppermute | solution.py:33
  16.9 1.6 %collective-permute-start.4 = (bf16[32,4096]{1,0:T(8,128)(2,1)S(1)}, bf16[32,4096]{1,0:T(8,128)(2,1)S(1)}, u32[]{:S(2)}, u32[]{:S(2)}) collective-permute-start(bf16[32,4096]{1,0:T(8,128)(2,1)S(1)} %pad_maximum_fusion.2), channel_id=1, source_target_pairs={{0,8},{1,17},{2,10},{3,19},{4,12},{5,21},{6,14},{7,23},{8,0},{9,25... | collective-permute-start | bytes 786440 | tf_op jit(solution)/shard_map/ppermute | solution.py:33
  19.4 1.6 %collective-permute-start.5 = (bf16[32,4096]{1,0:T(8,128)(2,1)S(1)}, bf16[32,4096]{1,0:T(8,128)(2,1)S(1)}, u32[]{:S(2)}, u32[]{:S(2)}) collective-permute-start(bf16[32,4096]{1,0:T(8,128)(2,1)S(1)} %pad_maximum_fusion.3), channel_id=1, source_target_pairs={{0,16},{1,9},{2,18},{3,11},{4,20},{5,13},{6,22},{7,15},{8,24},{9,1... | collective-permute-start | bytes 786440 | tf_op jit(solution)/shard_map/ppermute | solution.py:33
  21.2 3.0 %collective-permute-start.20 = (bf16[16,4096]{1,0:T(8,128)(2,1)S(1)}, bf16[16,4096]{1,0:T(8,128)(2,1)S(1)}, u32[]{:S(2)}, u32[]{:S(2)}) collective-permute-start(bf16[16,4096]{1,0:T(8,128)(2,1)S(1)} %copy-done), channel_id=1, source_target_pairs={{0,6},{1,7},{2,4},{3,5},{4,2},{5,3},{6,0},{7,1},{8,14},{9,15},{10,... | collective-permute-start | bytes 393224 | tf_op jit(solution)/shard_map/ppermute | solution.py:33
  29.6 4.6 %shard_map.127 = (bf16[8,192,4096]{2,1,0:T(8,128)(2,1)S(1)}, f32[8,128]{1,0:T(8,128)S(1)}) custom-call(bf16[8,192,4096]{2,1,0:T(8,128)(2,1)} %source, bf16[16,4096]{1,0:T(8,128)(2,1)S(1)} %collective-permute-done.3.after), custom_call_target="tpu_custom_call" | custom-call | bytes 12582912 | tf_op jit(solution)/shard_map/pallas_call | solution.py:272
  34.3 2.9 %collective-permute-done.10 = bf16[64,4096]{1,0:T(8,128)(2,1)S(1)} collective-permute-done((bf16[64,4096]{1,0:T(8,128)(2,1)S(1)}, bf16[64,4096]{1,0:T(8,128)(2,1)S(1)}, u32[]{:S(2)}, u32[]{:S(2)}) %collective-permute-start.10) | collective-permute-done | bytes 524320 | tf_op jit(solution)/shard_map/ppermute | solution.py:33
  39.5 2.9 %collective-permute-done.18 = bf16[16,4096]{1,0:T(8,128)(2,1)S(1)} collective-permute-done((bf16[16,4096]{1,0:T(8,128)(2,1)S(1)}, bf16[16,4096]{1,0:T(8,128)(2,1)S(1)}, u32[]{:S(2)}, u32[]{:S(2)}) %collective-permute-start.18) | collective-permute-done | bytes 131104 | tf_op jit(solution)/shard_map/ppermute | solution.py:33
  43.2 4.6 %shard_map.128 = (bf16[8,192,4096]{2,1,0:T(8,128)(2,1)S(1)}, f32[8,128]{1,0:T(8,128)S(1)}) custom-call(bf16[8,192,4096]{2,1,0:T(8,128)(2,1)} %source.1, f32[8,128]{1,0:T(8,128)S(1)} %get-tuple-element.112.after), custom_call_target="tpu_custom_call" | custom-call | bytes 12582912 | tf_op jit(solution)/shard_map/pallas_call | solution.py:272
  50.0 4.0 %shard_map.129 = (bf16[8,96,4096]{2,1,0:T(8,128)(2,1)S(1)}, bf16[2,256,384]{2,1,0:T(8,128)(2,1)S(1)}, bf16[2,384,256]{2,1,0:T(8,128)(2,1)S(1)}, f32[8,1,96]{2,1,0:T(1,128)S(1)}) custom-call(bf16[64,4096]{1,0:T(8,128)(2,1)S(1)} %constant_dynamic-update-slice_fusion.refs_0_, bf16[128,4096]{1,0:T(8,128)(2,1)S(1)} %constant_dynamic-update-slice_fusion.3.refs_1_, ...), custom_call_target="tpu_custom_call" | custom-call | flops 1610612736 | bytes 11705344 | tf_op jit(solution)/shard_map/pallas_call | solution.py:252
  55.4 10.3 %shard_map.130 = (f32[8,192,96]{2,1,0:T(8,128)S(1)}, f32[8,192,96]{2,1,0:T(8,128)S(1)}, bf16[8,96,192]{2,1,0:T(8,128)(2,1)S(1)}, bf16[8,192,96]{2,1,0:T(8,128)(2,1)S(1)}) custom-call(bf16[8,96,4096]{2,1,0:T(8,128)(2,1)S(1)} %get-tuple-element.121.x_ref, f32[8,1,96]{2,1,0:T(1,128)S(1)} %get-tuple-element.122.prob_ref, ...), custom_call_target="tpu_custom_call" | custom-call | flops 2415919104 | bytes 33229824 | tf_op jit(solution)/shard_map/pallas_call | solution.py:252
  65.7 3.6 %collective-permute-done.22.own1 = bf16[128,4096]{1,0:T(8,128)(2,1)S(1)} collective-permute-done((bf16[128,4096]{1,0:T(8,128)(2,1)S(1)}, bf16[128,4096]{1,0:T(8,128)(2,1)S(1)}, u32[]{:S(2)}, u32[]{:S(2)}) %collective-permute-start.22) | collective-permute-done | bytes 1048608 | tf_op jit(solution)/shard_map/ppermute | solution.py:33
  69.3 7.7 %shard_map.131 = (bf16[256,4096]{1,0:T(8,128)(2,1)S(1)}, bf16[256,4096]{1,0:T(8,128)(2,1)S(1)}) custom-call(bf16[2,256,384]{2,1,0:T(8,128)(2,1)S(1)} %get-tuple-element.118.put_ref, bf16[8,96,192]{2,1,0:T(8,128)(2,1)S(1)} %get-tuple-element.127.refs_0_, bf16[8,192,4096]{2,1,0:T(8,128)(2,1)} %down_ref.1), custom_call_target="tpu_custom_call" | custom-call | flops 2818572288 | bytes 17465344 | tf_op jit(solution)/shard_map/pallas_call | solution.py:252
  77.6 4.6 %shard_map.132 = (bf16[8,96,4096]{2,1,0:T(8,128)(2,1)S(1)}, bf16[8,96,4096]{2,1,0:T(8,128)(2,1)}) custom-call(bf16[128,4096]{1,0:T(8,128)(2,1)S(1)} %constant_dynamic-update-slice_fusion.21.own0, bf16[128,4096]{1,0:T(8,128)(2,1)S(1)} %collective-permute-done.22.own1, bf16[128,4096]{1,0:T(8,128)(2,1)S(1)} %collective-permute-done.23.other0, ...), custom_call_target="tpu_custom_call" | custom-call | flops 1610612736 | bytes 17170432 | tf_op jit(solution)/shard_map/pallas_call | solution.py:252
  84.8 8.5 %shard_map.133 = (bf16[8,96,192]{2,1,0:T(8,128)(2,1)S(1)}, bf16[8,96,192]{2,1,0:T(8,128)(2,1)S(1)}, bf16[8,192,96]{2,1,0:T(8,128)(2,1)S(1)}, bf16[8,192,96]{2,1,0:T(8,128)(2,1)S(1)}, bf16[2,256,128]{2,1,0:T(8,128)(2,1)S(1)}) custom-call(bf16[8,96,4096]{2,1,0:T(8,128)(2,1)S(1)} %get-tuple-element.137.x_ref, ...), custom_call_target="tpu_custom_call" | custom-call | flops 1207959552 | bytes 21859328 | tf_op jit(solution)/shard_map/pallas_call | solution.py:252
  93.2 4.8 %shard_map.134 = (bf16[256,2048]{1,0:T(8,128)(2,1)S(1)}, bf16[256,2048]{1,0:T(8,128)(2,1)S(1)}) custom-call(bf16[2,256,384]{2,1,0:T(8,128)(2,1)S(1)} %get-tuple-element.118.put_ref, bf16[8,96,192]{2,1,0:T(8,128)(2,1)S(1)} %get-tuple-element.147.refs_0_, bf16[8,96,192]{2,1,0:T(8,128)(2,1)S(1)} %get-tuple-element.148.refs_1_, ...), custom_call_target="tpu_custom_call" | custom-call | flops 2013265920 | bytes 28246016 | tf_op jit(solution)/shard_map/pallas_call | solution.py:252
  99.7 1.6 %collective-permute-start.27 = (bf16[64,4096]{1,0:T(8,128)(2,1)S(1)}, bf16[64,4096]{1,0:T(8,128)(2,1)S(1)}, u32[]{:S(2)}, u32[]{:S(2)}) collective-permute-start(bf16[64,4096]{1,0:T(8,128)(2,1)S(1)} %add_convert_fusion.3), channel_id=1, source_target_pairs={{0,8},{1,17},{2,10},{3,19},{4,12},{5,21},{6,14},{7,23},{8,0},{9,25... | collective-permute-start | bytes 1572872 | tf_op jit(solution)/shard_map/ppermute | solution.py:33
  101.3 5.2 %shard_map.135 = (bf16[256,2176]{1,0:T(8,128)(2,1)S(1)}, bf16[256,2176]{1,0:T(8,128)(2,1)S(1)}) custom-call(bf16[2,256,384]{2,1,0:T(8,128)(2,1)S(1)} %get-tuple-element.118.put_ref, bf16[8,96,192]{2,1,0:T(8,128)(2,1)S(1)} %get-tuple-element.147.refs_0_, bf16[8,96,192]{2,1,0:T(8,128)(2,1)S(1)} %get-tuple-element.148.refs_1_, ...), custom_call_target="tpu_custom_call" | custom-call | flops 2013265920 | bytes 28508160 | tf_op jit(solution)/shard_map/pallas_call | solution.py:252
  107.6 1.5 collective-permute-done.27
  110.9 7.4 %shard_map.136 = bf16[8,192,4096]{2,1,0:T(8,128)(2,1)} custom-call(bf16[8,96,4096]{2,1,0:T(8,128)(2,1)S(1)} %bitcast.1, bf16[8,192,96]{2,1,0:T(8,128)(2,1)S(1)} %get-tuple-element.160.left), custom_call_target="tpu_custom_call" | custom-call | flops 1207959552 | bytes 19169280 | tf_op jit(solution)/shard_map/pallas_call | solution.py:396
  120.3 1.8 %collective-permute-start.34 = (bf16[64,2048]{1,0:T(8,128)(2,1)S(1)}, bf16[64,2048]{1,0:T(8,128)(2,1)S(1)}, u32[]{:S(2)}, u32[]{:S(2)}) collective-permute-start(bf16[64,2048]{1,0:T(8,128)(2,1)S(1)} %add_convert_fusion.5), channel_id=1, source_target_pairs={{0,8},{1,17},{2,10},{3,19},{4,12},{5,21},{6,14},{7,23},{8,0},{9,25... | collective-permute-start | bytes 786440 | tf_op jit(solution)/shard_map/ppermute | solution.py:33
  122.1 7.3 %shard_map.137 = bf16[8,192,4096]{2,1,0:T(8,128)(2,1)} custom-call(bf16[8,96,4096]{2,1,0:T(8,128)(2,1)S(1)} %get-tuple-element.121.x_ref, bf16[8,192,96]{2,1,0:T(8,128)(2,1)S(1)} %get-tuple-element.169.left), custom_call_target="tpu_custom_call" | custom-call | flops 1207959552 | bytes 19169280 | tf_op jit(solution)/shard_map/pallas_call | solution.py:396
  131.7 1.6 %collective-permute-start.36 = (bf16[32,2048]{1,0:T(8,128)(2,1)S(1)}, bf16[32,2048]{1,0:T(8,128)(2,1)S(1)}, u32[]{:S(2)}, u32[]{:S(2)}) collective-permute-start(bf16[32,2048]{1,0:T(8,128)(2,1)S(1)} %add_convert_fusion.8), channel_id=1, source_target_pairs={{0,2},{1,3},{2,0},{3,1},{4,6},{5,7},{6,4},{7,5},{8,10},{9,11},{10,... | collective-permute-start | bytes 393224 | tf_op jit(solution)/shard_map/ppermute | solution.py:33
  133.3 4.0 %shard_map.138.refs_0_ = bf16[8,192,4096]{2,1,0:T(8,128)(2,1)} custom-call(bf16[8,96,4096]{2,1,0:T(8,128)(2,1)S(1)} %get-tuple-element.121.x_ref, bf16[8,192,96]{2,1,0:T(8,128)(2,1)S(1)} %get-tuple-element.180.left), custom_call_target="tpu_custom_call" | custom-call | flops 603979776 | bytes 9584640 | tf_op jit(solution)/shard_map/pallas_call | solution.py:396
  137.7 1.7 %collective-permute-start.38 = (bf16[32,2176]{1,0:T(8,128)(2,1)S(1)}, bf16[32,2176]{1,0:T(8,128)(2,1)S(1)}, u32[]{:S(2)}, u32[]{:S(2)}) collective-permute-start(bf16[32,2176]{1,0:T(8,128)(2,1)S(1)} %add_convert_fusion.7), channel_id=1, source_target_pairs={{0,2},{1,3},{2,0},{3,1},{4,6},{5,7},{6,4},{7,5},{8,10},{9,11},{10,... | collective-permute-start | bytes 417800 | tf_op jit(solution)/shard_map/ppermute | solution.py:33
  139.5 1.9 %collective-permute-done.32 = bf16[16,4096]{1,0:T(8,128)(2,1)S(1)} collective-permute-done((bf16[16,4096]{1,0:T(8,128)(2,1)S(1)}, bf16[16,4096]{1,0:T(8,128)(2,1)S(1)}, u32[]{:S(2)}, u32[]{:S(2)}) %collective-permute-start.32) | collective-permute-done | bytes 131104 | tf_op jit(solution)/shard_map/ppermute | solution.py:33
  141.4 1.7 %add_convert_fusion.9 = bf16[16,4096]{1,0:T(8,128)(2,1)} fusion(bf16[16,4096]{1,0:T(8,128)(2,1)S(1)} %collective-permute-done.32, bf16[64,4096]{1,0:T(8,128)(2,1)S(1)} %collective-permute-done.27, bf16[32,4096]{1,0:T(8,128)(2,1)S(1)} %collective-permute-done.31, bf16[128,4096]{1,0:T(8,128)(2,1)S(1)} %collective-permute-done.26, ...), kind=kLoop, calls=%fused_computation.14 | loop fusion | flops 786432 | bytes 917504 | tf_op jit(solution)/shard_map/convert_element_type | solution.py:40
  143.5 4.0 %shard_map.139 = bf16[8,192,4096]{2,1,0:T(8,128)(2,1)} custom-call(bf16[8,96,4096]{2,1,0:T(8,128)(2,1)S(1)} %get-tuple-element.121.x_ref, bf16[8,192,96]{2,1,0:T(8,128)(2,1)S(1)} %get-tuple-element.180.left, bf16[8,192,4096]{2,1,0:T(8,128)(2,1)} %shard_map.138.refs_0_), custom_call_target="tpu_custom_call", output_to_operand_aliasing={{}: (2, {})} | custom-call | flops 603979776 | bytes 9584640 | tf_op jit(solution)/shard_map/pallas_call | solution.py:396
  147.6 2.5 %collective-permute-start.39 = (bf16[16,2176]{1,0:T(8,128)(2,1)S(1)}, bf16[16,2176]{1,0:T(8,128)(2,1)S(1)}, u32[]{:S(2)}, u32[]{:S(2)}) collective-permute-start(bf16[16,2176]{1,0:T(8,128)(2,1)S(1)} %add_convert_fusion.12), channel_id=1, source_target_pairs={{0,4},{1,5},{2,6},{3,7},{4,0},{5,1},{6,2},{7,3},{8,12},{9,13},{10,... | collective-permute-start | bytes 208904 | tf_op jit(solution)/shard_map/ppermute | solution.py:33
  150.1 3.4 %collective-permute-done.39 = bf16[16,2176]{1,0:T(8,128)(2,1)S(1)} collective-permute-done((bf16[16,2176]{1,0:T(8,128)(2,1)S(1)}, bf16[16,2176]{1,0:T(8,128)(2,1)S(1)}, u32[]{:S(2)}, u32[]{:S(2)}) %collective-permute-start.39) | collective-permute-done | bytes 69664 | tf_op jit(solution)/shard_map/ppermute | solution.py:33
  (127 shorter events, 33.3 us)
Async XLA Ops:
  0.6 11.2 %collective-permute-start.2 = (bf16[16,4096]{1,0:T(8,128)(2,1)}, bf16[16,4096]{1,0:T(8,128)(2,1)S(1)}, u32[]{:S(2)}, u32[]{:S(2)}) collective-permute-start(bf16[16,4096]{1,0:T(8,128)(2,1)} %param.8), channel_id=1, source_target_pairs={{0,4},{1,5},{2,6},{3,7},{4,0},{5,1},{6,2},{7,3},{8,12},{9,13},{10,... | collective-permute-start | bytes 393224 | tf_op jit(solution)/shard_map/ppermute | solution.py:33
  4.7 7.1 %collective-permute-start.1 = (bf16[16,4096]{1,0:T(8,128)(2,1)}, bf16[16,4096]{1,0:T(8,128)(2,1)S(1)}, u32[]{:S(2)}, u32[]{:S(2)}) collective-permute-start(bf16[16,4096]{1,0:T(8,128)(2,1)} %param.8), channel_id=1, source_target_pairs={{0,2},{1,3},{2,0},{3,1},{4,6},{5,7},{6,4},{7,5},{8,10},{9,11},{10,... | collective-permute-start | bytes 393224 | tf_op jit(solution)/shard_map/ppermute | solution.py:33
  6.3 12.1 %collective-permute-start = (bf16[16,4096]{1,0:T(8,128)(2,1)}, bf16[16,4096]{1,0:T(8,128)(2,1)S(1)}, u32[]{:S(2)}, u32[]{:S(2)}) collective-permute-start(bf16[16,4096]{1,0:T(8,128)(2,1)} %param.8), channel_id=1, source_target_pairs={{0,8},{1,17},{2,10},{3,19},{4,12},{5,21},{6,14},{7,23},{8,0},{9,25... | collective-permute-start | bytes 393224 | tf_op jit(solution)/shard_map/ppermute | solution.py:33
  11.8 9.4 %collective-permute-start.8 = (bf16[16,128]{1,0:T(8,128)(2,1)S(1)}, bf16[16,128]{1,0:T(8,128)(2,1)S(1)}, u32[]{:S(2)}, u32[]{:S(2)}) collective-permute-start(bf16[16,128]{1,0:T(8,128)(2,1)S(1)} %pad_maximum_fusion.7), channel_id=1, source_target_pairs={{0,6},{1,7},{2,4},{3,5},{4,2},{5,3},{6,0},{7,1},{8,14},{9,15},{10,... | collective-permute-start | bytes 12296 | tf_op jit(solution)/shard_map/ppermute | solution.py:33
  14.8 9.4 %collective-permute-start.7 = (bf16[16,128]{1,0:T(8,128)(2,1)S(1)}, bf16[16,128]{1,0:T(8,128)(2,1)S(1)}, u32[]{:S(2)}, u32[]{:S(2)}) collective-permute-start(bf16[16,128]{1,0:T(8,128)(2,1)S(1)} %pad_maximum_fusion.7), channel_id=1, source_target_pairs={{0,2},{1,3},{2,0},{3,1},{4,6},{5,7},{6,4},{7,5},{8,10},{9,11},{10,... | collective-permute-start | bytes 12296 | tf_op jit(solution)/shard_map/ppermute | solution.py:33
  16.9 9.0 %collective-permute-start.4 = (bf16[32,4096]{1,0:T(8,128)(2,1)S(1)}, bf16[32,4096]{1,0:T(8,128)(2,1)S(1)}, u32[]{:S(2)}, u32[]{:S(2)}) collective-permute-start(bf16[32,4096]{1,0:T(8,128)(2,1)S(1)} %pad_maximum_fusion.2), channel_id=1, source_target_pairs={{0,8},{1,17},{2,10},{3,19},{4,12},{5,21},{6,14},{7,23},{8,0},{9,25... | collective-permute-start | bytes 786440 | tf_op jit(solution)/shard_map/ppermute | solution.py:33
  21.2 17.5 %collective-permute-start.20 = (bf16[16,4096]{1,0:T(8,128)(2,1)S(1)}, bf16[16,4096]{1,0:T(8,128)(2,1)S(1)}, u32[]{:S(2)}, u32[]{:S(2)}) collective-permute-start(bf16[16,4096]{1,0:T(8,128)(2,1)S(1)} %copy-done), channel_id=1, source_target_pairs={{0,6},{1,7},{2,4},{3,5},{4,2},{5,3},{6,0},{7,1},{8,14},{9,15},{10,... | collective-permute-start | bytes 393224 | tf_op jit(solution)/shard_map/ppermute | solution.py:33
  24.2 15.3 %collective-permute-start.19 = (bf16[16,4096]{1,0:T(8,128)(2,1)S(1)}, bf16[16,4096]{1,0:T(8,128)(2,1)S(1)}, u32[]{:S(2)}, u32[]{:S(2)}) collective-permute-start(bf16[16,4096]{1,0:T(8,128)(2,1)S(1)} %copy-done), channel_id=1, source_target_pairs={{0,2},{1,3},{2,0},{3,1},{4,6},{5,7},{6,4},{7,5},{8,10},{9,11},{10,... | collective-permute-start | bytes 393224 | tf_op jit(solution)/shard_map/ppermute | solution.py:33
  25.9 8.3 %collective-permute-start.11 = (bf16[64,128]{1,0:T(8,128)(2,1)S(1)}, bf16[64,128]{1,0:T(8,128)(2,1)S(1)}, u32[]{:S(2)}, u32[]{:S(2)}) collective-permute-start(bf16[64,128]{1,0:T(8,128)(2,1)S(1)} %pad_maximum_fusion.6), channel_id=1, source_target_pairs={{0,8},{1,17},{2,10},{3,19},{4,12},{5,21},{6,14},{7,23},{8,0},{9,25... | collective-permute-start | bytes 49160 | tf_op jit(solution)/shard_map/ppermute | solution.py:33
  27.3 7.0 %collective-permute-start.9 = (bf16[16,4096]{1,0:T(8,128)(2,1)S(1)}, bf16[16,4096]{1,0:T(8,128)(2,1)S(1)}, u32[]{:S(2)}, u32[]{:S(2)}) collective-permute-start(bf16[16,4096]{1,0:T(8,128)(2,1)S(1)} %collective-permute-done.3.after), channel_id=1, source_target_pairs={{0,8},{1,17},{2,10},{3,19},{4,12},{5,21},{6,14},{7,23},{8,0},{9,25... | collective-permute-start | bytes 393224 | tf_op jit(solution)/shard_map/ppermute | solution.py:33
  28.0 9.2 %collective-permute-start.10 = (bf16[64,4096]{1,0:T(8,128)(2,1)S(1)}, bf16[64,4096]{1,0:T(8,128)(2,1)S(1)}, u32[]{:S(2)}, u32[]{:S(2)}) collective-permute-start(bf16[64,4096]{1,0:T(8,128)(2,1)S(1)} %pad_maximum_fusion), channel_id=1, source_target_pairs={{0,16},{1,9},{2,18},{3,11},{4,20},{5,13},{6,22},{7,15},{8,24},{9,1... | collective-permute-start | bytes 1572872 | tf_op jit(solution)/shard_map/ppermute | solution.py:33
  34.2 8.2 %collective-permute-start.18 = (bf16[16,4096]{1,0:T(8,128)(2,1)S(1)}, bf16[16,4096]{1,0:T(8,128)(2,1)S(1)}, u32[]{:S(2)}, u32[]{:S(2)}) collective-permute-start(bf16[16,4096]{1,0:T(8,128)(2,1)S(1)} %copy-done), channel_id=1, source_target_pairs={{0,4},{1,5},{2,6},{3,7},{4,0},{5,1},{6,2},{7,3},{8,12},{9,13},{10,... | collective-permute-start | bytes 393224 | tf_op jit(solution)/shard_map/ppermute | solution.py:33
  34.3 14.2 %collective-permute-start.14 = (bf16[64,4096]{1,0:T(8,128)(2,1)S(1)}, bf16[64,4096]{1,0:T(8,128)(2,1)S(1)}, u32[]{:S(2)}, u32[]{:S(2)}) collective-permute-start(bf16[64,4096]{1,0:T(8,128)(2,1)S(1)} %constant_dynamic-update-slice_fusion.refs_0_), channel_id=1, source_target_pairs={{0,1},{1,0},{2,3},{3,2},{4,5},{5,4},{6,7},{7,6},{8,9},{9,8},{10,11... | collective-permute-start | bytes 1572872 | tf_op jit(solution)/shard_map/ppermute | solution.py:33
  37.3 10.5 %collective-permute-start.13 = (bf16[128,128]{1,0:T(8,128)(2,1)S(1)}, bf16[128,128]{1,0:T(8,128)(2,1)S(1)}, u32[]{:S(2)}, u32[]{:S(2)}) collective-permute-start(bf16[128,128]{1,0:T(8,128)(2,1)S(1)} %get-tuple-element.193), channel_id=1, source_target_pairs={{0,16},{1,9},{2,18},{3,11},{4,20},{5,13},{6,22},{7,15},{8,24},{9,1... | collective-permute-start | bytes 98312 | tf_op jit(solution)/shard_map/ppermute | solution.py:33
  38.8 9.0 %collective-permute-start.12 = (bf16[32,4096]{1,0:T(8,128)(2,1)S(1)}, bf16[32,4096]{1,0:T(8,128)(2,1)S(1)}, u32[]{:S(2)}, u32[]{:S(2)}) collective-permute-start(bf16[32,4096]{1,0:T(8,128)(2,1)S(1)} %pad_maximum_fusion.4), channel_id=1, source_target_pairs={{0,16},{1,9},{2,18},{3,11},{4,20},{5,13},{6,22},{7,15},{8,24},{9,1... | collective-permute-start | bytes 786440 | tf_op jit(solution)/shard_map/ppermute | solution.py:33
  42.4 11.6 %collective-permute-start.21 = (bf16[64,4096]{1,0:T(8,128)(2,1)S(1)}, bf16[64,4096]{1,0:T(8,128)(2,1)S(1)}, u32[]{:S(2)}, u32[]{:S(2)}) collective-permute-start(bf16[64,4096]{1,0:T(8,128)(2,1)S(1)} %pad_maximum_fusion.1), channel_id=1, source_target_pairs={{0,8},{1,17},{2,10},{3,19},{4,12},{5,21},{6,14},{7,23},{8,0},{9,25... | collective-permute-start | bytes 1572872 | tf_op jit(solution)/shard_map/ppermute | solution.py:33
  43.1 7.0 %collective-permute-start.15 = (bf16[128,4096]{1,0:T(8,128)(2,1)S(1)}, bf16[128,4096]{1,0:T(8,128)(2,1)S(1)}, u32[]{:S(2)}, u32[]{:S(2)}) collective-permute-start(bf16[128,4096]{1,0:T(8,128)(2,1)S(1)} %constant_dynamic-update-slice_fusion.3.refs_1_), channel_id=1, source_target_pairs={{0,1},{1,0},{2,3},{3,2},{4,5},{5,4},{6,7},{7,6},{8,9},{9,8},{10,11... | collective-permute-start | bytes 3145736 | tf_op jit(solution)/shard_map/ppermute | solution.py:33
  54.0 11.6 %collective-permute-start.23 = (bf16[128,4096]{1,0:T(8,128)(2,1)S(1)}, bf16[128,4096]{1,0:T(8,128)(2,1)S(1)}, u32[]{:S(2)}, u32[]{:S(2)}) collective-permute-start(bf16[128,4096]{1,0:T(8,128)(2,1)S(1)} %constant_dynamic-update-slice_fusion.21.own0), channel_id=1, source_target_pairs={{0,1},{1,0},{2,3},{3,2},{4,5},{5,4},{6,7},{7,6},{8,9},{9,8},{10,11... | collective-permute-start | bytes 3145736 | tf_op jit(solution)/shard_map/ppermute | solution.py:33
  54.5 14.8 %collective-permute-start.22 = (bf16[128,4096]{1,0:T(8,128)(2,1)S(1)}, bf16[128,4096]{1,0:T(8,128)(2,1)S(1)}, u32[]{:S(2)}, u32[]{:S(2)}) collective-permute-start(bf16[128,4096]{1,0:T(8,128)(2,1)S(1)} %constant_dynamic-update-slice_fusion.21.own0), channel_id=1, source_target_pairs={{0,16},{1,9},{2,18},{3,11},{4,20},{5,13},{6,22},{7,15},{8,24},{9,1... | collective-permute-start | bytes 3145736 | tf_op jit(solution)/shard_map/ppermute | solution.py:33
  69.3 7.7 %collective-permute-start.24 = (bf16[128,4096]{1,0:T(8,128)(2,1)S(1)}, bf16[128,4096]{1,0:T(8,128)(2,1)S(1)}, u32[]{:S(2)}, u32[]{:S(2)}) collective-permute-start(bf16[128,4096]{1,0:T(8,128)(2,1)S(1)} %collective-permute-done.22.own1), channel_id=1, source_target_pairs={{0,1},{1,0},{2,3},{3,2},{4,5},{5,4},{6,7},{7,6},{8,9},{9,8},{10,11... | collective-permute-start | bytes 3145736 | tf_op jit(solution)/shard_map/ppermute | solution.py:33
  83.6 14.9 %collective-permute-start.26 = (bf16[128,4096]{1,0:T(8,128)(2,1)S(1)}, bf16[128,4096]{1,0:T(8,128)(2,1)S(1)}, u32[]{:S(2)}, u32[]{:S(2)}) collective-permute-start(bf16[128,4096]{1,0:T(8,128)(2,1)S(1)} %add_convert_fusion), channel_id=1, source_target_pairs={{0,16},{1,9},{2,18},{3,11},{4,20},{5,13},{6,22},{7,15},{8,24},{9,1... | collective-permute-start | bytes 3145736 | tf_op jit(solution)/shard_map/ppermute | solution.py:33
  98.1 8.4 %collective-permute-start.29 = (bf16[256,2048]{1,0:T(8,128)(2,1)S(1)}, bf16[256,2048]{1,0:T(8,128)(2,1)S(1)}, u32[]{:S(2)}, u32[]{:S(2)}) collective-permute-start(bf16[256,2048]{1,0:T(8,128)(2,1)S(1)} %get-tuple-element.153), channel_id=1, source_target_pairs={{0,1},{1,0},{2,3},{3,2},{4,5},{5,4},{6,7},{7,6},{8,9},{9,8},{10,11... | collective-permute-start | bytes 3145736 | tf_op jit(solution)/shard_map/ppermute | solution.py:33
  99.7 9.4 %collective-permute-start.27 = (bf16[64,4096]{1,0:T(8,128)(2,1)S(1)}, bf16[64,4096]{1,0:T(8,128)(2,1)S(1)}, u32[]{:S(2)}, u32[]{:S(2)}) collective-permute-start(bf16[64,4096]{1,0:T(8,128)(2,1)S(1)} %add_convert_fusion.3), channel_id=1, source_target_pairs={{0,8},{1,17},{2,10},{3,19},{4,12},{5,21},{6,14},{7,23},{8,0},{9,25... | collective-permute-start | bytes 1572872 | tf_op jit(solution)/shard_map/ppermute | solution.py:33
  106.6 11.7 %collective-permute-start.30 = (bf16[128,2048]{1,0:T(8,128)(2,1)S(1)}, bf16[128,2048]{1,0:T(8,128)(2,1)S(1)}, u32[]{:S(2)}, u32[]{:S(2)}) collective-permute-start(bf16[128,2048]{1,0:T(8,128)(2,1)S(1)} %add_convert_fusion.2), channel_id=1, source_target_pairs={{0,16},{1,9},{2,18},{3,11},{4,20},{5,13},{6,22},{7,15},{8,24},{9,1... | collective-permute-start | bytes 1572872 | tf_op jit(solution)/shard_map/ppermute | solution.py:33
  107.6 10.7 %collective-permute-start.28 = (bf16[256,2176]{1,0:T(8,128)(2,1)S(1)}, bf16[256,2176]{1,0:T(8,128)(2,1)S(1)}, u32[]{:S(2)}, u32[]{:S(2)}) collective-permute-start(bf16[256,2176]{1,0:T(8,128)(2,1)S(1)} %get-tuple-element.150), channel_id=1, source_target_pairs={{0,1},{1,0},{2,3},{3,2},{4,5},{5,4},{6,7},{7,6},{8,9},{9,8},{10,11... | collective-permute-start | bytes 3342344 | tf_op jit(solution)/shard_map/ppermute | solution.py:33
  110.2 8.0 %collective-permute-start.31 = (bf16[32,4096]{1,0:T(8,128)(2,1)S(1)}, bf16[32,4096]{1,0:T(8,128)(2,1)S(1)}, u32[]{:S(2)}, u32[]{:S(2)}) collective-permute-start(bf16[32,4096]{1,0:T(8,128)(2,1)S(1)} %add_convert_fusion.6), channel_id=1, source_target_pairs={{0,2},{1,3},{2,0},{3,1},{4,6},{5,7},{6,4},{7,5},{8,10},{9,11},{10,... | collective-permute-start | bytes 786440 | tf_op jit(solution)/shard_map/ppermute | solution.py:33
  119.5 11.3 %collective-permute-start.33 = (bf16[128,2176]{1,0:T(8,128)(2,1)S(1)}, bf16[128,2176]{1,0:T(8,128)(2,1)S(1)}, u32[]{:S(2)}, u32[]{:S(2)}) collective-permute-start(bf16[128,2176]{1,0:T(8,128)(2,1)S(1)} %add_convert_fusion.1), channel_id=1, source_target_pairs={{0,16},{1,9},{2,18},{3,11},{4,20},{5,13},{6,22},{7,15},{8,24},{9,1... | collective-permute-start | bytes 1671176 | tf_op jit(solution)/shard_map/ppermute | solution.py:33
  120.3 9.2 %collective-permute-start.34 = (bf16[64,2048]{1,0:T(8,128)(2,1)S(1)}, bf16[64,2048]{1,0:T(8,128)(2,1)S(1)}, u32[]{:S(2)}, u32[]{:S(2)}) collective-permute-start(bf16[64,2048]{1,0:T(8,128)(2,1)S(1)} %add_convert_fusion.5), channel_id=1, source_target_pairs={{0,8},{1,17},{2,10},{3,19},{4,12},{5,21},{6,14},{7,23},{8,0},{9,25... | collective-permute-start | bytes 786440 | tf_op jit(solution)/shard_map/ppermute | solution.py:33
  131.0 6.6 %collective-permute-start.35 = (bf16[64,2176]{1,0:T(8,128)(2,1)S(1)}, bf16[64,2176]{1,0:T(8,128)(2,1)S(1)}, u32[]{:S(2)}, u32[]{:S(2)}) collective-permute-start(bf16[64,2176]{1,0:T(8,128)(2,1)S(1)} %add_convert_fusion.4), channel_id=1, source_target_pairs={{0,8},{1,17},{2,10},{3,19},{4,12},{5,21},{6,14},{7,23},{8,0},{9,25... | collective-permute-start | bytes 835592 | tf_op jit(solution)/shard_map/ppermute | solution.py:33
  133.3 8.1 %collective-permute-start.32 = (bf16[16,4096]{1,0:T(8,128)(2,1)S(1)}, bf16[16,4096]{1,0:T(8,128)(2,1)S(1)}, u32[]{:S(2)}, u32[]{:S(2)}) collective-permute-start(bf16[16,4096]{1,0:T(8,128)(2,1)S(1)} %add_convert_fusion.10), channel_id=1, source_target_pairs={{0,4},{1,5},{2,6},{3,7},{4,0},{5,1},{6,2},{7,3},{8,12},{9,13},{10,... | collective-permute-start | bytes 393224 | tf_op jit(solution)/shard_map/ppermute | solution.py:33
  137.7 9.8 %collective-permute-start.38 = (bf16[32,2176]{1,0:T(8,128)(2,1)S(1)}, bf16[32,2176]{1,0:T(8,128)(2,1)S(1)}, u32[]{:S(2)}, u32[]{:S(2)}) collective-permute-start(bf16[32,2176]{1,0:T(8,128)(2,1)S(1)} %add_convert_fusion.7), channel_id=1, source_target_pairs={{0,2},{1,3},{2,0},{3,1},{4,6},{5,7},{6,4},{7,5},{8,10},{9,11},{10,... | collective-permute-start | bytes 417800 | tf_op jit(solution)/shard_map/ppermute | solution.py:33
  143.1 7.0 %collective-permute-start.37 = (bf16[16,2048]{1,0:T(8,128)(2,1)S(1)}, bf16[16,2048]{1,0:T(8,128)(2,1)S(1)}, u32[]{:S(2)}, u32[]{:S(2)}) collective-permute-start(bf16[16,2048]{1,0:T(8,128)(2,1)S(1)} %add_convert_fusion.14), channel_id=1, source_target_pairs={{0,4},{1,5},{2,6},{3,7},{4,0},{5,1},{6,2},{7,3},{8,12},{9,13},{10,... | collective-permute-start | bytes 196616 | tf_op jit(solution)/shard_map/ppermute | solution.py:33
  (11 other events, 78.2 us)
